TPU v7x, 256 devices: a whole 4x4x8 slice. The times are simulated.
256 devices in a mesh: region: 32 (over x, y, core), batch: 8 (over z).
Axes of the slice: x: 4, y: 4, z: 8, core: 2. Of those that a mesh axis runs over, the one named last changes fastest.
Arguments:
- child_values: int32 [512, 32], P('batch'), may hold values from 0 to 255
- parent_values: int32 [512, 32], P('batch'), may hold values from 0 to 255
- child_logits: bfloat16 [32, 256, 4096], P(None, None, 'region'), may hold values from -254 to 12
- parent_logits: bfloat16 [32, 256, 4096], P(None, None, 'region'), may hold values from -254 to 12
- prior_logits: float32 [32, 4096], P(None, 'region'), may hold values from -8 to 8
- weights: bfloat16 [32, 32, 4, 128, 128], P(None, 'region'), may hold values from 0.049804688 to 1
- block_cols: int32 [32, 32, 4], P(None, 'region'), may hold values from 0 to 31, as said below
- parent_map: int32 [32], replicated, may hold values from 0 to 31
Outputs:
- counts: bfloat16 [32, 32, 4, 128, 128], P(None, 'region', None, 'batch')
- loglik: float32 [512], P('batch')
Inputs may be any that keep to these rules, and one draw needn't show every extreme that they name: `block_cols`: the 4 block columns of one block row are different.
All inputs are finite; a program needn't handle non-finite values.
Results may differ from a plain program's by a relative error of at most 0.015.
Values may be sent and summed in bfloat16 or wider, within the bound.
No kernel may reach another device: no remote copies, remote signals or barrier semaphores. Data moves between devices by JAX's collectives and lax.ppermute only.
A program may use at most 128 MiB of HBM per device.

v0:
```python
import jax
import jax.numpy as jnp
from jax import lax
from jax.sharding import PartitionSpec as P

K = 4096
BLK = 128
NZ = 4
C = 32
P_SIZE = 32


precise = lax.Precision.HIGHEST


def emission_input(values, logits):
    logit_table = logits.astype(jnp.float32)
    log_norm = jax.nn.logsumexp(logit_table, axis=1)
    one_hot = (values[:, :, None] == jnp.arange(logits.shape[1], dtype=jnp.int32)).astype(
        jnp.bfloat16
    )
    looked = jnp.einsum("srx,rxk->srk", one_hot, logits, preferred_element_type=jnp.float32)
    return looked - log_norm[None]


def pick_blocks(blocked, column_ids):
    return blocked[:, column_ids]


def body(
    child_values,
    parent_values,
    child_logits,
    parent_logits,
    prior_logits,
    weights,
    block_cols,
    parent_map,
):
    samples = child_values.shape[0]
    local_rows = weights.shape[1]
    local_width = local_rows * BLK
    inputs = emission_input(child_values, child_logits)
    peak_value = lax.pmax(jnp.max(inputs, axis=2), "region")
    scaled = jnp.exp(inputs - peak_value[:, :, None]).astype(jnp.bfloat16)
    scaled = lax.all_gather(scaled, "region", axis=2, tiled=True)
    blocked = scaled.reshape(samples, C, K // BLK, BLK)
    picked = jax.vmap(pick_blocks, in_axes=(1, 0), out_axes=1)(blocked, block_cols)
    row_sums = jnp.einsum("cizrj,scizj->scir", weights, picked, preferred_element_type=jnp.float32)
    row_sums = row_sums.reshape(samples, C, local_width)
    message = jnp.log(row_sums) + peak_value[:, :, None]
    owner_hot = (parent_map[:, None] == jnp.arange(P_SIZE, dtype=jnp.int32)[None, :]).astype(
        jnp.float32
    )
    incoming = jnp.einsum("sck,cp->spk", message, owner_hot, precision=precise)
    root_raw = emission_input(parent_values, parent_logits) + incoming + prior_logits[None]
    peaks = lax.pmax((jnp.max(root_raw, axis=2), jnp.max(prior_logits, axis=1)), "region")
    root_sum = jnp.sum(jnp.exp(root_raw - peaks[0][:, :, None]), axis=2)
    prior_sum = jnp.sum(jnp.exp(prior_logits - peaks[1][:, None]), axis=1)
    totals = lax.psum((root_sum, prior_sum), "region")
    root_norm = jnp.log(totals[0]) + peaks[0]
    prior_norm = jnp.log(totals[1]) + peaks[1]
    loglik = jnp.sum(root_norm - prior_norm[None, :], axis=1) / (C + P_SIZE)
    posterior = jnp.exp(root_raw - root_norm[:, :, None]).astype(jnp.bfloat16)
    child_post = posterior[:, parent_map]
    share_rows = (child_post.astype(jnp.float32) / row_sums).astype(jnp.bfloat16)
    share_rows = share_rows.reshape(samples, C, local_rows, BLK)
    partial_flow = jnp.einsum(
        "scir,scizj->cizrj", share_rows, picked, preferred_element_type=jnp.float32
    )
    partial_flow = partial_flow * weights.astype(jnp.float32)
    flows = lax.psum_scatter(
        partial_flow.astype(jnp.bfloat16), "batch", scatter_dimension=3, tiled=True
    ).astype(jnp.float32)
    factor = K * NZ * BLK / (samples * lax.axis_size("batch"))
    return ((flows * factor).astype(jnp.bfloat16), loglik)


def solution(mesh):
    return jax.shard_map(
        body,
        mesh=mesh,
        in_specs=(
            P("batch", None),
            P("batch", None),
            P(None, None, "region"),
            P(None, None, "region"),
            P(None, "region"),
            P(None, "region", None, None, None),
            P(None, "region", None),
            P(),
        ),
        out_specs=(P(None, "region", None, "batch", None), P("batch")),
        check_vma=False,
    )
```

profile of v0, /device:TPU:32, one launch (start us, length us, event | category | flops | bytes accessed | tf_op | source)
XLA Modules:
  0.0 586.1 jit_solution(15239011513195922804)
XLA Ops:
  7.2 0.0 copy-start
  7.2 0.0 copy-start.4
  7.2 0.0 all-gather.2.cloned.1.call-start
  7.2 2.1 reduce_max.55
  9.3 0.0 copy-start.6
  9.3 2.4 exponential_reduce_fusion.1
  11.7 0.0 copy-done
  11.8 0.0 copy-done.4
  11.8 0.9 fusion.28
  12.7 128.4 %pmax.21 = f32[64,32]{0,1:T(8,128)S(1)} all-reduce(f32[64,32]{0,1:T(8,128)S(1)} %get-tuple-element.14), channel_id=1, replica_groups=mesh['region'=32,'batch'=8] {'region'}, use_global_device_ids=true, to_apply=%region_3.0 | all-reduce | flops 2048 | bytes 16384 | tf_op jit(solution)/shard_map/pmax | solution.py:44
  141.1 1.1 exponential_convert_fusion.1
  142.2 0.0 all-gather.2.cloned.1.call-update
  142.2 0.0 reduce-scatter.2.cloned.1.call-start
  142.3 0.0 copy-done.6
  142.3 0.1 copy.23
  142.4 0.1 reshape.85
  142.5 1.9 reduce_max.58
  144.5 0.0 copy-start.3
  144.5 0.0 copy-start.7
  144.5 0.0 copy-start.1
  144.5 6.6 %copy.26 = bf16[32,1,4,128,128]{3,4,2,0,1:T(8,128)(2,1)} copy(bf16[32,1,4,128,128]{4,3,2,1,0:T(8,128)(2,1)} %param.13) | data formatting | bytes 8388608 | tf_op args[5]
  151.1 0.0 copy-done.3
  151.1 0.1 reduce_max.61
  151.2 0.0 copy-done.7
  151.3 0.0 copy-done.1
  151.3 0.8 exponential_reduce_fusion
  152.1 73.9 %all-gather.2.cloned.1.call-done = bf16[64,32,4096]{2,0,1:T(8,128)(2,1)} async-done(((bf16[64,32,128]{2,0,1:T(8,128)(2,1)}), bf16[64,32,4096]{2,0,1:T(8,128)(2,1)}) %all-gather.2.cloned.1.call-update) | async-done | bytes 16777232 | tf_op jit(solution)/shard_map/all_gather | solution.py:46
  226.0 15.3 %bitcast_bitcast_fusion = bf16[32,64,32,128]{3,1,2,0:T(8,128)(2,1)} fusion(bf16[64,32,4096]{2,0,1:T(8,128)(2,1)} %all-gather.2.cloned.1.call-done), kind=kLoop, calls=%fused_computation.2 | loop fusion | bytes 33554432 | tf_op jit(solution)/shard_map/vmap()/transpose | solution.py:27
  241.3 8.1 %gather_fusion.1 = bf16[128,64,128]{2,1,0:T(8,128)(2,1)} fusion(bf16[32,64,32,128]{3,1,2,0:T(8,128)(2,1)} %bitcast_bitcast_fusion, s32[128]{0:T(128)S(1)} %reshape.85), kind=kCustom, calls=%fused_computation.1 | custom fusion | bytes 4195328 | tf_op jit(solution)/shard_map/vmap()/gather | solution.py:27
  249.3 5.4 bitcast_add_fusion
  254.7 1.3 fusion.15
  256.0 0.0 copy-done.5
  256.0 1.7 fusion.29
  257.7 0.0 copy-start.2
  257.7 127.1 %all-reduce.1 = (f32[64,32]{0,1:T(8,128)S(1)}, f32[32]{0:T(128)S(1)}) all-reduce(f32[64,32]{0,1:T(8,128)S(1)} %get-tuple-element.18, f32[32]{0:T(128)S(1)} %reduce_max.61), channel_id=1, replica_groups=mesh['region'=32,'batch'=8] {'region'}, use_global_device_ids=true, to_apply=%region_7.0 | all-reduce | flops 2080 | bytes 16640 | tf_op jit(solution)/shard_map/pmax | solution.py:57
  384.8 0.2 exponential_reduce_fusion.3
  384.9 0.7 exponential_reduce_fusion.2
  385.6 124.0 %all-reduce = (f32[64,32]{0,1:T(8,128)S(1)}, f32[32]{0:T(128)S(1)}) all-reduce(f32[64,32]{0,1:T(8,128)S(1)} %exponential_reduce_fusion.2, f32[32]{0:T(128)S(1)} %exponential_reduce_fusion.3), channel_id=1, replica_groups=mesh['region'=32,'batch'=8] {'region'}, use_global_device_ids=true, to_apply=%region_9.0 | all-reduce | flops 2080 | bytes 16640 | tf_op jit(solution)/shard_map/psum | solution.py:60
  509.6 0.1 subtract_reduce_fusion
  509.7 1.1 exponential_convert_fusion
  510.8 1.7 gather_fusion
  512.5 6.3 %fusion = bf16[32,1,4,128,128]{3,4,2,0,1:T(8,128)(2,1)} fusion(bf16[32,1,4,128,128]{3,4,2,0,1:T(8,128)(2,1)} %copy.26, bf16[64,32,4,128]{3,0,2,1:T(8,128)(2,1)S(1)} %bitcast.70, f32[64,32,1,128]{3,0,1,2:T(8,128)} %get-tuple-element.17, bf16[32,64,128]{2,1,0:T(8,128)(2,1)S(1)} %gather_fusion), kind=kOutput, calls=%fused_computation.4 | convolution fusion | flops 275513344 | bytes 12058624 | tf_op jit(solution)/shard_map/scir,scizj->cizrj/dot_general | solution.py:68
  518.9 8.0 %copy.27 = bf16[32,1,4,128,128]{4,0,2,1,3:T(8,128)(2,1)} copy(bf16[32,1,4,128,128]{3,4,2,0,1:T(8,128)(2,1)} %fusion) | data formatting | bytes 8388608 | tf_op jit(solution)/shard_map/convert_element_type | solution.py:73
  526.9 0.0 reduce-scatter.2.cloned.1.call-update
  526.9 0.5 broadcast_multiply_fusion
  527.4 49.6 %reduce-scatter.2.cloned.1.call-done = bf16[32,1,4,16,128]{4,0,2,1,3:T(8,128)(2,1)} async-done(((bf16[32,1,4,128,128]{4,0,2,1,3:T(8,128)(2,1)}), bf16[32,1,4,16,128]{4,0,2,1,3:T(8,128)(2,1)}) %reduce-scatter.2.cloned.1.call-update) | async-done | bytes 524304 | tf_op jit(solution)/shard_map/reduce_scatter | solution.py:72
  577.0 1.2 multiply_convert_fusion
  578.2 1.1 copy.28
  (13 shorter events, 0.1 us)
Async XLA Ops:
  7.2 4.6 copy-start
  7.2 4.6 copy-start.4
  7.2 218.8 %all-gather.2.cloned.1.call-start = ((), (), s32[]{:S(2)}) async-start(), calls=%async_computation.1 | async-start | bytes 17301504 | tf_op jit(solution)/shard_map/all_gather | solution.py:46
  9.3 133.0 %copy-start.6 = (s32[32,1,4]{0,2,1:T(4,128)S(1)}, s32[32,1,4]{0,2,1:T(4,128)}, u32[]{:S(2)}) copy-start(s32[32,1,4]{0,2,1:T(4,128)} %param.14) | copy-start | bytes 1540
  142.2 434.8 %reduce-scatter.2.cloned.1.call-start = ((), (), s32[]{:S(2)}) async-start(), calls=%async_computation.2 | async-start | bytes 4718592 | tf_op jit(solution)/shard_map/reduce_scatter | solution.py:72
  144.5 6.7 %copy-start.3 = (f32[32,128]{1,0:T(8,128)S(1)}, f32[32,128]{1,0:T(8,128)}, u32[]{:S(2)}) copy-start(f32[32,128]{1,0:T(8,128)} %param.12) | copy-start | bytes 49156
  144.5 6.8 %copy-start.7 = (s32[32]{0:T(128)S(1)}, s32[32]{0:T(128)}, u32[]{:S(2)}) copy-start(s32[32]{0:T(128)} %param.15) | copy-start | bytes 388
  144.5 6.8 %copy-start.1 = (bf16[32,256,128]{2,1,0:T(8,128)(2,1)S(1)}, bf16[32,256,128]{2,1,0:T(8,128)(2,1)}, u32[]{:S(2)}) copy-start(bf16[32,256,128]{2,1,0:T(8,128)(2,1)} %param.11) | copy-start | bytes 6291460
  249.3 6.6 %copy-start.5 = (s32[64,32]{0,1:T(8,128)S(1)}, s32[64,32]{0,1:T(8,128)}, u32[]{:S(2)}) copy-start(s32[64,32]{0,1:T(8,128)} %param.9) | copy-start | bytes 24580
  257.7 254.8 %copy-start.2 = (bf16[128,64,128]{2,1,0:T(8,128)(2,1)S(1)}, bf16[128,64,128]{2,1,0:T(8,128)(2,1)}, u32[]{:S(2)}) copy-start(bf16[128,64,128]{2,1,0:T(8,128)(2,1)} %gather_fusion.1) | copy-start | bytes 6291460
Sparse Core Ops, SparseCore 0:
  142.3 83.6 all-gather.1
  527.0 49.9 reduce-scatter.1
where the time goes:
time: 590 us; the launch traced here: 586 us
  blocking collectives  379 us (64%)
  waiting for transfers between devices  124 us (21%)
  local copies, waits for them, and re-layouts  41 us (7%)
  matrix products  15.5 us (3%)
  between operations  14.3 us (2%)
  other arithmetic  12.3 us (2%)
    pmax x1, blocking collectives, body(): peak_value = lax.pmax(jnp.max(inputs, axis=2), 'region')  128 us
    pmax x1, blocking collectives, body(): lax.pmax((jnp.max(root_raw, axis=2), jnp.max(prior_logits, axis=1)), 'reg...  127 us
    psum x1, blocking collectives, body(): totals = lax.psum((root_sum, prior_sum), 'region')  124 us
    all_gather x1, waiting for transfers between devices, body(): scaled = lax.all_gather(scaled, 'region', axis=2, tiled=True)  73.9 us
    reduce_scatter x1, waiting for transfers between devices, body(): lax.psum_scatter(partial_flow.astype(jnp.bfloat16), 'batch', scatter_dime...  49.6 us
    transpose x1, local copies, waits for them, and re-layouts, pick_blocks(): return blocked[:, column_ids]  15.3 us
  transfers between devices with their start and end apart: 2, of which 2 were waited for; matrix products, arithmetic and copies ran while one was open for 2% of the time, Pallas kernels for 0%

commit v1 on v0

v1 whole, which is shorter than its diff:
```python
import jax
import jax.numpy as jnp
from jax import lax
from jax.experimental import pallas as pl
from jax.experimental.pallas import tpu as pltpu
from jax.sharding import PartitionSpec as P

K = 4096
BLK = 128
NZ = 4
C = 32
P_SIZE = 32
S_LOC = 64
LN2 = 0.6931471805599453
LOG2E = 1.4426950408889634
GROUP = 8
VMEM = pl.BlockSpec(memory_space=pltpu.VMEM)
SMEM = pl.BlockSpec(memory_space=pltpu.SMEM)
ANY = pl.BlockSpec(memory_space=pl.ANY)


def lane_of(shape):
    return lax.broadcasted_iota(jnp.int32, shape, len(shape) - 1)


def look_up(values, table_ref, index):
    table = table_ref[index]
    wide = table.astype(jnp.float32)
    top = jnp.max(wide, axis=0, keepdims=True)
    log_norm = jnp.log(jnp.sum(jnp.exp(wide - top), axis=0, keepdims=True)) + top
    hot = (values[:, index : index + 1] == lane_of((S_LOC, table.shape[0]))).astype(jnp.float32)
    looked = jnp.dot(hot.astype(jnp.bfloat16), table, preferred_element_type=jnp.float32)
    return looked - log_norm


def child_kernel(values_ref, table_ref, out_ref):
    values = values_ref[...]
    powers = jnp.zeros((S_LOC, BLK), jnp.float32)
    lanes = lane_of((S_LOC, BLK))
    for c in range(C):
        inputs = look_up(values, table_ref, c)
        power = jnp.ceil(jnp.max(inputs, axis=1, keepdims=True) * LOG2E)
        power = power.astype(jnp.bfloat16).astype(jnp.float32)
        out_ref[c] = jnp.exp(inputs - power * LN2).astype(jnp.bfloat16)
        powers = jnp.where(lanes == c, power, powers)
    out_ref[C] = powers.astype(jnp.bfloat16)


def parent_kernel(values_ref, table_ref, prior_ref, out_ref):
    values = values_ref[...]
    for p in range(P_SIZE):
        out_ref[p] = look_up(values, table_ref, p) + prior_ref[p : p + 1, :]


def sums_kernel(
    cols_ref, map_ref, gathered_ref, weights_ref, parent_ref, prior_ref,
    stats_ref, root_ref, sums_ref, picked_ref,
    slots, powers, slot_sem, power_sem,
):
    for g in range(C // GROUP):
        def fetch(k, carry, g=g):
            c = g * GROUP + k // NZ
            z = k % NZ
            source = cols_ref[c, z] * (C + 1) + c
            pltpu.make_async_copy(
                gathered_ref.at[source], slots.at[c, z], slot_sem.at[g]
            ).start()
            return carry

        if g == 0:
            def fetch_power(r, carry):
                pltpu.make_async_copy(
                    gathered_ref.at[r * (C + 1) + C], powers.at[r], power_sem
                ).start()
                return carry

            lax.fori_loop(0, powers.shape[0], fetch_power, 0)
        lax.fori_loop(0, GROUP * NZ, fetch, 0)
    root_ref[...] = parent_ref[...]
    pltpu.make_async_copy(powers, powers, power_sem).wait()
    for g in range(C // GROUP):
        part = slots.at[pl.ds(g * GROUP, GROUP)]
        pltpu.make_async_copy(part, part, slot_sem.at[g]).wait()
        for c in range(g * GROUP, (g + 1) * GROUP):
            power = [powers[cols_ref[c, z]].astype(jnp.float32)[:, c : c + 1] for z in range(NZ)]
            top = jnp.maximum(jnp.maximum(power[0], power[1]), jnp.maximum(power[2], power[3]))
            row_sums = None
            for z in range(NZ):
                factor = jnp.broadcast_to(jnp.exp2(power[z] - top), (S_LOC, BLK))
                block = (slots[c, z].astype(jnp.float32) * factor).astype(jnp.bfloat16)
                picked_ref[c, :, z * BLK : (z + 1) * BLK] = block
                term = lax.dot_general(
                    block, weights_ref[c, z], (((1,), (1,)), ((), ())),
                    preferred_element_type=jnp.float32,
                )
                row_sums = term if row_sums is None else row_sums + term
            sums_ref[c] = row_sums
            owner = map_ref[c]
            root_ref[owner] = root_ref[owner] + (jnp.log(row_sums) + top * LN2)
    lanes = lane_of((S_LOC, BLK))
    prior = prior_ref[...]
    prior_peak = jnp.max(prior, axis=1, keepdims=True)
    prior_total = jnp.sum(jnp.exp(prior - prior_peak), axis=1, keepdims=True)
    eye = lax.broadcasted_iota(jnp.int32, (P_SIZE, BLK), 0)
    wide = lane_of((P_SIZE, BLK))
    stats = jnp.sum(
        jnp.where(wide == eye + 2 * P_SIZE, prior_peak, 0.0)
        + jnp.where(wide == eye + 3 * P_SIZE, prior_total, 0.0),
        axis=0, keepdims=True,
    )
    stats = jnp.broadcast_to(stats, (S_LOC, BLK))
    for p in range(P_SIZE):
        root = root_ref[p]
        peak = jnp.max(root, axis=1, keepdims=True)
        total = jnp.sum(jnp.exp(root - peak), axis=1, keepdims=True)
        stats = jnp.where(lanes == p, peak, stats)
        stats = jnp.where(lanes == P_SIZE + p, total, stats)
    stats_ref[...] = stats


def merge(stats):
    is_peak = lane_of((S_LOC, BLK)) % (2 * P_SIZE) < P_SIZE
    peaks = [jnp.where(is_peak, s, pltpu.roll(s, P_SIZE, 1)) for s in stats]
    best = peaks[0]
    for p in peaks[1:]:
        best = jnp.maximum(best, p)
    total = None
    for s, p in zip(stats, peaks):
        term = s * jnp.exp(p - best)
        total = term if total is None else total + term
    return jnp.where(is_peak, best, total)


def merge_kernel(*refs):
    refs[-1][...] = merge([r[...] for r in refs[:-1]])


def counts_kernel(scale, n_stats, map_ref, *refs):
    stats_refs = refs[:n_stats]
    root_ref, sums_ref, picked_ref, weights_ref, out_ref, loglik_ref, posterior = refs[n_stats:]
    stats = merge([r[...] for r in stats_refs])
    lanes = lane_of((S_LOC, BLK))
    norm = stats + pltpu.roll(jnp.log(stats), BLK - P_SIZE, 1)
    signed = jnp.where(lanes < P_SIZE, norm, 0.0) - jnp.where(
        (lanes >= 2 * P_SIZE) & (lanes < 3 * P_SIZE), norm, 0.0
    )
    loglik = jnp.sum(signed, axis=1, keepdims=True) / (C + P_SIZE)
    loglik_ref[...] = jnp.broadcast_to(loglik, (S_LOC, BLK))
    for p in range(P_SIZE):
        posterior[p] = jnp.exp(root_ref[p] - norm[:, p : p + 1]).astype(jnp.bfloat16)
    parts, _, _, rows, _ = out_ref.shape
    for c in range(C):
        share = (posterior[map_ref[c]].astype(jnp.float32) / sums_ref[c]).astype(jnp.bfloat16)
        flow = lax.dot_general(
            share, picked_ref[c], (((0,), (0,)), ((), ())), preferred_element_type=jnp.float32
        )
        for z in range(NZ):
            block = flow[:, z * BLK : (z + 1) * BLK] * (weights_ref[c, z].astype(jnp.float32) * scale)
            out_ref[:, c, z] = block.astype(jnp.bfloat16).reshape(parts, rows, BLK)


def params(mib):
    return pltpu.CompilerParams(vmem_limit_bytes=mib << 20)


def cost(flops, moved, transcendentals):
    return pl.CostEstimate(flops=flops, bytes_accessed=moved, transcendentals=transcendentals)


def along(axis, step):
    pairs = []
    for i in range(32):
        x, y, core = i // 8, i // 2 % 4, i % 2
        if axis == "x":
            x = (x + step) % 4
        elif axis == "y":
            y = (y + step) % 4
        else:
            core = (core + step) % 2
        pairs.append((i, x * 8 + y * 2 + core))
    return pairs


def body(
    child_values,
    parent_values,
    child_logits,
    parent_logits,
    prior_logits,
    weights,
    block_cols,
    parent_map,
):
    f32, bf16 = jnp.float32, jnp.bfloat16
    shape = jax.ShapeDtypeStruct
    devices = lax.axis_size("region")
    parts = lax.axis_size("batch")
    weights = weights[:, 0]
    scaled = pl.pallas_call(
        child_kernel,
        out_shape=shape((C + 1, S_LOC, BLK), bf16),
        in_specs=[VMEM, VMEM],
        out_specs=VMEM,
        compiler_params=params(16),
        cost_estimate=cost(1 << 28, 3 << 20, 1 << 21),
        name="child_scores",
    )(child_values, child_logits)
    gathered = lax.all_gather(scaled.reshape(-1, BLK), "region")
    parent_in = pl.pallas_call(
        parent_kernel,
        out_shape=shape((P_SIZE, S_LOC, BLK), f32),
        in_specs=[VMEM, VMEM, VMEM],
        out_specs=VMEM,
        compiler_params=params(16),
        cost_estimate=cost(1 << 28, 3 << 20, 1 << 21),
        name="parent_scores",
    )(parent_values, parent_logits, prior_logits)
    stats, root, sums, picked = pl.pallas_call(
        sums_kernel,
        out_shape=(
            shape((S_LOC, BLK), f32),
            shape((P_SIZE, S_LOC, BLK), f32),
            shape((C, S_LOC, BLK), f32),
            shape((C, S_LOC, NZ * BLK), bf16),
        ),
        in_specs=[SMEM, SMEM, ANY, VMEM, VMEM, VMEM],
        out_specs=(VMEM,) * 4,
        scratch_shapes=[
            pltpu.VMEM((C, NZ, S_LOC, BLK), bf16),
            pltpu.VMEM((devices, S_LOC, BLK), bf16),
            pltpu.SemaphoreType.DMA((C // GROUP,)),
            pltpu.SemaphoreType.DMA,
        ],
        compiler_params=params(24),
        cost_estimate=cost(1 << 29, 12 << 20, 1 << 20),
        name="row_sums",
    )(
        block_cols[:, 0],
        parent_map,
        gathered.reshape(-1, S_LOC, BLK),
        weights,
        parent_in,
        prior_logits,
    )

    def send(axis, step):
        return lax.ppermute(stats, "region", along(axis, step))

    for axis, steps in (("core", (1,)), ("x", (1, 3, 2))):
        others = [send(axis, step) for step in steps]
        stats = pl.pallas_call(
            merge_kernel,
            out_shape=shape((S_LOC, BLK), f32),
            in_specs=[VMEM] * (1 + len(others)),
            out_specs=VMEM,
            compiler_params=params(4),
            name="merge_" + axis,
        )(stats, *others)
    others = [send("y", step) for step in (1, 3, 2)]
    scale = K * NZ * BLK / (S_LOC * parts)
    flows, loglik = pl.pallas_call(
        lambda *refs: counts_kernel(scale, 1 + len(others), *refs),
        out_shape=(shape((parts, C, NZ, BLK // parts, BLK), bf16), shape((S_LOC, BLK), f32)),
        in_specs=[SMEM] + [VMEM] * (5 + len(others)),
        out_specs=(VMEM, VMEM),
        scratch_shapes=[pltpu.VMEM((P_SIZE, S_LOC, BLK), bf16)],
        compiler_params=params(24),
        cost_estimate=cost(1 << 29, 13 << 20, 1 << 19),
        name="counts",
    )(parent_map, stats, *others, root, sums, picked, weights)
    flows = lax.psum_scatter(flows.reshape(parts, -1, BLK), "batch")
    return (flows.reshape(C, 1, NZ, BLK // parts, BLK), loglik[:, 0])


def solution(mesh):
    return jax.shard_map(
        body,
        mesh=mesh,
        in_specs=(
            P("batch", None),
            P("batch", None),
            P(None, None, "region"),
            P(None, None, "region"),
            P(None, "region"),
            P(None, "region", None, None, None),
            P(None, "region", None),
            P(),
        ),
        out_specs=(P(None, "region", None, "batch", None), P("batch")),
        check_vma=False,
    )
```

time: 590 us -> 200 us (0.34)
  blocking collectives: 379 us -> 0 us
  local copies, waits for them, and re-layouts: 41 us -> 13.3 us
  Pallas kernels: 0 us -> 21 us
  matrix products: 15.5 us -> 0 us
  waiting for transfers between devices: 124 us -> 139 us
  other arithmetic: 12.3 us -> 0 us
  starting transfers between devices: 0.08 us -> 8.9 us
    pmax x2 -> x0, blocking collectives: 255 us -> none  [the longest x1 128 us: body(): peak_value = lax.pmax(jnp.max(inputs, axis=2), 'region')]
    psum x1 -> x0, blocking collectives: 124 us -> none  [body(): totals = lax.psum((root_sum, prior_sum), 'region')]
    pallas_call x0 -> x6, Pallas kernels: none -> 21 us  [the longest x1 11 us: body(): pl.pallas_call(sums_kernel, out_shape=(shape((S_LOC, BLK), f32), shape((P...]
    dot_general x5 -> x0, matrix products: 15.5 us -> none  [the longest x1 6.34 us: body(): jnp.einsum('scir,scizj->cizrj', share_rows, picked, preferred_element_typ...]
    transpose x1 -> x0, local copies, waits for them, and re-layouts: 15.3 us -> none  [pick_blocks(): return blocked[:, column_ids]]
    gather x4 -> x0, local copies, waits for them, and re-layouts: 9.94 us -> none  [the longest x3 8.25 us: pick_blocks(): return blocked[:, column_ids]]
    ppermute x0 -> x7, waiting for transfers between devices: none -> 9.75 us  [send(): return lax.ppermute(stats, 'region', along(axis, step))]
    ppermute x0 -> x7, starting transfers between devices: none -> 8.82 us  [send(): return lax.ppermute(stats, 'region', along(axis, step))]
  transfers between devices with their start and end apart: 2 -> 9, of which waited for: 2 -> 8; matrix products, arithmetic and copies ran while one was open for 2% -> 0% of each run, Pallas kernels for 0% -> 1%
where the time goes in v1:
time: 200 us; the launch traced here: 196 us
  waiting for transfers between devices  139 us (70%)
  Pallas kernels  21 us (10%)
  between operations  14.1 us (7%)
  local copies, waits for them, and re-layouts  13.3 us (7%)
  starting transfers between devices  8.9 us (4%)
    all_gather x1, waiting for transfers between devices, body(): gathered = lax.all_gather(scaled.reshape(-1, BLK), 'region')  79.8 us
    reduce_scatter x1, waiting for transfers between devices, body(): flows = lax.psum_scatter(flows.reshape(parts, -1, BLK), 'batch')  49.5 us
    unnamed x20, local copies, waits for them, and re-layouts  12.5 us
    pallas_call x1, Pallas kernels, body(): pl.pallas_call(sums_kernel, out_shape=(shape((S_LOC, BLK), f32), shape((P...  11 us
    ppermute x7, waiting for transfers between devices, send(): return lax.ppermute(stats, 'region', along(axis, step))  9.75 us
    ppermute x7, starting transfers between devices, send(): return lax.ppermute(stats, 'region', along(axis, step))  8.82 us
    pallas_call x1, Pallas kernels, body(): pl.pallas_call(child_kernel, out_shape=shape((C + 1, S_LOC, BLK), bf16),...  5.99 us
  transfers between devices with their start and end apart: 9, of which 8 were waited for; matrix products, arithmetic and copies ran while one was open for 0% of the time, Pallas kernels for 1%

profile of v1, /device:TPU:32, one launch (start us, length us, event | category | flops | bytes accessed | tf_op | source)
XLA Modules:
  0.0 196.4 jit_solution(4259914342180252503)
XLA Ops:
  7.2 0.0 copy-start.8
  7.2 0.0 copy-start.7
  7.2 0.0 copy-start.3
  7.2 0.0 all-gather.2.cloned.1.call-start
  7.2 0.8 copy.16.values_ref
  8.0 0.0 copy-start.5
  8.0 1.6 copy-done.5
  9.6 0.0 copy-start.6
  9.6 0.0 copy-start.4
  9.6 6.0 %child_scores.1 = bf16[33,64,128]{2,1,0:T(8,128)(2,1)} custom-call(s32[64,32]{1,0:T(8,128)S(1)} %copy.16.values_ref, bf16[32,256,128]{2,1,0:T(8,128)(2,1)S(1)} %copy-done.5), custom_call_target="tpu_custom_call" | custom-call | flops 268435456 | bytes 3145728 | tf_op jit(solution)/shard_map/child_scores/pallas_call | solution.py:199
  15.6 0.0 all-gather.2.cloned.1.call-update
  15.7 0.0 reduce-scatter.2.cloned.1.call-start
  15.7 0.0 copy-done.8
  15.7 0.1 copy.18.cols_ref
  15.8 0.0 copy-done.7
  15.8 0.1 copy.17.values_ref
  15.9 0.0 copy-done.3
  15.9 0.0 copy-done.6
  15.9 1.4 parent_scores.1.parent_ref
  17.3 79.8 %all-gather.2.cloned.1.call-done = bf16[32,2112,128]{2,1,0:T(8,128)(2,1)} async-done(((bf16[1,2112,128]{2,1,0:T(8,128)(2,1)}), bf16[32,2112,128]{2,1,0:T(8,128)(2,1)}) %all-gather.2.cloned.1.call-update) | async-done | bytes 17301520 | tf_op jit(solution)/shard_map/all_gather | solution.py:208
  97.1 0.0 copy-done.4
  97.1 0.0 copy-start
  97.1 5.9 %copy-done = bf16[32,2112,128]{2,1,0:T(8,128)(2,1)S(1)} copy-done((bf16[32,2112,128]{2,1,0:T(8,128)(2,1)S(1)}, bf16[32,2112,128]{2,1,0:T(8,128)(2,1)}, u32[]{:S(2)}) %copy-start) | copy-done | bytes 17301528
  103.1 0.0 copy-start.1
  103.1 2.2 %copy-done.1 = bf16[32,1,4,128,128]{4,3,2,1,0:T(8,128)(2,1)S(1)} copy-done((bf16[32,1,4,128,128]{4,3,2,1,0:T(8,128)(2,1)S(1)}, bf16[32,1,4,128,128]{4,3,2,1,0:T(8,128)(2,1)}, u32[]{:S(2)}) %copy-start.1) | copy-done | bytes 4194328
  105.2 11.0 %row_sums.1 = (f32[64,128]{1,0:T(8,128)S(1)}, f32[32,64,128]{2,1,0:T(8,128)S(1)}, f32[32,64,128]{2,1,0:T(8,128)S(1)}, bf16[32,64,512]{2,1,0:T(8,128)(2,1)S(1)}) custom-call(s32[32,4]{1,0:T(8,128)S(1)} %copy.18.cols_ref, s32[32]{0:T(128)S(1)} %copy-done.4, bf16[1056,64,128]{2,1,0:T(8,128)(2,1)S(1)} %bitcast.6, bf16[32,4,128,128]{3,2,1,0:T(8,128)(2,1)S(1)} %bitcast.7, ...), custom_call_target="tpu_custom_call" | custom-call | flops 536870912 | bytes 12582912 | tf_op jit(solution)/shard_map/row_sums/pallas_call | solution.py:218
  116.2 0.3 collective-permute-start
  116.6 0.9 collective-permute-done.refs_1_
  117.5 0.1 merge_core.1.refs_0_
  117.6 3.1 %collective-permute-start.3 = (f32[64,128]{1,0:T(8,128)S(1)}, f32[64,128]{1,0:T(8,128)S(1)}, u32[]{:S(2)}, u32[]{:S(2)}) collective-permute-start(f32[64,128]{1,0:T(8,128)S(1)} %merge_core.1.refs_0_), channel_id=1, source_target_pairs={{0,128},{8,136},{16,144},{24,152},{32,160},{40,168},{48,176},{56,1... | collective-permute-start | bytes 98312 | tf_op jit(solution)/shard_map/ppermute | solution.py:247
  120.7 1.2 collective-permute-start.2
  121.8 0.9 collective-permute-start.1
  122.7 0.4 collective-permute-done.3.refs_3_
  123.1 1.5 collective-permute-done.2.refs_2_
  124.6 2.4 %collective-permute-done.1.refs_1_ = f32[64,128]{1,0:T(8,128)S(1)} collective-permute-done((f32[64,128]{1,0:T(8,128)S(1)}, f32[64,128]{1,0:T(8,128)S(1)}, u32[]{:S(2)}, u32[]{:S(2)}) %collective-permute-start.1) | collective-permute-done | bytes 32800 | tf_op jit(solution)/shard_map/ppermute | solution.py:247
  127.0 0.1 merge_x.1.refs_1_
  127.1 1.4 collective-permute-start.6
  128.5 1.4 collective-permute-start.5
  129.9 0.6 collective-permute-start.4
  130.5 2.1 %collective-permute-done.6.refs_4_ = f32[64,128]{1,0:T(8,128)S(1)} collective-permute-done((f32[64,128]{1,0:T(8,128)S(1)}, f32[64,128]{1,0:T(8,128)S(1)}, u32[]{:S(2)}, u32[]{:S(2)}) %collective-permute-start.6) | collective-permute-done | bytes 32800 | tf_op jit(solution)/shard_map/ppermute | solution.py:247
  132.6 0.0 collective-permute-done.5.refs_3_
  132.6 2.4 %collective-permute-done.4.refs_2_ = f32[64,128]{1,0:T(8,128)S(1)} collective-permute-done((f32[64,128]{1,0:T(8,128)S(1)}, f32[64,128]{1,0:T(8,128)S(1)}, u32[]{:S(2)}, u32[]{:S(2)}) %collective-permute-start.4) | collective-permute-done | bytes 32800 | tf_op jit(solution)/shard_map/ppermute | solution.py:247
  135.0 2.5 %counts.1 = (bf16[8,32,4,16,128]{4,3,2,1,0:T(8,128)(2,1)S(1)}, f32[64,128]{1,0:T(8,128)S(1)}) custom-call(s32[32]{0:T(128)S(1)} %copy-done.4, f32[64,128]{1,0:T(8,128)S(1)} %merge_x.1.refs_1_, f32[64,128]{1,0:T(8,128)S(1)} %collective-permute-done.4.refs_2_, f32[64,128]{1,0:T(8,128)S(1)} %collective-permute-done.5.refs_3_, ...), custom_call_target="tpu_custom_call" | custom-call | flops 536870912 | bytes 13631488 | tf_op jit(solution)/shard_map/counts/pallas_call | solution.py:261
  137.5 0.0 copy-start.2
  137.5 1.9 copy-done.2
  139.4 0.0 reduce-scatter.2.cloned.1.call-update
  139.5 0.6 slice_reduce_fusion
  140.1 49.5 %reduce-scatter.2.cloned.1.call-done = bf16[1,2048,128]{2,1,0:T(8,128)(2,1)} async-done(((bf16[8,2048,128]{2,1,0:T(8,128)(2,1)}), bf16[1,2048,128]{2,1,0:T(8,128)(2,1)}) %reduce-scatter.2.cloned.1.call-update) | async-done | bytes 524304 | tf_op jit(solution)/shard_map/reduce_scatter | solution.py:271
Async XLA Ops:
  7.2 8.5 %copy-start.8 = (s32[32,1,4]{0,2,1:T(4,128)S(1)}, s32[32,1,4]{0,2,1:T(4,128)}, u32[]{:S(2)}) copy-start(s32[32,1,4]{0,2,1:T(4,128)} %param.14) | copy-start | bytes 1540
  7.2 8.6 %copy-start.7 = (s32[64,32]{0,1:T(8,128)S(1)}, s32[64,32]{0,1:T(8,128)}, u32[]{:S(2)}) copy-start(s32[64,32]{0,1:T(8,128)} %param.9) | copy-start | bytes 24580
  7.2 8.7 %copy-start.3 = (f32[32,128]{1,0:T(8,128)S(1)}, f32[32,128]{1,0:T(8,128)}, u32[]{:S(2)}) copy-start(f32[32,128]{1,0:T(8,128)} %prior_ref.3) | copy-start | bytes 49156
  7.2 89.9 %all-gather.2.cloned.1.call-start = ((), (), s32[]{:S(2)}) async-start(), calls=%async_computation.1 | async-start | bytes 17842176 | tf_op jit(solution)/shard_map/all_gather | solution.py:208
  8.0 1.6 copy-start.5
  9.6 6.3 %copy-start.6 = (bf16[32,256,128]{2,1,0:T(8,128)(2,1)S(1)}, bf16[32,256,128]{2,1,0:T(8,128)(2,1)}, u32[]{:S(2)}) copy-start(bf16[32,256,128]{2,1,0:T(8,128)(2,1)} %table_ref.3) | copy-start | bytes 6291460
  9.6 87.5 %copy-start.4 = (s32[32]{0:T(128)S(1)}, s32[32]{0:T(128)}, u32[]{:S(2)}) copy-start(s32[32]{0:T(128)} %refs_0_.1) | copy-start | bytes 388
  15.7 173.9 %reduce-scatter.2.cloned.1.call-start = ((), (), s32[]{:S(2)}) async-start(), calls=%async_computation.2 | async-start | bytes 4718592 | tf_op jit(solution)/shard_map/reduce_scatter | solution.py:271
  97.1 5.9 %copy-start = (bf16[32,2112,128]{2,1,0:T(8,128)(2,1)S(1)}, bf16[32,2112,128]{2,1,0:T(8,128)(2,1)}, u32[]{:S(2)}) copy-start(bf16[32,2112,128]{2,1,0:T(8,128)(2,1)} %all-gather.2.cloned.1.call-done) | copy-start | bytes 51904516
  103.1 2.2 %copy-start.1 = (bf16[32,1,4,128,128]{4,3,2,1,0:T(8,128)(2,1)S(1)}, bf16[32,1,4,128,128]{4,3,2,1,0:T(8,128)(2,1)}, u32[]{:S(2)}) copy-start(bf16[32,1,4,128,128]{4,3,2,1,0:T(8,128)(2,1)} %param.13) | copy-start | bytes 12582916
  116.2 1.3 collective-permute-start
  117.6 5.5 %collective-permute-start.3 = (f32[64,128]{1,0:T(8,128)S(1)}, f32[64,128]{1,0:T(8,128)S(1)}, u32[]{:S(2)}, u32[]{:S(2)}) collective-permute-start(f32[64,128]{1,0:T(8,128)S(1)} %merge_core.1.refs_0_), channel_id=1, source_target_pairs={{0,128},{8,136},{16,144},{24,152},{32,160},{40,168},{48,176},{56,1... | collective-permute-start | bytes 98312 | tf_op jit(solution)/shard_map/ppermute | solution.py:247
  120.7 3.9 %collective-permute-start.2 = (f32[64,128]{1,0:T(8,128)S(1)}, f32[64,128]{1,0:T(8,128)S(1)}, u32[]{:S(2)}, u32[]{:S(2)}) collective-permute-start(f32[64,128]{1,0:T(8,128)S(1)} %merge_core.1.refs_0_), channel_id=1, source_target_pairs={{0,192},{8,200},{16,208},{24,216},{32,224},{40,232},{48,240},{56,2... | collective-permute-start | bytes 98312 | tf_op jit(solution)/shard_map/ppermute | solution.py:247
  121.8 5.1 %collective-permute-start.1 = (f32[64,128]{1,0:T(8,128)S(1)}, f32[64,128]{1,0:T(8,128)S(1)}, u32[]{:S(2)}, u32[]{:S(2)}) collective-permute-start(f32[64,128]{1,0:T(8,128)S(1)} %merge_core.1.refs_0_), channel_id=1, source_target_pairs={{0,64},{8,72},{16,80},{24,88},{32,96},{40,104},{48,112},{56,120},{... | collective-permute-start | bytes 98312 | tf_op jit(solution)/shard_map/ppermute | solution.py:247
  127.1 5.5 %collective-permute-start.6 = (f32[64,128]{1,0:T(8,128)S(1)}, f32[64,128]{1,0:T(8,128)S(1)}, u32[]{:S(2)}, u32[]{:S(2)}) collective-permute-start(f32[64,128]{1,0:T(8,128)S(1)} %merge_x.1.refs_1_), channel_id=1, source_target_pairs={{0,32},{8,40},{16,48},{24,56},{32,0},{40,8},{48,16},{56,24},{64,96... | collective-permute-start | bytes 98312 | tf_op jit(solution)/shard_map/ppermute | solution.py:247
  128.5 4.1 %collective-permute-start.5 = (f32[64,128]{1,0:T(8,128)S(1)}, f32[64,128]{1,0:T(8,128)S(1)}, u32[]{:S(2)}, u32[]{:S(2)}) collective-permute-start(f32[64,128]{1,0:T(8,128)S(1)} %merge_x.1.refs_1_), channel_id=1, source_target_pairs={{0,48},{8,56},{16,0},{24,8},{32,16},{40,24},{48,32},{56,40},{64,11... | collective-permute-start | bytes 98312 | tf_op jit(solution)/shard_map/ppermute | solution.py:247
  129.9 5.1 %collective-permute-start.4 = (f32[64,128]{1,0:T(8,128)S(1)}, f32[64,128]{1,0:T(8,128)S(1)}, u32[]{:S(2)}, u32[]{:S(2)}) collective-permute-start(f32[64,128]{1,0:T(8,128)S(1)} %merge_x.1.refs_1_), channel_id=1, source_target_pairs={{0,16},{8,24},{16,32},{24,40},{32,48},{40,56},{48,0},{56,8},{64,80... | collective-permute-start | bytes 98312 | tf_op jit(solution)/shard_map/ppermute | solution.py:247
  137.5 2.0 copy-start.2
Sparse Core Ops, SparseCore 0:
  15.8 81.3 all-gather.1
  139.6 49.9 reduce-scatter.1

commit v2 on v1

v2 whole, which is shorter than its diff:
```python
import jax
import jax.numpy as jnp
from jax import lax
from jax.experimental import pallas as pl
from jax.experimental.pallas import tpu as pltpu
from jax.sharding import PartitionSpec as P

K = 4096
BLK = 128
NZ = 4
C = 32
P_SIZE = 32
S_LOC = 64
LN2 = 0.6931471805599453
LOG2E = 1.4426950408889634
HALF = C // 2
PIECE = 2 * HALF + 1
VMEM = pl.BlockSpec(memory_space=pltpu.VMEM)
SMEM = pl.BlockSpec(memory_space=pltpu.SMEM)
ANY = pl.BlockSpec(memory_space=pl.ANY)


def lane_of(shape):
    return lax.broadcasted_iota(jnp.int32, shape, len(shape) - 1)


def look_up(values, table):
    wide = table.astype(jnp.float32)
    top = jnp.max(wide, axis=0, keepdims=True)
    log_norm = jnp.log(jnp.sum(jnp.exp(wide - top), axis=0, keepdims=True)) + top
    hot = (values == lane_of((S_LOC, table.shape[0]))).astype(jnp.float32)
    looked = jnp.dot(hot.astype(jnp.bfloat16), table, preferred_element_type=jnp.float32)
    return looked - log_norm


def child_kernel(half_ref, values_ref, table_ref, out_ref, inputs):
    half = half_ref[0]
    values = values_ref[...]
    values = jnp.where(half == 0, values[:, :HALF], values[:, HALF:])
    for k in range(HALF):
        inputs[k] = look_up(values[:, k : k + 1], table_ref[half * HALF + k])
    powers = jnp.zeros((S_LOC, BLK), jnp.float32)
    lanes = lane_of((S_LOC, BLK))
    for k in range(HALF):
        powers = jnp.where(lanes == k, jnp.max(inputs[k], axis=1, keepdims=True), powers)
    powers = jnp.ceil(powers * LOG2E).astype(jnp.bfloat16)
    out_ref[HALF] = powers
    powers = powers.astype(jnp.float32) * LN2
    for k in range(HALF):
        out_ref[k] = jnp.exp(inputs[k] - powers[:, k : k + 1]).astype(jnp.bfloat16)


def pack_kernel(core_ref, own_ref, other_ref, out_ref):
    core = core_ref[0]
    out_ref[pl.ds(core * HALF, HALF)] = own_ref[:HALF]
    out_ref[pl.ds((1 - core) * HALF, HALF)] = other_ref[:HALF]
    own = own_ref[HALF].astype(jnp.float32)
    other = other_ref[HALF].astype(jnp.float32)
    low = jnp.where(core == 0, own, other)
    high = jnp.where(core == 0, other, own)
    powers = jnp.where(lane_of((S_LOC, BLK)) < HALF, low, pltpu.roll(high, HALF, 1))
    out_ref[2 * HALF] = powers.astype(jnp.bfloat16)


def parent_kernel(values_ref, table_ref, prior_ref, out_ref):
    values = values_ref[...]
    for p in range(P_SIZE):
        out_ref[p] = look_up(values[:, p : p + 1], table_ref[p]) + prior_ref[p : p + 1, :]


PLACES = (
    ((0, 0),),
    ((3, 0), (1, 0), (2, 0)),
    ((0, 3),),
    ((0, 1),),
    ((3, 3), (1, 3), (2, 3)),
    ((3, 1), (1, 1), (2, 1)),
    ((3, 2), (1, 2)),
    ((0, 2), (2, 2)),
)


def pick_kernel(code_ref, *refs):
    sources = refs[: len(PLACES)]
    out_refs, pool, powers = refs[len(PLACES) : -2], refs[-2], refs[-1]

    def collect(k, carry):
        for source, places in zip(sources, PLACES):
            for n, (a, b) in enumerate(places):
                pool[(a * 4 + b) * PIECE + k] = source[n * PIECE + k]
        return carry

    lax.fori_loop(0, PIECE, collect, 0)
    for piece in range(16):
        both = pool[piece * PIECE + 2 * HALF].astype(jnp.float32)
        powers[2 * piece] = both
        powers[2 * piece + 1] = pltpu.roll(both, BLK - HALF, 1)
    lanes = lane_of((S_LOC, BLK))
    tops = [jnp.zeros((S_LOC, BLK), jnp.float32)] * 2
    for k in range(HALF):
        for row, out_ref in enumerate(out_refs):
            codes = [code_ref[row * C * NZ // 2 + k * NZ + z] for z in range(NZ)]
            power = [powers[code][:, k : k + 1] for code in codes]
            top = jnp.maximum(jnp.maximum(power[0], power[1]), jnp.maximum(power[2], power[3]))
            tops[row] = jnp.where(lanes == k, top, tops[row])
            for z in range(NZ):
                code = codes[z]
                factor = jnp.broadcast_to(jnp.exp2(power[z] - top), (S_LOC, BLK))
                block = pool[(code // 2) * PIECE + (code % 2) * HALF + k]
                out_ref[k * NZ + z] = (block.astype(jnp.float32) * factor).astype(jnp.bfloat16)
    for row, out_ref in enumerate(out_refs):
        out_ref[HALF * NZ] = tops[row].astype(jnp.bfloat16)


def child_at(core, half, k):
    return jnp.where(core == half, k, HALF + k)


def sums_kernel(
    core_ref, map_ref, own_ref, other_ref, weights_ref, parent_ref, prior_ref,
    stats_ref, root_ref, sums_ref,
):
    core = core_ref[0]
    root_ref[...] = parent_ref[...]
    for half, picked_ref in enumerate((own_ref, other_ref)):
        tops = picked_ref[HALF * NZ].astype(jnp.float32) * LN2
        for k in range(HALF):
            child = child_at(core, half, k)
            row_sums = None
            for z in range(0, NZ, 2):
                picked = jnp.concatenate([picked_ref[k * NZ + z], picked_ref[k * NZ + z + 1]], axis=1)
                wide = jnp.concatenate([weights_ref[child, z], weights_ref[child, z + 1]], axis=1)
                term = lax.dot_general(
                    picked, wide, (((1,), (1,)), ((), ())), preferred_element_type=jnp.float32
                )
                row_sums = term if row_sums is None else row_sums + term
            sums_ref[half * HALF + k] = row_sums
    for half, picked_ref in enumerate((own_ref, other_ref)):
        tops = picked_ref[HALF * NZ].astype(jnp.float32) * LN2
        for k in range(HALF):
            owner = map_ref[child_at(core, half, k)]
            message = jnp.log(sums_ref[half * HALF + k]) + tops[:, k : k + 1]
            root_ref[owner] = root_ref[owner] + message
    lanes = lane_of((S_LOC, BLK))
    prior = prior_ref[...]
    prior_peak = jnp.max(prior, axis=1, keepdims=True)
    prior_total = jnp.sum(jnp.exp(prior - prior_peak), axis=1, keepdims=True)
    eye = lax.broadcasted_iota(jnp.int32, (P_SIZE, BLK), 0)
    wide = lane_of((P_SIZE, BLK))
    stats = jnp.sum(
        jnp.where(wide == eye + 2 * P_SIZE, prior_peak, 0.0)
        + jnp.where(wide == eye + 3 * P_SIZE, prior_total, 0.0),
        axis=0, keepdims=True,
    )
    stats = jnp.broadcast_to(stats, (S_LOC, BLK))
    for p in range(P_SIZE):
        stats = jnp.where(lanes == p, jnp.max(root_ref[p], axis=1, keepdims=True), stats)
    peaks = stats
    for p in range(P_SIZE):
        total = jnp.sum(jnp.exp(root_ref[p] - peaks[:, p : p + 1]), axis=1, keepdims=True)
        stats = jnp.where(lanes == P_SIZE + p, total, stats)
    stats_ref[...] = stats


def merge(stats):
    is_peak = lane_of((S_LOC, BLK)) % (2 * P_SIZE) < P_SIZE
    peaks = [jnp.where(is_peak, s, pltpu.roll(s, P_SIZE, 1)) for s in stats]
    best = peaks[0]
    for p in peaks[1:]:
        best = jnp.maximum(best, p)
    total = None
    for s, p in zip(stats, peaks):
        term = s * jnp.exp(p - best)
        total = term if total is None else total + term
    return jnp.where(is_peak, best, total)


def merge_kernel(*refs):
    refs[-1][...] = merge([r[...] for r in refs[:-1]])


def counts_kernel(scale, n_stats, place_ref, map_ref, *refs):
    stats_refs, refs = refs[:n_stats], refs[n_stats:]
    root_ref, sums_ref, own_ref, other_ref, weights_ref = refs[:5]
    near, far, loglik_ref, posterior = refs[5:12], refs[12:14], refs[14], refs[15]
    core, place = place_ref[0], place_ref[1]
    stats = merge([r[...] for r in stats_refs])
    lanes = lane_of((S_LOC, BLK))
    norm = stats + pltpu.roll(jnp.log(stats), BLK - P_SIZE, 1)
    signed = jnp.where(lanes < P_SIZE, norm, 0.0) - jnp.where(
        (lanes >= 2 * P_SIZE) & (lanes < 3 * P_SIZE), norm, 0.0
    )
    loglik = jnp.sum(signed, axis=1, keepdims=True) / (C + P_SIZE)
    loglik_ref[...] = jnp.broadcast_to(loglik, (S_LOC, BLK))
    for p in range(P_SIZE):
        posterior[p] = jnp.exp(root_ref[p] - norm[:, p : p + 1]).astype(jnp.bfloat16)
    rows = near[0].shape[2]
    parts = BLK // rows
    starts = [pl.multiple_of(lax.rem(place + k, parts) * rows, rows) for k in range(parts)]
    turn = lax.rem(parts - place, parts) * rows
    for half, picked_ref in enumerate((own_ref, other_ref)):
        for k in range(HALF):
            child = child_at(core, half, k)
            share = posterior[map_ref[child]].astype(jnp.float32) / sums_ref[half * HALF + k]
            share = pltpu.roll(share, turn, 1).astype(jnp.bfloat16)
            picked = jnp.concatenate([picked_ref[k * NZ + z] for z in range(NZ)], axis=1)
            flow = lax.dot_general(
                share, picked, (((0,), (0,)), ((), ())), preferred_element_type=jnp.float32
            )
            for distance in range(parts):
                for z in range(NZ):
                    weight = weights_ref[child, z, pl.ds(starts[distance], rows), :]
                    block = flow[distance * rows : (distance + 1) * rows, z * BLK : (z + 1) * BLK]
                    block = (block * (weight.astype(jnp.float32) * scale)).astype(jnp.bfloat16)
                    if distance == 4:
                        far[half][k, z] = block
                    else:
                        near[distance if distance < 4 else distance - 1][half * HALF + k, z] = block


def first_step_kernel(up_ref, down_ref, up_in_ref, down_in_ref, up_out_ref, down_out_ref):
    f32 = jnp.float32
    low, high = pl.ds(0, HALF), pl.ds(HALF, HALF)
    up_out_ref[low] = (up_ref[low].astype(f32) + up_in_ref[...].astype(f32)).astype(jnp.bfloat16)
    up_out_ref[high] = up_ref[high]
    down_out_ref[low] = down_ref[low]
    down_out_ref[high] = (down_ref[high].astype(f32) + down_in_ref[...].astype(f32)).astype(
        jnp.bfloat16
    )


def step_kernel(up_ref, down_ref, up_in_ref, down_in_ref, up_out_ref, down_out_ref):
    f32 = jnp.float32
    up_out_ref[...] = (up_ref[...].astype(f32) + up_in_ref[...].astype(f32)).astype(jnp.bfloat16)
    down_out_ref[...] = (down_ref[...].astype(f32) + down_in_ref[...].astype(f32)).astype(
        jnp.bfloat16
    )


def last_kernel(core_ref, own_ref, up_in_ref, down_in_ref, out_ref):
    f32 = jnp.float32
    core = core_ref[0]
    for half in range(2):
        part = pl.ds(half * HALF, HALF)
        total = own_ref[part].astype(f32) + up_in_ref[part].astype(f32) + down_in_ref[part].astype(f32)
        out_ref[pl.ds(jnp.where(core == half, 0, HALF), HALF)] = total.astype(jnp.bfloat16)


def params(mib):
    return pltpu.CompilerParams(vmem_limit_bytes=mib << 20)


def cost(flops, moved, transcendentals):
    return pl.CostEstimate(flops=flops, bytes_accessed=moved, transcendentals=transcendentals)


def along(a, b):
    pairs = []
    for i in range(32):
        x, y, core = i // 8, i // 2 % 4, i % 2
        dx, dy = (a, b) if core == 0 else (b, a)
        pairs.append((i, (x + dx) % 4 * 8 + (y + dy) % 4 * 2 + core))
    return pairs


SWAP = [(i, i ^ 1) for i in range(32)]


def body(
    child_values,
    parent_values,
    child_logits,
    parent_logits,
    prior_logits,
    weights,
    block_cols,
    parent_map,
):
    f32, bf16, i32 = jnp.float32, jnp.bfloat16, jnp.int32
    shape = jax.ShapeDtypeStruct
    parts = lax.axis_size("batch")
    rows = BLK // parts
    weights = weights[:, 0]
    region = lax.axis_index("region").astype(i32)
    core = lax.rem(region, 2)
    place = jnp.stack([core, lax.axis_index("batch").astype(i32)])

    def scores(half):
        return pl.pallas_call(
            child_kernel,
            out_shape=shape((HALF + 1, S_LOC, BLK), bf16),
            in_specs=[SMEM, VMEM, VMEM],
            out_specs=VMEM,
            scratch_shapes=[pltpu.VMEM((HALF, S_LOC, BLK), f32)],
            compiler_params=params(16),
            cost_estimate=cost(1 << 27, 2 << 20, 1 << 20),
            name="child_scores",
        )(half.reshape(1), child_values, child_logits)

    given = lax.ppermute(scores(1 - core), "region", SWAP)
    kept = scores(core)
    own = pl.pallas_call(
        pack_kernel,
        out_shape=shape((PIECE, S_LOC, BLK), bf16),
        in_specs=[SMEM, VMEM, VMEM],
        out_specs=VMEM,
        compiler_params=params(8),
        name="pack",
    )(place, kept, given)

    def send(value, a, b):
        return lax.ppermute(value, "region", along(a, b))

    a1, a3, a2, b1, b3 = lax.optimization_barrier(
        (send(own, 1, 0), send(own, -1, 0), send(own, 2, 0), send(own, 0, 1), send(own, 0, -1))
    )
    line = jnp.concatenate([a1, a3, a2])
    q1, q3 = send(line, 0, 1), send(line, 0, -1)
    t1 = send(q1[: 2 * PIECE], 0, 1)
    t3 = send(jnp.concatenate([b3, q3[2 * PIECE :]]), 0, -1)

    parent_in = pl.pallas_call(
        parent_kernel,
        out_shape=shape((P_SIZE, S_LOC, BLK), f32),
        in_specs=[VMEM, VMEM, VMEM],
        out_specs=VMEM,
        compiler_params=params(16),
        cost_estimate=cost(1 << 28, 3 << 20, 1 << 21),
        name="parent_scores",
    )(parent_values, parent_logits, prior_logits)

    columns = block_cols[:, 0]
    columns = jnp.stack([columns, lax.ppermute(columns, "region", SWAP)])
    columns = lax.dynamic_slice_in_dim(columns, core * HALF, HALF, axis=1).reshape(-1)
    x, y = columns // 8 - region // 8 + 4, columns // 2 % 4 - region // 2 % 4 + 4
    x, y = x % 4, y % 4
    code = jnp.where(core == 0, x * 4 + y, y * 4 + x) * 2 + columns % 2
    picked, for_other = pl.pallas_call(
        pick_kernel,
        out_shape=(shape((HALF * NZ + 1, S_LOC, BLK), bf16),) * 2,
        in_specs=[SMEM] + [VMEM] * len(PLACES),
        out_specs=(VMEM, VMEM),
        scratch_shapes=[
            pltpu.VMEM((16 * PIECE, S_LOC, BLK), bf16),
            pltpu.VMEM((32, S_LOC, BLK), f32),
        ],
        compiler_params=params(32),
        cost_estimate=cost(1 << 22, 20 << 20, 1 << 20),
        name="pick",
    )(code, own, line, b1, b3, q1, q3, t1, t3)
    other = lax.ppermute(for_other, "region", SWAP)
    stats, root, sums = pl.pallas_call(
        sums_kernel,
        out_shape=(
            shape((S_LOC, BLK), f32),
            shape((P_SIZE, S_LOC, BLK), f32),
            shape((C, S_LOC, BLK), f32),
        ),
        in_specs=[SMEM, SMEM] + [VMEM] * 5,
        out_specs=(VMEM,) * 3,
        compiler_params=params(16),
        cost_estimate=cost(1 << 29, 12 << 20, 1 << 20),
        name="row_sums",
    )(place, parent_map, picked, other, weights, parent_in, prior_logits)

    for axis, pairs in (
        ("core", (SWAP,)),
        ("a", tuple(along(step, 0) for step in (1, 3, 2))),
        ("b", tuple(along(0, step) for step in (1, 3, 2))),
    ):
        others = [lax.ppermute(stats, "region", p) for p in pairs]
        if axis == "b":
            break
        stats = pl.pallas_call(
            merge_kernel,
            out_shape=shape((S_LOC, BLK), f32),
            in_specs=[VMEM] * (1 + len(others)),
            out_specs=VMEM,
            compiler_params=params(4),
            name="merge_" + axis,
        )(stats, *others)
    scale = K * NZ * BLK / (S_LOC * parts)
    whole, half_set = shape((C, NZ, rows, BLK), bf16), shape((HALF, NZ, rows, BLK), bf16)
    n0, n1, n2, n3, n5, n6, n7, far_up, far_down, loglik = pl.pallas_call(
        lambda *refs: counts_kernel(scale, 1 + len(others), *refs),
        out_shape=(whole,) * 7 + (half_set,) * 2 + (shape((S_LOC, BLK), f32),),
        in_specs=[SMEM, SMEM] + [VMEM] * (6 + len(others)),
        out_specs=(VMEM,) * 10,
        scratch_shapes=[pltpu.VMEM((P_SIZE, S_LOC, BLK), bf16)],
        compiler_params=params(24),
        cost_estimate=cost(1 << 29, 13 << 20, 1 << 19),
        name="counts",
    )(place, parent_map, stats, *others, root, sums, picked, other, weights)

    def ring(up, down):
        shift = lambda step: [(i, (i + step) % parts) for i in range(parts)]
        return lax.ppermute(up, "batch", shift(1)), lax.ppermute(down, "batch", shift(-1))

    up, down = ring(far_up, far_down)
    for kernel, here_up, here_down in (
        (first_step_kernel, n3, n5),
        (step_kernel, n2, n6),
        (step_kernel, n1, n7),
    ):
        up, down = ring(
            *pl.pallas_call(
                kernel,
                out_shape=(whole, whole),
                in_specs=[VMEM] * 4,
                out_specs=(VMEM, VMEM),
                compiler_params=params(8),
                name="ring_add",
            )(here_up, here_down, up, down)
        )
    counts = pl.pallas_call(
        last_kernel,
        out_shape=whole,
        in_specs=[SMEM] + [VMEM] * 3,
        out_specs=VMEM,
        compiler_params=params(8),
        name="ring_last",
    )(place, n0, up, down)
    return (counts[:, None], loglik[:, 0])


def solution(mesh):
    return jax.shard_map(
        body,
        mesh=mesh,
        in_specs=(
            P("batch", None),
            P("batch", None),
            P(None, None, "region"),
            P(None, None, "region"),
            P(None, "region"),
            P(None, "region", None, None, None),
            P(None, "region", None),
            P(),
        ),
        out_specs=(P(None, "region", None, "batch", None), P("batch")),
        check_vma=False,
    )
```

time: 200 us -> 169 us (0.84); the launches traced: 196 us -> 168 us
  waiting for transfers between devices: 139 us -> 98.3 us
  starting transfers between devices: 8.9 us -> 32.6 us
  between operations: 14.1 us -> 0.88 us
  local copies, waits for them, and re-layouts: 13.3 us -> 16.8 us
  Pallas kernels: 21 us -> 18.4 us
    ppermute x7 -> x27, waiting for transfers between devices: 9.75 us -> 98.3 us  [the longest x9 47.3 us: send(): return lax.ppermute(value, 'region', along(a, b))]
    all_gather x1 -> x0, waiting for transfers between devices: 79.8 us -> none  [body(): gathered = lax.all_gather(scaled.reshape(-1, BLK), 'region')]
    reduce_scatter x1 -> x0, waiting for transfers between devices: 49.5 us -> none  [body(): flows = lax.psum_scatter(flows.reshape(parts, -1, BLK), 'batch')]
    ppermute x7 -> x27, starting transfers between devices: 8.82 us -> 32.6 us  [the longest x9 15.1 us: send(): return lax.ppermute(value, 'region', along(a, b))]
    pallas_call x1, Pallas kernels: 11 us -> 4.4 us  [body(): pl.pallas_call(sums_kernel, out_shape=(shape((S_LOC, BLK), f32), shape((P...]
    pallas_call x1 -> x8, Pallas kernels: 5.99 us -> 9.75 us  [the longest x1 4.7 us: body(): pl.pallas_call(pick_kernel, out_shape=(shape((HALF * NZ + 1, S_LOC, BLK),...]
    unnamed x20 -> x38, local copies, waits for them, and re-layouts: 12.5 us -> 14.8 us
  transfers between devices with their start and end apart: 9 -> 27, of which waited for: 8 -> 21; matrix products, arithmetic and copies ran while one was open for 0% -> 2% of each run, Pallas kernels for 1% -> 2%
where the time goes in v2:
time: 169 us; the launch traced here: 168 us
  waiting for transfers between devices  98.3 us (58%)
  starting transfers between devices  32.6 us (19%)
  Pallas kernels  18.4 us (11%)
  local copies, waits for them, and re-layouts  16.8 us (10%)
    ppermute x9, waiting for transfers between devices, send(): return lax.ppermute(value, 'region', along(a, b))  47.3 us
    ppermute x4, waiting for transfers between devices, ring(): lax.ppermute(up, 'batch', shift(1))  27.5 us
    ppermute x9, starting transfers between devices, send(): return lax.ppermute(value, 'region', along(a, b))  15.1 us
    unnamed x38, local copies, waits for them, and re-layouts  14.8 us
    ppermute x7, waiting for transfers between devices, body(): others = [lax.ppermute(stats, 'region', p) for p in pairs]  11.3 us
    ppermute x4, waiting for transfers between devices, ring(): lax.ppermute(down, 'batch', shift(-1))  11 us
    ppermute x4, starting transfers between devices, ring(): lax.ppermute(up, 'batch', shift(1))  9.63 us
    ppermute x7, starting transfers between devices, body(): others = [lax.ppermute(stats, 'region', p) for p in pairs]  7.56 us
  transfers between devices with their start and end apart: 27, of which 21 were waited for; matrix products, arithmetic and copies ran while one was open for 2% of the time, Pallas kernels for 2%

profile of v2, /device:TPU:32, one launch (start us, length us, event | category | flops | bytes accessed | tf_op | source)
XLA Modules:
  0.0 168.2 jit_solution(14146008684375702479)
XLA Ops:
  1.4 1.6 copy-done.2
  3.0 1.1 child_scores.3
  4.6 1.1 child_scores.2.own_ref
  6.5 1.5 collective-permute-start.2
  8.0 1.7 %collective-permute-start.3 = (bf16[33,64,128]{2,1,0:T(8,128)(2,1)S(1)}, bf16[33,64,128]{2,1,0:T(8,128)(2,1)S(1)}, u32[]{:S(2)}, u32[]{:S(2)}) collective-permute-start(bf16[33,64,128]{2,1,0:T(8,128)(2,1)S(1)} %pack.1.refs_0_), channel_id=1, source_target_pairs={{0,192},{8,56},{16,208},{24,8},{32,224},{40,24},{48,240},{56,40},{... | collective-permute-start | bytes 1622024 | tf_op jit(solution)/shard_map/ppermute | solution.py:312
  9.8 1.8 %collective-permute-start.4 = (bf16[33,64,128]{2,1,0:T(8,128)(2,1)S(1)}, bf16[33,64,128]{2,1,0:T(8,128)(2,1)S(1)}, u32[]{:S(2)}, u32[]{:S(2)}) collective-permute-start(bf16[33,64,128]{2,1,0:T(8,128)(2,1)S(1)} %pack.1.refs_0_), channel_id=1, source_target_pairs={{0,128},{8,40},{16,144},{24,56},{32,160},{40,8},{48,176},{56,24},{... | collective-permute-start | bytes 1622024 | tf_op jit(solution)/shard_map/ppermute | solution.py:312
  11.6 1.6 collective-permute-start.5
  13.2 1.7 collective-permute-start.6
  14.8 4.4 %collective-permute-done.2 = bf16[33,64,128]{2,1,0:T(8,128)(2,1)S(1)} collective-permute-done((bf16[33,64,128]{2,1,0:T(8,128)(2,1)S(1)}, bf16[33,64,128]{2,1,0:T(8,128)(2,1)S(1)}, u32[]{:S(2)}, u32[]{:S(2)}) %collective-permute-start.2) | collective-permute-done | bytes 540704 | tf_op jit(solution)/shard_map/ppermute | solution.py:312
  19.8 9.9 %collective-permute-done.4 = bf16[33,64,128]{2,1,0:T(8,128)(2,1)S(1)} collective-permute-done((bf16[33,64,128]{2,1,0:T(8,128)(2,1)S(1)}, bf16[33,64,128]{2,1,0:T(8,128)(2,1)S(1)}, u32[]{:S(2)}, u32[]{:S(2)}) %collective-permute-start.4) | collective-permute-done | bytes 540704 | tf_op jit(solution)/shard_map/ppermute | solution.py:312
  30.7 3.1 %collective-permute-start.8 = (bf16[99,64,128]{2,1,0:T(8,128)(2,1)S(1)}, bf16[99,64,128]{2,1,0:T(8,128)(2,1)S(1)}, u32[]{:S(2)}, u32[]{:S(2)}) collective-permute-start(bf16[99,64,128]{2,1,0:T(8,128)(2,1)S(1)} %constant_dynamic-update-slice_fusion.refs_1_), channel_id=1, source_target_pairs={{0,48},{8,200},{16,0},{24,216},{32,16},{40,232},{48,32},{56,248},{... | collective-permute-start | bytes 4866056 | tf_op jit(solution)/shard_map/ppermute | solution.py:312
  33.8 1.2 copy-done.6
  35.0 17.3 %collective-permute-done.8.refs_5_ = bf16[99,64,128]{2,1,0:T(8,128)(2,1)S(1)} collective-permute-done((bf16[99,64,128]{2,1,0:T(8,128)(2,1)S(1)}, bf16[99,64,128]{2,1,0:T(8,128)(2,1)S(1)}, u32[]{:S(2)}, u32[]{:S(2)}) %collective-permute-start.8) | collective-permute-done | bytes 1622048 | tf_op jit(solution)/shard_map/ppermute | solution.py:312
  52.3 1.1 copy-done.4
  53.5 1.1 pad_maximum_fusion
  54.6 3.7 %collective-permute-start.10 = (bf16[66,64,128]{2,1,0:T(8,128)(2,1)}, bf16[66,64,128]{2,1,0:T(8,128)(2,1)}, u32[]{:S(2)}, u32[]{:S(2)}) collective-permute-start(bf16[66,64,128]{2,1,0:T(8,128)(2,1)} %pad_maximum_fusion), channel_id=1, source_target_pairs={{0,48},{8,200},{16,0},{24,216},{32,16},{40,232},{48,32},{56,248},{... | collective-permute-start | bytes 3244040 | tf_op jit(solution)/shard_map/ppermute | solution.py:312
  58.3 1.1 slice.12
  59.4 1.1 collective-permute-done
  60.8 10.4 %collective-permute-done.10.refs_7_ = bf16[66,64,128]{2,1,0:T(8,128)(2,1)} collective-permute-done((bf16[66,64,128]{2,1,0:T(8,128)(2,1)}, bf16[66,64,128]{2,1,0:T(8,128)(2,1)}, u32[]{:S(2)}, u32[]{:S(2)}) %collective-permute-start.10) | collective-permute-done | bytes 1081376 | tf_op jit(solution)/shard_map/ppermute | solution.py:312
  71.3 4.8 %collective-permute-done.9.refs_6_ = bf16[66,64,128]{2,1,0:T(8,128)(2,1)} collective-permute-done((bf16[66,64,128]{2,1,0:T(8,128)(2,1)}, bf16[66,64,128]{2,1,0:T(8,128)(2,1)}, u32[]{:S(2)}, u32[]{:S(2)}) %collective-permute-start.9) | collective-permute-done | bytes 1081376 | tf_op jit(solution)/shard_map/ppermute | solution.py:312
  76.0 1.4 copy-done.5
  77.4 1.4 copy-done.7
  81.0 4.7 %pick.1 = (bf16[65,64,128]{2,1,0:T(8,128)(2,1)S(1)}, bf16[65,64,128]{2,1,0:T(8,128)(2,1)}) custom-call(s32[128]{0:T(128)S(1)} %fusion.code_ref, bf16[33,64,128]{2,1,0:T(8,128)(2,1)S(1)} %pack.1.refs_0_, bf16[99,64,128]{2,1,0:T(8,128)(2,1)S(1)} %copy-done.7, bf16[33,64,128]{2,1,0:T(8,128)(2,1)S(1)} %copy-done.11, bf16[33,64,128]{2,1,0:T(8,128)(2,1)S(1)} %copy-done.9, ...), custom_call_target="tpu_custom_call" | custom-call | flops 4194304 | bytes 20971520 | tf_op jit(solution)/shard_map/pick/pallas_call | solution.py:338
  85.8 1.6 copy-done.14
  87.4 1.4 parent_scores.1.parent_ref
  88.8 2.2 %copy-done = bf16[32,1,4,128,128]{4,3,2,1,0:T(8,128)(2,1)S(1)} copy-done((bf16[32,1,4,128,128]{4,3,2,1,0:T(8,128)(2,1)S(1)}, bf16[32,1,4,128,128]{4,3,2,1,0:T(8,128)(2,1)}, u32[]{:S(2)}) %copy-start) | copy-done | bytes 4194328
  91.0 4.4 %row_sums.1 = (f32[64,128]{1,0:T(8,128)S(1)}, f32[32,64,128]{2,1,0:T(8,128)S(1)}, f32[32,64,128]{2,1,0:T(8,128)S(1)}) custom-call(s32[2]{0:T(128)S(1)} %pad_add_fusion.core_ref.refs_0_, s32[32]{0:T(128)S(1)} %copy-done.13, bf16[65,64,128]{2,1,0:T(8,128)(2,1)S(1)} %get-tuple-element.33.own_ref.refs_8_, ...), custom_call_target="tpu_custom_call" | custom-call | flops 536870912 | bytes 12582912 | tf_op jit(solution)/shard_map/row_sums/pallas_call | solution.py:352
  96.9 1.5 collective-permute-start.13
  98.4 1.8 %collective-permute-start.14 = (f32[64,128]{1,0:T(8,128)S(1)}, f32[64,128]{1,0:T(8,128)S(1)}, u32[]{:S(2)}, u32[]{:S(2)}) collective-permute-start(f32[64,128]{1,0:T(8,128)S(1)} %merge_core.1.refs_0_), channel_id=1, source_target_pairs={{0,192},{8,56},{16,208},{24,8},{32,224},{40,24},{48,240},{56,40},{... | collective-permute-start | bytes 98312 | tf_op jit(solution)/shard_map/ppermute | solution.py:371
  100.6 1.5 collective-permute-done.13.refs_1_
  102.3 3.3 %collective-permute-done.15.refs_3_ = f32[64,128]{1,0:T(8,128)S(1)} collective-permute-done((f32[64,128]{1,0:T(8,128)S(1)}, f32[64,128]{1,0:T(8,128)S(1)}, u32[]{:S(2)}, u32[]{:S(2)}) %collective-permute-start.15) | collective-permute-done | bytes 32800 | tf_op jit(solution)/shard_map/ppermute | solution.py:371
  105.9 3.2 %collective-permute-start.17 = (f32[64,128]{1,0:T(8,128)S(1)}, f32[64,128]{1,0:T(8,128)S(1)}, u32[]{:S(2)}, u32[]{:S(2)}) collective-permute-start(f32[64,128]{1,0:T(8,128)S(1)} %merge_a.1.refs_2_), channel_id=1, source_target_pairs={{0,48},{8,200},{16,0},{24,216},{32,16},{40,232},{48,32},{56,248},{... | collective-permute-start | bytes 98312 | tf_op jit(solution)/shard_map/ppermute | solution.py:371
  109.1 1.9 %collective-permute-done.16.refs_3_ = f32[64,128]{1,0:T(8,128)S(1)} collective-permute-done((f32[64,128]{1,0:T(8,128)S(1)}, f32[64,128]{1,0:T(8,128)S(1)}, u32[]{:S(2)}, u32[]{:S(2)}) %collective-permute-start.16) | collective-permute-done | bytes 32800 | tf_op jit(solution)/shard_map/ppermute | solution.py:371
  111.0 3.5 %collective-permute-done.18.refs_5_ = f32[64,128]{1,0:T(8,128)S(1)} collective-permute-done((f32[64,128]{1,0:T(8,128)S(1)}, f32[64,128]{1,0:T(8,128)S(1)}, u32[]{:S(2)}, u32[]{:S(2)}) %collective-permute-start.18) | collective-permute-done | bytes 32800 | tf_op jit(solution)/shard_map/ppermute | solution.py:371
  114.5 2.6 %counts.1 = (bf16[32,4,16,128]{3,2,1,0:T(8,128)(2,1)S(1)}, bf16[32,4,16,128]{3,2,1,0:T(8,128)(2,1)S(1)}, bf16[32,4,16,128]{3,2,1,0:T(8,128)(2,1)S(1)}, bf16[32,4...) custom-call(s32[2]{0:T(128)S(1)} %pad_add_fusion.core_ref.refs_0_, ...), custom_call_target="tpu_custom_call" | custom-call | flops 536870912 | bytes 13631488 | tf_op jit(solution)/shard_map/counts/pallas_call | solution.py:384
  117.1 2.0 %collective-permute-start.19 = (bf16[16,4,16,128]{3,2,1,0:T(8,128)(2,1)S(1)}, bf16[16,4,16,128]{3,2,1,0:T(8,128)(2,1)S(1)}, u32[]{:S(2)}, u32[]{:S(2)}) collective-permute-start(bf16[16,4,16,128]{3,2,1,0:T(8,128)(2,1)S(1)} %get-tuple-element.45), channel_id=1, source_target_pairs={{0,1},{1,2},{2,3},{3,4},{4,5},{5,6},{6,7},{7,0},{8,9},{9,10},{10,1... | collective-permute-start | bytes 786440 | tf_op jit(solution)/shard_map/ppermute | solution.py:397
  119.2 4.3 %collective-permute-done.19.up_in_ref = bf16[16,4,16,128]{3,2,1,0:T(8,128)(2,1)S(1)} collective-permute-done((bf16[16,4,16,128]{3,2,1,0:T(8,128)(2,1)S(1)}, bf16[16,4,16,128]{3,2,1,0:T(8,128)(2,1)S(1)}, u32[]{:S(2)}, u32[]{:S(2)}) %collective-permute-start.19) | collective-permute-done | bytes 262176 | tf_op jit(solution)/shard_map/ppermute | solution.py:397
  123.6 1.9 %collective-permute-done.20.down_in_ref = bf16[16,4,16,128]{3,2,1,0:T(8,128)(2,1)S(1)} collective-permute-done((bf16[16,4,16,128]{3,2,1,0:T(8,128)(2,1)S(1)}, bf16[16,4,16,128]{3,2,1,0:T(8,128)(2,1)S(1)}, u32[]{:S(2)}, u32[]{:S(2)}) %collective-permute-start.20) | collective-permute-done | bytes 262176 | tf_op jit(solution)/shard_map/ppermute | solution.py:397
  125.6 3.1 %collective-permute-start.21 = (bf16[32,4,16,128]{3,2,1,0:T(8,128)(2,1)S(1)}, bf16[32,4,16,128]{3,2,1,0:T(8,128)(2,1)S(1)}, u32[]{:S(2)}, u32[]{:S(2)}) collective-permute-start(bf16[32,4,16,128]{3,2,1,0:T(8,128)(2,1)S(1)} %get-tuple-element.47), channel_id=1, source_target_pairs={{0,1},{1,2},{2,3},{3,4},{4,5},{5,6},{6,7},{7,0},{8,9},{9,10},{10,1... | collective-permute-start | bytes 1572872 | tf_op jit(solution)/shard_map/ppermute | solution.py:397
  128.8 7.6 %collective-permute-done.21.up_in_ref = bf16[32,4,16,128]{3,2,1,0:T(8,128)(2,1)S(1)} collective-permute-done((bf16[32,4,16,128]{3,2,1,0:T(8,128)(2,1)S(1)}, bf16[32,4,16,128]{3,2,1,0:T(8,128)(2,1)S(1)}, u32[]{:S(2)}, u32[]{:S(2)}) %collective-permute-start.21) | collective-permute-done | bytes 524320 | tf_op jit(solution)/shard_map/ppermute | solution.py:397
  136.3 4.3 %collective-permute-done.22.down_in_ref = bf16[32,4,16,128]{3,2,1,0:T(8,128)(2,1)S(1)} collective-permute-done((bf16[32,4,16,128]{3,2,1,0:T(8,128)(2,1)S(1)}, bf16[32,4,16,128]{3,2,1,0:T(8,128)(2,1)S(1)}, u32[]{:S(2)}, u32[]{:S(2)}) %collective-permute-start.22) | collective-permute-done | bytes 524320 | tf_op jit(solution)/shard_map/ppermute | solution.py:397
  140.9 2.5 %collective-permute-start.23 = (bf16[32,4,16,128]{3,2,1,0:T(8,128)(2,1)S(1)}, bf16[32,4,16,128]{3,2,1,0:T(8,128)(2,1)S(1)}, u32[]{:S(2)}, u32[]{:S(2)}) collective-permute-start(bf16[32,4,16,128]{3,2,1,0:T(8,128)(2,1)S(1)} %get-tuple-element.49), channel_id=1, source_target_pairs={{0,1},{1,2},{2,3},{3,4},{4,5},{5,6},{6,7},{7,0},{8,9},{9,10},{10,1... | collective-permute-start | bytes 1572872 | tf_op jit(solution)/shard_map/ppermute | solution.py:397
  143.4 9.1 %collective-permute-done.23.up_in_ref = bf16[32,4,16,128]{3,2,1,0:T(8,128)(2,1)S(1)} collective-permute-done((bf16[32,4,16,128]{3,2,1,0:T(8,128)(2,1)S(1)}, bf16[32,4,16,128]{3,2,1,0:T(8,128)(2,1)S(1)}, u32[]{:S(2)}, u32[]{:S(2)}) %collective-permute-start.23) | collective-permute-done | bytes 524320 | tf_op jit(solution)/shard_map/ppermute | solution.py:397
  152.4 2.8 %collective-permute-done.24.down_in_ref = bf16[32,4,16,128]{3,2,1,0:T(8,128)(2,1)S(1)} collective-permute-done((bf16[32,4,16,128]{3,2,1,0:T(8,128)(2,1)S(1)}, bf16[32,4,16,128]{3,2,1,0:T(8,128)(2,1)S(1)}, u32[]{:S(2)}, u32[]{:S(2)}) %collective-permute-start.24) | collective-permute-done | bytes 524320 | tf_op jit(solution)/shard_map/ppermute | solution.py:397
  155.4 2.1 %collective-permute-start.25 = (bf16[32,4,16,128]{3,2,1,0:T(8,128)(2,1)S(1)}, bf16[32,4,16,128]{3,2,1,0:T(8,128)(2,1)S(1)}, u32[]{:S(2)}, u32[]{:S(2)}) collective-permute-start(bf16[32,4,16,128]{3,2,1,0:T(8,128)(2,1)S(1)} %get-tuple-element.51), channel_id=1, source_target_pairs={{0,1},{1,2},{2,3},{3,4},{4,5},{5,6},{6,7},{7,0},{8,9},{9,10},{10,1... | collective-permute-start | bytes 1572872 | tf_op jit(solution)/shard_map/ppermute | solution.py:397
  158.2 6.5 %collective-permute-done.25.up_in_ref = bf16[32,4,16,128]{3,2,1,0:T(8,128)(2,1)S(1)} collective-permute-done((bf16[32,4,16,128]{3,2,1,0:T(8,128)(2,1)S(1)}, bf16[32,4,16,128]{3,2,1,0:T(8,128)(2,1)S(1)}, u32[]{:S(2)}, u32[]{:S(2)}) %collective-permute-start.25) | collective-permute-done | bytes 524320 | tf_op jit(solution)/shard_map/ppermute | solution.py:397
  164.7 2.0 %collective-permute-done.26.down_in_ref = bf16[32,4,16,128]{3,2,1,0:T(8,128)(2,1)S(1)} collective-permute-done((bf16[32,4,16,128]{3,2,1,0:T(8,128)(2,1)S(1)}, bf16[32,4,16,128]{3,2,1,0:T(8,128)(2,1)S(1)}, u32[]{:S(2)}, u32[]{:S(2)}) %collective-permute-start.26) | collective-permute-done | bytes 524320 | tf_op jit(solution)/shard_map/ppermute | solution.py:397
  166.7 1.5 ring_last.1
  (67 shorter events, 9.8 us)
Async XLA Ops:
  1.4 1.6 copy-start.2
  3.0 1.6 copy-start.3
  4.2 1.7 collective-permute-start.1
  6.5 12.8 %collective-permute-start.2 = (bf16[33,64,128]{2,1,0:T(8,128)(2,1)S(1)}, bf16[33,64,128]{2,1,0:T(8,128)(2,1)S(1)}, u32[]{:S(2)}, u32[]{:S(2)}) collective-permute-start(bf16[33,64,128]{2,1,0:T(8,128)(2,1)S(1)} %pack.1.refs_0_), channel_id=1, source_target_pairs={{0,64},{8,24},{16,80},{24,40},{32,96},{40,56},{48,112},{56,8},{64,... | collective-permute-start | bytes 1622024 | tf_op jit(solution)/shard_map/ppermute | solution.py:312
  8.0 11.8 %collective-permute-start.3 = (bf16[33,64,128]{2,1,0:T(8,128)(2,1)S(1)}, bf16[33,64,128]{2,1,0:T(8,128)(2,1)S(1)}, u32[]{:S(2)}, u32[]{:S(2)}) collective-permute-start(bf16[33,64,128]{2,1,0:T(8,128)(2,1)S(1)} %pack.1.refs_0_), channel_id=1, source_target_pairs={{0,192},{8,56},{16,208},{24,8},{32,224},{40,24},{48,240},{56,40},{... | collective-permute-start | bytes 1622024 | tf_op jit(solution)/shard_map/ppermute | solution.py:312
  9.8 19.9 %collective-permute-start.4 = (bf16[33,64,128]{2,1,0:T(8,128)(2,1)S(1)}, bf16[33,64,128]{2,1,0:T(8,128)(2,1)S(1)}, u32[]{:S(2)}, u32[]{:S(2)}) collective-permute-start(bf16[33,64,128]{2,1,0:T(8,128)(2,1)S(1)} %pack.1.refs_0_), channel_id=1, source_target_pairs={{0,128},{8,40},{16,144},{24,56},{32,160},{40,8},{48,176},{56,24},{... | collective-permute-start | bytes 1622024 | tf_op jit(solution)/shard_map/ppermute | solution.py:312
  11.6 18.1 %collective-permute-start.5 = (bf16[33,64,128]{2,1,0:T(8,128)(2,1)S(1)}, bf16[33,64,128]{2,1,0:T(8,128)(2,1)S(1)}, u32[]{:S(2)}, u32[]{:S(2)}) collective-permute-start(bf16[33,64,128]{2,1,0:T(8,128)(2,1)S(1)} %pack.1.refs_0_), channel_id=1, source_target_pairs={{0,16},{8,72},{16,32},{24,88},{32,48},{40,104},{48,0},{56,120},{64... | collective-permute-start | bytes 1622024 | tf_op jit(solution)/shard_map/ppermute | solution.py:312
  13.2 17.4 %collective-permute-start.6 = (bf16[33,64,128]{2,1,0:T(8,128)(2,1)S(1)}, bf16[33,64,128]{2,1,0:T(8,128)(2,1)S(1)}, u32[]{:S(2)}, u32[]{:S(2)}) collective-permute-start(bf16[33,64,128]{2,1,0:T(8,128)(2,1)S(1)} %pack.1.refs_0_), channel_id=1, source_target_pairs={{0,48},{8,200},{16,0},{24,216},{32,16},{40,232},{48,32},{56,248},{... | collective-permute-start | bytes 1622024 | tf_op jit(solution)/shard_map/ppermute | solution.py:312
  29.7 0.9 copy-start.10
  30.5 21.8 %copy-start.8 = (bf16[33,64,128]{2,1,0:T(8,128)(2,1)}, bf16[33,64,128]{2,1,0:T(8,128)(2,1)S(1)}, u32[]{:S(2)}) copy-start(bf16[33,64,128]{2,1,0:T(8,128)(2,1)S(1)} %collective-permute-done.6.refs_3_) | copy-start | bytes 1622020
  30.7 21.6 %collective-permute-start.8 = (bf16[99,64,128]{2,1,0:T(8,128)(2,1)S(1)}, bf16[99,64,128]{2,1,0:T(8,128)(2,1)S(1)}, u32[]{:S(2)}, u32[]{:S(2)}) collective-permute-start(bf16[99,64,128]{2,1,0:T(8,128)(2,1)S(1)} %constant_dynamic-update-slice_fusion.refs_1_), channel_id=1, source_target_pairs={{0,48},{8,200},{16,0},{24,216},{32,16},{40,232},{48,32},{56,248},{... | collective-permute-start | bytes 4866056 | tf_op jit(solution)/shard_map/ppermute | solution.py:312
  33.8 24.5 %collective-permute-start.7 = (bf16[99,64,128]{2,1,0:T(8,128)(2,1)S(1)}, bf16[99,64,128]{2,1,0:T(8,128)(2,1)S(1)}, u32[]{:S(2)}, u32[]{:S(2)}) collective-permute-start(bf16[99,64,128]{2,1,0:T(8,128)(2,1)S(1)} %constant_dynamic-update-slice_fusion.refs_1_), channel_id=1, source_target_pairs={{0,16},{8,72},{16,32},{24,88},{32,48},{40,104},{48,0},{56,120},{64... | collective-permute-start | bytes 4866056 | tf_op jit(solution)/shard_map/ppermute | solution.py:312
  33.8 1.2 copy-start.6
  52.3 1.1 copy-start.4
  54.6 4.8 %copy-start.16 = (s32[32,1,4]{0,2,1:T(4,128)S(1)}, s32[32,1,4]{0,2,1:T(4,128)}, u32[]{:S(2)}) copy-start(s32[32,1,4]{0,2,1:T(4,128)} %param.14) | copy-start | bytes 1540
  54.6 16.7 %collective-permute-start.10 = (bf16[66,64,128]{2,1,0:T(8,128)(2,1)}, bf16[66,64,128]{2,1,0:T(8,128)(2,1)}, u32[]{:S(2)}, u32[]{:S(2)}) collective-permute-start(bf16[66,64,128]{2,1,0:T(8,128)(2,1)} %pad_maximum_fusion), channel_id=1, source_target_pairs={{0,48},{8,200},{16,0},{24,216},{32,16},{40,232},{48,32},{56,248},{... | collective-permute-start | bytes 3244040 | tf_op jit(solution)/shard_map/ppermute | solution.py:312
  59.3 16.7 %collective-permute-start.9 = (bf16[66,64,128]{2,1,0:T(8,128)(2,1)}, bf16[66,64,128]{2,1,0:T(8,128)(2,1)}, u32[]{:S(2)}, u32[]{:S(2)}) collective-permute-start(bf16[66,64,128]{2,1,0:T(8,128)(2,1)} %slice.12), channel_id=1, source_target_pairs={{0,16},{8,72},{16,32},{24,88},{32,48},{40,104},{48,0},{56,120},{64... | collective-permute-start | bytes 3244040 | tf_op jit(solution)/shard_map/ppermute | solution.py:312
  59.3 1.2 collective-permute-start
  76.0 1.4 copy-start.5
  77.4 1.4 copy-start.7
  78.9 1.0 copy-start.9
  79.9 1.0 copy-start.11
  81.0 4.7 %copy-start.15 = (s32[64,32]{0,1:T(8,128)S(1)}, s32[64,32]{0,1:T(8,128)}, u32[]{:S(2)}) copy-start(s32[64,32]{0,1:T(8,128)} %param.9) | copy-start | bytes 24580
  81.0 4.8 %copy-start.12 = (f32[32,128]{1,0:T(8,128)S(1)}, f32[32,128]{1,0:T(8,128)}, u32[]{:S(2)}) copy-start(f32[32,128]{1,0:T(8,128)} %prior_ref.3) | copy-start | bytes 49156
  85.7 3.1 %collective-permute-start.11 = (bf16[65,64,128]{2,1,0:T(8,128)(2,1)}, bf16[65,64,128]{2,1,0:T(8,128)(2,1)S(1)}, u32[]{:S(2)}, u32[]{:S(2)}) collective-permute-start(bf16[65,64,128]{2,1,0:T(8,128)(2,1)} %get-tuple-element.34), channel_id=1, source_target_pairs={{0,8},{8,0},{16,24},{24,16},{32,40},{40,32},{48,56},{56,48},{64,72... | collective-permute-start | bytes 3194888 | tf_op jit(solution)/shard_map/ppermute | solution.py:351
  85.8 1.6 copy-start.14
  87.4 1.4 copy-start.13
  88.8 2.2 %copy-start = (bf16[32,1,4,128,128]{4,3,2,1,0:T(8,128)(2,1)S(1)}, bf16[32,1,4,128,128]{4,3,2,1,0:T(8,128)(2,1)}, u32[]{:S(2)}) copy-start(bf16[32,1,4,128,128]{4,3,2,1,0:T(8,128)(2,1)} %param.13) | copy-start | bytes 12582916
  91.0 23.6 %copy-start.1 = (bf16[32,1,4,128,128]{4,3,2,1,0:T(8,128)(2,1)S(1)}, bf16[32,1,4,128,128]{4,3,2,1,0:T(8,128)(2,1)}, u32[]{:S(2)}) copy-start(bf16[32,1,4,128,128]{4,3,2,1,0:T(8,128)(2,1)} %param.13) | copy-start | bytes 12582916
  95.4 1.5 collective-permute-start.12
  96.9 5.2 %collective-permute-start.13 = (f32[64,128]{1,0:T(8,128)S(1)}, f32[64,128]{1,0:T(8,128)S(1)}, u32[]{:S(2)}, u32[]{:S(2)}) collective-permute-start(f32[64,128]{1,0:T(8,128)S(1)} %merge_core.1.refs_0_), channel_id=1, source_target_pairs={{0,64},{8,24},{16,80},{24,40},{32,96},{40,56},{48,112},{56,8},{64,... | collective-permute-start | bytes 98312 | tf_op jit(solution)/shard_map/ppermute | solution.py:371
  98.4 3.9 %collective-permute-start.14 = (f32[64,128]{1,0:T(8,128)S(1)}, f32[64,128]{1,0:T(8,128)S(1)}, u32[]{:S(2)}, u32[]{:S(2)}) collective-permute-start(f32[64,128]{1,0:T(8,128)S(1)} %merge_core.1.refs_0_), channel_id=1, source_target_pairs={{0,192},{8,56},{16,208},{24,8},{32,224},{40,24},{48,240},{56,40},{... | collective-permute-start | bytes 98312 | tf_op jit(solution)/shard_map/ppermute | solution.py:371
  100.2 5.4 %collective-permute-start.15 = (f32[64,128]{1,0:T(8,128)S(1)}, f32[64,128]{1,0:T(8,128)S(1)}, u32[]{:S(2)}, u32[]{:S(2)}) collective-permute-start(f32[64,128]{1,0:T(8,128)S(1)} %merge_core.1.refs_0_), channel_id=1, source_target_pairs={{0,128},{8,40},{16,144},{24,56},{32,160},{40,8},{48,176},{56,24},{... | collective-permute-start | bytes 98312 | tf_op jit(solution)/shard_map/ppermute | solution.py:371
  105.8 5.2 %collective-permute-start.16 = (f32[64,128]{1,0:T(8,128)S(1)}, f32[64,128]{1,0:T(8,128)S(1)}, u32[]{:S(2)}, u32[]{:S(2)}) collective-permute-start(f32[64,128]{1,0:T(8,128)S(1)} %merge_a.1.refs_2_), channel_id=1, source_target_pairs={{0,16},{8,72},{16,32},{24,88},{32,48},{40,104},{48,0},{56,120},{64... | collective-permute-start | bytes 98312 | tf_op jit(solution)/shard_map/ppermute | solution.py:371
  105.9 5.1 %collective-permute-start.17 = (f32[64,128]{1,0:T(8,128)S(1)}, f32[64,128]{1,0:T(8,128)S(1)}, u32[]{:S(2)}, u32[]{:S(2)}) collective-permute-start(f32[64,128]{1,0:T(8,128)S(1)} %merge_a.1.refs_2_), channel_id=1, source_target_pairs={{0,48},{8,200},{16,0},{24,216},{32,16},{40,232},{48,32},{56,248},{... | collective-permute-start | bytes 98312 | tf_op jit(solution)/shard_map/ppermute | solution.py:371
  109.1 5.4 %collective-permute-start.18 = (f32[64,128]{1,0:T(8,128)S(1)}, f32[64,128]{1,0:T(8,128)S(1)}, u32[]{:S(2)}, u32[]{:S(2)}) collective-permute-start(f32[64,128]{1,0:T(8,128)S(1)} %merge_a.1.refs_2_), channel_id=1, source_target_pairs={{0,32},{8,136},{16,48},{24,152},{32,0},{40,168},{48,16},{56,184},{... | collective-permute-start | bytes 98312 | tf_op jit(solution)/shard_map/ppermute | solution.py:371
  117.1 6.4 %collective-permute-start.19 = (bf16[16,4,16,128]{3,2,1,0:T(8,128)(2,1)S(1)}, bf16[16,4,16,128]{3,2,1,0:T(8,128)(2,1)S(1)}, u32[]{:S(2)}, u32[]{:S(2)}) collective-permute-start(bf16[16,4,16,128]{3,2,1,0:T(8,128)(2,1)S(1)} %get-tuple-element.45), channel_id=1, source_target_pairs={{0,1},{1,2},{2,3},{3,4},{4,5},{5,6},{6,7},{7,0},{8,9},{9,10},{10,1... | collective-permute-start | bytes 786440 | tf_op jit(solution)/shard_map/ppermute | solution.py:397
  119.1 6.4 %collective-permute-start.20 = (bf16[16,4,16,128]{3,2,1,0:T(8,128)(2,1)S(1)}, bf16[16,4,16,128]{3,2,1,0:T(8,128)(2,1)S(1)}, u32[]{:S(2)}, u32[]{:S(2)}) collective-permute-start(bf16[16,4,16,128]{3,2,1,0:T(8,128)(2,1)S(1)} %get-tuple-element.46), channel_id=1, source_target_pairs={{0,7},{1,0},{2,1},{3,2},{4,3},{5,4},{6,5},{7,6},{8,15},{9,8},{10,9... | collective-permute-start | bytes 786440 | tf_op jit(solution)/shard_map/ppermute | solution.py:397
  125.6 10.7 %collective-permute-start.21 = (bf16[32,4,16,128]{3,2,1,0:T(8,128)(2,1)S(1)}, bf16[32,4,16,128]{3,2,1,0:T(8,128)(2,1)S(1)}, u32[]{:S(2)}, u32[]{:S(2)}) collective-permute-start(bf16[32,4,16,128]{3,2,1,0:T(8,128)(2,1)S(1)} %get-tuple-element.47), channel_id=1, source_target_pairs={{0,1},{1,2},{2,3},{3,4},{4,5},{5,6},{6,7},{7,0},{8,9},{9,10},{10,1... | collective-permute-start | bytes 1572872 | tf_op jit(solution)/shard_map/ppermute | solution.py:397
  128.8 11.9 %collective-permute-start.22 = (bf16[32,4,16,128]{3,2,1,0:T(8,128)(2,1)S(1)}, bf16[32,4,16,128]{3,2,1,0:T(8,128)(2,1)S(1)}, u32[]{:S(2)}, u32[]{:S(2)}) collective-permute-start(bf16[32,4,16,128]{3,2,1,0:T(8,128)(2,1)S(1)} %get-tuple-element.48), channel_id=1, source_target_pairs={{0,7},{1,0},{2,1},{3,2},{4,3},{5,4},{6,5},{7,6},{8,15},{9,8},{10,9... | collective-permute-start | bytes 1572872 | tf_op jit(solution)/shard_map/ppermute | solution.py:397
  140.9 11.5 %collective-permute-start.23 = (bf16[32,4,16,128]{3,2,1,0:T(8,128)(2,1)S(1)}, bf16[32,4,16,128]{3,2,1,0:T(8,128)(2,1)S(1)}, u32[]{:S(2)}, u32[]{:S(2)}) collective-permute-start(bf16[32,4,16,128]{3,2,1,0:T(8,128)(2,1)S(1)} %get-tuple-element.49), channel_id=1, source_target_pairs={{0,1},{1,2},{2,3},{3,4},{4,5},{5,6},{6,7},{7,0},{8,9},{9,10},{10,1... | collective-permute-start | bytes 1572872 | tf_op jit(solution)/shard_map/ppermute | solution.py:397
  143.4 11.8 %collective-permute-start.24 = (bf16[32,4,16,128]{3,2,1,0:T(8,128)(2,1)S(1)}, bf16[32,4,16,128]{3,2,1,0:T(8,128)(2,1)S(1)}, u32[]{:S(2)}, u32[]{:S(2)}) collective-permute-start(bf16[32,4,16,128]{3,2,1,0:T(8,128)(2,1)S(1)} %get-tuple-element.50), channel_id=1, source_target_pairs={{0,7},{1,0},{2,1},{3,2},{4,3},{5,4},{6,5},{7,6},{8,15},{9,8},{10,9... | collective-permute-start | bytes 1572872 | tf_op jit(solution)/shard_map/ppermute | solution.py:397
  155.4 9.3 %collective-permute-start.25 = (bf16[32,4,16,128]{3,2,1,0:T(8,128)(2,1)S(1)}, bf16[32,4,16,128]{3,2,1,0:T(8,128)(2,1)S(1)}, u32[]{:S(2)}, u32[]{:S(2)}) collective-permute-start(bf16[32,4,16,128]{3,2,1,0:T(8,128)(2,1)S(1)} %get-tuple-element.51), channel_id=1, source_target_pairs={{0,1},{1,2},{2,3},{3,4},{4,5},{5,6},{6,7},{7,0},{8,9},{9,10},{10,1... | collective-permute-start | bytes 1572872 | tf_op jit(solution)/shard_map/ppermute | solution.py:397
  157.5 9.2 %collective-permute-start.26 = (bf16[32,4,16,128]{3,2,1,0:T(8,128)(2,1)S(1)}, bf16[32,4,16,128]{3,2,1,0:T(8,128)(2,1)S(1)}, u32[]{:S(2)}, u32[]{:S(2)}) collective-permute-start(bf16[32,4,16,128]{3,2,1,0:T(8,128)(2,1)S(1)} %get-tuple-element.52), channel_id=1, source_target_pairs={{0,7},{1,0},{2,1},{3,2},{4,3},{5,4},{6,5},{7,6},{8,15},{9,8},{10,9... | collective-permute-start | bytes 1572872 | tf_op jit(solution)/shard_map/ppermute | solution.py:397

commit v3 on v2

--- a/solution.py
+++ b/solution.py
@@ -69,14 +69,14 @@
 
 
 PLACES = (
-    ((0, 0),),
-    ((3, 0), (1, 0), (2, 0)),
-    ((0, 3),),
-    ((0, 1),),
-    ((3, 3), (1, 3), (2, 3)),
-    ((3, 1), (1, 1), (2, 1)),
-    ((3, 2), (1, 2)),
-    ((0, 2), (2, 2)),
+    ((0, 0), (3, 0)),
+    ((1, 0), (2, 0)),
+    ((0, 3), (3, 3)),
+    ((1, 3), (2, 3)),
+    ((0, 1), (3, 1)),
+    ((1, 1), (2, 1)),
+    ((0, 2), (3, 2)),
+    ((1, 2), (2, 2)),
 )
 
 
@@ -311,30 +311,30 @@
     def send(value, a, b):
         return lax.ppermute(value, "region", along(a, b))
 
-    a1, a3, a2, b1, b3 = lax.optimization_barrier(
-        (send(own, 1, 0), send(own, -1, 0), send(own, 2, 0), send(own, 0, 1), send(own, 0, -1))
-    )
-    line = jnp.concatenate([a1, a3, a2])
-    q1, q3 = send(line, 0, 1), send(line, 0, -1)
-    t1 = send(q1[: 2 * PIECE], 0, 1)
-    t3 = send(jnp.concatenate([b3, q3[2 * PIECE :]]), 0, -1)
-
     parent_in = pl.pallas_call(
         parent_kernel,
         out_shape=shape((P_SIZE, S_LOC, BLK), f32),
         in_specs=[VMEM, VMEM, VMEM],
         out_specs=VMEM,
-        compiler_params=params(16),
+        compiler_params=params(12),
         cost_estimate=cost(1 << 28, 3 << 20, 1 << 21),
         name="parent_scores",
     )(parent_values, parent_logits, prior_logits)
-
     columns = block_cols[:, 0]
     columns = jnp.stack([columns, lax.ppermute(columns, "region", SWAP)])
     columns = lax.dynamic_slice_in_dim(columns, core * HALF, HALF, axis=1).reshape(-1)
     x, y = columns // 8 - region // 8 + 4, columns // 2 % 4 - region // 2 % 4 + 4
     x, y = x % 4, y % 4
     code = jnp.where(core == 0, x * 4 + y, y * 4 + x) * 2 + columns % 2
+
+    a1, a3, a2 = send(own, 1, 0), send(own, -1, 0), send(own, 2, 0)
+    near = jnp.concatenate([own, a1])
+    near_up, near_down = send(near, 0, 1), send(near, 0, -1)
+    a3, a2, parent_in, code = lax.optimization_barrier((a3, a2, parent_in, code))
+    far = jnp.concatenate([a3, a2])
+    far_up, far_down = send(far, 0, 1), send(far, 0, -1)
+    next_up = send(near_up, 0, 1)
+    next_down = send(far_down, 0, -1)
     picked, for_other = pl.pallas_call(
         pick_kernel,
         out_shape=(shape((HALF * NZ + 1, S_LOC, BLK), bf16),) * 2,
@@ -344,10 +344,10 @@
             pltpu.VMEM((16 * PIECE, S_LOC, BLK), bf16),
             pltpu.VMEM((32, S_LOC, BLK), f32),
         ],
-        compiler_params=params(32),
+        compiler_params=params(22),
         cost_estimate=cost(1 << 22, 20 << 20, 1 << 20),
         name="pick",
-    )(code, own, line, b1, b3, q1, q3, t1, t3)
+    )(code, near, far, near_up, far_up, near_down, far_down, next_up, next_down)
     other = lax.ppermute(for_other, "region", SWAP)
     stats, root, sums = pl.pallas_call(
         sums_kernel,

time: 169 us -> 148 us (0.88)
  local copies, waits for them, and re-layouts: 16.8 us -> 5.36 us
  waiting for transfers between devices: 98.3 us -> 92.3 us
  Pallas kernels: 18.4 us -> 16.3 us
    unnamed x38 -> x19, local copies, waits for them, and re-layouts: 14.8 us -> 4.46 us
    ppermute x9, waiting for transfers between devices: 47.3 us -> 40.5 us  [send(): return lax.ppermute(value, 'region', along(a, b))]
    ppermute x1, waiting for transfers between devices: 0.01 us -> 2.67 us  [body(): other = lax.ppermute(for_other, 'region', SWAP)]
    pallas_call x1, Pallas kernels: 4.7 us -> 2.64 us  [body(): pl.pallas_call(pick_kernel, out_shape=(shape((HALF * NZ + 1, S_LOC, BLK),...]
  transfers between devices with their start and end apart: 27 -> 27, of which waited for: 21 -> 22; matrix products, arithmetic and copies ran while one was open for 2% -> 1% of each run, Pallas kernels for 2% -> 2%
where the time goes in v3:
time: 148 us; the launch traced here: 147 us
  waiting for transfers between devices  92.3 us (62%)
  starting transfers between devices  32 us (22%)
  Pallas kernels  16.3 us (11%)
  local copies, waits for them, and re-layouts  5.36 us (4%)
    ppermute x9, waiting for transfers between devices, send(): return lax.ppermute(value, 'region', along(a, b))  40.5 us
    ppermute x4, waiting for transfers between devices, ring(): lax.ppermute(up, 'batch', shift(1))  27.8 us
    ppermute x9, starting transfers between devices, send(): return lax.ppermute(value, 'region', along(a, b))  15.6 us
    ppermute x4, waiting for transfers between devices, ring(): lax.ppermute(down, 'batch', shift(-1))  10.7 us
    ppermute x7, waiting for transfers between devices, body(): others = [lax.ppermute(stats, 'region', p) for p in pairs]  10.7 us
    ppermute x4, starting transfers between devices, ring(): lax.ppermute(up, 'batch', shift(1))  8.6 us
    ppermute x7, starting transfers between devices, body(): others = [lax.ppermute(stats, 'region', p) for p in pairs]  6.55 us
    unnamed x19, local copies, waits for them, and re-layouts  4.46 us
  transfers between devices with their start and end apart: 27, of which 22 were waited for; matrix products, arithmetic and copies ran while one was open for 1% of the time, Pallas kernels for 2%

profile of v3, /device:TPU:32, one launch (start us, length us, event | category | flops | bytes accessed | tf_op | source)
XLA Modules:
  0.0 147.1 jit_solution(5752159792970620153)
XLA Ops:
  0.6 0.8 copy.15.values_ref
  1.4 1.6 %copy-done.1 = bf16[32,256,128]{2,1,0:T(8,128)(2,1)S(1)} copy-done((bf16[32,256,128]{2,1,0:T(8,128)(2,1)S(1)}, bf16[32,256,128]{2,1,0:T(8,128)(2,1)}, u32[]{:S(2)}) %copy-start.1) | copy-done | bytes 2097176
  3.0 1.1 child_scores.3
  4.6 1.1 child_scores.2.own_ref
  5.9 0.6 pack.1
  6.5 3.1 %collective-permute-start.2 = (bf16[33,64,128]{2,1,0:T(8,128)(2,1)S(1)}, bf16[33,64,128]{2,1,0:T(8,128)(2,1)S(1)}, u32[]{:S(2)}, u32[]{:S(2)}) collective-permute-start(bf16[33,64,128]{2,1,0:T(8,128)(2,1)S(1)} %pack.1), channel_id=1, source_target_pairs={{0,128},{8,40},{16,144},{24,56},{32,160},{40,8},{48,176},{56,24},{... | collective-permute-start | bytes 1622024 | tf_op jit(solution)/shard_map/ppermute | solution.py:312
  9.6 1.1 collective-permute-start.1
  10.8 1.6 %copy-done.5 = bf16[32,256,128]{2,1,0:T(8,128)(2,1)S(1)} copy-done((bf16[32,256,128]{2,1,0:T(8,128)(2,1)S(1)}, bf16[32,256,128]{2,1,0:T(8,128)(2,1)}, u32[]{:S(2)}) %copy-start.5) | copy-done | bytes 2097176
  12.4 1.4 parent_scores.1.parent_ref
  13.8 1.2 collective-permute-start.4
  15.4 2.0 %collective-permute-done.2 = bf16[33,64,128]{2,1,0:T(8,128)(2,1)S(1)} collective-permute-done((bf16[33,64,128]{2,1,0:T(8,128)(2,1)S(1)}, bf16[33,64,128]{2,1,0:T(8,128)(2,1)S(1)}, u32[]{:S(2)}, u32[]{:S(2)}) %collective-permute-start.2) | collective-permute-done | bytes 540704 | tf_op jit(solution)/shard_map/ppermute | solution.py:312
  17.4 5.9 %collective-permute-done.1 = bf16[33,64,128]{2,1,0:T(8,128)(2,1)S(1)} collective-permute-done((bf16[33,64,128]{2,1,0:T(8,128)(2,1)S(1)}, bf16[33,64,128]{2,1,0:T(8,128)(2,1)S(1)}, u32[]{:S(2)}, u32[]{:S(2)}) %collective-permute-start.1) | collective-permute-done | bytes 540704 | tf_op jit(solution)/shard_map/ppermute | solution.py:312
  23.5 3.1 %collective-permute-start.8 = (bf16[66,64,128]{2,1,0:T(8,128)(2,1)S(1)}, bf16[66,64,128]{2,1,0:T(8,128)(2,1)S(1)}, u32[]{:S(2)}, u32[]{:S(2)}) collective-permute-start(bf16[66,64,128]{2,1,0:T(8,128)(2,1)S(1)} %constant_dynamic-update-slice_fusion.refs_1_), channel_id=1, source_target_pairs={{0,48},{8,200},{16,0},{24,216},{32,16},{40,232},{48,32},{56,248},{... | collective-permute-start | bytes 3244040 | tf_op jit(solution)/shard_map/ppermute | solution.py:312
  26.8 1.1 collective-permute-start.6
  27.8 2.3 %collective-permute-start.7 = (bf16[66,64,128]{2,1,0:T(8,128)(2,1)S(1)}, bf16[66,64,128]{2,1,0:T(8,128)(2,1)S(1)}, u32[]{:S(2)}, u32[]{:S(2)}) collective-permute-start(bf16[66,64,128]{2,1,0:T(8,128)(2,1)S(1)} %pad_maximum_fusion.refs_0_), channel_id=1, source_target_pairs={{0,48},{8,200},{16,0},{24,216},{32,16},{40,232},{48,32},{56,248},{... | collective-permute-start | bytes 3244040 | tf_op jit(solution)/shard_map/ppermute | solution.py:312
  30.1 9.1 %collective-permute-done.8.refs_5_ = bf16[66,64,128]{2,1,0:T(8,128)(2,1)S(1)} collective-permute-done((bf16[66,64,128]{2,1,0:T(8,128)(2,1)S(1)}, bf16[66,64,128]{2,1,0:T(8,128)(2,1)S(1)}, u32[]{:S(2)}, u32[]{:S(2)}) %collective-permute-start.8) | collective-permute-done | bytes 1081376 | tf_op jit(solution)/shard_map/ppermute | solution.py:312
  39.2 3.7 %collective-permute-start.10 = (bf16[66,64,128]{2,1,0:T(8,128)(2,1)S(1)}, bf16[66,64,128]{2,1,0:T(8,128)(2,1)S(1)}, u32[]{:S(2)}, u32[]{:S(2)}) collective-permute-start(bf16[66,64,128]{2,1,0:T(8,128)(2,1)S(1)} %collective-permute-done.8.refs_5_), channel_id=1, source_target_pairs={{0,48},{8,200},{16,0},{24,216},{32,16},{40,232},{48,32},{56,248},{... | collective-permute-start | bytes 3244040 | tf_op jit(solution)/shard_map/ppermute | solution.py:312
  43.1 11.6 %collective-permute-done.6.refs_3_ = bf16[66,64,128]{2,1,0:T(8,128)(2,1)S(1)} collective-permute-done((bf16[66,64,128]{2,1,0:T(8,128)(2,1)S(1)}, bf16[66,64,128]{2,1,0:T(8,128)(2,1)S(1)}, u32[]{:S(2)}, u32[]{:S(2)}) %collective-permute-start.6) | collective-permute-done | bytes 1081376 | tf_op jit(solution)/shard_map/ppermute | solution.py:312
  54.7 7.7 %collective-permute-done.10.refs_7_ = bf16[66,64,128]{2,1,0:T(8,128)(2,1)S(1)} collective-permute-done((bf16[66,64,128]{2,1,0:T(8,128)(2,1)S(1)}, bf16[66,64,128]{2,1,0:T(8,128)(2,1)S(1)}, u32[]{:S(2)}, u32[]{:S(2)}) %collective-permute-start.10) | collective-permute-done | bytes 1081376 | tf_op jit(solution)/shard_map/ppermute | solution.py:312
  62.4 3.9 %collective-permute-done.9.refs_6_ = bf16[66,64,128]{2,1,0:T(8,128)(2,1)S(1)} collective-permute-done((bf16[66,64,128]{2,1,0:T(8,128)(2,1)S(1)}, bf16[66,64,128]{2,1,0:T(8,128)(2,1)S(1)}, u32[]{:S(2)}, u32[]{:S(2)}) %collective-permute-start.9) | collective-permute-done | bytes 1081376 | tf_op jit(solution)/shard_map/ppermute | solution.py:312
  66.3 2.6 %pick.1 = (bf16[65,64,128]{2,1,0:T(8,128)(2,1)S(1)}, bf16[65,64,128]{2,1,0:T(8,128)(2,1)S(1)}) custom-call(s32[128]{0:T(128)S(1)} %fusion.code_ref, bf16[66,64,128]{2,1,0:T(8,128)(2,1)S(1)} %pad_maximum_fusion.refs_0_, bf16[66,64,128]{2,1,0:T(8,128)(2,1)S(1)} %constant_dynamic-update-slice_fusion.refs_1_, ...), custom_call_target="tpu_custom_call" | custom-call | flops 4194304 | bytes 20971520 | tf_op jit(solution)/shard_map/pick/pallas_call | solution.py:338
  69.0 2.7 %collective-permute-done.11.other_ref.refs_9_ = bf16[65,64,128]{2,1,0:T(8,128)(2,1)S(1)} collective-permute-done((bf16[65,64,128]{2,1,0:T(8,128)(2,1)S(1)}, bf16[65,64,128]{2,1,0:T(8,128)(2,1)S(1)}, u32[]{:S(2)}, u32[]{:S(2)}) %collective-permute-start.11) | collective-permute-done | bytes 1064992 | tf_op jit(solution)/shard_map/ppermute | solution.py:351
  71.7 4.4 %row_sums.1 = (f32[64,128]{1,0:T(8,128)S(1)}, f32[32,64,128]{2,1,0:T(8,128)S(1)}, f32[32,64,128]{2,1,0:T(8,128)S(1)}) custom-call(s32[2]{0:T(128)S(1)} %pad_add_fusion.core_ref.refs_0_, s32[32]{0:T(128)S(1)} %copy-done.4, bf16[65,64,128]{2,1,0:T(8,128)(2,1)S(1)} %get-tuple-element.30.own_ref.refs_8_, ...), custom_call_target="tpu_custom_call" | custom-call | flops 536870912 | bytes 12582912 | tf_op jit(solution)/shard_map/row_sums/pallas_call | solution.py:352
  76.3 1.1 collective-permute-done.12.refs_1_
  77.5 2.1 %collective-permute-start.15 = (f32[64,128]{1,0:T(8,128)S(1)}, f32[64,128]{1,0:T(8,128)S(1)}, u32[]{:S(2)}, u32[]{:S(2)}) collective-permute-start(f32[64,128]{1,0:T(8,128)S(1)} %merge_core.1.refs_0_), channel_id=1, source_target_pairs={{0,128},{8,40},{16,144},{24,56},{32,160},{40,8},{48,176},{56,24},{... | collective-permute-start | bytes 98312 | tf_op jit(solution)/shard_map/ppermute | solution.py:371
  79.6 2.0 %collective-permute-start.14 = (f32[64,128]{1,0:T(8,128)S(1)}, f32[64,128]{1,0:T(8,128)S(1)}, u32[]{:S(2)}, u32[]{:S(2)}) collective-permute-start(f32[64,128]{1,0:T(8,128)S(1)} %merge_core.1.refs_0_), channel_id=1, source_target_pairs={{0,192},{8,56},{16,208},{24,8},{32,224},{40,24},{48,240},{56,40},{... | collective-permute-start | bytes 98312 | tf_op jit(solution)/shard_map/ppermute | solution.py:371
  81.6 1.4 collective-permute-done.15.refs_3_
  83.5 3.2 %collective-permute-done.13.refs_1_ = f32[64,128]{1,0:T(8,128)S(1)} collective-permute-done((f32[64,128]{1,0:T(8,128)S(1)}, f32[64,128]{1,0:T(8,128)S(1)}, u32[]{:S(2)}, u32[]{:S(2)}) %collective-permute-start.13) | collective-permute-done | bytes 32800 | tf_op jit(solution)/shard_map/ppermute | solution.py:371
  87.0 1.5 collective-permute-start.17
  88.4 0.6 collective-permute-start.16
  89.1 3.3 %collective-permute-done.18.refs_5_ = f32[64,128]{1,0:T(8,128)S(1)} collective-permute-done((f32[64,128]{1,0:T(8,128)S(1)}, f32[64,128]{1,0:T(8,128)S(1)}, u32[]{:S(2)}, u32[]{:S(2)}) %collective-permute-start.18) | collective-permute-done | bytes 32800 | tf_op jit(solution)/shard_map/ppermute | solution.py:371
  92.4 1.2 collective-permute-done.16.refs_3_
  93.5 2.6 %counts.1 = (bf16[32,4,16,128]{3,2,1,0:T(8,128)(2,1)S(1)}, bf16[32,4,16,128]{3,2,1,0:T(8,128)(2,1)S(1)}, bf16[32,4,16,128]{3,2,1,0:T(8,128)(2,1)S(1)}, bf16[32,4...) custom-call(s32[2]{0:T(128)S(1)} %pad_add_fusion.core_ref.refs_0_, ...), custom_call_target="tpu_custom_call" | custom-call | flops 536870912 | bytes 13631488 | tf_op jit(solution)/shard_map/counts/pallas_call | solution.py:384
  96.2 2.0 %collective-permute-start.19 = (bf16[16,4,16,128]{3,2,1,0:T(8,128)(2,1)S(1)}, bf16[16,4,16,128]{3,2,1,0:T(8,128)(2,1)S(1)}, u32[]{:S(2)}, u32[]{:S(2)}) collective-permute-start(bf16[16,4,16,128]{3,2,1,0:T(8,128)(2,1)S(1)} %get-tuple-element.43), channel_id=1, source_target_pairs={{0,1},{1,2},{2,3},{3,4},{4,5},{5,6},{6,7},{7,0},{8,9},{9,10},{10,1... | collective-permute-start | bytes 786440 | tf_op jit(solution)/shard_map/ppermute | solution.py:397
  98.3 4.3 %collective-permute-done.19.up_in_ref = bf16[16,4,16,128]{3,2,1,0:T(8,128)(2,1)S(1)} collective-permute-done((bf16[16,4,16,128]{3,2,1,0:T(8,128)(2,1)S(1)}, bf16[16,4,16,128]{3,2,1,0:T(8,128)(2,1)S(1)}, u32[]{:S(2)}, u32[]{:S(2)}) %collective-permute-start.19) | collective-permute-done | bytes 262176 | tf_op jit(solution)/shard_map/ppermute | solution.py:397
  102.6 2.0 %collective-permute-done.20.down_in_ref = bf16[16,4,16,128]{3,2,1,0:T(8,128)(2,1)S(1)} collective-permute-done((bf16[16,4,16,128]{3,2,1,0:T(8,128)(2,1)S(1)}, bf16[16,4,16,128]{3,2,1,0:T(8,128)(2,1)S(1)}, u32[]{:S(2)}, u32[]{:S(2)}) %collective-permute-start.20) | collective-permute-done | bytes 262176 | tf_op jit(solution)/shard_map/ppermute | solution.py:397
  104.7 3.1 %collective-permute-start.21 = (bf16[32,4,16,128]{3,2,1,0:T(8,128)(2,1)S(1)}, bf16[32,4,16,128]{3,2,1,0:T(8,128)(2,1)S(1)}, u32[]{:S(2)}, u32[]{:S(2)}) collective-permute-start(bf16[32,4,16,128]{3,2,1,0:T(8,128)(2,1)S(1)} %get-tuple-element.45), channel_id=1, source_target_pairs={{0,1},{1,2},{2,3},{3,4},{4,5},{5,6},{6,7},{7,0},{8,9},{9,10},{10,1... | collective-permute-start | bytes 1572872 | tf_op jit(solution)/shard_map/ppermute | solution.py:397
  107.8 7.4 %collective-permute-done.21.up_in_ref = bf16[32,4,16,128]{3,2,1,0:T(8,128)(2,1)S(1)} collective-permute-done((bf16[32,4,16,128]{3,2,1,0:T(8,128)(2,1)S(1)}, bf16[32,4,16,128]{3,2,1,0:T(8,128)(2,1)S(1)}, u32[]{:S(2)}, u32[]{:S(2)}) %collective-permute-start.21) | collective-permute-done | bytes 524320 | tf_op jit(solution)/shard_map/ppermute | solution.py:397
  115.2 5.0 %collective-permute-done.22.down_in_ref = bf16[32,4,16,128]{3,2,1,0:T(8,128)(2,1)S(1)} collective-permute-done((bf16[32,4,16,128]{3,2,1,0:T(8,128)(2,1)S(1)}, bf16[32,4,16,128]{3,2,1,0:T(8,128)(2,1)S(1)}, u32[]{:S(2)}, u32[]{:S(2)}) %collective-permute-start.22) | collective-permute-done | bytes 524320 | tf_op jit(solution)/shard_map/ppermute | solution.py:397
  120.4 2.4 %collective-permute-start.23 = (bf16[32,4,16,128]{3,2,1,0:T(8,128)(2,1)S(1)}, bf16[32,4,16,128]{3,2,1,0:T(8,128)(2,1)S(1)}, u32[]{:S(2)}, u32[]{:S(2)}) collective-permute-start(bf16[32,4,16,128]{3,2,1,0:T(8,128)(2,1)S(1)} %get-tuple-element.47), channel_id=1, source_target_pairs={{0,1},{1,2},{2,3},{3,4},{4,5},{5,6},{6,7},{7,0},{8,9},{9,10},{10,1... | collective-permute-start | bytes 1572872 | tf_op jit(solution)/shard_map/ppermute | solution.py:397
  122.8 9.5 %collective-permute-done.23.up_in_ref = bf16[32,4,16,128]{3,2,1,0:T(8,128)(2,1)S(1)} collective-permute-done((bf16[32,4,16,128]{3,2,1,0:T(8,128)(2,1)S(1)}, bf16[32,4,16,128]{3,2,1,0:T(8,128)(2,1)S(1)}, u32[]{:S(2)}, u32[]{:S(2)}) %collective-permute-start.23) | collective-permute-done | bytes 524320 | tf_op jit(solution)/shard_map/ppermute | solution.py:397
  132.3 2.8 %collective-permute-done.24.down_in_ref = bf16[32,4,16,128]{3,2,1,0:T(8,128)(2,1)S(1)} collective-permute-done((bf16[32,4,16,128]{3,2,1,0:T(8,128)(2,1)S(1)}, bf16[32,4,16,128]{3,2,1,0:T(8,128)(2,1)S(1)}, u32[]{:S(2)}, u32[]{:S(2)}) %collective-permute-start.24) | collective-permute-done | bytes 524320 | tf_op jit(solution)/shard_map/ppermute | solution.py:397
  135.3 1.1 collective-permute-start.25
  136.4 1.0 collective-permute-start.26
  137.4 0.6 slice_reduce_fusion
  138.0 6.5 %collective-permute-done.25.up_in_ref = bf16[32,4,16,128]{3,2,1,0:T(8,128)(2,1)S(1)} collective-permute-done((bf16[32,4,16,128]{3,2,1,0:T(8,128)(2,1)S(1)}, bf16[32,4,16,128]{3,2,1,0:T(8,128)(2,1)S(1)}, u32[]{:S(2)}, u32[]{:S(2)}) %collective-permute-start.25) | collective-permute-done | bytes 524320 | tf_op jit(solution)/shard_map/ppermute | solution.py:397
  144.6 1.1 collective-permute-done.26.down_in_ref
  145.6 1.5 %ring_last.1 = bf16[32,4,16,128]{3,2,1,0:T(8,128)(2,1)} custom-call(s32[2]{0:T(128)S(1)} %pad_add_fusion.core_ref.refs_0_, bf16[32,4,16,128]{3,2,1,0:T(8,128)(2,1)S(1)} %get-tuple-element.36.own_ref, bf16[32,4,16,128]{3,2,1,0:T(8,128)(2,1)S(1)} %collective-permute-done.25.up_in_ref, bf16[32,4,16,128]{3,2,1,0:T(8,128)(2,1)S(1)} %collective-permute-done.26.down_in_ref), custom_call_target="tpu_custom_call" | custom-call | tf_op jit(solution)/shard_map/ring_last/pallas_call | solution.py:415
  (46 shorter events, 3.3 us)
Async XLA Ops:
  1.4 1.6 %copy-start.1 = (bf16[32,256,128]{2,1,0:T(8,128)(2,1)S(1)}, bf16[32,256,128]{2,1,0:T(8,128)(2,1)}, u32[]{:S(2)}) copy-start(bf16[32,256,128]{2,1,0:T(8,128)(2,1)} %table_ref.4) | copy-start | bytes 6291460
  3.0 1.6 %copy-start.2 = (bf16[32,256,128]{2,1,0:T(8,128)(2,1)S(1)}, bf16[32,256,128]{2,1,0:T(8,128)(2,1)}, u32[]{:S(2)}) copy-start(bf16[32,256,128]{2,1,0:T(8,128)(2,1)} %table_ref.4) | copy-start | bytes 6291460
  4.2 1.7 %collective-permute-start = (bf16[17,64,128]{2,1,0:T(8,128)(2,1)S(1)}, bf16[17,64,128]{2,1,0:T(8,128)(2,1)S(1)}, u32[]{:S(2)}, u32[]{:S(2)}) collective-permute-start(bf16[17,64,128]{2,1,0:T(8,128)(2,1)S(1)} %child_scores.3), channel_id=1, source_target_pairs={{0,8},{8,0},{16,24},{24,16},{32,40},{40,32},{48,56},{56,48},{64,72... | collective-permute-start | bytes 835592 | tf_op jit(solution)/shard_map/ppermute | solution.py:300
  5.8 5.0 %copy-start.7 = (s32[32,1,4]{0,2,1:T(4,128)S(1)}, s32[32,1,4]{0,2,1:T(4,128)}, u32[]{:S(2)}) copy-start(s32[32,1,4]{0,2,1:T(4,128)} %param.14) | copy-start | bytes 1540
  5.8 5.0 %copy-start.6 = (s32[64,32]{0,1:T(8,128)S(1)}, s32[64,32]{0,1:T(8,128)}, u32[]{:S(2)}) copy-start(s32[64,32]{0,1:T(8,128)} %param.9) | copy-start | bytes 24580
  5.8 5.0 %copy-start.3 = (f32[32,128]{1,0:T(8,128)S(1)}, f32[32,128]{1,0:T(8,128)}, u32[]{:S(2)}) copy-start(f32[32,128]{1,0:T(8,128)} %prior_ref.3) | copy-start | bytes 49156
  6.5 10.9 %collective-permute-start.2 = (bf16[33,64,128]{2,1,0:T(8,128)(2,1)S(1)}, bf16[33,64,128]{2,1,0:T(8,128)(2,1)S(1)}, u32[]{:S(2)}, u32[]{:S(2)}) collective-permute-start(bf16[33,64,128]{2,1,0:T(8,128)(2,1)S(1)} %pack.1), channel_id=1, source_target_pairs={{0,128},{8,40},{16,144},{24,56},{32,160},{40,8},{48,176},{56,24},{... | collective-permute-start | bytes 1622024 | tf_op jit(solution)/shard_map/ppermute | solution.py:312
  9.6 13.8 %collective-permute-start.1 = (bf16[33,64,128]{2,1,0:T(8,128)(2,1)S(1)}, bf16[33,64,128]{2,1,0:T(8,128)(2,1)S(1)}, u32[]{:S(2)}, u32[]{:S(2)}) collective-permute-start(bf16[33,64,128]{2,1,0:T(8,128)(2,1)S(1)} %pack.1), channel_id=1, source_target_pairs={{0,192},{8,56},{16,208},{24,8},{32,224},{40,24},{48,240},{56,40},{... | collective-permute-start | bytes 1622024 | tf_op jit(solution)/shard_map/ppermute | solution.py:312
  10.7 4.3 %collective-permute-start.3 = (s32[32,4]{0,1:T(4,128)S(1)}, s32[32,4]{0,1:T(4,128)S(1)}, u32[]{:S(2)}, u32[]{:S(2)}) collective-permute-start(s32[32,4]{0,1:T(4,128)S(1)} %bitcast.13), channel_id=1, source_target_pairs={{0,8},{8,0},{16,24},{24,16},{32,40},{40,32},{48,56},{56,48},{64,72... | collective-permute-start | bytes 1544 | tf_op jit(solution)/shard_map/ppermute | solution.py:324
  10.8 1.6 %copy-start.5 = (bf16[32,256,128]{2,1,0:T(8,128)(2,1)S(1)}, bf16[32,256,128]{2,1,0:T(8,128)(2,1)}, u32[]{:S(2)}) copy-start(bf16[32,256,128]{2,1,0:T(8,128)(2,1)} %table_ref.5) | copy-start | bytes 6291460
  13.8 12.7 %collective-permute-start.4 = (bf16[33,64,128]{2,1,0:T(8,128)(2,1)S(1)}, bf16[33,64,128]{2,1,0:T(8,128)(2,1)S(1)}, u32[]{:S(2)}, u32[]{:S(2)}) collective-permute-start(bf16[33,64,128]{2,1,0:T(8,128)(2,1)S(1)} %pack.1), channel_id=1, source_target_pairs={{0,64},{8,24},{16,80},{24,40},{32,96},{40,56},{48,112},{56,8},{64,... | collective-permute-start | bytes 1622024 | tf_op jit(solution)/shard_map/ppermute | solution.py:312
  23.5 15.8 %collective-permute-start.8 = (bf16[66,64,128]{2,1,0:T(8,128)(2,1)S(1)}, bf16[66,64,128]{2,1,0:T(8,128)(2,1)S(1)}, u32[]{:S(2)}, u32[]{:S(2)}) collective-permute-start(bf16[66,64,128]{2,1,0:T(8,128)(2,1)S(1)} %constant_dynamic-update-slice_fusion.refs_1_), channel_id=1, source_target_pairs={{0,48},{8,200},{16,0},{24,216},{32,16},{40,232},{48,32},{56,248},{... | collective-permute-start | bytes 3244040 | tf_op jit(solution)/shard_map/ppermute | solution.py:312
  26.7 45.0 %copy-start.4 = (s32[32]{0:T(128)S(1)}, s32[32]{0:T(128)}, u32[]{:S(2)}) copy-start(s32[32]{0:T(128)} %refs_1_.1) | copy-start | bytes 388
  26.7 16.4 %collective-permute-start.5 = (bf16[66,64,128]{2,1,0:T(8,128)(2,1)S(1)}, bf16[66,64,128]{2,1,0:T(8,128)(2,1)S(1)}, u32[]{:S(2)}, u32[]{:S(2)}) collective-permute-start(bf16[66,64,128]{2,1,0:T(8,128)(2,1)S(1)} %pad_maximum_fusion.refs_0_), channel_id=1, source_target_pairs={{0,16},{8,72},{16,32},{24,88},{32,48},{40,104},{48,0},{56,120},{64... | collective-permute-start | bytes 3244040 | tf_op jit(solution)/shard_map/ppermute | solution.py:312
  26.8 27.9 %collective-permute-start.6 = (bf16[66,64,128]{2,1,0:T(8,128)(2,1)S(1)}, bf16[66,64,128]{2,1,0:T(8,128)(2,1)S(1)}, u32[]{:S(2)}, u32[]{:S(2)}) collective-permute-start(bf16[66,64,128]{2,1,0:T(8,128)(2,1)S(1)} %constant_dynamic-update-slice_fusion.refs_1_), channel_id=1, source_target_pairs={{0,16},{8,72},{16,32},{24,88},{32,48},{40,104},{48,0},{56,120},{64... | collective-permute-start | bytes 3244040 | tf_op jit(solution)/shard_map/ppermute | solution.py:312
  27.8 26.9 %collective-permute-start.7 = (bf16[66,64,128]{2,1,0:T(8,128)(2,1)S(1)}, bf16[66,64,128]{2,1,0:T(8,128)(2,1)S(1)}, u32[]{:S(2)}, u32[]{:S(2)}) collective-permute-start(bf16[66,64,128]{2,1,0:T(8,128)(2,1)S(1)} %pad_maximum_fusion.refs_0_), channel_id=1, source_target_pairs={{0,48},{8,200},{16,0},{24,216},{32,16},{40,232},{48,32},{56,248},{... | collective-permute-start | bytes 3244040 | tf_op jit(solution)/shard_map/ppermute | solution.py:312
  39.2 23.2 %collective-permute-start.10 = (bf16[66,64,128]{2,1,0:T(8,128)(2,1)S(1)}, bf16[66,64,128]{2,1,0:T(8,128)(2,1)S(1)}, u32[]{:S(2)}, u32[]{:S(2)}) collective-permute-start(bf16[66,64,128]{2,1,0:T(8,128)(2,1)S(1)} %collective-permute-done.8.refs_5_), channel_id=1, source_target_pairs={{0,48},{8,200},{16,0},{24,216},{32,16},{40,232},{48,32},{56,248},{... | collective-permute-start | bytes 3244040 | tf_op jit(solution)/shard_map/ppermute | solution.py:312
  43.1 23.2 %collective-permute-start.9 = (bf16[66,64,128]{2,1,0:T(8,128)(2,1)S(1)}, bf16[66,64,128]{2,1,0:T(8,128)(2,1)S(1)}, u32[]{:S(2)}, u32[]{:S(2)}) collective-permute-start(bf16[66,64,128]{2,1,0:T(8,128)(2,1)S(1)} %collective-permute-done.5.refs_2_), channel_id=1, source_target_pairs={{0,16},{8,72},{16,32},{24,88},{32,48},{40,104},{48,0},{56,120},{64... | collective-permute-start | bytes 3244040 | tf_op jit(solution)/shard_map/ppermute | solution.py:312
  66.3 5.4 %copy-start = (bf16[32,1,4,128,128]{4,3,2,1,0:T(8,128)(2,1)S(1)}, bf16[32,1,4,128,128]{4,3,2,1,0:T(8,128)(2,1)}, u32[]{:S(2)}) copy-start(bf16[32,1,4,128,128]{4,3,2,1,0:T(8,128)(2,1)} %param.13) | copy-start | bytes 12582916
  68.9 2.8 %collective-permute-start.11 = (bf16[65,64,128]{2,1,0:T(8,128)(2,1)S(1)}, bf16[65,64,128]{2,1,0:T(8,128)(2,1)S(1)}, u32[]{:S(2)}, u32[]{:S(2)}) collective-permute-start(bf16[65,64,128]{2,1,0:T(8,128)(2,1)S(1)} %get-tuple-element.31), channel_id=1, source_target_pairs={{0,8},{8,0},{16,24},{24,16},{32,40},{40,32},{48,56},{56,48},{64,72... | collective-permute-start | bytes 3194888 | tf_op jit(solution)/shard_map/ppermute | solution.py:351
  76.1 1.3 collective-permute-start.12
  77.5 5.5 %collective-permute-start.15 = (f32[64,128]{1,0:T(8,128)S(1)}, f32[64,128]{1,0:T(8,128)S(1)}, u32[]{:S(2)}, u32[]{:S(2)}) collective-permute-start(f32[64,128]{1,0:T(8,128)S(1)} %merge_core.1.refs_0_), channel_id=1, source_target_pairs={{0,128},{8,40},{16,144},{24,56},{32,160},{40,8},{48,176},{56,24},{... | collective-permute-start | bytes 98312 | tf_op jit(solution)/shard_map/ppermute | solution.py:371
  79.6 3.9 %collective-permute-start.14 = (f32[64,128]{1,0:T(8,128)S(1)}, f32[64,128]{1,0:T(8,128)S(1)}, u32[]{:S(2)}, u32[]{:S(2)}) collective-permute-start(f32[64,128]{1,0:T(8,128)S(1)} %merge_core.1.refs_0_), channel_id=1, source_target_pairs={{0,192},{8,56},{16,208},{24,8},{32,224},{40,24},{48,240},{56,40},{... | collective-permute-start | bytes 98312 | tf_op jit(solution)/shard_map/ppermute | solution.py:371
  81.6 5.1 %collective-permute-start.13 = (f32[64,128]{1,0:T(8,128)S(1)}, f32[64,128]{1,0:T(8,128)S(1)}, u32[]{:S(2)}, u32[]{:S(2)}) collective-permute-start(f32[64,128]{1,0:T(8,128)S(1)} %merge_core.1.refs_0_), channel_id=1, source_target_pairs={{0,64},{8,24},{16,80},{24,40},{32,96},{40,56},{48,112},{56,8},{64,... | collective-permute-start | bytes 98312 | tf_op jit(solution)/shard_map/ppermute | solution.py:371
  86.9 5.5 %collective-permute-start.18 = (f32[64,128]{1,0:T(8,128)S(1)}, f32[64,128]{1,0:T(8,128)S(1)}, u32[]{:S(2)}, u32[]{:S(2)}) collective-permute-start(f32[64,128]{1,0:T(8,128)S(1)} %merge_a.1.refs_2_), channel_id=1, source_target_pairs={{0,32},{8,136},{16,48},{24,152},{32,0},{40,168},{48,16},{56,184},{... | collective-permute-start | bytes 98312 | tf_op jit(solution)/shard_map/ppermute | solution.py:371
  87.0 5.4 %collective-permute-start.17 = (f32[64,128]{1,0:T(8,128)S(1)}, f32[64,128]{1,0:T(8,128)S(1)}, u32[]{:S(2)}, u32[]{:S(2)}) collective-permute-start(f32[64,128]{1,0:T(8,128)S(1)} %merge_a.1.refs_2_), channel_id=1, source_target_pairs={{0,48},{8,200},{16,0},{24,216},{32,16},{40,232},{48,32},{56,248},{... | collective-permute-start | bytes 98312 | tf_op jit(solution)/shard_map/ppermute | solution.py:371
  88.4 5.1 %collective-permute-start.16 = (f32[64,128]{1,0:T(8,128)S(1)}, f32[64,128]{1,0:T(8,128)S(1)}, u32[]{:S(2)}, u32[]{:S(2)}) collective-permute-start(f32[64,128]{1,0:T(8,128)S(1)} %merge_a.1.refs_2_), channel_id=1, source_target_pairs={{0,16},{8,72},{16,32},{24,88},{32,48},{40,104},{48,0},{56,120},{64... | collective-permute-start | bytes 98312 | tf_op jit(solution)/shard_map/ppermute | solution.py:371
  96.2 6.4 %collective-permute-start.19 = (bf16[16,4,16,128]{3,2,1,0:T(8,128)(2,1)S(1)}, bf16[16,4,16,128]{3,2,1,0:T(8,128)(2,1)S(1)}, u32[]{:S(2)}, u32[]{:S(2)}) collective-permute-start(bf16[16,4,16,128]{3,2,1,0:T(8,128)(2,1)S(1)} %get-tuple-element.43), channel_id=1, source_target_pairs={{0,1},{1,2},{2,3},{3,4},{4,5},{5,6},{6,7},{7,0},{8,9},{9,10},{10,1... | collective-permute-start | bytes 786440 | tf_op jit(solution)/shard_map/ppermute | solution.py:397
  98.2 6.4 %collective-permute-start.20 = (bf16[16,4,16,128]{3,2,1,0:T(8,128)(2,1)S(1)}, bf16[16,4,16,128]{3,2,1,0:T(8,128)(2,1)S(1)}, u32[]{:S(2)}, u32[]{:S(2)}) collective-permute-start(bf16[16,4,16,128]{3,2,1,0:T(8,128)(2,1)S(1)} %get-tuple-element.44), channel_id=1, source_target_pairs={{0,7},{1,0},{2,1},{3,2},{4,3},{5,4},{6,5},{7,6},{8,15},{9,8},{10,9... | collective-permute-start | bytes 786440 | tf_op jit(solution)/shard_map/ppermute | solution.py:397
  104.7 10.4 %collective-permute-start.21 = (bf16[32,4,16,128]{3,2,1,0:T(8,128)(2,1)S(1)}, bf16[32,4,16,128]{3,2,1,0:T(8,128)(2,1)S(1)}, u32[]{:S(2)}, u32[]{:S(2)}) collective-permute-start(bf16[32,4,16,128]{3,2,1,0:T(8,128)(2,1)S(1)} %get-tuple-element.45), channel_id=1, source_target_pairs={{0,1},{1,2},{2,3},{3,4},{4,5},{5,6},{6,7},{7,0},{8,9},{9,10},{10,1... | collective-permute-start | bytes 1572872 | tf_op jit(solution)/shard_map/ppermute | solution.py:397
  107.8 12.4 %collective-permute-start.22 = (bf16[32,4,16,128]{3,2,1,0:T(8,128)(2,1)S(1)}, bf16[32,4,16,128]{3,2,1,0:T(8,128)(2,1)S(1)}, u32[]{:S(2)}, u32[]{:S(2)}) collective-permute-start(bf16[32,4,16,128]{3,2,1,0:T(8,128)(2,1)S(1)} %get-tuple-element.46), channel_id=1, source_target_pairs={{0,7},{1,0},{2,1},{3,2},{4,3},{5,4},{6,5},{7,6},{8,15},{9,8},{10,9... | collective-permute-start | bytes 1572872 | tf_op jit(solution)/shard_map/ppermute | solution.py:397
  120.4 11.9 %collective-permute-start.23 = (bf16[32,4,16,128]{3,2,1,0:T(8,128)(2,1)S(1)}, bf16[32,4,16,128]{3,2,1,0:T(8,128)(2,1)S(1)}, u32[]{:S(2)}, u32[]{:S(2)}) collective-permute-start(bf16[32,4,16,128]{3,2,1,0:T(8,128)(2,1)S(1)} %get-tuple-element.47), channel_id=1, source_target_pairs={{0,1},{1,2},{2,3},{3,4},{4,5},{5,6},{6,7},{7,0},{8,9},{9,10},{10,1... | collective-permute-start | bytes 1572872 | tf_op jit(solution)/shard_map/ppermute | solution.py:397
  122.8 12.3 %collective-permute-start.24 = (bf16[32,4,16,128]{3,2,1,0:T(8,128)(2,1)S(1)}, bf16[32,4,16,128]{3,2,1,0:T(8,128)(2,1)S(1)}, u32[]{:S(2)}, u32[]{:S(2)}) collective-permute-start(bf16[32,4,16,128]{3,2,1,0:T(8,128)(2,1)S(1)} %get-tuple-element.48), channel_id=1, source_target_pairs={{0,7},{1,0},{2,1},{3,2},{4,3},{5,4},{6,5},{7,6},{8,15},{9,8},{10,9... | collective-permute-start | bytes 1572872 | tf_op jit(solution)/shard_map/ppermute | solution.py:397
  135.3 9.3 %collective-permute-start.25 = (bf16[32,4,16,128]{3,2,1,0:T(8,128)(2,1)S(1)}, bf16[32,4,16,128]{3,2,1,0:T(8,128)(2,1)S(1)}, u32[]{:S(2)}, u32[]{:S(2)}) collective-permute-start(bf16[32,4,16,128]{3,2,1,0:T(8,128)(2,1)S(1)} %get-tuple-element.49), channel_id=1, source_target_pairs={{0,1},{1,2},{2,3},{3,4},{4,5},{5,6},{6,7},{7,0},{8,9},{9,10},{10,1... | collective-permute-start | bytes 1572872 | tf_op jit(solution)/shard_map/ppermute | solution.py:397
  136.4 9.2 %collective-permute-start.26 = (bf16[32,4,16,128]{3,2,1,0:T(8,128)(2,1)S(1)}, bf16[32,4,16,128]{3,2,1,0:T(8,128)(2,1)S(1)}, u32[]{:S(2)}, u32[]{:S(2)}) collective-permute-start(bf16[32,4,16,128]{3,2,1,0:T(8,128)(2,1)S(1)} %get-tuple-element.50), channel_id=1, source_target_pairs={{0,7},{1,0},{2,1},{3,2},{4,3},{5,4},{6,5},{7,6},{8,15},{9,8},{10,9... | collective-permute-start | bytes 1572872 | tf_op jit(solution)/shard_map/ppermute | solution.py:397

commit v4 on v3

--- a/solution.py
+++ b/solution.py
@@ -35,7 +35,7 @@
 
 def child_kernel(half_ref, values_ref, table_ref, out_ref, inputs):
     half = half_ref[0]
-    values = values_ref[...]
+    values = values_ref[...].T
     values = jnp.where(half == 0, values[:, :HALF], values[:, HALF:])
     for k in range(HALF):
         inputs[k] = look_up(values[:, k : k + 1], table_ref[half * HALF + k])
@@ -63,7 +63,7 @@
 
 
 def parent_kernel(values_ref, table_ref, prior_ref, out_ref):
-    values = values_ref[...]
+    values = values_ref[...].T
     for p in range(P_SIZE):
         out_ref[p] = look_up(values[:, p : p + 1], table_ref[p]) + prior_ref[p : p + 1, :]
 
@@ -80,9 +80,31 @@
 )
 
 
-def pick_kernel(code_ref, *refs):
-    sources = refs[: len(PLACES)]
-    out_refs, pool, powers = refs[len(PLACES) : -2], refs[-2], refs[-1]
+def codes_of(place_ref, columns_ref, k):
+    core = place_ref[0]
+    codes = []
+    for z in range(NZ):
+        column = columns_ref[z, core * HALF + k]
+        x, y = lax.shift_right_logical(column, 3), lax.shift_right_logical(column, 1) & 3
+        a = (jnp.where(core == 0, x, y) - place_ref[2]) & 3
+        b = (jnp.where(core == 0, y, x) - place_ref[3]) & 3
+        codes.append((a * 4 + b) * 2 + (column & 1))
+    return codes
+
+
+def pick_child(codes, k, pool, powers):
+    power = [powers[code][:, k : k + 1] for code in codes]
+    top = jnp.maximum(jnp.maximum(power[0], power[1]), jnp.maximum(power[2], power[3]))
+    blocks = []
+    for code, mine in zip(codes, power):
+        factor = jnp.broadcast_to(jnp.exp2(mine - top), (S_LOC, BLK))
+        block = pool[lax.shift_right_logical(code, 1) * PIECE + (code & 1) * HALF + k]
+        blocks.append((block.astype(jnp.float32) * factor).astype(jnp.bfloat16))
+    return blocks, top
+
+
+def pick_other_kernel(place_ref, columns_ref, *refs):
+    sources, (out_ref, pool, powers) = refs[: len(PLACES)], refs[len(PLACES) :]
 
     def collect(k, carry):
         for source, places in zip(sources, PLACES):
@@ -96,20 +118,37 @@
         powers[2 * piece] = both
         powers[2 * piece + 1] = pltpu.roll(both, BLK - HALF, 1)
     lanes = lane_of((S_LOC, BLK))
-    tops = [jnp.zeros((S_LOC, BLK), jnp.float32)] * 2
-    for k in range(HALF):
-        for row, out_ref in enumerate(out_refs):
-            codes = [code_ref[row * C * NZ // 2 + k * NZ + z] for z in range(NZ)]
-            power = [powers[code][:, k : k + 1] for code in codes]
-            top = jnp.maximum(jnp.maximum(power[0], power[1]), jnp.maximum(power[2], power[3]))
-            tops[row] = jnp.where(lanes == k, top, tops[row])
-            for z in range(NZ):
-                code = codes[z]
-                factor = jnp.broadcast_to(jnp.exp2(power[z] - top), (S_LOC, BLK))
-                block = pool[(code // 2) * PIECE + (code % 2) * HALF + k]
-                out_ref[k * NZ + z] = (block.astype(jnp.float32) * factor).astype(jnp.bfloat16)
-    for row, out_ref in enumerate(out_refs):
-        out_ref[HALF * NZ] = tops[row].astype(jnp.bfloat16)
+    tops = jnp.zeros((S_LOC, BLK), jnp.float32)
+    for k in range(HALF):
+        blocks, top = pick_child(codes_of(place_ref, columns_ref, k), k, pool, powers)
+        tops = jnp.where(lanes == k, top, tops)
+        for z in range(NZ):
+            out_ref[k * NZ + z] = blocks[z]
+    out_ref[HALF * NZ] = tops.astype(jnp.bfloat16)
+
+
+def row_sum(blocks, weights_ref, child):
+    total = None
+    for z in range(0, NZ, 2):
+        picked = jnp.concatenate(blocks[z : z + 2], axis=1)
+        wide = jnp.concatenate([weights_ref[child, z], weights_ref[child, z + 1]], axis=1)
+        term = lax.dot_general(
+            picked, wide, (((1,), (1,)), ((), ())), preferred_element_type=jnp.float32
+        )
+        total = term if total is None else total + term
+    return total
+
+
+def own_sums_kernel(place_ref, columns_ref, pool, powers, weights_ref, out_ref, sums_ref):
+    lanes = lane_of((S_LOC, BLK))
+    tops = jnp.zeros((S_LOC, BLK), jnp.float32)
+    for k in range(HALF):
+        blocks, top = pick_child(codes_of(place_ref, columns_ref, k), k, pool, powers)
+        tops = jnp.where(lanes == k, top, tops)
+        for z in range(NZ):
+            out_ref[k * NZ + z] = blocks[z]
+        sums_ref[k] = row_sum(blocks, weights_ref, child_at(place_ref[0], 0, k))
+    out_ref[HALF * NZ] = tops.astype(jnp.bfloat16)
 
 
 def child_at(core, half, k):
@@ -117,24 +156,15 @@
 
 
 def sums_kernel(
-    core_ref, map_ref, own_ref, other_ref, weights_ref, parent_ref, prior_ref,
+    core_ref, map_ref, own_ref, other_ref, own_sums_ref, weights_ref, parent_ref, prior_ref,
     stats_ref, root_ref, sums_ref,
 ):
     core = core_ref[0]
     root_ref[...] = parent_ref[...]
-    for half, picked_ref in enumerate((own_ref, other_ref)):
-        tops = picked_ref[HALF * NZ].astype(jnp.float32) * LN2
-        for k in range(HALF):
-            child = child_at(core, half, k)
-            row_sums = None
-            for z in range(0, NZ, 2):
-                picked = jnp.concatenate([picked_ref[k * NZ + z], picked_ref[k * NZ + z + 1]], axis=1)
-                wide = jnp.concatenate([weights_ref[child, z], weights_ref[child, z + 1]], axis=1)
-                term = lax.dot_general(
-                    picked, wide, (((1,), (1,)), ((), ())), preferred_element_type=jnp.float32
-                )
-                row_sums = term if row_sums is None else row_sums + term
-            sums_ref[half * HALF + k] = row_sums
+    for k in range(HALF):
+        sums_ref[k] = own_sums_ref[k]
+        blocks = [other_ref[k * NZ + z] for z in range(NZ)]
+        sums_ref[HALF + k] = row_sum(blocks, weights_ref, child_at(core, 1, k))
     for half, picked_ref in enumerate((own_ref, other_ref)):
         tops = picked_ref[HALF * NZ].astype(jnp.float32) * LN2
         for k in range(HALF):
@@ -283,7 +313,17 @@
     weights = weights[:, 0]
     region = lax.axis_index("region").astype(i32)
     core = lax.rem(region, 2)
-    place = jnp.stack([core, lax.axis_index("batch").astype(i32)])
+    x, y = lax.shift_right_logical(region, 3), lax.shift_right_logical(region, 1) & 3
+    place = jnp.stack(
+        [
+            core,
+            lax.axis_index("batch").astype(i32),
+            jnp.where(core == 0, x, y),
+            jnp.where(core == 0, y, x),
+        ]
+    )
+
+    columns = block_cols[:, 0].T
 
     def scores(half):
         return pl.pallas_call(
@@ -295,9 +335,11 @@
             compiler_params=params(16),
             cost_estimate=cost(1 << 27, 2 << 20, 1 << 20),
             name="child_scores",
-        )(half.reshape(1), child_values, child_logits)
-
-    given = lax.ppermute(scores(1 - core), "region", SWAP)
+        )(half.reshape(1), child_values.T, child_logits)
+
+    given, other_columns = lax.optimization_barrier(
+        (lax.ppermute(scores(1 - core), "region", SWAP), lax.ppermute(columns, "region", SWAP))
+    )
     kept = scores(core)
     own = pl.pallas_call(
         pack_kernel,
@@ -319,36 +361,40 @@
         compiler_params=params(12),
         cost_estimate=cost(1 << 28, 3 << 20, 1 << 21),
         name="parent_scores",
-    )(parent_values, parent_logits, prior_logits)
-    columns = block_cols[:, 0]
-    columns = jnp.stack([columns, lax.ppermute(columns, "region", SWAP)])
-    columns = lax.dynamic_slice_in_dim(columns, core * HALF, HALF, axis=1).reshape(-1)
-    x, y = columns // 8 - region // 8 + 4, columns // 2 % 4 - region // 2 % 4 + 4
-    x, y = x % 4, y % 4
-    code = jnp.where(core == 0, x * 4 + y, y * 4 + x) * 2 + columns % 2
-
-    a1, a3, a2 = send(own, 1, 0), send(own, -1, 0), send(own, 2, 0)
+    )(parent_values.T, parent_logits, prior_logits)
+    a1, a3 = send(own, 1, 0), send(own, -1, 0)
+    a1, own = lax.optimization_barrier((a1, own))
+    a2 = send(own, 2, 0)
     near = jnp.concatenate([own, a1])
     near_up, near_down = send(near, 0, 1), send(near, 0, -1)
-    a3, a2, parent_in, code = lax.optimization_barrier((a3, a2, parent_in, code))
     far = jnp.concatenate([a3, a2])
     far_up, far_down = send(far, 0, 1), send(far, 0, -1)
     next_up = send(near_up, 0, 1)
     next_down = send(far_down, 0, -1)
-    picked, for_other = pl.pallas_call(
-        pick_kernel,
-        out_shape=(shape((HALF * NZ + 1, S_LOC, BLK), bf16),) * 2,
-        in_specs=[SMEM] + [VMEM] * len(PLACES),
-        out_specs=(VMEM, VMEM),
-        scratch_shapes=[
-            pltpu.VMEM((16 * PIECE, S_LOC, BLK), bf16),
-            pltpu.VMEM((32, S_LOC, BLK), f32),
-        ],
+    slots = shape((HALF * NZ + 1, S_LOC, BLK), bf16)
+    for_other, pool, powers = pl.pallas_call(
+        pick_other_kernel,
+        out_shape=(
+            slots,
+            shape((16 * PIECE, S_LOC, BLK), bf16),
+            shape((32, S_LOC, BLK), f32),
+        ),
+        in_specs=[SMEM, SMEM] + [VMEM] * len(PLACES),
+        out_specs=(VMEM, VMEM, VMEM),
         compiler_params=params(22),
         cost_estimate=cost(1 << 22, 20 << 20, 1 << 20),
-        name="pick",
-    )(code, near, far, near_up, far_up, near_down, far_down, next_up, next_down)
+        name="pick_other",
+    )(place, other_columns, near, far, near_up, far_up, near_down, far_down, next_up, next_down)
     other = lax.ppermute(for_other, "region", SWAP)
+    picked, own_sums = pl.pallas_call(
+        own_sums_kernel,
+        out_shape=(slots, shape((HALF, S_LOC, BLK), f32)),
+        in_specs=[SMEM, SMEM] + [VMEM] * 3,
+        out_specs=(VMEM, VMEM),
+        compiler_params=params(20),
+        cost_estimate=cost(1 << 28, 8 << 20, 1 << 19),
+        name="own_sums",
+    )(place, columns, pool, powers, weights)
     stats, root, sums = pl.pallas_call(
         sums_kernel,
         out_shape=(
@@ -356,12 +402,12 @@
             shape((P_SIZE, S_LOC, BLK), f32),
             shape((C, S_LOC, BLK), f32),
         ),
-        in_specs=[SMEM, SMEM] + [VMEM] * 5,
+        in_specs=[SMEM, SMEM] + [VMEM] * 6,
         out_specs=(VMEM,) * 3,
         compiler_params=params(16),
         cost_estimate=cost(1 << 29, 12 << 20, 1 << 20),
         name="row_sums",
-    )(place, parent_map, picked, other, weights, parent_in, prior_logits)
+    )(place, parent_map, picked, other, own_sums, weights, parent_in, prior_logits)
 
     for axis, pairs in (
         ("core", (SWAP,)),

time: 148 us -> 155 us (1.047)
  starting transfers between devices: 32 us -> 36.6 us
  waiting for transfers between devices: 92.3 us -> 96.8 us
  local copies, waits for them, and re-layouts: 5.36 us -> 3.18 us
    ppermute x9, waiting for transfers between devices: 40.5 us -> 49.6 us  [send(): return lax.ppermute(value, 'region', along(a, b))]
    ppermute x7, starting transfers between devices: 6.55 us -> 9.76 us  [body(): others = [lax.ppermute(stats, 'region', p) for p in pairs]]
    ppermute x1, waiting for transfers between devices: 2.67 us -> 0.01 us  [body(): other = lax.ppermute(for_other, 'region', SWAP)]
    unnamed x19 -> x22, local copies, waits for them, and re-layouts: 4.46 us -> 2.41 us
    pallas_call x1 -> x2, Pallas kernels: 2.64 us -> 3.7 us  [the longest x1 2.09 us: body(): pl.pallas_call(pick_other_kernel, out_shape=(slots, shape((16 * PIECE, S_...]
  transfers between devices with their start and end apart: 27 -> 27, of which waited for: 22 -> 19; matrix products, arithmetic and copies ran while one was open for 1% -> 1% of each run, Pallas kernels for 2% -> 3%
where the time goes in v4:
time: 155 us
  waiting for transfers between devices  96.8 us (62%)
  starting transfers between devices  36.6 us (24%)
  Pallas kernels  17.7 us (11%)
  local copies, waits for them, and re-layouts  3.18 us (2%)
    ppermute x9, waiting for transfers between devices, send(): return lax.ppermute(value, 'region', along(a, b))  49.6 us
    ppermute x4, waiting for transfers between devices, ring(): lax.ppermute(up, 'batch', shift(1))  27.4 us
    ppermute x9, starting transfers between devices, send(): return lax.ppermute(value, 'region', along(a, b))  16.5 us
    ppermute x4, waiting for transfers between devices, ring(): lax.ppermute(down, 'batch', shift(-1))  10.1 us
    ppermute x7, starting transfers between devices, body(): others = [lax.ppermute(stats, 'region', p) for p in pairs]  9.76 us
    ppermute x7, waiting for transfers between devices, body(): others = [lax.ppermute(stats, 'region', p) for p in pairs]  9.66 us
    ppermute x4, starting transfers between devices, ring(): lax.ppermute(up, 'batch', shift(1))  9.16 us
    pallas_call x1, Pallas kernels, body(): pl.pallas_call(sums_kernel, out_shape=(shape((S_LOC, BLK), f32), shape((P...  4.49 us
  transfers between devices with their start and end apart: 27, of which 19 were waited for; matrix products, arithmetic and copies ran while one was open for 1% of the time, Pallas kernels for 3%

profile of v4, /device:TPU:32, one launch (start us, length us, event | category | flops | bytes accessed | tf_op | source)
XLA Modules:
  0.0 155.2 jit_solution(14354622243415801630)
XLA Ops:
  0.6 1.6 %copy-done.1 = bf16[32,256,128]{2,1,0:T(8,128)(2,1)S(1)} copy-done((bf16[32,256,128]{2,1,0:T(8,128)(2,1)S(1)}, bf16[32,256,128]{2,1,0:T(8,128)(2,1)}, u32[]{:S(2)}) %copy-start.1) | copy-done | bytes 2097176
  2.2 0.7 copy-done.3
  3.0 1.2 child_scores.2
  4.9 1.2 child_scores.3.own_ref
  6.1 0.6 pack.1
  6.7 1.5 collective-permute-start.2
  8.3 1.7 %collective-permute-start.3 = (bf16[33,64,128]{2,1,0:T(8,128)(2,1)S(1)}, bf16[33,64,128]{2,1,0:T(8,128)(2,1)S(1)}, u32[]{:S(2)}, u32[]{:S(2)}) collective-permute-start(bf16[33,64,128]{2,1,0:T(8,128)(2,1)S(1)} %pack.1), channel_id=1, source_target_pairs={{0,192},{8,56},{16,208},{24,8},{32,224},{40,24},{48,240},{56,40},{... | collective-permute-start | bytes 1622024 | tf_op jit(solution)/shard_map/ppermute | solution.py:354
  10.0 7.3 %collective-permute-done.2 = bf16[33,64,128]{2,1,0:T(8,128)(2,1)S(1)} collective-permute-done((bf16[33,64,128]{2,1,0:T(8,128)(2,1)S(1)}, bf16[33,64,128]{2,1,0:T(8,128)(2,1)S(1)}, u32[]{:S(2)}, u32[]{:S(2)}) %collective-permute-start.2) | collective-permute-done | bytes 540704 | tf_op jit(solution)/shard_map/ppermute | solution.py:354
  17.4 1.8 %collective-permute-start.4 = (bf16[33,64,128]{2,1,0:T(8,128)(2,1)S(1)}, bf16[33,64,128]{2,1,0:T(8,128)(2,1)S(1)}, u32[]{:S(2)}, u32[]{:S(2)}) collective-permute-start(bf16[33,64,128]{2,1,0:T(8,128)(2,1)S(1)} %pack.1), channel_id=1, source_target_pairs={{0,128},{8,40},{16,144},{24,56},{32,160},{40,8},{48,176},{56,24},{... | collective-permute-start | bytes 1622024 | tf_op jit(solution)/shard_map/ppermute | solution.py:354
  19.3 1.7 %collective-permute-start.5 = (bf16[66,64,128]{2,1,0:T(8,128)(2,1)S(1)}, bf16[66,64,128]{2,1,0:T(8,128)(2,1)S(1)}, u32[]{:S(2)}, u32[]{:S(2)}) collective-permute-start(bf16[66,64,128]{2,1,0:T(8,128)(2,1)S(1)} %constant_dynamic-update-slice_fusion.refs_0_), channel_id=1, source_target_pairs={{0,16},{8,72},{16,32},{24,88},{32,48},{40,104},{48,0},{56,120},{64... | collective-permute-start | bytes 3244040 | tf_op jit(solution)/shard_map/ppermute | solution.py:354
  21.0 12.2 %collective-permute-done.4 = bf16[33,64,128]{2,1,0:T(8,128)(2,1)S(1)} collective-permute-done((bf16[33,64,128]{2,1,0:T(8,128)(2,1)S(1)}, bf16[33,64,128]{2,1,0:T(8,128)(2,1)S(1)}, u32[]{:S(2)}, u32[]{:S(2)}) %collective-permute-start.4) | collective-permute-done | bytes 540704 | tf_op jit(solution)/shard_map/ppermute | solution.py:354
  33.3 4.0 %collective-permute-start.8 = (bf16[66,64,128]{2,1,0:T(8,128)(2,1)S(1)}, bf16[66,64,128]{2,1,0:T(8,128)(2,1)S(1)}, u32[]{:S(2)}, u32[]{:S(2)}) collective-permute-start(bf16[66,64,128]{2,1,0:T(8,128)(2,1)S(1)} %constant_dynamic-update-slice_fusion.2.refs_1_), channel_id=1, source_target_pairs={{0,48},{8,200},{16,0},{24,216},{32,16},{40,232},{48,32},{56,248},{... | collective-permute-start | bytes 3244040 | tf_op jit(solution)/shard_map/ppermute | solution.py:354
  37.2 0.7 collective-permute-start.7
  37.9 1.3 collective-permute-start.6
  39.3 10.6 %collective-permute-done.8.refs_5_ = bf16[66,64,128]{2,1,0:T(8,128)(2,1)S(1)} collective-permute-done((bf16[66,64,128]{2,1,0:T(8,128)(2,1)S(1)}, bf16[66,64,128]{2,1,0:T(8,128)(2,1)S(1)}, u32[]{:S(2)}, u32[]{:S(2)}) %collective-permute-start.8) | collective-permute-done | bytes 1081376 | tf_op jit(solution)/shard_map/ppermute | solution.py:354
  49.9 3.7 %collective-permute-start.10 = (bf16[66,64,128]{2,1,0:T(8,128)(2,1)S(1)}, bf16[66,64,128]{2,1,0:T(8,128)(2,1)S(1)}, u32[]{:S(2)}, u32[]{:S(2)}) collective-permute-start(bf16[66,64,128]{2,1,0:T(8,128)(2,1)S(1)} %collective-permute-done.8.refs_5_), channel_id=1, source_target_pairs={{0,48},{8,200},{16,0},{24,216},{32,16},{40,232},{48,32},{56,248},{... | collective-permute-start | bytes 3244040 | tf_op jit(solution)/shard_map/ppermute | solution.py:354
  53.6 7.9 %collective-permute-done.7.refs_4_ = bf16[66,64,128]{2,1,0:T(8,128)(2,1)S(1)} collective-permute-done((bf16[66,64,128]{2,1,0:T(8,128)(2,1)S(1)}, bf16[66,64,128]{2,1,0:T(8,128)(2,1)S(1)}, u32[]{:S(2)}, u32[]{:S(2)}) %collective-permute-start.7) | collective-permute-done | bytes 1081376 | tf_op jit(solution)/shard_map/ppermute | solution.py:354
  61.5 4.4 %collective-permute-done.9.refs_6_ = bf16[66,64,128]{2,1,0:T(8,128)(2,1)S(1)} collective-permute-done((bf16[66,64,128]{2,1,0:T(8,128)(2,1)S(1)}, bf16[66,64,128]{2,1,0:T(8,128)(2,1)S(1)}, u32[]{:S(2)}, u32[]{:S(2)}) %collective-permute-start.9) | collective-permute-done | bytes 1081376 | tf_op jit(solution)/shard_map/ppermute | solution.py:354
  65.9 7.2 %collective-permute-done.10.refs_7_ = bf16[66,64,128]{2,1,0:T(8,128)(2,1)S(1)} collective-permute-done((bf16[66,64,128]{2,1,0:T(8,128)(2,1)S(1)}, bf16[66,64,128]{2,1,0:T(8,128)(2,1)S(1)}, u32[]{:S(2)}, u32[]{:S(2)}) %collective-permute-start.10) | collective-permute-done | bytes 1081376 | tf_op jit(solution)/shard_map/ppermute | solution.py:354
  73.1 2.1 %pick_other.1 = (bf16[65,64,128]{2,1,0:T(8,128)(2,1)S(1)}, bf16[528,64,128]{2,1,0:T(8,128)(2,1)S(1)}, f32[32,64,128]{2,1,0:T(8,128)S(1)}) custom-call(s32[4]{0:T(128)S(1)} %pad_add_fusion.core_ref.place_ref.refs_0_, s32[4,32]{1,0:T(4,128)S(1)} %collective-permute-done.1.columns_ref, bf16[66,64,128]{2,1,0:T(8,128)(2,1)S(1)} %constant_dynamic-update-slice_fusion.refs_0_, ...), custom_call_target="tpu_custom_call" | custom-call | flops 4194304 | bytes 20971520 | tf_op jit(solution)/shard_map/pick_other/pallas_call | solution.py:375
  75.5 1.4 parent_scores.1.parent_ref
  76.9 1.6 %own_sums.1 = (bf16[65,64,128]{2,1,0:T(8,128)(2,1)S(1)}, f32[16,64,128]{2,1,0:T(8,128)S(1)}) custom-call(s32[4]{0:T(128)S(1)} %pad_add_fusion.core_ref.place_ref.refs_0_, s32[4,32]{1,0:T(4,128)S(1)} %bitcast.20, bf16[528,64,128]{2,1,0:T(8,128)(2,1)S(1)} %get-tuple-element.34.pool, f32[32,64,128]{2,1,0:T(8,128)S(1)} %get-tuple-element.35.powers, ...), custom_call_target="tpu_custom_call" | custom-call | flops 268435456 | bytes 8388608 | tf_op jit(solution)/shard_map/own_sums/pallas_call | solution.py:389
  78.6 4.5 %row_sums.1 = (f32[64,128]{1,0:T(8,128)S(1)}, f32[32,64,128]{2,1,0:T(8,128)S(1)}, f32[32,64,128]{2,1,0:T(8,128)S(1)}) custom-call(s32[4]{0:T(128)S(1)} %pad_add_fusion.core_ref.place_ref.refs_0_, s32[32]{0:T(128)S(1)} %copy-done.7, bf16[65,64,128]{2,1,0:T(8,128)(2,1)S(1)} %get-tuple-element.36.own_ref.refs_8_, ...), custom_call_target="tpu_custom_call" | custom-call | flops 536870912 | bytes 12582912 | tf_op jit(solution)/shard_map/row_sums/pallas_call | solution.py:398
  83.1 0.6 collective-permute-start.12
  83.6 0.9 collective-permute-done.12.refs_1_
  84.7 3.2 %collective-permute-start.14 = (f32[64,128]{1,0:T(8,128)S(1)}, f32[64,128]{1,0:T(8,128)S(1)}, u32[]{:S(2)}, u32[]{:S(2)}) collective-permute-start(f32[64,128]{1,0:T(8,128)S(1)} %merge_core.1.refs_0_), channel_id=1, source_target_pairs={{0,192},{8,56},{16,208},{24,8},{32,224},{40,24},{48,240},{56,40},{... | collective-permute-start | bytes 98312 | tf_op jit(solution)/shard_map/ppermute | solution.py:417
  87.9 0.7 collective-permute-start.15
  88.6 1.2 collective-permute-done.13.refs_1_
  89.8 3.5 %collective-permute-done.15.refs_3_ = f32[64,128]{1,0:T(8,128)S(1)} collective-permute-done((f32[64,128]{1,0:T(8,128)S(1)}, f32[64,128]{1,0:T(8,128)S(1)}, u32[]{:S(2)}, u32[]{:S(2)}) %collective-permute-start.15) | collective-permute-done | bytes 32800 | tf_op jit(solution)/shard_map/ppermute | solution.py:417
  93.5 1.1 collective-permute-start.16
  94.6 2.7 %collective-permute-start.17 = (f32[64,128]{1,0:T(8,128)S(1)}, f32[64,128]{1,0:T(8,128)S(1)}, u32[]{:S(2)}, u32[]{:S(2)}) collective-permute-start(f32[64,128]{1,0:T(8,128)S(1)} %merge_a.1.refs_2_), channel_id=1, source_target_pairs={{0,48},{8,200},{16,0},{24,216},{32,16},{40,232},{48,32},{56,248},{... | collective-permute-start | bytes 98312 | tf_op jit(solution)/shard_map/ppermute | solution.py:417
  97.3 1.4 collective-permute-start.18
  99.1 3.6 %collective-permute-done.18.refs_5_ = f32[64,128]{1,0:T(8,128)S(1)} collective-permute-done((f32[64,128]{1,0:T(8,128)S(1)}, f32[64,128]{1,0:T(8,128)S(1)}, u32[]{:S(2)}, u32[]{:S(2)}) %collective-permute-start.18) | collective-permute-done | bytes 32800 | tf_op jit(solution)/shard_map/ppermute | solution.py:417
  102.7 2.6 %counts.1 = (bf16[32,4,16,128]{3,2,1,0:T(8,128)(2,1)S(1)}, bf16[32,4,16,128]{3,2,1,0:T(8,128)(2,1)S(1)}, bf16[32,4,16,128]{3,2,1,0:T(8,128)(2,1)S(1)}, bf16[32,4...) custom-call(s32[4]{0:T(128)S(1)} %pad_add_fusion.core_ref.place_ref., ...), custom_call_target="tpu_custom_call" | custom-call | flops 536870912 | bytes 13631488 | tf_op jit(solution)/shard_map/counts/pallas_call | solution.py:430
  105.4 2.0 %collective-permute-start.19 = (bf16[16,4,16,128]{3,2,1,0:T(8,128)(2,1)S(1)}, bf16[16,4,16,128]{3,2,1,0:T(8,128)(2,1)S(1)}, u32[]{:S(2)}, u32[]{:S(2)}) collective-permute-start(bf16[16,4,16,128]{3,2,1,0:T(8,128)(2,1)S(1)} %get-tuple-element.49), channel_id=1, source_target_pairs={{0,1},{1,2},{2,3},{3,4},{4,5},{5,6},{6,7},{7,0},{8,9},{9,10},{10,1... | collective-permute-start | bytes 786440 | tf_op jit(solution)/shard_map/ppermute | solution.py:443
  107.5 4.3 %collective-permute-done.19.up_in_ref = bf16[16,4,16,128]{3,2,1,0:T(8,128)(2,1)S(1)} collective-permute-done((bf16[16,4,16,128]{3,2,1,0:T(8,128)(2,1)S(1)}, bf16[16,4,16,128]{3,2,1,0:T(8,128)(2,1)S(1)}, u32[]{:S(2)}, u32[]{:S(2)}) %collective-permute-start.19) | collective-permute-done | bytes 262176 | tf_op jit(solution)/shard_map/ppermute | solution.py:443
  111.8 2.0 %collective-permute-done.20.down_in_ref = bf16[16,4,16,128]{3,2,1,0:T(8,128)(2,1)S(1)} collective-permute-done((bf16[16,4,16,128]{3,2,1,0:T(8,128)(2,1)S(1)}, bf16[16,4,16,128]{3,2,1,0:T(8,128)(2,1)S(1)}, u32[]{:S(2)}, u32[]{:S(2)}) %collective-permute-start.20) | collective-permute-done | bytes 262176 | tf_op jit(solution)/shard_map/ppermute | solution.py:443
  113.9 3.1 %collective-permute-start.21 = (bf16[32,4,16,128]{3,2,1,0:T(8,128)(2,1)S(1)}, bf16[32,4,16,128]{3,2,1,0:T(8,128)(2,1)S(1)}, u32[]{:S(2)}, u32[]{:S(2)}) collective-permute-start(bf16[32,4,16,128]{3,2,1,0:T(8,128)(2,1)S(1)} %get-tuple-element.51), channel_id=1, source_target_pairs={{0,1},{1,2},{2,3},{3,4},{4,5},{5,6},{6,7},{7,0},{8,9},{9,10},{10,1... | collective-permute-start | bytes 1572872 | tf_op jit(solution)/shard_map/ppermute | solution.py:443
  117.0 7.8 %collective-permute-done.21.up_in_ref = bf16[32,4,16,128]{3,2,1,0:T(8,128)(2,1)S(1)} collective-permute-done((bf16[32,4,16,128]{3,2,1,0:T(8,128)(2,1)S(1)}, bf16[32,4,16,128]{3,2,1,0:T(8,128)(2,1)S(1)}, u32[]{:S(2)}, u32[]{:S(2)}) %collective-permute-start.21) | collective-permute-done | bytes 524320 | tf_op jit(solution)/shard_map/ppermute | solution.py:443
  124.8 4.0 %collective-permute-done.22.down_in_ref = bf16[32,4,16,128]{3,2,1,0:T(8,128)(2,1)S(1)} collective-permute-done((bf16[32,4,16,128]{3,2,1,0:T(8,128)(2,1)S(1)}, bf16[32,4,16,128]{3,2,1,0:T(8,128)(2,1)S(1)}, u32[]{:S(2)}, u32[]{:S(2)}) %collective-permute-start.22) | collective-permute-done | bytes 524320 | tf_op jit(solution)/shard_map/ppermute | solution.py:443
  129.0 1.8 %collective-permute-start.23 = (bf16[32,4,16,128]{3,2,1,0:T(8,128)(2,1)S(1)}, bf16[32,4,16,128]{3,2,1,0:T(8,128)(2,1)S(1)}, u32[]{:S(2)}, u32[]{:S(2)}) collective-permute-start(bf16[32,4,16,128]{3,2,1,0:T(8,128)(2,1)S(1)} %get-tuple-element.53), channel_id=1, source_target_pairs={{0,1},{1,2},{2,3},{3,4},{4,5},{5,6},{6,7},{7,0},{8,9},{9,10},{10,1... | collective-permute-start | bytes 1572872 | tf_op jit(solution)/shard_map/ppermute | solution.py:443
  131.1 8.9 %collective-permute-done.23.up_in_ref = bf16[32,4,16,128]{3,2,1,0:T(8,128)(2,1)S(1)} collective-permute-done((bf16[32,4,16,128]{3,2,1,0:T(8,128)(2,1)S(1)}, bf16[32,4,16,128]{3,2,1,0:T(8,128)(2,1)S(1)}, u32[]{:S(2)}, u32[]{:S(2)}) %collective-permute-start.23) | collective-permute-done | bytes 524320 | tf_op jit(solution)/shard_map/ppermute | solution.py:443
  140.0 2.0 %collective-permute-done.24.down_in_ref = bf16[32,4,16,128]{3,2,1,0:T(8,128)(2,1)S(1)} collective-permute-done((bf16[32,4,16,128]{3,2,1,0:T(8,128)(2,1)S(1)}, bf16[32,4,16,128]{3,2,1,0:T(8,128)(2,1)S(1)}, u32[]{:S(2)}, u32[]{:S(2)}) %collective-permute-start.24) | collective-permute-done | bytes 524320 | tf_op jit(solution)/shard_map/ppermute | solution.py:443
  142.2 2.2 %collective-permute-start.25 = (bf16[32,4,16,128]{3,2,1,0:T(8,128)(2,1)S(1)}, bf16[32,4,16,128]{3,2,1,0:T(8,128)(2,1)S(1)}, u32[]{:S(2)}, u32[]{:S(2)}) collective-permute-start(bf16[32,4,16,128]{3,2,1,0:T(8,128)(2,1)S(1)} %get-tuple-element.55), channel_id=1, source_target_pairs={{0,1},{1,2},{2,3},{3,4},{4,5},{5,6},{6,7},{7,0},{8,9},{9,10},{10,1... | collective-permute-start | bytes 1572872 | tf_op jit(solution)/shard_map/ppermute | solution.py:443
  144.5 0.6 slice_reduce_fusion
  145.1 6.4 %collective-permute-done.25.up_in_ref = bf16[32,4,16,128]{3,2,1,0:T(8,128)(2,1)S(1)} collective-permute-done((bf16[32,4,16,128]{3,2,1,0:T(8,128)(2,1)S(1)}, bf16[32,4,16,128]{3,2,1,0:T(8,128)(2,1)S(1)}, u32[]{:S(2)}, u32[]{:S(2)}) %collective-permute-start.25) | collective-permute-done | bytes 524320 | tf_op jit(solution)/shard_map/ppermute | solution.py:443
  151.5 2.2 %collective-permute-done.26.down_in_ref = bf16[32,4,16,128]{3,2,1,0:T(8,128)(2,1)S(1)} collective-permute-done((bf16[32,4,16,128]{3,2,1,0:T(8,128)(2,1)S(1)}, bf16[32,4,16,128]{3,2,1,0:T(8,128)(2,1)S(1)}, u32[]{:S(2)}, u32[]{:S(2)}) %collective-permute-start.26) | collective-permute-done | bytes 524320 | tf_op jit(solution)/shard_map/ppermute | solution.py:443
  153.7 1.5 ring_last.1
  (46 shorter events, 2.9 us)
Async XLA Ops:
  0.6 1.6 %copy-start.1 = (bf16[32,256,128]{2,1,0:T(8,128)(2,1)S(1)}, bf16[32,256,128]{2,1,0:T(8,128)(2,1)}, u32[]{:S(2)}) copy-start(bf16[32,256,128]{2,1,0:T(8,128)(2,1)} %table_ref.4) | copy-start | bytes 6291460
  2.2 0.7 copy-start.3
  2.9 1.3 copy-start.6
  3.0 1.9 %copy-start.2 = (bf16[32,256,128]{2,1,0:T(8,128)(2,1)S(1)}, bf16[32,256,128]{2,1,0:T(8,128)(2,1)}, u32[]{:S(2)}) copy-start(bf16[32,256,128]{2,1,0:T(8,128)(2,1)} %table_ref.4) | copy-start | bytes 6291460
  3.0 1.9 %copy-start.4 = (s32[64,32]{0,1:T(8,128)S(1)}, s32[64,32]{0,1:T(8,128)}, u32[]{:S(2)}) copy-start(s32[64,32]{0,1:T(8,128)} %param.8) | copy-start | bytes 24580
  4.2 1.9 %collective-permute-start = (bf16[17,64,128]{2,1,0:T(8,128)(2,1)S(1)}, bf16[17,64,128]{2,1,0:T(8,128)(2,1)S(1)}, u32[]{:S(2)}, u32[]{:S(2)}) collective-permute-start(bf16[17,64,128]{2,1,0:T(8,128)(2,1)S(1)} %child_scores.2), channel_id=1, source_target_pairs={{0,8},{8,0},{16,24},{24,16},{32,40},{40,32},{48,56},{56,48},{64,72... | collective-permute-start | bytes 835592 | tf_op jit(solution)/shard_map/ppermute | solution.py:341
  4.3 1.8 %collective-permute-start.1 = (s32[4,32]{1,0:T(4,128)S(1)}, s32[4,32]{1,0:T(4,128)S(1)}, u32[]{:S(2)}, u32[]{:S(2)}) collective-permute-start(s32[4,32]{1,0:T(4,128)S(1)} %bitcast.19), channel_id=1, source_target_pairs={{0,8},{8,0},{16,24},{24,16},{32,40},{40,32},{48,56},{56,48},{64,72... | collective-permute-start | bytes 1544 | tf_op jit(solution)/shard_map/ppermute | solution.py:341
  6.7 10.6 %collective-permute-start.2 = (bf16[33,64,128]{2,1,0:T(8,128)(2,1)S(1)}, bf16[33,64,128]{2,1,0:T(8,128)(2,1)S(1)}, u32[]{:S(2)}, u32[]{:S(2)}) collective-permute-start(bf16[33,64,128]{2,1,0:T(8,128)(2,1)S(1)} %pack.1), channel_id=1, source_target_pairs={{0,64},{8,24},{16,80},{24,40},{32,96},{40,56},{48,112},{56,8},{64,... | collective-permute-start | bytes 1622024 | tf_op jit(solution)/shard_map/ppermute | solution.py:354
  8.3 12.7 %collective-permute-start.3 = (bf16[33,64,128]{2,1,0:T(8,128)(2,1)S(1)}, bf16[33,64,128]{2,1,0:T(8,128)(2,1)S(1)}, u32[]{:S(2)}, u32[]{:S(2)}) collective-permute-start(bf16[33,64,128]{2,1,0:T(8,128)(2,1)S(1)} %pack.1), channel_id=1, source_target_pairs={{0,192},{8,56},{16,208},{24,8},{32,224},{40,24},{48,240},{56,40},{... | collective-permute-start | bytes 1622024 | tf_op jit(solution)/shard_map/ppermute | solution.py:354
  17.4 15.8 %collective-permute-start.4 = (bf16[33,64,128]{2,1,0:T(8,128)(2,1)S(1)}, bf16[33,64,128]{2,1,0:T(8,128)(2,1)S(1)}, u32[]{:S(2)}, u32[]{:S(2)}) collective-permute-start(bf16[33,64,128]{2,1,0:T(8,128)(2,1)S(1)} %pack.1), channel_id=1, source_target_pairs={{0,128},{8,40},{16,144},{24,56},{32,160},{40,8},{48,176},{56,24},{... | collective-permute-start | bytes 1622024 | tf_op jit(solution)/shard_map/ppermute | solution.py:354
  19.3 20.0 %collective-permute-start.5 = (bf16[66,64,128]{2,1,0:T(8,128)(2,1)S(1)}, bf16[66,64,128]{2,1,0:T(8,128)(2,1)S(1)}, u32[]{:S(2)}, u32[]{:S(2)}) collective-permute-start(bf16[66,64,128]{2,1,0:T(8,128)(2,1)S(1)} %constant_dynamic-update-slice_fusion.refs_0_), channel_id=1, source_target_pairs={{0,16},{8,72},{16,32},{24,88},{32,48},{40,104},{48,0},{56,120},{64... | collective-permute-start | bytes 3244040 | tf_op jit(solution)/shard_map/ppermute | solution.py:354
  33.2 42.2 %copy-start.5 = (f32[32,128]{1,0:T(8,128)S(1)}, f32[32,128]{1,0:T(8,128)}, u32[]{:S(2)}) copy-start(f32[32,128]{1,0:T(8,128)} %prior_ref.3) | copy-start | bytes 49156
  33.2 42.2 %copy-start.8 = (bf16[32,256,128]{2,1,0:T(8,128)(2,1)S(1)}, bf16[32,256,128]{2,1,0:T(8,128)(2,1)}, u32[]{:S(2)}) copy-start(bf16[32,256,128]{2,1,0:T(8,128)(2,1)} %table_ref.5) | copy-start | bytes 6291460
  33.3 42.2 %copy-start.9 = (s32[64,32]{0,1:T(8,128)S(1)}, s32[64,32]{0,1:T(8,128)}, u32[]{:S(2)}) copy-start(s32[64,32]{0,1:T(8,128)} %param.9) | copy-start | bytes 24580
  33.3 16.6 %collective-permute-start.8 = (bf16[66,64,128]{2,1,0:T(8,128)(2,1)S(1)}, bf16[66,64,128]{2,1,0:T(8,128)(2,1)S(1)}, u32[]{:S(2)}, u32[]{:S(2)}) collective-permute-start(bf16[66,64,128]{2,1,0:T(8,128)(2,1)S(1)} %constant_dynamic-update-slice_fusion.2.refs_1_), channel_id=1, source_target_pairs={{0,48},{8,200},{16,0},{24,216},{32,16},{40,232},{48,32},{56,248},{... | collective-permute-start | bytes 3244040 | tf_op jit(solution)/shard_map/ppermute | solution.py:354
  37.2 24.3 %collective-permute-start.7 = (bf16[66,64,128]{2,1,0:T(8,128)(2,1)S(1)}, bf16[66,64,128]{2,1,0:T(8,128)(2,1)S(1)}, u32[]{:S(2)}, u32[]{:S(2)}) collective-permute-start(bf16[66,64,128]{2,1,0:T(8,128)(2,1)S(1)} %constant_dynamic-update-slice_fusion.refs_0_), channel_id=1, source_target_pairs={{0,48},{8,200},{16,0},{24,216},{32,16},{40,232},{48,32},{56,248},{... | collective-permute-start | bytes 3244040 | tf_op jit(solution)/shard_map/ppermute | solution.py:354
  37.9 23.6 %collective-permute-start.6 = (bf16[66,64,128]{2,1,0:T(8,128)(2,1)S(1)}, bf16[66,64,128]{2,1,0:T(8,128)(2,1)S(1)}, u32[]{:S(2)}, u32[]{:S(2)}) collective-permute-start(bf16[66,64,128]{2,1,0:T(8,128)(2,1)S(1)} %constant_dynamic-update-slice_fusion.2.refs_1_), channel_id=1, source_target_pairs={{0,16},{8,72},{16,32},{24,88},{32,48},{40,104},{48,0},{56,120},{64... | collective-permute-start | bytes 3244040 | tf_op jit(solution)/shard_map/ppermute | solution.py:354
  39.3 26.6 %collective-permute-start.9 = (bf16[66,64,128]{2,1,0:T(8,128)(2,1)S(1)}, bf16[66,64,128]{2,1,0:T(8,128)(2,1)S(1)}, u32[]{:S(2)}, u32[]{:S(2)}) collective-permute-start(bf16[66,64,128]{2,1,0:T(8,128)(2,1)S(1)} %collective-permute-done.5.refs_2_), channel_id=1, source_target_pairs={{0,16},{8,72},{16,32},{24,88},{32,48},{40,104},{48,0},{56,120},{64... | collective-permute-start | bytes 3244040 | tf_op jit(solution)/shard_map/ppermute | solution.py:354
  49.9 23.2 %collective-permute-start.10 = (bf16[66,64,128]{2,1,0:T(8,128)(2,1)S(1)}, bf16[66,64,128]{2,1,0:T(8,128)(2,1)S(1)}, u32[]{:S(2)}, u32[]{:S(2)}) collective-permute-start(bf16[66,64,128]{2,1,0:T(8,128)(2,1)S(1)} %collective-permute-done.8.refs_5_), channel_id=1, source_target_pairs={{0,48},{8,200},{16,0},{24,216},{32,16},{40,232},{48,32},{56,248},{... | collective-permute-start | bytes 3244040 | tf_op jit(solution)/shard_map/ppermute | solution.py:354
  73.1 3.9 %copy-start = (bf16[32,1,4,128,128]{4,3,2,1,0:T(8,128)(2,1)S(1)}, bf16[32,1,4,128,128]{4,3,2,1,0:T(8,128)(2,1)}, u32[]{:S(2)}) copy-start(bf16[32,1,4,128,128]{4,3,2,1,0:T(8,128)(2,1)} %param.13) | copy-start | bytes 12582916
  75.2 3.4 %collective-permute-start.11 = (bf16[65,64,128]{2,1,0:T(8,128)(2,1)S(1)}, bf16[65,64,128]{2,1,0:T(8,128)(2,1)S(1)}, u32[]{:S(2)}, u32[]{:S(2)}) collective-permute-start(bf16[65,64,128]{2,1,0:T(8,128)(2,1)S(1)} %get-tuple-element.37), channel_id=1, source_target_pairs={{0,8},{8,0},{16,24},{24,16},{32,40},{40,32},{48,56},{56,48},{64,72... | collective-permute-start | bytes 3194888 | tf_op jit(solution)/shard_map/ppermute | solution.py:388
  76.9 1.6 %copy-start.7 = (s32[32]{0:T(128)S(1)}, s32[32]{0:T(128)}, u32[]{:S(2)}) copy-start(s32[32]{0:T(128)} %refs_1_.1) | copy-start | bytes 388
  83.1 1.4 collective-permute-start.12
  84.6 5.2 %collective-permute-start.13 = (f32[64,128]{1,0:T(8,128)S(1)}, f32[64,128]{1,0:T(8,128)S(1)}, u32[]{:S(2)}, u32[]{:S(2)}) collective-permute-start(f32[64,128]{1,0:T(8,128)S(1)} %merge_core.1.refs_0_), channel_id=1, source_target_pairs={{0,64},{8,24},{16,80},{24,40},{32,96},{40,56},{48,112},{56,8},{64,... | collective-permute-start | bytes 98312 | tf_op jit(solution)/shard_map/ppermute | solution.py:417
  84.7 5.1 %collective-permute-start.14 = (f32[64,128]{1,0:T(8,128)S(1)}, f32[64,128]{1,0:T(8,128)S(1)}, u32[]{:S(2)}, u32[]{:S(2)}) collective-permute-start(f32[64,128]{1,0:T(8,128)S(1)} %merge_core.1.refs_0_), channel_id=1, source_target_pairs={{0,192},{8,56},{16,208},{24,8},{32,224},{40,24},{48,240},{56,40},{... | collective-permute-start | bytes 98312 | tf_op jit(solution)/shard_map/ppermute | solution.py:417
  87.9 5.4 %collective-permute-start.15 = (f32[64,128]{1,0:T(8,128)S(1)}, f32[64,128]{1,0:T(8,128)S(1)}, u32[]{:S(2)}, u32[]{:S(2)}) collective-permute-start(f32[64,128]{1,0:T(8,128)S(1)} %merge_core.1.refs_0_), channel_id=1, source_target_pairs={{0,128},{8,40},{16,144},{24,56},{32,160},{40,8},{48,176},{56,24},{... | collective-permute-start | bytes 98312 | tf_op jit(solution)/shard_map/ppermute | solution.py:417
  93.5 5.7 %collective-permute-start.16 = (f32[64,128]{1,0:T(8,128)S(1)}, f32[64,128]{1,0:T(8,128)S(1)}, u32[]{:S(2)}, u32[]{:S(2)}) collective-permute-start(f32[64,128]{1,0:T(8,128)S(1)} %merge_a.1.refs_2_), channel_id=1, source_target_pairs={{0,16},{8,72},{16,32},{24,88},{32,48},{40,104},{48,0},{56,120},{64... | collective-permute-start | bytes 98312 | tf_op jit(solution)/shard_map/ppermute | solution.py:417
  94.6 4.6 %collective-permute-start.17 = (f32[64,128]{1,0:T(8,128)S(1)}, f32[64,128]{1,0:T(8,128)S(1)}, u32[]{:S(2)}, u32[]{:S(2)}) collective-permute-start(f32[64,128]{1,0:T(8,128)S(1)} %merge_a.1.refs_2_), channel_id=1, source_target_pairs={{0,48},{8,200},{16,0},{24,216},{32,16},{40,232},{48,32},{56,248},{... | collective-permute-start | bytes 98312 | tf_op jit(solution)/shard_map/ppermute | solution.py:417
  97.3 5.4 %collective-permute-start.18 = (f32[64,128]{1,0:T(8,128)S(1)}, f32[64,128]{1,0:T(8,128)S(1)}, u32[]{:S(2)}, u32[]{:S(2)}) collective-permute-start(f32[64,128]{1,0:T(8,128)S(1)} %merge_a.1.refs_2_), channel_id=1, source_target_pairs={{0,32},{8,136},{16,48},{24,152},{32,0},{40,168},{48,16},{56,184},{... | collective-permute-start | bytes 98312 | tf_op jit(solution)/shard_map/ppermute | solution.py:417
  105.4 6.4 %collective-permute-start.19 = (bf16[16,4,16,128]{3,2,1,0:T(8,128)(2,1)S(1)}, bf16[16,4,16,128]{3,2,1,0:T(8,128)(2,1)S(1)}, u32[]{:S(2)}, u32[]{:S(2)}) collective-permute-start(bf16[16,4,16,128]{3,2,1,0:T(8,128)(2,1)S(1)} %get-tuple-element.49), channel_id=1, source_target_pairs={{0,1},{1,2},{2,3},{3,4},{4,5},{5,6},{6,7},{7,0},{8,9},{9,10},{10,1... | collective-permute-start | bytes 786440 | tf_op jit(solution)/shard_map/ppermute | solution.py:443
  107.4 6.4 %collective-permute-start.20 = (bf16[16,4,16,128]{3,2,1,0:T(8,128)(2,1)S(1)}, bf16[16,4,16,128]{3,2,1,0:T(8,128)(2,1)S(1)}, u32[]{:S(2)}, u32[]{:S(2)}) collective-permute-start(bf16[16,4,16,128]{3,2,1,0:T(8,128)(2,1)S(1)} %get-tuple-element.50), channel_id=1, source_target_pairs={{0,7},{1,0},{2,1},{3,2},{4,3},{5,4},{6,5},{7,6},{8,15},{9,8},{10,9... | collective-permute-start | bytes 786440 | tf_op jit(solution)/shard_map/ppermute | solution.py:443
  113.9 10.9 %collective-permute-start.21 = (bf16[32,4,16,128]{3,2,1,0:T(8,128)(2,1)S(1)}, bf16[32,4,16,128]{3,2,1,0:T(8,128)(2,1)S(1)}, u32[]{:S(2)}, u32[]{:S(2)}) collective-permute-start(bf16[32,4,16,128]{3,2,1,0:T(8,128)(2,1)S(1)} %get-tuple-element.51), channel_id=1, source_target_pairs={{0,1},{1,2},{2,3},{3,4},{4,5},{5,6},{6,7},{7,0},{8,9},{9,10},{10,1... | collective-permute-start | bytes 1572872 | tf_op jit(solution)/shard_map/ppermute | solution.py:443
  117.0 11.8 %collective-permute-start.22 = (bf16[32,4,16,128]{3,2,1,0:T(8,128)(2,1)S(1)}, bf16[32,4,16,128]{3,2,1,0:T(8,128)(2,1)S(1)}, u32[]{:S(2)}, u32[]{:S(2)}) collective-permute-start(bf16[32,4,16,128]{3,2,1,0:T(8,128)(2,1)S(1)} %get-tuple-element.52), channel_id=1, source_target_pairs={{0,7},{1,0},{2,1},{3,2},{4,3},{5,4},{6,5},{7,6},{8,15},{9,8},{10,9... | collective-permute-start | bytes 1572872 | tf_op jit(solution)/shard_map/ppermute | solution.py:443
  129.0 11.0 %collective-permute-start.23 = (bf16[32,4,16,128]{3,2,1,0:T(8,128)(2,1)S(1)}, bf16[32,4,16,128]{3,2,1,0:T(8,128)(2,1)S(1)}, u32[]{:S(2)}, u32[]{:S(2)}) collective-permute-start(bf16[32,4,16,128]{3,2,1,0:T(8,128)(2,1)S(1)} %get-tuple-element.53), channel_id=1, source_target_pairs={{0,1},{1,2},{2,3},{3,4},{4,5},{5,6},{6,7},{7,0},{8,9},{9,10},{10,1... | collective-permute-start | bytes 1572872 | tf_op jit(solution)/shard_map/ppermute | solution.py:443
  130.8 11.2 %collective-permute-start.24 = (bf16[32,4,16,128]{3,2,1,0:T(8,128)(2,1)S(1)}, bf16[32,4,16,128]{3,2,1,0:T(8,128)(2,1)S(1)}, u32[]{:S(2)}, u32[]{:S(2)}) collective-permute-start(bf16[32,4,16,128]{3,2,1,0:T(8,128)(2,1)S(1)} %get-tuple-element.54), channel_id=1, source_target_pairs={{0,7},{1,0},{2,1},{3,2},{4,3},{5,4},{6,5},{7,6},{8,15},{9,8},{10,9... | collective-permute-start | bytes 1572872 | tf_op jit(solution)/shard_map/ppermute | solution.py:443
  142.2 9.3 %collective-permute-start.25 = (bf16[32,4,16,128]{3,2,1,0:T(8,128)(2,1)S(1)}, bf16[32,4,16,128]{3,2,1,0:T(8,128)(2,1)S(1)}, u32[]{:S(2)}, u32[]{:S(2)}) collective-permute-start(bf16[32,4,16,128]{3,2,1,0:T(8,128)(2,1)S(1)} %get-tuple-element.55), channel_id=1, source_target_pairs={{0,1},{1,2},{2,3},{3,4},{4,5},{5,6},{6,7},{7,0},{8,9},{9,10},{10,1... | collective-permute-start | bytes 1572872 | tf_op jit(solution)/shard_map/ppermute | solution.py:443
  144.5 9.2 %collective-permute-start.26 = (bf16[32,4,16,128]{3,2,1,0:T(8,128)(2,1)S(1)}, bf16[32,4,16,128]{3,2,1,0:T(8,128)(2,1)S(1)}, u32[]{:S(2)}, u32[]{:S(2)}) collective-permute-start(bf16[32,4,16,128]{3,2,1,0:T(8,128)(2,1)S(1)} %get-tuple-element.56), channel_id=1, source_target_pairs={{0,7},{1,0},{2,1},{3,2},{4,3},{5,4},{6,5},{7,6},{8,15},{9,8},{10,9... | collective-permute-start | bytes 1572872 | tf_op jit(solution)/shard_map/ppermute | solution.py:443

commit v5 on v4

--- a/solution.py
+++ b/solution.py
@@ -139,38 +139,38 @@
     return total
 
 
-def own_sums_kernel(place_ref, columns_ref, pool, powers, weights_ref, out_ref, sums_ref):
-    lanes = lane_of((S_LOC, BLK))
-    tops = jnp.zeros((S_LOC, BLK), jnp.float32)
-    for k in range(HALF):
+def child_at(core, half, k):
+    return jnp.where(core == half, k, HALF + k)
+
+
+def own_sums_kernel(
+    place_ref, columns_ref, map_ref, pool, powers, weights_ref, parent_ref,
+    out_ref, sums_ref, root_ref,
+):
+    root_ref[...] = parent_ref[...]
+    for k in range(HALF):
+        child = child_at(place_ref[0], 0, k)
         blocks, top = pick_child(codes_of(place_ref, columns_ref, k), k, pool, powers)
-        tops = jnp.where(lanes == k, top, tops)
         for z in range(NZ):
             out_ref[k * NZ + z] = blocks[z]
-        sums_ref[k] = row_sum(blocks, weights_ref, child_at(place_ref[0], 0, k))
-    out_ref[HALF * NZ] = tops.astype(jnp.bfloat16)
-
-
-def child_at(core, half, k):
-    return jnp.where(core == half, k, HALF + k)
+        row_sums = row_sum(blocks, weights_ref, child)
+        sums_ref[k] = row_sums
+        owner = map_ref[child]
+        root_ref[owner] = root_ref[owner] + (jnp.log(row_sums) + top * LN2)
 
 
 def sums_kernel(
-    core_ref, map_ref, own_ref, other_ref, own_sums_ref, weights_ref, parent_ref, prior_ref,
+    place_ref, map_ref, other_ref, weights_ref, own_root_ref, prior_ref,
     stats_ref, root_ref, sums_ref,
 ):
-    core = core_ref[0]
-    root_ref[...] = parent_ref[...]
-    for k in range(HALF):
-        sums_ref[k] = own_sums_ref[k]
-        blocks = [other_ref[k * NZ + z] for z in range(NZ)]
-        sums_ref[HALF + k] = row_sum(blocks, weights_ref, child_at(core, 1, k))
-    for half, picked_ref in enumerate((own_ref, other_ref)):
-        tops = picked_ref[HALF * NZ].astype(jnp.float32) * LN2
-        for k in range(HALF):
-            owner = map_ref[child_at(core, half, k)]
-            message = jnp.log(sums_ref[half * HALF + k]) + tops[:, k : k + 1]
-            root_ref[owner] = root_ref[owner] + message
+    root_ref[...] = own_root_ref[...]
+    tops = other_ref[HALF * NZ].astype(jnp.float32) * LN2
+    for k in range(HALF):
+        child = child_at(place_ref[0], 1, k)
+        row_sums = row_sum([other_ref[k * NZ + z] for z in range(NZ)], weights_ref, child)
+        sums_ref[k] = row_sums
+        owner = map_ref[child]
+        root_ref[owner] = root_ref[owner] + (jnp.log(row_sums) + tops[:, k : k + 1])
     lanes = lane_of((S_LOC, BLK))
     prior = prior_ref[...]
     prior_peak = jnp.max(prior, axis=1, keepdims=True)
@@ -183,11 +183,10 @@
         axis=0, keepdims=True,
     )
     stats = jnp.broadcast_to(stats, (S_LOC, BLK))
+    peaks = [jnp.max(root_ref[p], axis=1, keepdims=True) for p in range(P_SIZE)]
     for p in range(P_SIZE):
-        stats = jnp.where(lanes == p, jnp.max(root_ref[p], axis=1, keepdims=True), stats)
-    peaks = stats
-    for p in range(P_SIZE):
-        total = jnp.sum(jnp.exp(root_ref[p] - peaks[:, p : p + 1]), axis=1, keepdims=True)
+        total = jnp.sum(jnp.exp(root_ref[p] - peaks[p]), axis=1, keepdims=True)
+        stats = jnp.where(lanes == p, peaks[p], stats)
         stats = jnp.where(lanes == P_SIZE + p, total, stats)
     stats_ref[...] = stats
 
@@ -211,8 +210,8 @@
 
 def counts_kernel(scale, n_stats, place_ref, map_ref, *refs):
     stats_refs, refs = refs[:n_stats], refs[n_stats:]
-    root_ref, sums_ref, own_ref, other_ref, weights_ref = refs[:5]
-    near, far, loglik_ref, posterior = refs[5:12], refs[12:14], refs[14], refs[15]
+    root_ref, own_sums_ref, other_sums_ref, own_ref, other_ref, weights_ref = refs[:6]
+    near, far, loglik_ref, posterior = refs[6:13], refs[13:15], refs[15], refs[16]
     core, place = place_ref[0], place_ref[1]
     stats = merge([r[...] for r in stats_refs])
     lanes = lane_of((S_LOC, BLK))
@@ -228,10 +227,12 @@
     parts = BLK // rows
     starts = [pl.multiple_of(lax.rem(place + k, parts) * rows, rows) for k in range(parts)]
     turn = lax.rem(parts - place, parts) * rows
-    for half, picked_ref in enumerate((own_ref, other_ref)):
+    for half, (picked_ref, sums_ref) in enumerate(
+        ((own_ref, own_sums_ref), (other_ref, other_sums_ref))
+    ):
         for k in range(HALF):
             child = child_at(core, half, k)
-            share = posterior[map_ref[child]].astype(jnp.float32) / sums_ref[half * HALF + k]
+            share = posterior[map_ref[child]].astype(jnp.float32) / sums_ref[k]
             share = pltpu.roll(share, turn, 1).astype(jnp.bfloat16)
             picked = jnp.concatenate([picked_ref[k * NZ + z] for z in range(NZ)], axis=1)
             flow = lax.dot_general(
@@ -362,13 +363,12 @@
         cost_estimate=cost(1 << 28, 3 << 20, 1 << 21),
         name="parent_scores",
     )(parent_values.T, parent_logits, prior_logits)
-    a1, a3 = send(own, 1, 0), send(own, -1, 0)
-    a1, own = lax.optimization_barrier((a1, own))
-    a2 = send(own, 2, 0)
+    a1, a3, a2 = lax.optimization_barrier((send(own, 1, 0), send(own, -1, 0), send(own, 2, 0)))
     near = jnp.concatenate([own, a1])
     near_up, near_down = send(near, 0, 1), send(near, 0, -1)
     far = jnp.concatenate([a3, a2])
     far_up, far_down = send(far, 0, 1), send(far, 0, -1)
+    near_up, far_down = lax.optimization_barrier((near_up, far_down))
     next_up = send(near_up, 0, 1)
     next_down = send(far_down, 0, -1)
     slots = shape((HALF * NZ + 1, S_LOC, BLK), bf16)
@@ -386,28 +386,26 @@
         name="pick_other",
     )(place, other_columns, near, far, near_up, far_up, near_down, far_down, next_up, next_down)
     other = lax.ppermute(for_other, "region", SWAP)
-    picked, own_sums = pl.pallas_call(
+    half_sums = shape((HALF, S_LOC, BLK), f32)
+    scores_all = shape((P_SIZE, S_LOC, BLK), f32)
+    picked, own_sums, own_root = pl.pallas_call(
         own_sums_kernel,
-        out_shape=(slots, shape((HALF, S_LOC, BLK), f32)),
-        in_specs=[SMEM, SMEM] + [VMEM] * 3,
-        out_specs=(VMEM, VMEM),
+        out_shape=(shape((HALF * NZ, S_LOC, BLK), bf16), half_sums, scores_all),
+        in_specs=[SMEM, SMEM, SMEM] + [VMEM] * 4,
+        out_specs=(VMEM,) * 3,
         compiler_params=params(20),
         cost_estimate=cost(1 << 28, 8 << 20, 1 << 19),
         name="own_sums",
-    )(place, columns, pool, powers, weights)
-    stats, root, sums = pl.pallas_call(
+    )(place, columns, parent_map, pool, powers, weights, parent_in)
+    stats, root, other_sums = pl.pallas_call(
         sums_kernel,
-        out_shape=(
-            shape((S_LOC, BLK), f32),
-            shape((P_SIZE, S_LOC, BLK), f32),
-            shape((C, S_LOC, BLK), f32),
-        ),
-        in_specs=[SMEM, SMEM] + [VMEM] * 6,
+        out_shape=(shape((S_LOC, BLK), f32), scores_all, half_sums),
+        in_specs=[SMEM, SMEM] + [VMEM] * 4,
         out_specs=(VMEM,) * 3,
         compiler_params=params(16),
-        cost_estimate=cost(1 << 29, 12 << 20, 1 << 20),
+        cost_estimate=cost(1 << 28, 8 << 20, 1 << 20),
         name="row_sums",
-    )(place, parent_map, picked, other, own_sums, weights, parent_in, prior_logits)
+    )(place, parent_map, other, weights, own_root, prior_logits)
 
     for axis, pairs in (
         ("core", (SWAP,)),
@@ -430,13 +428,13 @@
     n0, n1, n2, n3, n5, n6, n7, far_up, far_down, loglik = pl.pallas_call(
         lambda *refs: counts_kernel(scale, 1 + len(others), *refs),
         out_shape=(whole,) * 7 + (half_set,) * 2 + (shape((S_LOC, BLK), f32),),
-        in_specs=[SMEM, SMEM] + [VMEM] * (6 + len(others)),
+        in_specs=[SMEM, SMEM] + [VMEM] * (7 + len(others)),
         out_specs=(VMEM,) * 10,
         scratch_shapes=[pltpu.VMEM((P_SIZE, S_LOC, BLK), bf16)],
         compiler_params=params(24),
         cost_estimate=cost(1 << 29, 13 << 20, 1 << 19),
         name="counts",
-    )(place, parent_map, stats, *others, root, sums, picked, other, weights)
+    )(place, parent_map, stats, *others, root, own_sums, other_sums, picked, other, weights)
 
     def ring(up, down):
         shift = lambda step: [(i, (i + step) % parts) for i in range(parts)]

time: 155 us -> 148 us (0.955)
  starting transfers between devices: 36.6 us -> 32.3 us
  Pallas kernels: 17.7 us -> 15.4 us
    ppermute x9, waiting for transfers between devices: 49.6 us -> 46.5 us  [send(): return lax.ppermute(value, 'region', along(a, b))]
    ppermute x9, starting transfers between devices: 16.5 us -> 13.6 us  [send(): return lax.ppermute(value, 'region', along(a, b))]
    pallas_call x2, Pallas kernels: 6.1 us -> 3.78 us  [the longest x1 2.07 us: body(): pl.pallas_call(sums_kernel, out_shape=(shape((S_LOC, BLK), f32), scores_a...]
    ppermute x7, starting transfers between devices: 9.76 us -> 7.66 us  [body(): others = [lax.ppermute(stats, 'region', p) for p in pairs]]
  transfers between devices with their start and end apart: 27 -> 27, of which waited for: 19 -> 22; matrix products, arithmetic and copies ran while one was open for 1% -> 1% of each run, Pallas kernels for 3% -> 3%
where the time goes in v5:
time: 148 us; the launch traced here: 147 us
  waiting for transfers between devices  95.6 us (65%)
  starting transfers between devices  32.3 us (22%)
  Pallas kernels  15.4 us (10%)
  local copies, waits for them, and re-layouts  3.07 us (2%)
    ppermute x9, waiting for transfers between devices, send(): return lax.ppermute(value, 'region', along(a, b))  46.5 us
    ppermute x4, waiting for transfers between devices, ring(): lax.ppermute(up, 'batch', shift(1))  27.5 us
    ppermute x9, starting transfers between devices, send(): return lax.ppermute(value, 'region', along(a, b))  13.6 us
    ppermute x7, waiting for transfers between devices, body(): others = [lax.ppermute(stats, 'region', p) for p in pairs]  11.2 us
    ppermute x4, waiting for transfers between devices, ring(): lax.ppermute(down, 'batch', shift(-1))  10.5 us
    ppermute x4, starting transfers between devices, ring(): lax.ppermute(up, 'batch', shift(1))  9.76 us
    ppermute x7, starting transfers between devices, body(): others = [lax.ppermute(stats, 'region', p) for p in pairs]  7.66 us
  transfers between devices with their start and end apart: 27, of which 22 were waited for; matrix products, arithmetic and copies ran while one was open for 1% of the time, Pallas kernels for 3%

profile of v5, /device:TPU:32, one launch (start us, length us, event | category | flops | bytes accessed | tf_op | source)
XLA Modules:
  0.0 147.4 jit_solution(14875475996770440755)
XLA Ops:
  0.6 1.6 %copy-done.1 = bf16[32,256,128]{2,1,0:T(8,128)(2,1)S(1)} copy-done((bf16[32,256,128]{2,1,0:T(8,128)(2,1)S(1)}, bf16[32,256,128]{2,1,0:T(8,128)(2,1)}, u32[]{:S(2)}) %copy-start.1) | copy-done | bytes 2097176
  2.2 0.7 copy-done.3
  3.0 1.2 child_scores.2
  4.9 1.2 child_scores.3.own_ref
  6.1 0.6 pack.1
  6.7 1.5 %collective-permute-start.2 = (bf16[33,64,128]{2,1,0:T(8,128)(2,1)S(1)}, bf16[33,64,128]{2,1,0:T(8,128)(2,1)S(1)}, u32[]{:S(2)}, u32[]{:S(2)}) collective-permute-start(bf16[33,64,128]{2,1,0:T(8,128)(2,1)S(1)} %pack.1), channel_id=1, source_target_pairs={{0,64},{8,24},{16,80},{24,40},{32,96},{40,56},{48,112},{56,8},{64,... | collective-permute-start | bytes 1622024 | tf_op jit(solution)/shard_map/ppermute | solution.py:355
  8.3 1.7 %collective-permute-start.3 = (bf16[33,64,128]{2,1,0:T(8,128)(2,1)S(1)}, bf16[33,64,128]{2,1,0:T(8,128)(2,1)S(1)}, u32[]{:S(2)}, u32[]{:S(2)}) collective-permute-start(bf16[33,64,128]{2,1,0:T(8,128)(2,1)S(1)} %pack.1), channel_id=1, source_target_pairs={{0,192},{8,56},{16,208},{24,8},{32,224},{40,24},{48,240},{56,40},{... | collective-permute-start | bytes 1622024 | tf_op jit(solution)/shard_map/ppermute | solution.py:355
  10.0 1.8 %collective-permute-start.4 = (bf16[33,64,128]{2,1,0:T(8,128)(2,1)S(1)}, bf16[33,64,128]{2,1,0:T(8,128)(2,1)S(1)}, u32[]{:S(2)}, u32[]{:S(2)}) collective-permute-start(bf16[33,64,128]{2,1,0:T(8,128)(2,1)S(1)} %pack.1), channel_id=1, source_target_pairs={{0,128},{8,40},{16,144},{24,56},{32,160},{40,8},{48,176},{56,24},{... | collective-permute-start | bytes 1622024 | tf_op jit(solution)/shard_map/ppermute | solution.py:355
  11.8 5.5 %collective-permute-done.2 = bf16[33,64,128]{2,1,0:T(8,128)(2,1)S(1)} collective-permute-done((bf16[33,64,128]{2,1,0:T(8,128)(2,1)S(1)}, bf16[33,64,128]{2,1,0:T(8,128)(2,1)S(1)}, u32[]{:S(2)}, u32[]{:S(2)}) %collective-permute-start.2) | collective-permute-done | bytes 540704 | tf_op jit(solution)/shard_map/ppermute | solution.py:355
  17.4 5.4 %collective-permute-done.3 = bf16[33,64,128]{2,1,0:T(8,128)(2,1)S(1)} collective-permute-done((bf16[33,64,128]{2,1,0:T(8,128)(2,1)S(1)}, bf16[33,64,128]{2,1,0:T(8,128)(2,1)S(1)}, u32[]{:S(2)}, u32[]{:S(2)}) %collective-permute-start.3) | collective-permute-done | bytes 540704 | tf_op jit(solution)/shard_map/ppermute | solution.py:355
  22.7 1.4 collective-permute-done.4
  24.3 3.1 %collective-permute-start.6 = (bf16[66,64,128]{2,1,0:T(8,128)(2,1)S(1)}, bf16[66,64,128]{2,1,0:T(8,128)(2,1)S(1)}, u32[]{:S(2)}, u32[]{:S(2)}) collective-permute-start(bf16[66,64,128]{2,1,0:T(8,128)(2,1)S(1)} %constant_dynamic-update-slice_fusion.refs_1_), channel_id=1, source_target_pairs={{0,48},{8,200},{16,0},{24,216},{32,16},{40,232},{48,32},{56,248},{... | collective-permute-start | bytes 3244040 | tf_op jit(solution)/shard_map/ppermute | solution.py:355
  27.6 0.6 collective-permute-start.7
  28.1 2.7 %collective-permute-start.8 = (bf16[66,64,128]{2,1,0:T(8,128)(2,1)S(1)}, bf16[66,64,128]{2,1,0:T(8,128)(2,1)S(1)}, u32[]{:S(2)}, u32[]{:S(2)}) collective-permute-start(bf16[66,64,128]{2,1,0:T(8,128)(2,1)S(1)} %pad_maximum_fusion.refs_0_), channel_id=1, source_target_pairs={{0,48},{8,200},{16,0},{24,216},{32,16},{40,232},{48,32},{56,248},{... | collective-permute-start | bytes 3244040 | tf_op jit(solution)/shard_map/ppermute | solution.py:355
  30.9 9.1 %collective-permute-done.6.refs_5_ = bf16[66,64,128]{2,1,0:T(8,128)(2,1)S(1)} collective-permute-done((bf16[66,64,128]{2,1,0:T(8,128)(2,1)S(1)}, bf16[66,64,128]{2,1,0:T(8,128)(2,1)S(1)}, u32[]{:S(2)}, u32[]{:S(2)}) %collective-permute-start.6) | collective-permute-done | bytes 1081376 | tf_op jit(solution)/shard_map/ppermute | solution.py:355
  40.0 3.9 %collective-permute-done.5.refs_2_ = bf16[66,64,128]{2,1,0:T(8,128)(2,1)S(1)} collective-permute-done((bf16[66,64,128]{2,1,0:T(8,128)(2,1)S(1)}, bf16[66,64,128]{2,1,0:T(8,128)(2,1)S(1)}, u32[]{:S(2)}, u32[]{:S(2)}) %collective-permute-start.5) | collective-permute-done | bytes 1081376 | tf_op jit(solution)/shard_map/ppermute | solution.py:355
  43.9 2.0 %collective-permute-start.9 = (bf16[66,64,128]{2,1,0:T(8,128)(2,1)S(1)}, bf16[66,64,128]{2,1,0:T(8,128)(2,1)S(1)}, u32[]{:S(2)}, u32[]{:S(2)}) collective-permute-start(bf16[66,64,128]{2,1,0:T(8,128)(2,1)S(1)} %collective-permute-done.5.refs_2_), channel_id=1, source_target_pairs={{0,16},{8,72},{16,32},{24,88},{32,48},{40,104},{48,0},{56,120},{64... | collective-permute-start | bytes 3244040 | tf_op jit(solution)/shard_map/ppermute | solution.py:355
  45.9 9.6 %collective-permute-done.7.refs_3_ = bf16[66,64,128]{2,1,0:T(8,128)(2,1)S(1)} collective-permute-done((bf16[66,64,128]{2,1,0:T(8,128)(2,1)S(1)}, bf16[66,64,128]{2,1,0:T(8,128)(2,1)S(1)}, u32[]{:S(2)}, u32[]{:S(2)}) %collective-permute-start.7) | collective-permute-done | bytes 1081376 | tf_op jit(solution)/shard_map/ppermute | solution.py:355
  55.5 7.7 %collective-permute-done.10.refs_7_ = bf16[66,64,128]{2,1,0:T(8,128)(2,1)S(1)} collective-permute-done((bf16[66,64,128]{2,1,0:T(8,128)(2,1)S(1)}, bf16[66,64,128]{2,1,0:T(8,128)(2,1)S(1)}, u32[]{:S(2)}, u32[]{:S(2)}) %collective-permute-start.10) | collective-permute-done | bytes 1081376 | tf_op jit(solution)/shard_map/ppermute | solution.py:355
  63.2 3.9 %collective-permute-done.9.refs_6_ = bf16[66,64,128]{2,1,0:T(8,128)(2,1)S(1)} collective-permute-done((bf16[66,64,128]{2,1,0:T(8,128)(2,1)S(1)}, bf16[66,64,128]{2,1,0:T(8,128)(2,1)S(1)}, u32[]{:S(2)}, u32[]{:S(2)}) %collective-permute-start.9) | collective-permute-done | bytes 1081376 | tf_op jit(solution)/shard_map/ppermute | solution.py:355
  67.1 2.1 %pick_other.1 = (bf16[65,64,128]{2,1,0:T(8,128)(2,1)S(1)}, bf16[528,64,128]{2,1,0:T(8,128)(2,1)S(1)}, f32[32,64,128]{2,1,0:T(8,128)S(1)}) custom-call(s32[4]{0:T(128)S(1)} %pad_add_fusion.core_ref.place_ref.refs_0_, s32[4,32]{1,0:T(4,128)S(1)} %collective-permute-done.1.columns_ref, bf16[66,64,128]{2,1,0:T(8,128)(2,1)S(1)} %pad_maximum_fusion.refs_0_, ...), custom_call_target="tpu_custom_call" | custom-call | flops 4194304 | bytes 20971520 | tf_op jit(solution)/shard_map/pick_other/pallas_call | solution.py:375
  69.5 1.4 parent_scores.1.parent_ref
  71.0 1.7 %own_sums.1 = (bf16[64,64,128]{2,1,0:T(8,128)(2,1)S(1)}, f32[16,64,128]{2,1,0:T(8,128)S(1)}, f32[32,64,128]{2,1,0:T(8,128)S(1)}) custom-call(s32[4]{0:T(128)S(1)} %pad_add_fusion.core_ref.place_ref.refs_0_, s32[4,32]{1,0:T(4,128)S(1)} %bitcast.20, s32[32]{0:T(128)S(1)} %copy-done.6, bf16[528,64,128]{2,1,0:T(8,128)(2,1)S(1)} %get-tuple-element.42.pool, ...), custom_call_target="tpu_custom_call" | custom-call | flops 268435456 | bytes 8388608 | tf_op jit(solution)/shard_map/own_sums/pallas_call | solution.py:391
  72.7 2.1 %row_sums.1 = (f32[64,128]{1,0:T(8,128)S(1)}, f32[32,64,128]{2,1,0:T(8,128)S(1)}, f32[16,64,128]{2,1,0:T(8,128)S(1)}) custom-call(s32[4]{0:T(128)S(1)} %pad_add_fusion.core_ref.place_ref.refs_0_, s32[32]{0:T(128)S(1)} %copy-done.6, bf16[65,64,128]{2,1,0:T(8,128)(2,1)S(1)} %collective-permute-done.11.other_ref.refs_10_, ...), custom_call_target="tpu_custom_call" | custom-call | flops 268435456 | bytes 8388608 | tf_op jit(solution)/shard_map/row_sums/pallas_call | solution.py:400
  74.8 0.6 collective-permute-start.12
  75.3 0.9 collective-permute-done.12.refs_1_
  76.3 1.5 %collective-permute-start.13 = (f32[64,128]{1,0:T(8,128)S(1)}, f32[64,128]{1,0:T(8,128)S(1)}, u32[]{:S(2)}, u32[]{:S(2)}) collective-permute-start(f32[64,128]{1,0:T(8,128)S(1)} %merge_core.1.refs_0_), channel_id=1, source_target_pairs={{0,64},{8,24},{16,80},{24,40},{32,96},{40,56},{48,112},{56,8},{64,... | collective-permute-start | bytes 98312 | tf_op jit(solution)/shard_map/ppermute | solution.py:415
  77.8 1.8 %collective-permute-start.14 = (f32[64,128]{1,0:T(8,128)S(1)}, f32[64,128]{1,0:T(8,128)S(1)}, u32[]{:S(2)}, u32[]{:S(2)}) collective-permute-start(f32[64,128]{1,0:T(8,128)S(1)} %merge_core.1.refs_0_), channel_id=1, source_target_pairs={{0,192},{8,56},{16,208},{24,8},{32,224},{40,24},{48,240},{56,40},{... | collective-permute-start | bytes 98312 | tf_op jit(solution)/shard_map/ppermute | solution.py:415
  80.1 1.4 collective-permute-done.13.refs_1_
  81.7 3.3 %collective-permute-done.15.refs_3_ = f32[64,128]{1,0:T(8,128)S(1)} collective-permute-done((f32[64,128]{1,0:T(8,128)S(1)}, f32[64,128]{1,0:T(8,128)S(1)}, u32[]{:S(2)}, u32[]{:S(2)}) %collective-permute-start.15) | collective-permute-done | bytes 32800 | tf_op jit(solution)/shard_map/ppermute | solution.py:415
  85.2 3.2 %collective-permute-start.17 = (f32[64,128]{1,0:T(8,128)S(1)}, f32[64,128]{1,0:T(8,128)S(1)}, u32[]{:S(2)}, u32[]{:S(2)}) collective-permute-start(f32[64,128]{1,0:T(8,128)S(1)} %merge_a.1.refs_2_), channel_id=1, source_target_pairs={{0,48},{8,200},{16,0},{24,216},{32,16},{40,232},{48,32},{56,248},{... | collective-permute-start | bytes 98312 | tf_op jit(solution)/shard_map/ppermute | solution.py:415
  88.5 1.9 %collective-permute-done.16.refs_3_ = f32[64,128]{1,0:T(8,128)S(1)} collective-permute-done((f32[64,128]{1,0:T(8,128)S(1)}, f32[64,128]{1,0:T(8,128)S(1)}, u32[]{:S(2)}, u32[]{:S(2)}) %collective-permute-start.16) | collective-permute-done | bytes 32800 | tf_op jit(solution)/shard_map/ppermute | solution.py:415
  90.4 3.5 %collective-permute-done.18.refs_5_ = f32[64,128]{1,0:T(8,128)S(1)} collective-permute-done((f32[64,128]{1,0:T(8,128)S(1)}, f32[64,128]{1,0:T(8,128)S(1)}, u32[]{:S(2)}, u32[]{:S(2)}) %collective-permute-start.18) | collective-permute-done | bytes 32800 | tf_op jit(solution)/shard_map/ppermute | solution.py:415
  93.9 2.6 %counts.1 = (bf16[32,4,16,128]{3,2,1,0:T(8,128)(2,1)S(1)}, bf16[32,4,16,128]{3,2,1,0:T(8,128)(2,1)S(1)}, bf16[32,4,16,128]{3,2,1,0:T(8,128)(2,1)S(1)}, bf16[32,4...) custom-call(s32[4]{0:T(128)S(1)} %pad_add_fusion.core_ref.place_ref., ...), custom_call_target="tpu_custom_call" | custom-call | flops 536870912 | bytes 13631488 | tf_op jit(solution)/shard_map/counts/pallas_call | solution.py:428
  96.5 2.0 %collective-permute-start.19 = (bf16[16,4,16,128]{3,2,1,0:T(8,128)(2,1)S(1)}, bf16[16,4,16,128]{3,2,1,0:T(8,128)(2,1)S(1)}, u32[]{:S(2)}, u32[]{:S(2)}) collective-permute-start(bf16[16,4,16,128]{3,2,1,0:T(8,128)(2,1)S(1)} %get-tuple-element.57), channel_id=1, source_target_pairs={{0,1},{1,2},{2,3},{3,4},{4,5},{5,6},{6,7},{7,0},{8,9},{9,10},{10,1... | collective-permute-start | bytes 786440 | tf_op jit(solution)/shard_map/ppermute | solution.py:441
  98.6 4.3 %collective-permute-done.19.up_in_ref = bf16[16,4,16,128]{3,2,1,0:T(8,128)(2,1)S(1)} collective-permute-done((bf16[16,4,16,128]{3,2,1,0:T(8,128)(2,1)S(1)}, bf16[16,4,16,128]{3,2,1,0:T(8,128)(2,1)S(1)}, u32[]{:S(2)}, u32[]{:S(2)}) %collective-permute-start.19) | collective-permute-done | bytes 262176 | tf_op jit(solution)/shard_map/ppermute | solution.py:441
  103.0 1.9 %collective-permute-done.20.down_in_ref = bf16[16,4,16,128]{3,2,1,0:T(8,128)(2,1)S(1)} collective-permute-done((bf16[16,4,16,128]{3,2,1,0:T(8,128)(2,1)S(1)}, bf16[16,4,16,128]{3,2,1,0:T(8,128)(2,1)S(1)}, u32[]{:S(2)}, u32[]{:S(2)}) %collective-permute-start.20) | collective-permute-done | bytes 262176 | tf_op jit(solution)/shard_map/ppermute | solution.py:441
  105.0 3.3 %collective-permute-start.21 = (bf16[32,4,16,128]{3,2,1,0:T(8,128)(2,1)S(1)}, bf16[32,4,16,128]{3,2,1,0:T(8,128)(2,1)S(1)}, u32[]{:S(2)}, u32[]{:S(2)}) collective-permute-start(bf16[32,4,16,128]{3,2,1,0:T(8,128)(2,1)S(1)} %get-tuple-element.59), channel_id=1, source_target_pairs={{0,1},{1,2},{2,3},{3,4},{4,5},{5,6},{6,7},{7,0},{8,9},{9,10},{10,1... | collective-permute-start | bytes 1572872 | tf_op jit(solution)/shard_map/ppermute | solution.py:441
  108.4 7.6 %collective-permute-done.21.up_in_ref = bf16[32,4,16,128]{3,2,1,0:T(8,128)(2,1)S(1)} collective-permute-done((bf16[32,4,16,128]{3,2,1,0:T(8,128)(2,1)S(1)}, bf16[32,4,16,128]{3,2,1,0:T(8,128)(2,1)S(1)}, u32[]{:S(2)}, u32[]{:S(2)}) %collective-permute-start.21) | collective-permute-done | bytes 524320 | tf_op jit(solution)/shard_map/ppermute | solution.py:441
  115.9 4.0 %collective-permute-done.22.down_in_ref = bf16[32,4,16,128]{3,2,1,0:T(8,128)(2,1)S(1)} collective-permute-done((bf16[32,4,16,128]{3,2,1,0:T(8,128)(2,1)S(1)}, bf16[32,4,16,128]{3,2,1,0:T(8,128)(2,1)S(1)}, u32[]{:S(2)}, u32[]{:S(2)}) %collective-permute-start.22) | collective-permute-done | bytes 524320 | tf_op jit(solution)/shard_map/ppermute | solution.py:441
  120.2 2.6 %collective-permute-start.23 = (bf16[32,4,16,128]{3,2,1,0:T(8,128)(2,1)S(1)}, bf16[32,4,16,128]{3,2,1,0:T(8,128)(2,1)S(1)}, u32[]{:S(2)}, u32[]{:S(2)}) collective-permute-start(bf16[32,4,16,128]{3,2,1,0:T(8,128)(2,1)S(1)} %get-tuple-element.61), channel_id=1, source_target_pairs={{0,1},{1,2},{2,3},{3,4},{4,5},{5,6},{6,7},{7,0},{8,9},{9,10},{10,1... | collective-permute-start | bytes 1572872 | tf_op jit(solution)/shard_map/ppermute | solution.py:441
  122.8 9.1 %collective-permute-done.23.up_in_ref = bf16[32,4,16,128]{3,2,1,0:T(8,128)(2,1)S(1)} collective-permute-done((bf16[32,4,16,128]{3,2,1,0:T(8,128)(2,1)S(1)}, bf16[32,4,16,128]{3,2,1,0:T(8,128)(2,1)S(1)}, u32[]{:S(2)}, u32[]{:S(2)}) %collective-permute-start.23) | collective-permute-done | bytes 524320 | tf_op jit(solution)/shard_map/ppermute | solution.py:441
  131.8 2.8 %collective-permute-done.24.down_in_ref = bf16[32,4,16,128]{3,2,1,0:T(8,128)(2,1)S(1)} collective-permute-done((bf16[32,4,16,128]{3,2,1,0:T(8,128)(2,1)S(1)}, bf16[32,4,16,128]{3,2,1,0:T(8,128)(2,1)S(1)}, u32[]{:S(2)}, u32[]{:S(2)}) %collective-permute-start.24) | collective-permute-done | bytes 524320 | tf_op jit(solution)/shard_map/ppermute | solution.py:441
  134.9 1.8 %collective-permute-start.25 = (bf16[32,4,16,128]{3,2,1,0:T(8,128)(2,1)S(1)}, bf16[32,4,16,128]{3,2,1,0:T(8,128)(2,1)S(1)}, u32[]{:S(2)}, u32[]{:S(2)}) collective-permute-start(bf16[32,4,16,128]{3,2,1,0:T(8,128)(2,1)S(1)} %get-tuple-element.63), channel_id=1, source_target_pairs={{0,1},{1,2},{2,3},{3,4},{4,5},{5,6},{6,7},{7,0},{8,9},{9,10},{10,1... | collective-permute-start | bytes 1572872 | tf_op jit(solution)/shard_map/ppermute | solution.py:441
  137.0 0.6 slice_reduce_fusion
  137.6 6.5 %collective-permute-done.25.up_in_ref = bf16[32,4,16,128]{3,2,1,0:T(8,128)(2,1)S(1)} collective-permute-done((bf16[32,4,16,128]{3,2,1,0:T(8,128)(2,1)S(1)}, bf16[32,4,16,128]{3,2,1,0:T(8,128)(2,1)S(1)}, u32[]{:S(2)}, u32[]{:S(2)}) %collective-permute-start.25) | collective-permute-done | bytes 524320 | tf_op jit(solution)/shard_map/ppermute | solution.py:441
  144.1 1.8 %collective-permute-done.26.down_in_ref = bf16[32,4,16,128]{3,2,1,0:T(8,128)(2,1)S(1)} collective-permute-done((bf16[32,4,16,128]{3,2,1,0:T(8,128)(2,1)S(1)}, bf16[32,4,16,128]{3,2,1,0:T(8,128)(2,1)S(1)}, u32[]{:S(2)}, u32[]{:S(2)}) %collective-permute-start.26) | collective-permute-done | bytes 524320 | tf_op jit(solution)/shard_map/ppermute | solution.py:441
  145.9 1.5 %ring_last.1 = bf16[32,4,16,128]{3,2,1,0:T(8,128)(2,1)} custom-call(s32[4]{0:T(128)S(1)} %pad_add_fusion.core_ref.place_ref.refs_0_, bf16[32,4,16,128]{3,2,1,0:T(8,128)(2,1)S(1)} %get-tuple-element.50.own_ref, bf16[32,4,16,128]{3,2,1,0:T(8,128)(2,1)S(1)} %collective-permute-done.25.up_in_ref, bf16[32,4,16,128]{3,2,1,0:T(8,128)(2,1)S(1)} %collective-permute-done.26.down_in_ref), custom_call_target="tpu_custom_call" | custom-call | tf_op jit(solution)/shard_map/ring_last/pallas_call | solution.py:459
  (45 shorter events, 3.3 us)
Async XLA Ops:
  0.6 1.6 %copy-start.1 = (bf16[32,256,128]{2,1,0:T(8,128)(2,1)S(1)}, bf16[32,256,128]{2,1,0:T(8,128)(2,1)}, u32[]{:S(2)}) copy-start(bf16[32,256,128]{2,1,0:T(8,128)(2,1)} %table_ref.4) | copy-start | bytes 6291460
  2.2 0.7 copy-start.3
  2.9 1.3 copy-start.7
  3.0 1.9 %copy-start.2 = (bf16[32,256,128]{2,1,0:T(8,128)(2,1)S(1)}, bf16[32,256,128]{2,1,0:T(8,128)(2,1)}, u32[]{:S(2)}) copy-start(bf16[32,256,128]{2,1,0:T(8,128)(2,1)} %table_ref.4) | copy-start | bytes 6291460
  3.0 1.9 %copy-start.4 = (s32[64,32]{0,1:T(8,128)S(1)}, s32[64,32]{0,1:T(8,128)}, u32[]{:S(2)}) copy-start(s32[64,32]{0,1:T(8,128)} %param.8) | copy-start | bytes 24580
  4.2 1.9 %collective-permute-start = (bf16[17,64,128]{2,1,0:T(8,128)(2,1)S(1)}, bf16[17,64,128]{2,1,0:T(8,128)(2,1)S(1)}, u32[]{:S(2)}, u32[]{:S(2)}) collective-permute-start(bf16[17,64,128]{2,1,0:T(8,128)(2,1)S(1)} %child_scores.2), channel_id=1, source_target_pairs={{0,8},{8,0},{16,24},{24,16},{32,40},{40,32},{48,56},{56,48},{64,72... | collective-permute-start | bytes 835592 | tf_op jit(solution)/shard_map/ppermute | solution.py:342
  4.3 1.8 %collective-permute-start.1 = (s32[4,32]{1,0:T(4,128)S(1)}, s32[4,32]{1,0:T(4,128)S(1)}, u32[]{:S(2)}, u32[]{:S(2)}) collective-permute-start(s32[4,32]{1,0:T(4,128)S(1)} %bitcast.19), channel_id=1, source_target_pairs={{0,8},{8,0},{16,24},{24,16},{32,40},{40,32},{48,56},{56,48},{64,72... | collective-permute-start | bytes 1544 | tf_op jit(solution)/shard_map/ppermute | solution.py:342
  6.7 10.6 %collective-permute-start.2 = (bf16[33,64,128]{2,1,0:T(8,128)(2,1)S(1)}, bf16[33,64,128]{2,1,0:T(8,128)(2,1)S(1)}, u32[]{:S(2)}, u32[]{:S(2)}) collective-permute-start(bf16[33,64,128]{2,1,0:T(8,128)(2,1)S(1)} %pack.1), channel_id=1, source_target_pairs={{0,64},{8,24},{16,80},{24,40},{32,96},{40,56},{48,112},{56,8},{64,... | collective-permute-start | bytes 1622024 | tf_op jit(solution)/shard_map/ppermute | solution.py:355
  8.3 14.4 %collective-permute-start.3 = (bf16[33,64,128]{2,1,0:T(8,128)(2,1)S(1)}, bf16[33,64,128]{2,1,0:T(8,128)(2,1)S(1)}, u32[]{:S(2)}, u32[]{:S(2)}) collective-permute-start(bf16[33,64,128]{2,1,0:T(8,128)(2,1)S(1)} %pack.1), channel_id=1, source_target_pairs={{0,192},{8,56},{16,208},{24,8},{32,224},{40,24},{48,240},{56,40},{... | collective-permute-start | bytes 1622024 | tf_op jit(solution)/shard_map/ppermute | solution.py:355
  10.0 14.1 %collective-permute-start.4 = (bf16[33,64,128]{2,1,0:T(8,128)(2,1)S(1)}, bf16[33,64,128]{2,1,0:T(8,128)(2,1)S(1)}, u32[]{:S(2)}, u32[]{:S(2)}) collective-permute-start(bf16[33,64,128]{2,1,0:T(8,128)(2,1)S(1)} %pack.1), channel_id=1, source_target_pairs={{0,128},{8,40},{16,144},{24,56},{32,160},{40,8},{48,176},{56,24},{... | collective-permute-start | bytes 1622024 | tf_op jit(solution)/shard_map/ppermute | solution.py:355
  24.3 15.8 %collective-permute-start.6 = (bf16[66,64,128]{2,1,0:T(8,128)(2,1)S(1)}, bf16[66,64,128]{2,1,0:T(8,128)(2,1)S(1)}, u32[]{:S(2)}, u32[]{:S(2)}) collective-permute-start(bf16[66,64,128]{2,1,0:T(8,128)(2,1)S(1)} %constant_dynamic-update-slice_fusion.refs_1_), channel_id=1, source_target_pairs={{0,48},{8,200},{16,0},{24,216},{32,16},{40,232},{48,32},{56,248},{... | collective-permute-start | bytes 3244040 | tf_op jit(solution)/shard_map/ppermute | solution.py:355
  27.4 42.0 %copy-start.5 = (f32[32,128]{1,0:T(8,128)S(1)}, f32[32,128]{1,0:T(8,128)}, u32[]{:S(2)}) copy-start(f32[32,128]{1,0:T(8,128)} %prior_ref.3) | copy-start | bytes 49156
  27.5 42.0 %copy-start.8 = (bf16[32,256,128]{2,1,0:T(8,128)(2,1)S(1)}, bf16[32,256,128]{2,1,0:T(8,128)(2,1)}, u32[]{:S(2)}) copy-start(bf16[32,256,128]{2,1,0:T(8,128)(2,1)} %table_ref.5) | copy-start | bytes 6291460
  27.5 42.0 %copy-start.9 = (s32[64,32]{0,1:T(8,128)S(1)}, s32[64,32]{0,1:T(8,128)}, u32[]{:S(2)}) copy-start(s32[64,32]{0,1:T(8,128)} %param.9) | copy-start | bytes 24580
  27.5 16.4 %collective-permute-start.5 = (bf16[66,64,128]{2,1,0:T(8,128)(2,1)S(1)}, bf16[66,64,128]{2,1,0:T(8,128)(2,1)S(1)}, u32[]{:S(2)}, u32[]{:S(2)}) collective-permute-start(bf16[66,64,128]{2,1,0:T(8,128)(2,1)S(1)} %pad_maximum_fusion.refs_0_), channel_id=1, source_target_pairs={{0,16},{8,72},{16,32},{24,88},{32,48},{40,104},{48,0},{56,120},{64... | collective-permute-start | bytes 3244040 | tf_op jit(solution)/shard_map/ppermute | solution.py:355
  27.6 27.9 %collective-permute-start.7 = (bf16[66,64,128]{2,1,0:T(8,128)(2,1)S(1)}, bf16[66,64,128]{2,1,0:T(8,128)(2,1)S(1)}, u32[]{:S(2)}, u32[]{:S(2)}) collective-permute-start(bf16[66,64,128]{2,1,0:T(8,128)(2,1)S(1)} %constant_dynamic-update-slice_fusion.refs_1_), channel_id=1, source_target_pairs={{0,16},{8,72},{16,32},{24,88},{32,48},{40,104},{48,0},{56,120},{64... | collective-permute-start | bytes 3244040 | tf_op jit(solution)/shard_map/ppermute | solution.py:355
  28.1 27.4 %collective-permute-start.8 = (bf16[66,64,128]{2,1,0:T(8,128)(2,1)S(1)}, bf16[66,64,128]{2,1,0:T(8,128)(2,1)S(1)}, u32[]{:S(2)}, u32[]{:S(2)}) collective-permute-start(bf16[66,64,128]{2,1,0:T(8,128)(2,1)S(1)} %pad_maximum_fusion.refs_0_), channel_id=1, source_target_pairs={{0,48},{8,200},{16,0},{24,216},{32,16},{40,232},{48,32},{56,248},{... | collective-permute-start | bytes 3244040 | tf_op jit(solution)/shard_map/ppermute | solution.py:355
  43.9 19.3 %collective-permute-start.10 = (bf16[66,64,128]{2,1,0:T(8,128)(2,1)S(1)}, bf16[66,64,128]{2,1,0:T(8,128)(2,1)S(1)}, u32[]{:S(2)}, u32[]{:S(2)}) collective-permute-start(bf16[66,64,128]{2,1,0:T(8,128)(2,1)S(1)} %collective-permute-done.6.refs_5_), channel_id=1, source_target_pairs={{0,48},{8,200},{16,0},{24,216},{32,16},{40,232},{48,32},{56,248},{... | collective-permute-start | bytes 3244040 | tf_op jit(solution)/shard_map/ppermute | solution.py:355
  43.9 23.2 %collective-permute-start.9 = (bf16[66,64,128]{2,1,0:T(8,128)(2,1)S(1)}, bf16[66,64,128]{2,1,0:T(8,128)(2,1)S(1)}, u32[]{:S(2)}, u32[]{:S(2)}) collective-permute-start(bf16[66,64,128]{2,1,0:T(8,128)(2,1)S(1)} %collective-permute-done.5.refs_2_), channel_id=1, source_target_pairs={{0,16},{8,72},{16,32},{24,88},{32,48},{40,104},{48,0},{56,120},{64... | collective-permute-start | bytes 3244040 | tf_op jit(solution)/shard_map/ppermute | solution.py:355
  67.1 3.9 %copy-start = (bf16[32,1,4,128,128]{4,3,2,1,0:T(8,128)(2,1)S(1)}, bf16[32,1,4,128,128]{4,3,2,1,0:T(8,128)(2,1)}, u32[]{:S(2)}) copy-start(bf16[32,1,4,128,128]{4,3,2,1,0:T(8,128)(2,1)} %param.13) | copy-start | bytes 12582916
  69.2 3.5 %collective-permute-start.11 = (bf16[65,64,128]{2,1,0:T(8,128)(2,1)S(1)}, bf16[65,64,128]{2,1,0:T(8,128)(2,1)S(1)}, u32[]{:S(2)}, u32[]{:S(2)}) collective-permute-start(bf16[65,64,128]{2,1,0:T(8,128)(2,1)S(1)} %get-tuple-element.41), channel_id=1, source_target_pairs={{0,8},{8,0},{16,24},{24,16},{32,40},{40,32},{48,56},{56,48},{64,72... | collective-permute-start | bytes 3194888 | tf_op jit(solution)/shard_map/ppermute | solution.py:388
  69.5 1.5 copy-start.6
  74.8 1.4 collective-permute-start.12
  76.3 5.2 %collective-permute-start.13 = (f32[64,128]{1,0:T(8,128)S(1)}, f32[64,128]{1,0:T(8,128)S(1)}, u32[]{:S(2)}, u32[]{:S(2)}) collective-permute-start(f32[64,128]{1,0:T(8,128)S(1)} %merge_core.1.refs_0_), channel_id=1, source_target_pairs={{0,64},{8,24},{16,80},{24,40},{32,96},{40,56},{48,112},{56,8},{64,... | collective-permute-start | bytes 98312 | tf_op jit(solution)/shard_map/ppermute | solution.py:415
  77.8 3.9 %collective-permute-start.14 = (f32[64,128]{1,0:T(8,128)S(1)}, f32[64,128]{1,0:T(8,128)S(1)}, u32[]{:S(2)}, u32[]{:S(2)}) collective-permute-start(f32[64,128]{1,0:T(8,128)S(1)} %merge_core.1.refs_0_), channel_id=1, source_target_pairs={{0,192},{8,56},{16,208},{24,8},{32,224},{40,24},{48,240},{56,40},{... | collective-permute-start | bytes 98312 | tf_op jit(solution)/shard_map/ppermute | solution.py:415
  79.6 5.4 %collective-permute-start.15 = (f32[64,128]{1,0:T(8,128)S(1)}, f32[64,128]{1,0:T(8,128)S(1)}, u32[]{:S(2)}, u32[]{:S(2)}) collective-permute-start(f32[64,128]{1,0:T(8,128)S(1)} %merge_core.1.refs_0_), channel_id=1, source_target_pairs={{0,128},{8,40},{16,144},{24,56},{32,160},{40,8},{48,176},{56,24},{... | collective-permute-start | bytes 98312 | tf_op jit(solution)/shard_map/ppermute | solution.py:415
  85.2 5.2 %collective-permute-start.16 = (f32[64,128]{1,0:T(8,128)S(1)}, f32[64,128]{1,0:T(8,128)S(1)}, u32[]{:S(2)}, u32[]{:S(2)}) collective-permute-start(f32[64,128]{1,0:T(8,128)S(1)} %merge_a.1.refs_2_), channel_id=1, source_target_pairs={{0,16},{8,72},{16,32},{24,88},{32,48},{40,104},{48,0},{56,120},{64... | collective-permute-start | bytes 98312 | tf_op jit(solution)/shard_map/ppermute | solution.py:415
  85.2 5.1 %collective-permute-start.17 = (f32[64,128]{1,0:T(8,128)S(1)}, f32[64,128]{1,0:T(8,128)S(1)}, u32[]{:S(2)}, u32[]{:S(2)}) collective-permute-start(f32[64,128]{1,0:T(8,128)S(1)} %merge_a.1.refs_2_), channel_id=1, source_target_pairs={{0,48},{8,200},{16,0},{24,216},{32,16},{40,232},{48,32},{56,248},{... | collective-permute-start | bytes 98312 | tf_op jit(solution)/shard_map/ppermute | solution.py:415
  88.5 5.4 %collective-permute-start.18 = (f32[64,128]{1,0:T(8,128)S(1)}, f32[64,128]{1,0:T(8,128)S(1)}, u32[]{:S(2)}, u32[]{:S(2)}) collective-permute-start(f32[64,128]{1,0:T(8,128)S(1)} %merge_a.1.refs_2_), channel_id=1, source_target_pairs={{0,32},{8,136},{16,48},{24,152},{32,0},{40,168},{48,16},{56,184},{... | collective-permute-start | bytes 98312 | tf_op jit(solution)/shard_map/ppermute | solution.py:415
  96.5 6.4 %collective-permute-start.19 = (bf16[16,4,16,128]{3,2,1,0:T(8,128)(2,1)S(1)}, bf16[16,4,16,128]{3,2,1,0:T(8,128)(2,1)S(1)}, u32[]{:S(2)}, u32[]{:S(2)}) collective-permute-start(bf16[16,4,16,128]{3,2,1,0:T(8,128)(2,1)S(1)} %get-tuple-element.57), channel_id=1, source_target_pairs={{0,1},{1,2},{2,3},{3,4},{4,5},{5,6},{6,7},{7,0},{8,9},{9,10},{10,1... | collective-permute-start | bytes 786440 | tf_op jit(solution)/shard_map/ppermute | solution.py:441
  98.5 6.4 %collective-permute-start.20 = (bf16[16,4,16,128]{3,2,1,0:T(8,128)(2,1)S(1)}, bf16[16,4,16,128]{3,2,1,0:T(8,128)(2,1)S(1)}, u32[]{:S(2)}, u32[]{:S(2)}) collective-permute-start(bf16[16,4,16,128]{3,2,1,0:T(8,128)(2,1)S(1)} %get-tuple-element.58), channel_id=1, source_target_pairs={{0,7},{1,0},{2,1},{3,2},{4,3},{5,4},{6,5},{7,6},{8,15},{9,8},{10,9... | collective-permute-start | bytes 786440 | tf_op jit(solution)/shard_map/ppermute | solution.py:441
  105.0 10.9 %collective-permute-start.21 = (bf16[32,4,16,128]{3,2,1,0:T(8,128)(2,1)S(1)}, bf16[32,4,16,128]{3,2,1,0:T(8,128)(2,1)S(1)}, u32[]{:S(2)}, u32[]{:S(2)}) collective-permute-start(bf16[32,4,16,128]{3,2,1,0:T(8,128)(2,1)S(1)} %get-tuple-element.59), channel_id=1, source_target_pairs={{0,1},{1,2},{2,3},{3,4},{4,5},{5,6},{6,7},{7,0},{8,9},{9,10},{10,1... | collective-permute-start | bytes 1572872 | tf_op jit(solution)/shard_map/ppermute | solution.py:441
  108.4 11.6 %collective-permute-start.22 = (bf16[32,4,16,128]{3,2,1,0:T(8,128)(2,1)S(1)}, bf16[32,4,16,128]{3,2,1,0:T(8,128)(2,1)S(1)}, u32[]{:S(2)}, u32[]{:S(2)}) collective-permute-start(bf16[32,4,16,128]{3,2,1,0:T(8,128)(2,1)S(1)} %get-tuple-element.60), channel_id=1, source_target_pairs={{0,7},{1,0},{2,1},{3,2},{4,3},{5,4},{6,5},{7,6},{8,15},{9,8},{10,9... | collective-permute-start | bytes 1572872 | tf_op jit(solution)/shard_map/ppermute | solution.py:441
  120.2 11.7 %collective-permute-start.23 = (bf16[32,4,16,128]{3,2,1,0:T(8,128)(2,1)S(1)}, bf16[32,4,16,128]{3,2,1,0:T(8,128)(2,1)S(1)}, u32[]{:S(2)}, u32[]{:S(2)}) collective-permute-start(bf16[32,4,16,128]{3,2,1,0:T(8,128)(2,1)S(1)} %get-tuple-element.61), channel_id=1, source_target_pairs={{0,1},{1,2},{2,3},{3,4},{4,5},{5,6},{6,7},{7,0},{8,9},{9,10},{10,1... | collective-permute-start | bytes 1572872 | tf_op jit(solution)/shard_map/ppermute | solution.py:441
  122.8 11.8 %collective-permute-start.24 = (bf16[32,4,16,128]{3,2,1,0:T(8,128)(2,1)S(1)}, bf16[32,4,16,128]{3,2,1,0:T(8,128)(2,1)S(1)}, u32[]{:S(2)}, u32[]{:S(2)}) collective-permute-start(bf16[32,4,16,128]{3,2,1,0:T(8,128)(2,1)S(1)} %get-tuple-element.62), channel_id=1, source_target_pairs={{0,7},{1,0},{2,1},{3,2},{4,3},{5,4},{6,5},{7,6},{8,15},{9,8},{10,9... | collective-permute-start | bytes 1572872 | tf_op jit(solution)/shard_map/ppermute | solution.py:441
  134.9 9.3 %collective-permute-start.25 = (bf16[32,4,16,128]{3,2,1,0:T(8,128)(2,1)S(1)}, bf16[32,4,16,128]{3,2,1,0:T(8,128)(2,1)S(1)}, u32[]{:S(2)}, u32[]{:S(2)}) collective-permute-start(bf16[32,4,16,128]{3,2,1,0:T(8,128)(2,1)S(1)} %get-tuple-element.63), channel_id=1, source_target_pairs={{0,1},{1,2},{2,3},{3,4},{4,5},{5,6},{6,7},{7,0},{8,9},{9,10},{10,1... | collective-permute-start | bytes 1572872 | tf_op jit(solution)/shard_map/ppermute | solution.py:441
  136.7 9.2 %collective-permute-start.26 = (bf16[32,4,16,128]{3,2,1,0:T(8,128)(2,1)S(1)}, bf16[32,4,16,128]{3,2,1,0:T(8,128)(2,1)S(1)}, u32[]{:S(2)}, u32[]{:S(2)}) collective-permute-start(bf16[32,4,16,128]{3,2,1,0:T(8,128)(2,1)S(1)} %get-tuple-element.64), channel_id=1, source_target_pairs={{0,7},{1,0},{2,1},{3,2},{4,3},{5,4},{6,5},{7,6},{8,15},{9,8},{10,9... | collective-permute-start | bytes 1572872 | tf_op jit(solution)/shard_map/ppermute | solution.py:441

commit v6 on v5

--- a/solution.py
+++ b/solution.py
@@ -75,8 +75,10 @@
     ((1, 3), (2, 3)),
     ((0, 1), (3, 1)),
     ((1, 1), (2, 1)),
-    ((0, 2), (3, 2)),
-    ((1, 2), (2, 2)),
+    ((0, 2),),
+    ((3, 2),),
+    ((1, 2),),
+    ((2, 2),),
 )
 
 
@@ -363,14 +365,18 @@
         cost_estimate=cost(1 << 28, 3 << 20, 1 << 21),
         name="parent_scores",
     )(parent_values.T, parent_logits, prior_logits)
-    a1, a3, a2 = lax.optimization_barrier((send(own, 1, 0), send(own, -1, 0), send(own, 2, 0)))
+    cut = (PIECE + 1) // 2
+    a1, a3 = lax.optimization_barrier((send(own, 1, 0), send(own, -1, 0)))
+    c1, c3 = send(a1[:cut], 1, 0), send(a3[cut:], -1, 0)
     near = jnp.concatenate([own, a1])
     near_up, near_down = send(near, 0, 1), send(near, 0, -1)
-    far = jnp.concatenate([a3, a2])
+    c1, c3 = lax.optimization_barrier((c1, c3))
+    far = jnp.concatenate([a3, c1, c3])
     far_up, far_down = send(far, 0, 1), send(far, 0, -1)
-    near_up, far_down = lax.optimization_barrier((near_up, far_down))
-    next_up = send(near_up, 0, 1)
-    next_down = send(far_down, 0, -1)
+    near_up, near_down = lax.optimization_barrier((near_up, near_down))
+    next_up, next_down = send(near_up[:PIECE], 0, 1), send(near_down[PIECE:], 0, -1)
+    far_up, far_down, near_down = lax.optimization_barrier((far_up, far_down, near_down))
+    last_up, last_down = send(far_up[:PIECE], 0, 1), send(far_down[PIECE:], 0, -1)
     slots = shape((HALF * NZ + 1, S_LOC, BLK), bf16)
     for_other, pool, powers = pl.pallas_call(
         pick_other_kernel,
@@ -384,7 +390,7 @@
         compiler_params=params(22),
         cost_estimate=cost(1 << 22, 20 << 20, 1 << 20),
         name="pick_other",
-    )(place, other_columns, near, far, near_up, far_up, near_down, far_down, next_up, next_down)
+    )(place, other_columns, near, far, near_up, far_up, near_down, far_down, next_up, next_down, last_up, last_down)
     other = lax.ppermute(for_other, "region", SWAP)
     half_sums = shape((HALF, S_LOC, BLK), f32)
     scores_all = shape((P_SIZE, S_LOC, BLK), f32)

time: 148 us -> 141 us (0.953)
  waiting for transfers between devices: 95.6 us -> 80.9 us
  starting transfers between devices: 32.3 us -> 40.8 us
    ppermute x9 -> x12, waiting for transfers between devices: 46.5 us -> 33.2 us  [send(): return lax.ppermute(value, 'region', along(a, b))]
    ppermute x9 -> x12, starting transfers between devices: 13.6 us -> 20.7 us  [send(): return lax.ppermute(value, 'region', along(a, b))]
    ppermute x7, starting transfers between devices: 7.66 us -> 9.56 us  [body(): others = [lax.ppermute(stats, 'region', p) for p in pairs]]
    ppermute x7, waiting for transfers between devices: 11.2 us -> 9.32 us  [body(): others = [lax.ppermute(stats, 'region', p) for p in pairs]]
  transfers between devices with their start and end apart: 27 -> 30, of which waited for: 22 -> 25; matrix products, arithmetic and copies ran while one was open for 1% -> 1% of each run, Pallas kernels for 3% -> 3%
where the time goes in v6:
time: 141 us
  waiting for transfers between devices  80.9 us (57%)
  starting transfers between devices  40.8 us (29%)
  Pallas kernels  15.4 us (11%)
  local copies, waits for them, and re-layouts  3.25 us (2%)
    ppermute x12, waiting for transfers between devices, send(): return lax.ppermute(value, 'region', along(a, b))  33.2 us
    ppermute x4, waiting for transfers between devices, ring(): lax.ppermute(up, 'batch', shift(1))  27.5 us
    ppermute x12, starting transfers between devices, send(): return lax.ppermute(value, 'region', along(a, b))  20.7 us
    ppermute x4, waiting for transfers between devices, ring(): lax.ppermute(down, 'batch', shift(-1))  10.8 us
    ppermute x7, starting transfers between devices, body(): others = [lax.ppermute(stats, 'region', p) for p in pairs]  9.56 us
    ppermute x4, starting transfers between devices, ring(): lax.ppermute(up, 'batch', shift(1))  9.47 us
    ppermute x7, waiting for transfers between devices, body(): others = [lax.ppermute(stats, 'region', p) for p in pairs]  9.32 us
  transfers between devices with their start and end apart: 30, of which 25 were waited for; matrix products, arithmetic and copies ran while one was open for 1% of the time, Pallas kernels for 3%

profile of v6, /device:TPU:32, one launch (start us, length us, event | category | flops | bytes accessed | tf_op | source)
XLA Modules:
  0.0 141.3 jit_solution(15147512060416025896)
XLA Ops:
  0.6 1.6 %copy-done.1 = bf16[32,256,128]{2,1,0:T(8,128)(2,1)S(1)} copy-done((bf16[32,256,128]{2,1,0:T(8,128)(2,1)S(1)}, bf16[32,256,128]{2,1,0:T(8,128)(2,1)}, u32[]{:S(2)}) %copy-start.1) | copy-done | bytes 2097176
  2.2 0.7 copy-done.3
  3.0 1.2 child_scores.2
  4.9 1.2 child_scores.3.own_ref
  6.7 1.5 %collective-permute-start.2 = (bf16[33,64,128]{2,1,0:T(8,128)(2,1)S(1)}, bf16[33,64,128]{2,1,0:T(8,128)(2,1)S(1)}, u32[]{:S(2)}, u32[]{:S(2)}) collective-permute-start(bf16[33,64,128]{2,1,0:T(8,128)(2,1)S(1)} %pack.1), channel_id=1, source_target_pairs={{0,64},{8,24},{16,80},{24,40},{32,96},{40,56},{48,112},{56,8},{64,... | collective-permute-start | bytes 1622024 | tf_op jit(solution)/shard_map/ppermute | solution.py:357
  8.3 1.7 %collective-permute-start.3 = (bf16[33,64,128]{2,1,0:T(8,128)(2,1)S(1)}, bf16[33,64,128]{2,1,0:T(8,128)(2,1)S(1)}, u32[]{:S(2)}, u32[]{:S(2)}) collective-permute-start(bf16[33,64,128]{2,1,0:T(8,128)(2,1)S(1)} %pack.1), channel_id=1, source_target_pairs={{0,192},{8,56},{16,208},{24,8},{32,224},{40,24},{48,240},{56,40},{... | collective-permute-start | bytes 1622024 | tf_op jit(solution)/shard_map/ppermute | solution.py:357
  10.0 7.3 %collective-permute-done.2 = bf16[33,64,128]{2,1,0:T(8,128)(2,1)S(1)} collective-permute-done((bf16[33,64,128]{2,1,0:T(8,128)(2,1)S(1)}, bf16[33,64,128]{2,1,0:T(8,128)(2,1)S(1)}, u32[]{:S(2)}, u32[]{:S(2)}) %collective-permute-start.2) | collective-permute-done | bytes 540704 | tf_op jit(solution)/shard_map/ppermute | solution.py:357
  17.7 1.6 %collective-permute-start.4 = (bf16[17,64,128]{2,1,0:T(8,128)(2,1)S(1)}, bf16[17,64,128]{2,1,0:T(8,128)(2,1)S(1)}, u32[]{:S(2)}, u32[]{:S(2)}) collective-permute-start(bf16[17,64,128]{2,1,0:T(8,128)(2,1)S(1)} %slice.21), channel_id=1, source_target_pairs={{0,64},{8,24},{16,80},{24,40},{32,96},{40,56},{48,112},{56,8},{64,... | collective-permute-start | bytes 835592 | tf_op jit(solution)/shard_map/ppermute | solution.py:357
  19.2 1.8 %collective-permute-start.5 = (bf16[16,64,128]{2,1,0:T(8,128)(2,1)S(1)}, bf16[16,64,128]{2,1,0:T(8,128)(2,1)S(1)}, u32[]{:S(2)}, u32[]{:S(2)}) collective-permute-start(bf16[16,64,128]{2,1,0:T(8,128)(2,1)S(1)} %slice.22), channel_id=1, source_target_pairs={{0,192},{8,56},{16,208},{24,8},{32,224},{40,24},{48,240},{56,40},{... | collective-permute-start | bytes 786440 | tf_op jit(solution)/shard_map/ppermute | solution.py:357
  21.2 1.7 %collective-permute-start.6 = (bf16[66,64,128]{2,1,0:T(8,128)(2,1)S(1)}, bf16[66,64,128]{2,1,0:T(8,128)(2,1)S(1)}, u32[]{:S(2)}, u32[]{:S(2)}) collective-permute-start(bf16[66,64,128]{2,1,0:T(8,128)(2,1)S(1)} %pad_maximum_fusion.refs_0_), channel_id=1, source_target_pairs={{0,16},{8,72},{16,32},{24,88},{32,48},{40,104},{48,0},{56,120},{64... | collective-permute-start | bytes 3244040 | tf_op jit(solution)/shard_map/ppermute | solution.py:357
  22.8 1.7 %collective-permute-start.7 = (bf16[66,64,128]{2,1,0:T(8,128)(2,1)S(1)}, bf16[66,64,128]{2,1,0:T(8,128)(2,1)S(1)}, u32[]{:S(2)}, u32[]{:S(2)}) collective-permute-start(bf16[66,64,128]{2,1,0:T(8,128)(2,1)S(1)} %pad_maximum_fusion.refs_0_), channel_id=1, source_target_pairs={{0,48},{8,200},{16,0},{24,216},{32,16},{40,232},{48,32},{56,248},{... | collective-permute-start | bytes 3244040 | tf_op jit(solution)/shard_map/ppermute | solution.py:357
  24.5 3.4 %collective-permute-done.5 = bf16[16,64,128]{2,1,0:T(8,128)(2,1)S(1)} collective-permute-done((bf16[16,64,128]{2,1,0:T(8,128)(2,1)S(1)}, bf16[16,64,128]{2,1,0:T(8,128)(2,1)S(1)}, u32[]{:S(2)}, u32[]{:S(2)}) %collective-permute-start.5) | collective-permute-done | bytes 262176 | tf_op jit(solution)/shard_map/ppermute | solution.py:357
  28.0 2.2 %collective-permute-start.8 = (bf16[66,64,128]{2,1,0:T(8,128)(2,1)S(1)}, bf16[66,64,128]{2,1,0:T(8,128)(2,1)S(1)}, u32[]{:S(2)}, u32[]{:S(2)}) collective-permute-start(bf16[66,64,128]{2,1,0:T(8,128)(2,1)S(1)} %constant_dynamic-update-slice_fusion.refs_1_), channel_id=1, source_target_pairs={{0,16},{8,72},{16,32},{24,88},{32,48},{40,104},{48,0},{56,120},{64... | collective-permute-start | bytes 3244040 | tf_op jit(solution)/shard_map/ppermute | solution.py:357
  30.2 1.5 %collective-permute-start.9 = (bf16[66,64,128]{2,1,0:T(8,128)(2,1)S(1)}, bf16[66,64,128]{2,1,0:T(8,128)(2,1)S(1)}, u32[]{:S(2)}, u32[]{:S(2)}) collective-permute-start(bf16[66,64,128]{2,1,0:T(8,128)(2,1)S(1)} %constant_dynamic-update-slice_fusion.refs_1_), channel_id=1, source_target_pairs={{0,48},{8,200},{16,0},{24,216},{32,16},{40,232},{48,32},{56,248},{... | collective-permute-start | bytes 3244040 | tf_op jit(solution)/shard_map/ppermute | solution.py:357
  31.8 5.9 %collective-permute-done.6.refs_2_ = bf16[66,64,128]{2,1,0:T(8,128)(2,1)S(1)} collective-permute-done((bf16[66,64,128]{2,1,0:T(8,128)(2,1)S(1)}, bf16[66,64,128]{2,1,0:T(8,128)(2,1)S(1)}, u32[]{:S(2)}, u32[]{:S(2)}) %collective-permute-start.6) | collective-permute-done | bytes 1081376 | tf_op jit(solution)/shard_map/ppermute | solution.py:357
  38.0 1.7 %collective-permute-start.10 = (bf16[33,64,128]{2,1,0:T(8,128)(2,1)S(1)}, bf16[33,64,128]{2,1,0:T(8,128)(2,1)S(1)}, u32[]{:S(2)}, u32[]{:S(2)}) collective-permute-start(bf16[33,64,128]{2,1,0:T(8,128)(2,1)S(1)} %slice.23), channel_id=1, source_target_pairs={{0,16},{8,72},{16,32},{24,88},{32,48},{40,104},{48,0},{56,120},{64... | collective-permute-start | bytes 1622024 | tf_op jit(solution)/shard_map/ppermute | solution.py:357
  39.7 1.7 %collective-permute-start.11 = (bf16[33,64,128]{2,1,0:T(8,128)(2,1)S(1)}, bf16[33,64,128]{2,1,0:T(8,128)(2,1)S(1)}, u32[]{:S(2)}, u32[]{:S(2)}) collective-permute-start(bf16[33,64,128]{2,1,0:T(8,128)(2,1)S(1)} %slice.24), channel_id=1, source_target_pairs={{0,48},{8,200},{16,0},{24,216},{32,16},{40,232},{48,32},{56,248},{... | collective-permute-start | bytes 1622024 | tf_op jit(solution)/shard_map/ppermute | solution.py:357
  41.4 7.7 %collective-permute-done.8.refs_3_ = bf16[66,64,128]{2,1,0:T(8,128)(2,1)S(1)} collective-permute-done((bf16[66,64,128]{2,1,0:T(8,128)(2,1)S(1)}, bf16[66,64,128]{2,1,0:T(8,128)(2,1)S(1)}, u32[]{:S(2)}, u32[]{:S(2)}) %collective-permute-start.8) | collective-permute-done | bytes 1081376 | tf_op jit(solution)/shard_map/ppermute | solution.py:357
  49.6 1.8 %collective-permute-start.12 = (bf16[33,64,128]{2,1,0:T(8,128)(2,1)S(1)}, bf16[33,64,128]{2,1,0:T(8,128)(2,1)S(1)}, u32[]{:S(2)}, u32[]{:S(2)}) collective-permute-start(bf16[33,64,128]{2,1,0:T(8,128)(2,1)S(1)} %slice.25), channel_id=1, source_target_pairs={{0,16},{8,72},{16,32},{24,88},{32,48},{40,104},{48,0},{56,120},{64... | collective-permute-start | bytes 1622024 | tf_op jit(solution)/shard_map/ppermute | solution.py:357
  51.5 1.7 %collective-permute-start.13 = (bf16[33,64,128]{2,1,0:T(8,128)(2,1)S(1)}, bf16[33,64,128]{2,1,0:T(8,128)(2,1)S(1)}, u32[]{:S(2)}, u32[]{:S(2)}) collective-permute-start(bf16[33,64,128]{2,1,0:T(8,128)(2,1)S(1)} %slice.26), channel_id=1, source_target_pairs={{0,48},{8,200},{16,0},{24,216},{32,16},{40,232},{48,32},{56,248},{... | collective-permute-start | bytes 1622024 | tf_op jit(solution)/shard_map/ppermute | solution.py:357
  53.2 1.7 %collective-permute-done.10.refs_6_ = bf16[33,64,128]{2,1,0:T(8,128)(2,1)S(1)} collective-permute-done((bf16[33,64,128]{2,1,0:T(8,128)(2,1)S(1)}, bf16[33,64,128]{2,1,0:T(8,128)(2,1)S(1)}, u32[]{:S(2)}, u32[]{:S(2)}) %collective-permute-start.10) | collective-permute-done | bytes 540704 | tf_op jit(solution)/shard_map/ppermute | solution.py:357
  55.4 5.4 %collective-permute-done.12.refs_8_ = bf16[33,64,128]{2,1,0:T(8,128)(2,1)S(1)} collective-permute-done((bf16[33,64,128]{2,1,0:T(8,128)(2,1)S(1)}, bf16[33,64,128]{2,1,0:T(8,128)(2,1)S(1)}, u32[]{:S(2)}, u32[]{:S(2)}) %collective-permute-start.12) | collective-permute-done | bytes 540704 | tf_op jit(solution)/shard_map/ppermute | solution.py:357
  61.2 2.1 %pick_other.1 = (bf16[65,64,128]{2,1,0:T(8,128)(2,1)S(1)}, bf16[528,64,128]{2,1,0:T(8,128)(2,1)S(1)}, f32[32,64,128]{2,1,0:T(8,128)S(1)}) custom-call(s32[4]{0:T(128)S(1)} %pad_add_fusion.core_ref.place_ref.refs_0_, s32[4,32]{1,0:T(4,128)S(1)} %collective-permute-done.1.columns_ref, bf16[66,64,128]{2,1,0:T(8,128)(2,1)S(1)} %pad_maximum_fusion.refs_0_, ...), custom_call_target="tpu_custom_call" | custom-call | flops 4194304 | bytes 20971520 | tf_op jit(solution)/shard_map/pick_other/pallas_call | solution.py:381
  63.4 1.4 %parent_scores.1.parent_ref = f32[32,64,128]{2,1,0:T(8,128)S(1)} custom-call(s32[32,64]{1,0:T(8,128)S(1)} %bitcast.21, bf16[32,256,128]{2,1,0:T(8,128)(2,1)S(1)} %copy-done.8, f32[32,128]{1,0:T(8,128)S(1)} %copy-done.5), custom_call_target="tpu_custom_call" | custom-call | flops 268435456 | bytes 3145728 | tf_op jit(solution)/shard_map/parent_scores/pallas_call | solution.py:359
  64.9 1.7 %own_sums.1 = (bf16[64,64,128]{2,1,0:T(8,128)(2,1)S(1)}, f32[16,64,128]{2,1,0:T(8,128)S(1)}, f32[32,64,128]{2,1,0:T(8,128)S(1)}) custom-call(s32[4]{0:T(128)S(1)} %pad_add_fusion.core_ref.place_ref.refs_0_, s32[4,32]{1,0:T(4,128)S(1)} %bitcast.20, s32[32]{0:T(128)S(1)} %copy-done.6, bf16[528,64,128]{2,1,0:T(8,128)(2,1)S(1)} %get-tuple-element.50.pool, ...), custom_call_target="tpu_custom_call" | custom-call | flops 268435456 | bytes 8388608 | tf_op jit(solution)/shard_map/own_sums/pallas_call | solution.py:397
  66.6 2.1 %row_sums.1 = (f32[64,128]{1,0:T(8,128)S(1)}, f32[32,64,128]{2,1,0:T(8,128)S(1)}, f32[16,64,128]{2,1,0:T(8,128)S(1)}) custom-call(s32[4]{0:T(128)S(1)} %pad_add_fusion.core_ref.place_ref.refs_0_, s32[32]{0:T(128)S(1)} %copy-done.6, bf16[65,64,128]{2,1,0:T(8,128)(2,1)S(1)} %collective-permute-done.14.other_ref.refs_10_, ...), custom_call_target="tpu_custom_call" | custom-call | flops 268435456 | bytes 8388608 | tf_op jit(solution)/shard_map/row_sums/pallas_call | solution.py:406
  69.2 0.9 collective-permute-done.15.refs_1_
  70.6 3.0 %collective-permute-start.17 = (f32[64,128]{1,0:T(8,128)S(1)}, f32[64,128]{1,0:T(8,128)S(1)}, u32[]{:S(2)}, u32[]{:S(2)}) collective-permute-start(f32[64,128]{1,0:T(8,128)S(1)} %merge_core.1.refs_0_), channel_id=1, source_target_pairs={{0,192},{8,56},{16,208},{24,8},{32,224},{40,24},{48,240},{56,40},{... | collective-permute-start | bytes 98312 | tf_op jit(solution)/shard_map/ppermute | solution.py:421
  74.2 1.2 collective-permute-done.16.refs_1_
  75.4 3.5 %collective-permute-done.18.refs_3_ = f32[64,128]{1,0:T(8,128)S(1)} collective-permute-done((f32[64,128]{1,0:T(8,128)S(1)}, f32[64,128]{1,0:T(8,128)S(1)}, u32[]{:S(2)}, u32[]{:S(2)}) %collective-permute-start.18) | collective-permute-done | bytes 32800 | tf_op jit(solution)/shard_map/ppermute | solution.py:421
  79.1 1.7 %collective-permute-start.19 = (f32[64,128]{1,0:T(8,128)S(1)}, f32[64,128]{1,0:T(8,128)S(1)}, u32[]{:S(2)}, u32[]{:S(2)}) collective-permute-start(f32[64,128]{1,0:T(8,128)S(1)} %merge_a.1.refs_2_), channel_id=1, source_target_pairs={{0,16},{8,72},{16,32},{24,88},{32,48},{40,104},{48,0},{56,120},{64... | collective-permute-start | bytes 98312 | tf_op jit(solution)/shard_map/ppermute | solution.py:421
  80.7 1.7 %collective-permute-start.20 = (f32[64,128]{1,0:T(8,128)S(1)}, f32[64,128]{1,0:T(8,128)S(1)}, u32[]{:S(2)}, u32[]{:S(2)}) collective-permute-start(f32[64,128]{1,0:T(8,128)S(1)} %merge_a.1.refs_2_), channel_id=1, source_target_pairs={{0,48},{8,200},{16,0},{24,216},{32,16},{40,232},{48,32},{56,248},{... | collective-permute-start | bytes 98312 | tf_op jit(solution)/shard_map/ppermute | solution.py:421
  82.4 1.7 %collective-permute-start.21 = (f32[64,128]{1,0:T(8,128)S(1)}, f32[64,128]{1,0:T(8,128)S(1)}, u32[]{:S(2)}, u32[]{:S(2)}) collective-permute-start(f32[64,128]{1,0:T(8,128)S(1)} %merge_a.1.refs_2_), channel_id=1, source_target_pairs={{0,32},{8,136},{16,48},{24,152},{32,0},{40,168},{48,16},{56,184},{... | collective-permute-start | bytes 98312 | tf_op jit(solution)/shard_map/ppermute | solution.py:421
  84.6 3.2 %collective-permute-done.21.refs_5_ = f32[64,128]{1,0:T(8,128)S(1)} collective-permute-done((f32[64,128]{1,0:T(8,128)S(1)}, f32[64,128]{1,0:T(8,128)S(1)}, u32[]{:S(2)}, u32[]{:S(2)}) %collective-permute-start.21) | collective-permute-done | bytes 32800 | tf_op jit(solution)/shard_map/ppermute | solution.py:421
  87.8 2.6 %counts.1 = (bf16[32,4,16,128]{3,2,1,0:T(8,128)(2,1)S(1)}, bf16[32,4,16,128]{3,2,1,0:T(8,128)(2,1)S(1)}, bf16[32,4,16,128]{3,2,1,0:T(8,128)(2,1)S(1)}, bf16[32,4...) custom-call(s32[4]{0:T(128)S(1)} %pad_add_fusion.core_ref.place_ref., ...), custom_call_target="tpu_custom_call" | custom-call | flops 536870912 | bytes 13631488 | tf_op jit(solution)/shard_map/counts/pallas_call | solution.py:434
  90.4 2.0 %collective-permute-start.22 = (bf16[16,4,16,128]{3,2,1,0:T(8,128)(2,1)S(1)}, bf16[16,4,16,128]{3,2,1,0:T(8,128)(2,1)S(1)}, u32[]{:S(2)}, u32[]{:S(2)}) collective-permute-start(bf16[16,4,16,128]{3,2,1,0:T(8,128)(2,1)S(1)} %get-tuple-element.65), channel_id=1, source_target_pairs={{0,1},{1,2},{2,3},{3,4},{4,5},{5,6},{6,7},{7,0},{8,9},{9,10},{10,1... | collective-permute-start | bytes 786440 | tf_op jit(solution)/shard_map/ppermute | solution.py:447
  92.5 4.3 %collective-permute-done.22.up_in_ref = bf16[16,4,16,128]{3,2,1,0:T(8,128)(2,1)S(1)} collective-permute-done((bf16[16,4,16,128]{3,2,1,0:T(8,128)(2,1)S(1)}, bf16[16,4,16,128]{3,2,1,0:T(8,128)(2,1)S(1)}, u32[]{:S(2)}, u32[]{:S(2)}) %collective-permute-start.22) | collective-permute-done | bytes 262176 | tf_op jit(solution)/shard_map/ppermute | solution.py:447
  96.8 1.9 %collective-permute-done.23.down_in_ref = bf16[16,4,16,128]{3,2,1,0:T(8,128)(2,1)S(1)} collective-permute-done((bf16[16,4,16,128]{3,2,1,0:T(8,128)(2,1)S(1)}, bf16[16,4,16,128]{3,2,1,0:T(8,128)(2,1)S(1)}, u32[]{:S(2)}, u32[]{:S(2)}) %collective-permute-start.23) | collective-permute-done | bytes 262176 | tf_op jit(solution)/shard_map/ppermute | solution.py:447
  98.9 3.1 %collective-permute-start.24 = (bf16[32,4,16,128]{3,2,1,0:T(8,128)(2,1)S(1)}, bf16[32,4,16,128]{3,2,1,0:T(8,128)(2,1)S(1)}, u32[]{:S(2)}, u32[]{:S(2)}) collective-permute-start(bf16[32,4,16,128]{3,2,1,0:T(8,128)(2,1)S(1)} %get-tuple-element.67), channel_id=1, source_target_pairs={{0,1},{1,2},{2,3},{3,4},{4,5},{5,6},{6,7},{7,0},{8,9},{9,10},{10,1... | collective-permute-start | bytes 1572872 | tf_op jit(solution)/shard_map/ppermute | solution.py:447
  102.0 7.6 %collective-permute-done.24.up_in_ref = bf16[32,4,16,128]{3,2,1,0:T(8,128)(2,1)S(1)} collective-permute-done((bf16[32,4,16,128]{3,2,1,0:T(8,128)(2,1)S(1)}, bf16[32,4,16,128]{3,2,1,0:T(8,128)(2,1)S(1)}, u32[]{:S(2)}, u32[]{:S(2)}) %collective-permute-start.24) | collective-permute-done | bytes 524320 | tf_op jit(solution)/shard_map/ppermute | solution.py:447
  109.6 4.4 %collective-permute-done.25.down_in_ref = bf16[32,4,16,128]{3,2,1,0:T(8,128)(2,1)S(1)} collective-permute-done((bf16[32,4,16,128]{3,2,1,0:T(8,128)(2,1)S(1)}, bf16[32,4,16,128]{3,2,1,0:T(8,128)(2,1)S(1)}, u32[]{:S(2)}, u32[]{:S(2)}) %collective-permute-start.25) | collective-permute-done | bytes 524320 | tf_op jit(solution)/shard_map/ppermute | solution.py:447
  114.2 2.5 %collective-permute-start.26 = (bf16[32,4,16,128]{3,2,1,0:T(8,128)(2,1)S(1)}, bf16[32,4,16,128]{3,2,1,0:T(8,128)(2,1)S(1)}, u32[]{:S(2)}, u32[]{:S(2)}) collective-permute-start(bf16[32,4,16,128]{3,2,1,0:T(8,128)(2,1)S(1)} %get-tuple-element.69), channel_id=1, source_target_pairs={{0,1},{1,2},{2,3},{3,4},{4,5},{5,6},{6,7},{7,0},{8,9},{9,10},{10,1... | collective-permute-start | bytes 1572872 | tf_op jit(solution)/shard_map/ppermute | solution.py:447
  116.7 9.1 %collective-permute-done.26.up_in_ref = bf16[32,4,16,128]{3,2,1,0:T(8,128)(2,1)S(1)} collective-permute-done((bf16[32,4,16,128]{3,2,1,0:T(8,128)(2,1)S(1)}, bf16[32,4,16,128]{3,2,1,0:T(8,128)(2,1)S(1)}, u32[]{:S(2)}, u32[]{:S(2)}) %collective-permute-start.26) | collective-permute-done | bytes 524320 | tf_op jit(solution)/shard_map/ppermute | solution.py:447
  125.7 2.8 %collective-permute-done.27.down_in_ref = bf16[32,4,16,128]{3,2,1,0:T(8,128)(2,1)S(1)} collective-permute-done((bf16[32,4,16,128]{3,2,1,0:T(8,128)(2,1)S(1)}, bf16[32,4,16,128]{3,2,1,0:T(8,128)(2,1)S(1)}, u32[]{:S(2)}, u32[]{:S(2)}) %collective-permute-start.27) | collective-permute-done | bytes 524320 | tf_op jit(solution)/shard_map/ppermute | solution.py:447
  128.7 1.9 %collective-permute-start.28 = (bf16[32,4,16,128]{3,2,1,0:T(8,128)(2,1)S(1)}, bf16[32,4,16,128]{3,2,1,0:T(8,128)(2,1)S(1)}, u32[]{:S(2)}, u32[]{:S(2)}) collective-permute-start(bf16[32,4,16,128]{3,2,1,0:T(8,128)(2,1)S(1)} %get-tuple-element.71), channel_id=1, source_target_pairs={{0,1},{1,2},{2,3},{3,4},{4,5},{5,6},{6,7},{7,0},{8,9},{9,10},{10,1... | collective-permute-start | bytes 1572872 | tf_op jit(solution)/shard_map/ppermute | solution.py:447
  131.4 6.5 %collective-permute-done.28.up_in_ref = bf16[32,4,16,128]{3,2,1,0:T(8,128)(2,1)S(1)} collective-permute-done((bf16[32,4,16,128]{3,2,1,0:T(8,128)(2,1)S(1)}, bf16[32,4,16,128]{3,2,1,0:T(8,128)(2,1)S(1)}, u32[]{:S(2)}, u32[]{:S(2)}) %collective-permute-start.28) | collective-permute-done | bytes 524320 | tf_op jit(solution)/shard_map/ppermute | solution.py:447
  138.0 1.8 %collective-permute-done.29.down_in_ref = bf16[32,4,16,128]{3,2,1,0:T(8,128)(2,1)S(1)} collective-permute-done((bf16[32,4,16,128]{3,2,1,0:T(8,128)(2,1)S(1)}, bf16[32,4,16,128]{3,2,1,0:T(8,128)(2,1)S(1)}, u32[]{:S(2)}, u32[]{:S(2)}) %collective-permute-start.29) | collective-permute-done | bytes 524320 | tf_op jit(solution)/shard_map/ppermute | solution.py:447
  139.8 1.5 %ring_last.1 = bf16[32,4,16,128]{3,2,1,0:T(8,128)(2,1)} custom-call(s32[4]{0:T(128)S(1)} %pad_add_fusion.core_ref.place_ref.refs_0_, bf16[32,4,16,128]{3,2,1,0:T(8,128)(2,1)S(1)} %get-tuple-element.58.own_ref, bf16[32,4,16,128]{3,2,1,0:T(8,128)(2,1)S(1)} %collective-permute-done.28.up_in_ref, bf16[32,4,16,128]{3,2,1,0:T(8,128)(2,1)S(1)} %collective-permute-done.29.down_in_ref), custom_call_target="tpu_custom_call" | custom-call | tf_op jit(solution)/shard_map/ring_last/pallas_call | solution.py:465
  (58 shorter events, 7.5 us)
Async XLA Ops:
  0.6 1.6 %copy-start.1 = (bf16[32,256,128]{2,1,0:T(8,128)(2,1)S(1)}, bf16[32,256,128]{2,1,0:T(8,128)(2,1)}, u32[]{:S(2)}) copy-start(bf16[32,256,128]{2,1,0:T(8,128)(2,1)} %table_ref.4) | copy-start | bytes 6291460
  2.2 0.7 copy-start.3
  2.9 1.3 copy-start.7
  3.0 1.9 %copy-start.2 = (bf16[32,256,128]{2,1,0:T(8,128)(2,1)S(1)}, bf16[32,256,128]{2,1,0:T(8,128)(2,1)}, u32[]{:S(2)}) copy-start(bf16[32,256,128]{2,1,0:T(8,128)(2,1)} %table_ref.4) | copy-start | bytes 6291460
  3.0 1.9 %copy-start.4 = (s32[64,32]{0,1:T(8,128)S(1)}, s32[64,32]{0,1:T(8,128)}, u32[]{:S(2)}) copy-start(s32[64,32]{0,1:T(8,128)} %param.8) | copy-start | bytes 24580
  4.2 1.9 %collective-permute-start = (bf16[17,64,128]{2,1,0:T(8,128)(2,1)S(1)}, bf16[17,64,128]{2,1,0:T(8,128)(2,1)S(1)}, u32[]{:S(2)}, u32[]{:S(2)}) collective-permute-start(bf16[17,64,128]{2,1,0:T(8,128)(2,1)S(1)} %child_scores.2), channel_id=1, source_target_pairs={{0,8},{8,0},{16,24},{24,16},{32,40},{40,32},{48,56},{56,48},{64,72... | collective-permute-start | bytes 835592 | tf_op jit(solution)/shard_map/ppermute | solution.py:344
  4.3 1.8 %collective-permute-start.1 = (s32[4,32]{1,0:T(4,128)S(1)}, s32[4,32]{1,0:T(4,128)S(1)}, u32[]{:S(2)}, u32[]{:S(2)}) collective-permute-start(s32[4,32]{1,0:T(4,128)S(1)} %bitcast.19), channel_id=1, source_target_pairs={{0,8},{8,0},{16,24},{24,16},{32,40},{40,32},{48,56},{56,48},{64,72... | collective-permute-start | bytes 1544 | tf_op jit(solution)/shard_map/ppermute | solution.py:344
  6.7 10.6 %collective-permute-start.2 = (bf16[33,64,128]{2,1,0:T(8,128)(2,1)S(1)}, bf16[33,64,128]{2,1,0:T(8,128)(2,1)S(1)}, u32[]{:S(2)}, u32[]{:S(2)}) collective-permute-start(bf16[33,64,128]{2,1,0:T(8,128)(2,1)S(1)} %pack.1), channel_id=1, source_target_pairs={{0,64},{8,24},{16,80},{24,40},{32,96},{40,56},{48,112},{56,8},{64,... | collective-permute-start | bytes 1622024 | tf_op jit(solution)/shard_map/ppermute | solution.py:357
  8.3 9.4 %collective-permute-start.3 = (bf16[33,64,128]{2,1,0:T(8,128)(2,1)S(1)}, bf16[33,64,128]{2,1,0:T(8,128)(2,1)S(1)}, u32[]{:S(2)}, u32[]{:S(2)}) collective-permute-start(bf16[33,64,128]{2,1,0:T(8,128)(2,1)S(1)} %pack.1), channel_id=1, source_target_pairs={{0,192},{8,56},{16,208},{24,8},{32,224},{40,24},{48,240},{56,40},{... | collective-permute-start | bytes 1622024 | tf_op jit(solution)/shard_map/ppermute | solution.py:357
  17.7 10.2 %collective-permute-start.4 = (bf16[17,64,128]{2,1,0:T(8,128)(2,1)S(1)}, bf16[17,64,128]{2,1,0:T(8,128)(2,1)S(1)}, u32[]{:S(2)}, u32[]{:S(2)}) collective-permute-start(bf16[17,64,128]{2,1,0:T(8,128)(2,1)S(1)} %slice.21), channel_id=1, source_target_pairs={{0,64},{8,24},{16,80},{24,40},{32,96},{40,56},{48,112},{56,8},{64,... | collective-permute-start | bytes 835592 | tf_op jit(solution)/shard_map/ppermute | solution.py:357
  19.2 8.6 %collective-permute-start.5 = (bf16[16,64,128]{2,1,0:T(8,128)(2,1)S(1)}, bf16[16,64,128]{2,1,0:T(8,128)(2,1)S(1)}, u32[]{:S(2)}, u32[]{:S(2)}) collective-permute-start(bf16[16,64,128]{2,1,0:T(8,128)(2,1)S(1)} %slice.22), channel_id=1, source_target_pairs={{0,192},{8,56},{16,208},{24,8},{32,224},{40,24},{48,240},{56,40},{... | collective-permute-start | bytes 786440 | tf_op jit(solution)/shard_map/ppermute | solution.py:357
  21.2 16.4 %collective-permute-start.6 = (bf16[66,64,128]{2,1,0:T(8,128)(2,1)S(1)}, bf16[66,64,128]{2,1,0:T(8,128)(2,1)S(1)}, u32[]{:S(2)}, u32[]{:S(2)}) collective-permute-start(bf16[66,64,128]{2,1,0:T(8,128)(2,1)S(1)} %pad_maximum_fusion.refs_0_), channel_id=1, source_target_pairs={{0,16},{8,72},{16,32},{24,88},{32,48},{40,104},{48,0},{56,120},{64... | collective-permute-start | bytes 3244040 | tf_op jit(solution)/shard_map/ppermute | solution.py:357
  22.8 15.2 %collective-permute-start.7 = (bf16[66,64,128]{2,1,0:T(8,128)(2,1)S(1)}, bf16[66,64,128]{2,1,0:T(8,128)(2,1)S(1)}, u32[]{:S(2)}, u32[]{:S(2)}) collective-permute-start(bf16[66,64,128]{2,1,0:T(8,128)(2,1)S(1)} %pad_maximum_fusion.refs_0_), channel_id=1, source_target_pairs={{0,48},{8,200},{16,0},{24,216},{32,16},{40,232},{48,32},{56,248},{... | collective-permute-start | bytes 3244040 | tf_op jit(solution)/shard_map/ppermute | solution.py:357
  28.0 21.2 %collective-permute-start.8 = (bf16[66,64,128]{2,1,0:T(8,128)(2,1)S(1)}, bf16[66,64,128]{2,1,0:T(8,128)(2,1)S(1)}, u32[]{:S(2)}, u32[]{:S(2)}) collective-permute-start(bf16[66,64,128]{2,1,0:T(8,128)(2,1)S(1)} %constant_dynamic-update-slice_fusion.refs_1_), channel_id=1, source_target_pairs={{0,16},{8,72},{16,32},{24,88},{32,48},{40,104},{48,0},{56,120},{64... | collective-permute-start | bytes 3244040 | tf_op jit(solution)/shard_map/ppermute | solution.py:357
  30.2 19.3 %collective-permute-start.9 = (bf16[66,64,128]{2,1,0:T(8,128)(2,1)S(1)}, bf16[66,64,128]{2,1,0:T(8,128)(2,1)S(1)}, u32[]{:S(2)}, u32[]{:S(2)}) collective-permute-start(bf16[66,64,128]{2,1,0:T(8,128)(2,1)S(1)} %constant_dynamic-update-slice_fusion.refs_1_), channel_id=1, source_target_pairs={{0,48},{8,200},{16,0},{24,216},{32,16},{40,232},{48,32},{56,248},{... | collective-permute-start | bytes 3244040 | tf_op jit(solution)/shard_map/ppermute | solution.py:357
  38.0 17.0 %collective-permute-start.10 = (bf16[33,64,128]{2,1,0:T(8,128)(2,1)S(1)}, bf16[33,64,128]{2,1,0:T(8,128)(2,1)S(1)}, u32[]{:S(2)}, u32[]{:S(2)}) collective-permute-start(bf16[33,64,128]{2,1,0:T(8,128)(2,1)S(1)} %slice.23), channel_id=1, source_target_pairs={{0,16},{8,72},{16,32},{24,88},{32,48},{40,104},{48,0},{56,120},{64... | collective-permute-start | bytes 1622024 | tf_op jit(solution)/shard_map/ppermute | solution.py:357
  39.7 15.6 %collective-permute-start.11 = (bf16[33,64,128]{2,1,0:T(8,128)(2,1)S(1)}, bf16[33,64,128]{2,1,0:T(8,128)(2,1)S(1)}, u32[]{:S(2)}, u32[]{:S(2)}) collective-permute-start(bf16[33,64,128]{2,1,0:T(8,128)(2,1)S(1)} %slice.24), channel_id=1, source_target_pairs={{0,48},{8,200},{16,0},{24,216},{32,16},{40,232},{48,32},{56,248},{... | collective-permute-start | bytes 1622024 | tf_op jit(solution)/shard_map/ppermute | solution.py:357
  49.6 11.2 %collective-permute-start.12 = (bf16[33,64,128]{2,1,0:T(8,128)(2,1)S(1)}, bf16[33,64,128]{2,1,0:T(8,128)(2,1)S(1)}, u32[]{:S(2)}, u32[]{:S(2)}) collective-permute-start(bf16[33,64,128]{2,1,0:T(8,128)(2,1)S(1)} %slice.25), channel_id=1, source_target_pairs={{0,16},{8,72},{16,32},{24,88},{32,48},{40,104},{48,0},{56,120},{64... | collective-permute-start | bytes 1622024 | tf_op jit(solution)/shard_map/ppermute | solution.py:357
  51.5 11.9 %copy-start.5 = (f32[32,128]{1,0:T(8,128)S(1)}, f32[32,128]{1,0:T(8,128)}, u32[]{:S(2)}) copy-start(f32[32,128]{1,0:T(8,128)} %prior_ref.3) | copy-start | bytes 49156
  51.5 11.9 %copy-start.8 = (bf16[32,256,128]{2,1,0:T(8,128)(2,1)S(1)}, bf16[32,256,128]{2,1,0:T(8,128)(2,1)}, u32[]{:S(2)}) copy-start(bf16[32,256,128]{2,1,0:T(8,128)(2,1)} %table_ref.5) | copy-start | bytes 6291460
  51.5 11.9 %copy-start.9 = (s32[64,32]{0,1:T(8,128)S(1)}, s32[64,32]{0,1:T(8,128)}, u32[]{:S(2)}) copy-start(s32[64,32]{0,1:T(8,128)} %param.9) | copy-start | bytes 24580
  51.5 9.6 %collective-permute-start.13 = (bf16[33,64,128]{2,1,0:T(8,128)(2,1)S(1)}, bf16[33,64,128]{2,1,0:T(8,128)(2,1)S(1)}, u32[]{:S(2)}, u32[]{:S(2)}) collective-permute-start(bf16[33,64,128]{2,1,0:T(8,128)(2,1)S(1)} %slice.26), channel_id=1, source_target_pairs={{0,48},{8,200},{16,0},{24,216},{32,16},{40,232},{48,32},{56,248},{... | collective-permute-start | bytes 1622024 | tf_op jit(solution)/shard_map/ppermute | solution.py:357
  61.1 3.7 %copy-start = (bf16[32,1,4,128,128]{4,3,2,1,0:T(8,128)(2,1)S(1)}, bf16[32,1,4,128,128]{4,3,2,1,0:T(8,128)(2,1)}, u32[]{:S(2)}) copy-start(bf16[32,1,4,128,128]{4,3,2,1,0:T(8,128)(2,1)} %param.13) | copy-start | bytes 12582916
  63.2 3.3 %collective-permute-start.14 = (bf16[65,64,128]{2,1,0:T(8,128)(2,1)S(1)}, bf16[65,64,128]{2,1,0:T(8,128)(2,1)S(1)}, u32[]{:S(2)}, u32[]{:S(2)}) collective-permute-start(bf16[65,64,128]{2,1,0:T(8,128)(2,1)S(1)} %get-tuple-element.49), channel_id=1, source_target_pairs={{0,8},{8,0},{16,24},{24,16},{32,40},{40,32},{48,56},{56,48},{64,72... | collective-permute-start | bytes 3194888 | tf_op jit(solution)/shard_map/ppermute | solution.py:394
  63.4 1.5 %copy-start.6 = (s32[32]{0:T(128)S(1)}, s32[32]{0:T(128)}, u32[]{:S(2)}) copy-start(s32[32]{0:T(128)} %refs_1_.1) | copy-start | bytes 388
  68.7 1.4 %collective-permute-start.15 = (f32[64,128]{1,0:T(8,128)S(1)}, f32[64,128]{1,0:T(8,128)S(1)}, u32[]{:S(2)}, u32[]{:S(2)}) collective-permute-start(f32[64,128]{1,0:T(8,128)S(1)} %get-tuple-element.53.refs_0_), channel_id=1, source_target_pairs={{0,8},{8,0},{16,24},{24,16},{32,40},{40,32},{48,56},{56,48},{64,72... | collective-permute-start | bytes 98312 | tf_op jit(solution)/shard_map/ppermute | solution.py:421
  70.2 5.2 %collective-permute-start.16 = (f32[64,128]{1,0:T(8,128)S(1)}, f32[64,128]{1,0:T(8,128)S(1)}, u32[]{:S(2)}, u32[]{:S(2)}) collective-permute-start(f32[64,128]{1,0:T(8,128)S(1)} %merge_core.1.refs_0_), channel_id=1, source_target_pairs={{0,64},{8,24},{16,80},{24,40},{32,96},{40,56},{48,112},{56,8},{64,... | collective-permute-start | bytes 98312 | tf_op jit(solution)/shard_map/ppermute | solution.py:421
  70.6 4.8 %collective-permute-start.17 = (f32[64,128]{1,0:T(8,128)S(1)}, f32[64,128]{1,0:T(8,128)S(1)}, u32[]{:S(2)}, u32[]{:S(2)}) collective-permute-start(f32[64,128]{1,0:T(8,128)S(1)} %merge_core.1.refs_0_), channel_id=1, source_target_pairs={{0,192},{8,56},{16,208},{24,8},{32,224},{40,24},{48,240},{56,40},{... | collective-permute-start | bytes 98312 | tf_op jit(solution)/shard_map/ppermute | solution.py:421
  73.5 5.4 %collective-permute-start.18 = (f32[64,128]{1,0:T(8,128)S(1)}, f32[64,128]{1,0:T(8,128)S(1)}, u32[]{:S(2)}, u32[]{:S(2)}) collective-permute-start(f32[64,128]{1,0:T(8,128)S(1)} %merge_core.1.refs_0_), channel_id=1, source_target_pairs={{0,128},{8,40},{16,144},{24,56},{32,160},{40,8},{48,176},{56,24},{... | collective-permute-start | bytes 98312 | tf_op jit(solution)/shard_map/ppermute | solution.py:421
  79.1 5.2 %collective-permute-start.19 = (f32[64,128]{1,0:T(8,128)S(1)}, f32[64,128]{1,0:T(8,128)S(1)}, u32[]{:S(2)}, u32[]{:S(2)}) collective-permute-start(f32[64,128]{1,0:T(8,128)S(1)} %merge_a.1.refs_2_), channel_id=1, source_target_pairs={{0,16},{8,72},{16,32},{24,88},{32,48},{40,104},{48,0},{56,120},{64... | collective-permute-start | bytes 98312 | tf_op jit(solution)/shard_map/ppermute | solution.py:421
  80.7 3.9 %collective-permute-start.20 = (f32[64,128]{1,0:T(8,128)S(1)}, f32[64,128]{1,0:T(8,128)S(1)}, u32[]{:S(2)}, u32[]{:S(2)}) collective-permute-start(f32[64,128]{1,0:T(8,128)S(1)} %merge_a.1.refs_2_), channel_id=1, source_target_pairs={{0,48},{8,200},{16,0},{24,216},{32,16},{40,232},{48,32},{56,248},{... | collective-permute-start | bytes 98312 | tf_op jit(solution)/shard_map/ppermute | solution.py:421
  82.4 5.4 %collective-permute-start.21 = (f32[64,128]{1,0:T(8,128)S(1)}, f32[64,128]{1,0:T(8,128)S(1)}, u32[]{:S(2)}, u32[]{:S(2)}) collective-permute-start(f32[64,128]{1,0:T(8,128)S(1)} %merge_a.1.refs_2_), channel_id=1, source_target_pairs={{0,32},{8,136},{16,48},{24,152},{32,0},{40,168},{48,16},{56,184},{... | collective-permute-start | bytes 98312 | tf_op jit(solution)/shard_map/ppermute | solution.py:421
  90.4 6.4 %collective-permute-start.22 = (bf16[16,4,16,128]{3,2,1,0:T(8,128)(2,1)S(1)}, bf16[16,4,16,128]{3,2,1,0:T(8,128)(2,1)S(1)}, u32[]{:S(2)}, u32[]{:S(2)}) collective-permute-start(bf16[16,4,16,128]{3,2,1,0:T(8,128)(2,1)S(1)} %get-tuple-element.65), channel_id=1, source_target_pairs={{0,1},{1,2},{2,3},{3,4},{4,5},{5,6},{6,7},{7,0},{8,9},{9,10},{10,1... | collective-permute-start | bytes 786440 | tf_op jit(solution)/shard_map/ppermute | solution.py:447
  92.4 6.4 %collective-permute-start.23 = (bf16[16,4,16,128]{3,2,1,0:T(8,128)(2,1)S(1)}, bf16[16,4,16,128]{3,2,1,0:T(8,128)(2,1)S(1)}, u32[]{:S(2)}, u32[]{:S(2)}) collective-permute-start(bf16[16,4,16,128]{3,2,1,0:T(8,128)(2,1)S(1)} %get-tuple-element.66), channel_id=1, source_target_pairs={{0,7},{1,0},{2,1},{3,2},{4,3},{5,4},{6,5},{7,6},{8,15},{9,8},{10,9... | collective-permute-start | bytes 786440 | tf_op jit(solution)/shard_map/ppermute | solution.py:447
  98.9 10.7 %collective-permute-start.24 = (bf16[32,4,16,128]{3,2,1,0:T(8,128)(2,1)S(1)}, bf16[32,4,16,128]{3,2,1,0:T(8,128)(2,1)S(1)}, u32[]{:S(2)}, u32[]{:S(2)}) collective-permute-start(bf16[32,4,16,128]{3,2,1,0:T(8,128)(2,1)S(1)} %get-tuple-element.67), channel_id=1, source_target_pairs={{0,1},{1,2},{2,3},{3,4},{4,5},{5,6},{6,7},{7,0},{8,9},{9,10},{10,1... | collective-permute-start | bytes 1572872 | tf_op jit(solution)/shard_map/ppermute | solution.py:447
  102.0 11.9 %collective-permute-start.25 = (bf16[32,4,16,128]{3,2,1,0:T(8,128)(2,1)S(1)}, bf16[32,4,16,128]{3,2,1,0:T(8,128)(2,1)S(1)}, u32[]{:S(2)}, u32[]{:S(2)}) collective-permute-start(bf16[32,4,16,128]{3,2,1,0:T(8,128)(2,1)S(1)} %get-tuple-element.68), channel_id=1, source_target_pairs={{0,7},{1,0},{2,1},{3,2},{4,3},{5,4},{6,5},{7,6},{8,15},{9,8},{10,9... | collective-permute-start | bytes 1572872 | tf_op jit(solution)/shard_map/ppermute | solution.py:447
  114.2 11.5 %collective-permute-start.26 = (bf16[32,4,16,128]{3,2,1,0:T(8,128)(2,1)S(1)}, bf16[32,4,16,128]{3,2,1,0:T(8,128)(2,1)S(1)}, u32[]{:S(2)}, u32[]{:S(2)}) collective-permute-start(bf16[32,4,16,128]{3,2,1,0:T(8,128)(2,1)S(1)} %get-tuple-element.69), channel_id=1, source_target_pairs={{0,1},{1,2},{2,3},{3,4},{4,5},{5,6},{6,7},{7,0},{8,9},{9,10},{10,1... | collective-permute-start | bytes 1572872 | tf_op jit(solution)/shard_map/ppermute | solution.py:447
  116.6 11.8 %collective-permute-start.27 = (bf16[32,4,16,128]{3,2,1,0:T(8,128)(2,1)S(1)}, bf16[32,4,16,128]{3,2,1,0:T(8,128)(2,1)S(1)}, u32[]{:S(2)}, u32[]{:S(2)}) collective-permute-start(bf16[32,4,16,128]{3,2,1,0:T(8,128)(2,1)S(1)} %get-tuple-element.70), channel_id=1, source_target_pairs={{0,7},{1,0},{2,1},{3,2},{4,3},{5,4},{6,5},{7,6},{8,15},{9,8},{10,9... | collective-permute-start | bytes 1572872 | tf_op jit(solution)/shard_map/ppermute | solution.py:447
  128.7 9.3 %collective-permute-start.28 = (bf16[32,4,16,128]{3,2,1,0:T(8,128)(2,1)S(1)}, bf16[32,4,16,128]{3,2,1,0:T(8,128)(2,1)S(1)}, u32[]{:S(2)}, u32[]{:S(2)}) collective-permute-start(bf16[32,4,16,128]{3,2,1,0:T(8,128)(2,1)S(1)} %get-tuple-element.71), channel_id=1, source_target_pairs={{0,1},{1,2},{2,3},{3,4},{4,5},{5,6},{6,7},{7,0},{8,9},{9,10},{10,1... | collective-permute-start | bytes 1572872 | tf_op jit(solution)/shard_map/ppermute | solution.py:447
  130.6 9.2 %collective-permute-start.29 = (bf16[32,4,16,128]{3,2,1,0:T(8,128)(2,1)S(1)}, bf16[32,4,16,128]{3,2,1,0:T(8,128)(2,1)S(1)}, u32[]{:S(2)}, u32[]{:S(2)}) collective-permute-start(bf16[32,4,16,128]{3,2,1,0:T(8,128)(2,1)S(1)} %get-tuple-element.72), channel_id=1, source_target_pairs={{0,7},{1,0},{2,1},{3,2},{4,3},{5,4},{6,5},{7,6},{8,15},{9,8},{10,9... | collective-permute-start | bytes 1572872 | tf_op jit(solution)/shard_map/ppermute | solution.py:447

commit v7 on v6

--- a/solution.py
+++ b/solution.py
@@ -210,12 +210,11 @@
     refs[-1][...] = merge([r[...] for r in refs[:-1]])
 
 
-def counts_kernel(scale, n_stats, place_ref, map_ref, *refs):
-    stats_refs, refs = refs[:n_stats], refs[n_stats:]
+def counts_kernel(scale, place_ref, map_ref, stats_ref, *refs):
     root_ref, own_sums_ref, other_sums_ref, own_ref, other_ref, weights_ref = refs[:6]
     near, far, loglik_ref, posterior = refs[6:13], refs[13:15], refs[15], refs[16]
     core, place = place_ref[0], place_ref[1]
-    stats = merge([r[...] for r in stats_refs])
+    stats = merge([stats_ref[i] for i in range(stats_ref.shape[0])])
     lanes = lane_of((S_LOC, BLK))
     norm = stats + pltpu.roll(jnp.log(stats), BLK - P_SIZE, 1)
     signed = jnp.where(lanes < P_SIZE, norm, 0.0) - jnp.where(
@@ -413,34 +412,35 @@
         name="row_sums",
     )(place, parent_map, other, weights, own_root, prior_logits)
 
-    for axis, pairs in (
-        ("core", (SWAP,)),
-        ("a", tuple(along(step, 0) for step in (1, 3, 2))),
-        ("b", tuple(along(0, step) for step in (1, 3, 2))),
-    ):
-        others = [lax.ppermute(stats, "region", p) for p in pairs]
-        if axis == "b":
-            break
-        stats = pl.pallas_call(
+    def merged(name, *parts_of):
+        return pl.pallas_call(
             merge_kernel,
             out_shape=shape((S_LOC, BLK), f32),
-            in_specs=[VMEM] * (1 + len(others)),
+            in_specs=[VMEM] * len(parts_of),
             out_specs=VMEM,
             compiler_params=params(4),
-            name="merge_" + axis,
-        )(stats, *others)
+            name=name,
+        )(*parts_of)
+
+    stats = merged("merge_core", stats, lax.ppermute(stats, "region", SWAP))
+    same_core = [[2 * i + c for i in range(16)] for c in range(2)]
+    others = [
+        lax.all_to_all(
+            jnp.broadcast_to(stats[None], (16, S_LOC, BLK)), "region", 0, 0, axis_index_groups=same_core
+        )
+    ]
     scale = K * NZ * BLK / (S_LOC * parts)
     whole, half_set = shape((C, NZ, rows, BLK), bf16), shape((HALF, NZ, rows, BLK), bf16)
     n0, n1, n2, n3, n5, n6, n7, far_up, far_down, loglik = pl.pallas_call(
-        lambda *refs: counts_kernel(scale, 1 + len(others), *refs),
+        lambda *refs: counts_kernel(scale, *refs),
         out_shape=(whole,) * 7 + (half_set,) * 2 + (shape((S_LOC, BLK), f32),),
-        in_specs=[SMEM, SMEM] + [VMEM] * (7 + len(others)),
+        in_specs=[SMEM, SMEM] + [VMEM] * 7,
         out_specs=(VMEM,) * 10,
         scratch_shapes=[pltpu.VMEM((P_SIZE, S_LOC, BLK), bf16)],
         compiler_params=params(24),
         cost_estimate=cost(1 << 29, 13 << 20, 1 << 19),
         name="counts",
-    )(place, parent_map, stats, *others, root, own_sums, other_sums, picked, other, weights)
+    )(place, parent_map, *others, root, own_sums, other_sums, picked, other, weights)
 
     def ring(up, down):
         shift = lambda step: [(i, (i + step) % parts) for i in range(parts)]

time: 141 us -> 141 us (level); the launches traced: 141 us -> 139 us
  blocking collectives: 0 us -> 17.3 us
  waiting for transfers between devices: 80.9 us -> 70.2 us
  starting transfers between devices: 40.8 us -> 31.7 us
    all_to_all x0 -> x1, blocking collectives: none -> 17.3 us  [body(): lax.all_to_all(jnp.broadcast_to(stats[None], (16, S_LOC, BLK)), 'region',...]
    ppermute x7 -> x1, starting transfers between devices: 9.56 us -> 0.55 us  [body(): stats = merged('merge_core', stats, lax.ppermute(stats, 'region', SWAP))]
    ppermute x7 -> x1, waiting for transfers between devices: 9.32 us -> 0.86 us  [body(): stats = merged('merge_core', stats, lax.ppermute(stats, 'region', SWAP))]
    ppermute x4, waiting for transfers between devices: 10.8 us -> 8.11 us  [ring(): lax.ppermute(down, 'batch', shift(-1))]
    pallas_call x3 -> x2, Pallas kernels: 2.81 us -> 2.88 us  [the longest x1 2.79 us: body(): pl.pallas_call(lambda *refs: counts_kernel(scale, *refs), out_shape=(whol...]
  transfers between devices with their start and end apart: 30 -> 24, of which waited for: 25 -> 20; matrix products, arithmetic and copies ran while one was open for 1% -> 1% of each run, Pallas kernels for 3% -> 3%
where the time goes in v7:
time: 141 us; the launch traced here: 139 us
  waiting for transfers between devices  70.2 us (50%)
  starting transfers between devices  31.7 us (22%)
  blocking collectives  17.3 us (12%)
  Pallas kernels  15.4 us (11%)
  local copies, waits for them, and re-layouts  3.3 us (2%)
    ppermute x12, waiting for transfers between devices, send(): return lax.ppermute(value, 'region', along(a, b))  33.2 us
    ppermute x4, waiting for transfers between devices, ring(): lax.ppermute(up, 'batch', shift(1))  28 us
    ppermute x12, starting transfers between devices, send(): return lax.ppermute(value, 'region', along(a, b))  20.7 us
    all_to_all x1, blocking collectives, body(): lax.all_to_all(jnp.broadcast_to(stats[None], (16, S_LOC, BLK)), 'region',...  17.3 us
    ppermute x4, starting transfers between devices, ring(): lax.ppermute(up, 'batch', shift(1))  9.09 us
    ppermute x4, waiting for transfers between devices, ring(): lax.ppermute(down, 'batch', shift(-1))  8.11 us
  transfers between devices with their start and end apart: 24, of which 20 were waited for; matrix products, arithmetic and copies ran while one was open for 1% of the time, Pallas kernels for 3%

profile of v7, /device:TPU:32, one launch (start us, length us, event | category | flops | bytes accessed | tf_op | source)
XLA Modules:
  0.0 138.9 jit_solution(16536586856730601620)
XLA Ops:
  0.6 1.6 %copy-done.1 = bf16[32,256,128]{2,1,0:T(8,128)(2,1)S(1)} copy-done((bf16[32,256,128]{2,1,0:T(8,128)(2,1)S(1)}, bf16[32,256,128]{2,1,0:T(8,128)(2,1)}, u32[]{:S(2)}) %copy-start.1) | copy-done | bytes 2097176
  2.2 0.7 copy-done.3
  3.0 1.2 child_scores.2
  4.3 0.5 collective-permute-start.1
  4.9 1.2 child_scores.3.own_ref
  6.1 0.6 pack.1
  6.7 1.5 %collective-permute-start.2 = (bf16[33,64,128]{2,1,0:T(8,128)(2,1)S(1)}, bf16[33,64,128]{2,1,0:T(8,128)(2,1)S(1)}, u32[]{:S(2)}, u32[]{:S(2)}) collective-permute-start(bf16[33,64,128]{2,1,0:T(8,128)(2,1)S(1)} %pack.1), channel_id=1, source_target_pairs={{0,64},{8,24},{16,80},{24,40},{32,96},{40,56},{48,112},{56,8},{64,... | collective-permute-start | bytes 1622024 | tf_op jit(solution)/shard_map/ppermute | solution.py:356
  8.3 1.7 %collective-permute-start.3 = (bf16[33,64,128]{2,1,0:T(8,128)(2,1)S(1)}, bf16[33,64,128]{2,1,0:T(8,128)(2,1)S(1)}, u32[]{:S(2)}, u32[]{:S(2)}) collective-permute-start(bf16[33,64,128]{2,1,0:T(8,128)(2,1)S(1)} %pack.1), channel_id=1, source_target_pairs={{0,192},{8,56},{16,208},{24,8},{32,224},{40,24},{48,240},{56,40},{... | collective-permute-start | bytes 1622024 | tf_op jit(solution)/shard_map/ppermute | solution.py:356
  10.0 7.3 %collective-permute-done.2 = bf16[33,64,128]{2,1,0:T(8,128)(2,1)S(1)} collective-permute-done((bf16[33,64,128]{2,1,0:T(8,128)(2,1)S(1)}, bf16[33,64,128]{2,1,0:T(8,128)(2,1)S(1)}, u32[]{:S(2)}, u32[]{:S(2)}) %collective-permute-start.2) | collective-permute-done | bytes 540704 | tf_op jit(solution)/shard_map/ppermute | solution.py:356
  17.7 1.6 %collective-permute-start.4 = (bf16[17,64,128]{2,1,0:T(8,128)(2,1)S(1)}, bf16[17,64,128]{2,1,0:T(8,128)(2,1)S(1)}, u32[]{:S(2)}, u32[]{:S(2)}) collective-permute-start(bf16[17,64,128]{2,1,0:T(8,128)(2,1)S(1)} %slice.21), channel_id=1, source_target_pairs={{0,64},{8,24},{16,80},{24,40},{32,96},{40,56},{48,112},{56,8},{64,... | collective-permute-start | bytes 835592 | tf_op jit(solution)/shard_map/ppermute | solution.py:356
  19.2 1.8 %collective-permute-start.5 = (bf16[16,64,128]{2,1,0:T(8,128)(2,1)S(1)}, bf16[16,64,128]{2,1,0:T(8,128)(2,1)S(1)}, u32[]{:S(2)}, u32[]{:S(2)}) collective-permute-start(bf16[16,64,128]{2,1,0:T(8,128)(2,1)S(1)} %slice.22), channel_id=1, source_target_pairs={{0,192},{8,56},{16,208},{24,8},{32,224},{40,24},{48,240},{56,40},{... | collective-permute-start | bytes 786440 | tf_op jit(solution)/shard_map/ppermute | solution.py:356
  21.2 1.7 %collective-permute-start.6 = (bf16[66,64,128]{2,1,0:T(8,128)(2,1)S(1)}, bf16[66,64,128]{2,1,0:T(8,128)(2,1)S(1)}, u32[]{:S(2)}, u32[]{:S(2)}) collective-permute-start(bf16[66,64,128]{2,1,0:T(8,128)(2,1)S(1)} %pad_maximum_fusion.refs_0_), channel_id=1, source_target_pairs={{0,16},{8,72},{16,32},{24,88},{32,48},{40,104},{48,0},{56,120},{64... | collective-permute-start | bytes 3244040 | tf_op jit(solution)/shard_map/ppermute | solution.py:356
  22.8 1.7 %collective-permute-start.7 = (bf16[66,64,128]{2,1,0:T(8,128)(2,1)S(1)}, bf16[66,64,128]{2,1,0:T(8,128)(2,1)S(1)}, u32[]{:S(2)}, u32[]{:S(2)}) collective-permute-start(bf16[66,64,128]{2,1,0:T(8,128)(2,1)S(1)} %pad_maximum_fusion.refs_0_), channel_id=1, source_target_pairs={{0,48},{8,200},{16,0},{24,216},{32,16},{40,232},{48,32},{56,248},{... | collective-permute-start | bytes 3244040 | tf_op jit(solution)/shard_map/ppermute | solution.py:356
  24.5 3.4 %collective-permute-done.5 = bf16[16,64,128]{2,1,0:T(8,128)(2,1)S(1)} collective-permute-done((bf16[16,64,128]{2,1,0:T(8,128)(2,1)S(1)}, bf16[16,64,128]{2,1,0:T(8,128)(2,1)S(1)}, u32[]{:S(2)}, u32[]{:S(2)}) %collective-permute-start.5) | collective-permute-done | bytes 262176 | tf_op jit(solution)/shard_map/ppermute | solution.py:356
  28.0 2.2 %collective-permute-start.8 = (bf16[66,64,128]{2,1,0:T(8,128)(2,1)S(1)}, bf16[66,64,128]{2,1,0:T(8,128)(2,1)S(1)}, u32[]{:S(2)}, u32[]{:S(2)}) collective-permute-start(bf16[66,64,128]{2,1,0:T(8,128)(2,1)S(1)} %constant_dynamic-update-slice_fusion.refs_1_), channel_id=1, source_target_pairs={{0,16},{8,72},{16,32},{24,88},{32,48},{40,104},{48,0},{56,120},{64... | collective-permute-start | bytes 3244040 | tf_op jit(solution)/shard_map/ppermute | solution.py:356
  30.2 1.5 %collective-permute-start.9 = (bf16[66,64,128]{2,1,0:T(8,128)(2,1)S(1)}, bf16[66,64,128]{2,1,0:T(8,128)(2,1)S(1)}, u32[]{:S(2)}, u32[]{:S(2)}) collective-permute-start(bf16[66,64,128]{2,1,0:T(8,128)(2,1)S(1)} %constant_dynamic-update-slice_fusion.refs_1_), channel_id=1, source_target_pairs={{0,48},{8,200},{16,0},{24,216},{32,16},{40,232},{48,32},{56,248},{... | collective-permute-start | bytes 3244040 | tf_op jit(solution)/shard_map/ppermute | solution.py:356
  31.8 5.9 %collective-permute-done.6.refs_2_ = bf16[66,64,128]{2,1,0:T(8,128)(2,1)S(1)} collective-permute-done((bf16[66,64,128]{2,1,0:T(8,128)(2,1)S(1)}, bf16[66,64,128]{2,1,0:T(8,128)(2,1)S(1)}, u32[]{:S(2)}, u32[]{:S(2)}) %collective-permute-start.6) | collective-permute-done | bytes 1081376 | tf_op jit(solution)/shard_map/ppermute | solution.py:356
  37.6 0.4 collective-permute-done.7.refs_4_
  38.0 1.7 %collective-permute-start.10 = (bf16[33,64,128]{2,1,0:T(8,128)(2,1)S(1)}, bf16[33,64,128]{2,1,0:T(8,128)(2,1)S(1)}, u32[]{:S(2)}, u32[]{:S(2)}) collective-permute-start(bf16[33,64,128]{2,1,0:T(8,128)(2,1)S(1)} %slice.23), channel_id=1, source_target_pairs={{0,16},{8,72},{16,32},{24,88},{32,48},{40,104},{48,0},{56,120},{64... | collective-permute-start | bytes 1622024 | tf_op jit(solution)/shard_map/ppermute | solution.py:356
  39.7 1.7 %collective-permute-start.11 = (bf16[33,64,128]{2,1,0:T(8,128)(2,1)S(1)}, bf16[33,64,128]{2,1,0:T(8,128)(2,1)S(1)}, u32[]{:S(2)}, u32[]{:S(2)}) collective-permute-start(bf16[33,64,128]{2,1,0:T(8,128)(2,1)S(1)} %slice.24), channel_id=1, source_target_pairs={{0,48},{8,200},{16,0},{24,216},{32,16},{40,232},{48,32},{56,248},{... | collective-permute-start | bytes 1622024 | tf_op jit(solution)/shard_map/ppermute | solution.py:356
  41.4 7.7 %collective-permute-done.8.refs_3_ = bf16[66,64,128]{2,1,0:T(8,128)(2,1)S(1)} collective-permute-done((bf16[66,64,128]{2,1,0:T(8,128)(2,1)S(1)}, bf16[66,64,128]{2,1,0:T(8,128)(2,1)S(1)}, u32[]{:S(2)}, u32[]{:S(2)}) %collective-permute-start.8) | collective-permute-done | bytes 1081376 | tf_op jit(solution)/shard_map/ppermute | solution.py:356
  49.2 0.4 collective-permute-done.9.refs_5_
  49.6 1.8 %collective-permute-start.12 = (bf16[33,64,128]{2,1,0:T(8,128)(2,1)S(1)}, bf16[33,64,128]{2,1,0:T(8,128)(2,1)S(1)}, u32[]{:S(2)}, u32[]{:S(2)}) collective-permute-start(bf16[33,64,128]{2,1,0:T(8,128)(2,1)S(1)} %slice.25), channel_id=1, source_target_pairs={{0,16},{8,72},{16,32},{24,88},{32,48},{40,104},{48,0},{56,120},{64... | collective-permute-start | bytes 1622024 | tf_op jit(solution)/shard_map/ppermute | solution.py:356
  51.5 1.7 %collective-permute-start.13 = (bf16[33,64,128]{2,1,0:T(8,128)(2,1)S(1)}, bf16[33,64,128]{2,1,0:T(8,128)(2,1)S(1)}, u32[]{:S(2)}, u32[]{:S(2)}) collective-permute-start(bf16[33,64,128]{2,1,0:T(8,128)(2,1)S(1)} %slice.26), channel_id=1, source_target_pairs={{0,48},{8,200},{16,0},{24,216},{32,16},{40,232},{48,32},{56,248},{... | collective-permute-start | bytes 1622024 | tf_op jit(solution)/shard_map/ppermute | solution.py:356
  53.2 1.7 %collective-permute-done.10.refs_6_ = bf16[33,64,128]{2,1,0:T(8,128)(2,1)S(1)} collective-permute-done((bf16[33,64,128]{2,1,0:T(8,128)(2,1)S(1)}, bf16[33,64,128]{2,1,0:T(8,128)(2,1)S(1)}, u32[]{:S(2)}, u32[]{:S(2)}) %collective-permute-start.10) | collective-permute-done | bytes 540704 | tf_op jit(solution)/shard_map/ppermute | solution.py:356
  55.4 5.4 %collective-permute-done.12.refs_8_ = bf16[33,64,128]{2,1,0:T(8,128)(2,1)S(1)} collective-permute-done((bf16[33,64,128]{2,1,0:T(8,128)(2,1)S(1)}, bf16[33,64,128]{2,1,0:T(8,128)(2,1)S(1)}, u32[]{:S(2)}, u32[]{:S(2)}) %collective-permute-start.12) | collective-permute-done | bytes 540704 | tf_op jit(solution)/shard_map/ppermute | solution.py:356
  61.2 2.1 %pick_other.1 = (bf16[65,64,128]{2,1,0:T(8,128)(2,1)S(1)}, bf16[528,64,128]{2,1,0:T(8,128)(2,1)S(1)}, f32[32,64,128]{2,1,0:T(8,128)S(1)}) custom-call(s32[4]{0:T(128)S(1)} %pad_add_fusion.core_ref.place_ref.refs_0_, s32[4,32]{1,0:T(4,128)S(1)} %collective-permute-done.1.columns_ref, bf16[66,64,128]{2,1,0:T(8,128)(2,1)S(1)} %pad_maximum_fusion.refs_0_, ...), custom_call_target="tpu_custom_call" | custom-call | flops 4194304 | bytes 20971520 | tf_op jit(solution)/shard_map/pick_other/pallas_call | solution.py:380
  63.4 1.4 %parent_scores.1.parent_ref = f32[32,64,128]{2,1,0:T(8,128)S(1)} custom-call(s32[32,64]{1,0:T(8,128)S(1)} %bitcast.21, bf16[32,256,128]{2,1,0:T(8,128)(2,1)S(1)} %copy-done.8, f32[32,128]{1,0:T(8,128)S(1)} %copy-done.5), custom_call_target="tpu_custom_call" | custom-call | flops 268435456 | bytes 3145728 | tf_op jit(solution)/shard_map/parent_scores/pallas_call | solution.py:358
  64.9 1.7 %own_sums.1 = (bf16[64,64,128]{2,1,0:T(8,128)(2,1)S(1)}, f32[16,64,128]{2,1,0:T(8,128)S(1)}, f32[32,64,128]{2,1,0:T(8,128)S(1)}) custom-call(s32[4]{0:T(128)S(1)} %pad_add_fusion.core_ref.place_ref.refs_0_, s32[4,32]{1,0:T(4,128)S(1)} %bitcast.20, s32[32]{0:T(128)S(1)} %copy-done.6, bf16[528,64,128]{2,1,0:T(8,128)(2,1)S(1)} %get-tuple-element.50.pool, ...), custom_call_target="tpu_custom_call" | custom-call | flops 268435456 | bytes 8388608 | tf_op jit(solution)/shard_map/own_sums/pallas_call | solution.py:396
  66.6 2.1 %row_sums.1 = (f32[64,128]{1,0:T(8,128)S(1)}, f32[32,64,128]{2,1,0:T(8,128)S(1)}, f32[16,64,128]{2,1,0:T(8,128)S(1)}) custom-call(s32[4]{0:T(128)S(1)} %pad_add_fusion.core_ref.place_ref.refs_0_, s32[32]{0:T(128)S(1)} %copy-done.6, bf16[65,64,128]{2,1,0:T(8,128)(2,1)S(1)} %collective-permute-done.14.other_ref.refs_7_, ...), custom_call_target="tpu_custom_call" | custom-call | flops 268435456 | bytes 8388608 | tf_op jit(solution)/shard_map/row_sums/pallas_call | solution.py:405
  68.7 0.6 collective-permute-start.15
  69.2 0.9 collective-permute-done.15.refs_1_
  70.2 17.3 %all_to_all.5.refs_2_ = f32[16,64,128]{2,1,0:T(8,128)S(1)} all-to-all(f32[16,64,128]{2,1,0:T(8,128)S(1)} %broadcast_in_dim.4), channel_id=1, replica_groups={{0,16,32,48,64,80,96,112,128,144,160,176,192,208,224,240},{8,24,40,56,7..., dimensions={0} | all-to-all | bytes 1048576 | tf_op jit(solution)/shard_map/all_to_all | solution.py:428
  87.5 2.8 %counts.1 = (bf16[32,4,16,128]{3,2,1,0:T(8,128)(2,1)S(1)}, bf16[32,4,16,128]{3,2,1,0:T(8,128)(2,1)S(1)}, bf16[32,4,16,128]{3,2,1,0:T(8,128)(2,1)S(1)}, bf16[32,4...) custom-call(s32[4]{0:T(128)S(1)} %pad_add_fusion.core_ref.place_ref., ...), custom_call_target="tpu_custom_call" | custom-call | flops 536870912 | bytes 13631488 | tf_op jit(solution)/shard_map/counts/pallas_call | solution.py:434
  90.3 2.0 %collective-permute-start.16 = (bf16[16,4,16,128]{3,2,1,0:T(8,128)(2,1)S(1)}, bf16[16,4,16,128]{3,2,1,0:T(8,128)(2,1)S(1)}, u32[]{:S(2)}, u32[]{:S(2)}) collective-permute-start(bf16[16,4,16,128]{3,2,1,0:T(8,128)(2,1)S(1)} %get-tuple-element.65), channel_id=1, source_target_pairs={{0,1},{1,2},{2,3},{3,4},{4,5},{5,6},{6,7},{7,0},{8,9},{9,10},{10,1... | collective-permute-start | bytes 786440 | tf_op jit(solution)/shard_map/ppermute | solution.py:447
  92.4 4.5 %collective-permute-done.16.up_in_ref = bf16[16,4,16,128]{3,2,1,0:T(8,128)(2,1)S(1)} collective-permute-done((bf16[16,4,16,128]{3,2,1,0:T(8,128)(2,1)S(1)}, bf16[16,4,16,128]{3,2,1,0:T(8,128)(2,1)S(1)}, u32[]{:S(2)}, u32[]{:S(2)}) %collective-permute-start.16) | collective-permute-done | bytes 262176 | tf_op jit(solution)/shard_map/ppermute | solution.py:447
  97.0 1.7 %collective-permute-done.17.down_in_ref = bf16[16,4,16,128]{3,2,1,0:T(8,128)(2,1)S(1)} collective-permute-done((bf16[16,4,16,128]{3,2,1,0:T(8,128)(2,1)S(1)}, bf16[16,4,16,128]{3,2,1,0:T(8,128)(2,1)S(1)}, u32[]{:S(2)}, u32[]{:S(2)}) %collective-permute-start.17) | collective-permute-done | bytes 262176 | tf_op jit(solution)/shard_map/ppermute | solution.py:447
  98.8 3.2 %collective-permute-start.18 = (bf16[32,4,16,128]{3,2,1,0:T(8,128)(2,1)S(1)}, bf16[32,4,16,128]{3,2,1,0:T(8,128)(2,1)S(1)}, u32[]{:S(2)}, u32[]{:S(2)}) collective-permute-start(bf16[32,4,16,128]{3,2,1,0:T(8,128)(2,1)S(1)} %get-tuple-element.67), channel_id=1, source_target_pairs={{0,1},{1,2},{2,3},{3,4},{4,5},{5,6},{6,7},{7,0},{8,9},{9,10},{10,1... | collective-permute-start | bytes 1572872 | tf_op jit(solution)/shard_map/ppermute | solution.py:447
  102.1 9.0 %collective-permute-done.18.up_in_ref = bf16[32,4,16,128]{3,2,1,0:T(8,128)(2,1)S(1)} collective-permute-done((bf16[32,4,16,128]{3,2,1,0:T(8,128)(2,1)S(1)}, bf16[32,4,16,128]{3,2,1,0:T(8,128)(2,1)S(1)}, u32[]{:S(2)}, u32[]{:S(2)}) %collective-permute-start.18) | collective-permute-done | bytes 524320 | tf_op jit(solution)/shard_map/ppermute | solution.py:447
  111.0 2.8 %collective-permute-done.19.down_in_ref = bf16[32,4,16,128]{3,2,1,0:T(8,128)(2,1)S(1)} collective-permute-done((bf16[32,4,16,128]{3,2,1,0:T(8,128)(2,1)S(1)}, bf16[32,4,16,128]{3,2,1,0:T(8,128)(2,1)S(1)}, u32[]{:S(2)}, u32[]{:S(2)}) %collective-permute-start.19) | collective-permute-done | bytes 524320 | tf_op jit(solution)/shard_map/ppermute | solution.py:447
  114.1 2.0 %collective-permute-start.20 = (bf16[32,4,16,128]{3,2,1,0:T(8,128)(2,1)S(1)}, bf16[32,4,16,128]{3,2,1,0:T(8,128)(2,1)S(1)}, u32[]{:S(2)}, u32[]{:S(2)}) collective-permute-start(bf16[32,4,16,128]{3,2,1,0:T(8,128)(2,1)S(1)} %get-tuple-element.69), channel_id=1, source_target_pairs={{0,1},{1,2},{2,3},{3,4},{4,5},{5,6},{6,7},{7,0},{8,9},{9,10},{10,1... | collective-permute-start | bytes 1572872 | tf_op jit(solution)/shard_map/ppermute | solution.py:447
  116.4 8.0 %collective-permute-done.20.up_in_ref = bf16[32,4,16,128]{3,2,1,0:T(8,128)(2,1)S(1)} collective-permute-done((bf16[32,4,16,128]{3,2,1,0:T(8,128)(2,1)S(1)}, bf16[32,4,16,128]{3,2,1,0:T(8,128)(2,1)S(1)}, u32[]{:S(2)}, u32[]{:S(2)}) %collective-permute-start.20) | collective-permute-done | bytes 524320 | tf_op jit(solution)/shard_map/ppermute | solution.py:447
  124.4 1.8 %collective-permute-done.21.down_in_ref = bf16[32,4,16,128]{3,2,1,0:T(8,128)(2,1)S(1)} collective-permute-done((bf16[32,4,16,128]{3,2,1,0:T(8,128)(2,1)S(1)}, bf16[32,4,16,128]{3,2,1,0:T(8,128)(2,1)S(1)}, u32[]{:S(2)}, u32[]{:S(2)}) %collective-permute-start.21) | collective-permute-done | bytes 524320 | tf_op jit(solution)/shard_map/ppermute | solution.py:447
  126.4 1.8 %collective-permute-start.22 = (bf16[32,4,16,128]{3,2,1,0:T(8,128)(2,1)S(1)}, bf16[32,4,16,128]{3,2,1,0:T(8,128)(2,1)S(1)}, u32[]{:S(2)}, u32[]{:S(2)}) collective-permute-start(bf16[32,4,16,128]{3,2,1,0:T(8,128)(2,1)S(1)} %get-tuple-element.71), channel_id=1, source_target_pairs={{0,1},{1,2},{2,3},{3,4},{4,5},{5,6},{6,7},{7,0},{8,9},{9,10},{10,1... | collective-permute-start | bytes 1572872 | tf_op jit(solution)/shard_map/ppermute | solution.py:447
  128.5 0.6 slice_reduce_fusion
  129.2 6.5 %collective-permute-done.22.up_in_ref = bf16[32,4,16,128]{3,2,1,0:T(8,128)(2,1)S(1)} collective-permute-done((bf16[32,4,16,128]{3,2,1,0:T(8,128)(2,1)S(1)}, bf16[32,4,16,128]{3,2,1,0:T(8,128)(2,1)S(1)}, u32[]{:S(2)}, u32[]{:S(2)}) %collective-permute-start.22) | collective-permute-done | bytes 524320 | tf_op jit(solution)/shard_map/ppermute | solution.py:447
  135.7 1.7 %collective-permute-done.23.down_in_ref = bf16[32,4,16,128]{3,2,1,0:T(8,128)(2,1)S(1)} collective-permute-done((bf16[32,4,16,128]{3,2,1,0:T(8,128)(2,1)S(1)}, bf16[32,4,16,128]{3,2,1,0:T(8,128)(2,1)S(1)}, u32[]{:S(2)}, u32[]{:S(2)}) %collective-permute-start.23) | collective-permute-done | bytes 524320 | tf_op jit(solution)/shard_map/ppermute | solution.py:447
  137.4 1.5 %ring_last.1 = bf16[32,4,16,128]{3,2,1,0:T(8,128)(2,1)} custom-call(s32[4]{0:T(128)S(1)} %pad_add_fusion.core_ref.place_ref.refs_0_, bf16[32,4,16,128]{3,2,1,0:T(8,128)(2,1)S(1)} %get-tuple-element.58.own_ref, bf16[32,4,16,128]{3,2,1,0:T(8,128)(2,1)S(1)} %collective-permute-done.22.up_in_ref, bf16[32,4,16,128]{3,2,1,0:T(8,128)(2,1)S(1)} %collective-permute-done.23.down_in_ref), custom_call_target="tpu_custom_call" | custom-call | tf_op jit(solution)/shard_map/ring_last/pallas_call | solution.py:465
  (47 shorter events, 3.1 us)
Async XLA Ops:
  0.6 1.6 %copy-start.1 = (bf16[32,256,128]{2,1,0:T(8,128)(2,1)S(1)}, bf16[32,256,128]{2,1,0:T(8,128)(2,1)}, u32[]{:S(2)}) copy-start(bf16[32,256,128]{2,1,0:T(8,128)(2,1)} %table_ref.4) | copy-start | bytes 6291460
  2.2 0.7 copy-start.3
  2.9 1.3 copy-start.7
  3.0 1.9 %copy-start.2 = (bf16[32,256,128]{2,1,0:T(8,128)(2,1)S(1)}, bf16[32,256,128]{2,1,0:T(8,128)(2,1)}, u32[]{:S(2)}) copy-start(bf16[32,256,128]{2,1,0:T(8,128)(2,1)} %table_ref.4) | copy-start | bytes 6291460
  3.0 1.9 %copy-start.4 = (s32[64,32]{0,1:T(8,128)S(1)}, s32[64,32]{0,1:T(8,128)}, u32[]{:S(2)}) copy-start(s32[64,32]{0,1:T(8,128)} %param.8) | copy-start | bytes 24580
  4.2 1.9 %collective-permute-start = (bf16[17,64,128]{2,1,0:T(8,128)(2,1)S(1)}, bf16[17,64,128]{2,1,0:T(8,128)(2,1)S(1)}, u32[]{:S(2)}, u32[]{:S(2)}) collective-permute-start(bf16[17,64,128]{2,1,0:T(8,128)(2,1)S(1)} %child_scores.2), channel_id=1, source_target_pairs={{0,8},{8,0},{16,24},{24,16},{32,40},{40,32},{48,56},{56,48},{64,72... | collective-permute-start | bytes 835592 | tf_op jit(solution)/shard_map/ppermute | solution.py:343
  4.3 1.8 %collective-permute-start.1 = (s32[4,32]{1,0:T(4,128)S(1)}, s32[4,32]{1,0:T(4,128)S(1)}, u32[]{:S(2)}, u32[]{:S(2)}) collective-permute-start(s32[4,32]{1,0:T(4,128)S(1)} %bitcast.19), channel_id=1, source_target_pairs={{0,8},{8,0},{16,24},{24,16},{32,40},{40,32},{48,56},{56,48},{64,72... | collective-permute-start | bytes 1544 | tf_op jit(solution)/shard_map/ppermute | solution.py:343
  6.7 10.6 %collective-permute-start.2 = (bf16[33,64,128]{2,1,0:T(8,128)(2,1)S(1)}, bf16[33,64,128]{2,1,0:T(8,128)(2,1)S(1)}, u32[]{:S(2)}, u32[]{:S(2)}) collective-permute-start(bf16[33,64,128]{2,1,0:T(8,128)(2,1)S(1)} %pack.1), channel_id=1, source_target_pairs={{0,64},{8,24},{16,80},{24,40},{32,96},{40,56},{48,112},{56,8},{64,... | collective-permute-start | bytes 1622024 | tf_op jit(solution)/shard_map/ppermute | solution.py:356
  8.3 9.4 %collective-permute-start.3 = (bf16[33,64,128]{2,1,0:T(8,128)(2,1)S(1)}, bf16[33,64,128]{2,1,0:T(8,128)(2,1)S(1)}, u32[]{:S(2)}, u32[]{:S(2)}) collective-permute-start(bf16[33,64,128]{2,1,0:T(8,128)(2,1)S(1)} %pack.1), channel_id=1, source_target_pairs={{0,192},{8,56},{16,208},{24,8},{32,224},{40,24},{48,240},{56,40},{... | collective-permute-start | bytes 1622024 | tf_op jit(solution)/shard_map/ppermute | solution.py:356
  17.7 10.2 %collective-permute-start.4 = (bf16[17,64,128]{2,1,0:T(8,128)(2,1)S(1)}, bf16[17,64,128]{2,1,0:T(8,128)(2,1)S(1)}, u32[]{:S(2)}, u32[]{:S(2)}) collective-permute-start(bf16[17,64,128]{2,1,0:T(8,128)(2,1)S(1)} %slice.21), channel_id=1, source_target_pairs={{0,64},{8,24},{16,80},{24,40},{32,96},{40,56},{48,112},{56,8},{64,... | collective-permute-start | bytes 835592 | tf_op jit(solution)/shard_map/ppermute | solution.py:356
  19.2 8.6 %collective-permute-start.5 = (bf16[16,64,128]{2,1,0:T(8,128)(2,1)S(1)}, bf16[16,64,128]{2,1,0:T(8,128)(2,1)S(1)}, u32[]{:S(2)}, u32[]{:S(2)}) collective-permute-start(bf16[16,64,128]{2,1,0:T(8,128)(2,1)S(1)} %slice.22), channel_id=1, source_target_pairs={{0,192},{8,56},{16,208},{24,8},{32,224},{40,24},{48,240},{56,40},{... | collective-permute-start | bytes 786440 | tf_op jit(solution)/shard_map/ppermute | solution.py:356
  21.2 16.4 %collective-permute-start.6 = (bf16[66,64,128]{2,1,0:T(8,128)(2,1)S(1)}, bf16[66,64,128]{2,1,0:T(8,128)(2,1)S(1)}, u32[]{:S(2)}, u32[]{:S(2)}) collective-permute-start(bf16[66,64,128]{2,1,0:T(8,128)(2,1)S(1)} %pad_maximum_fusion.refs_0_), channel_id=1, source_target_pairs={{0,16},{8,72},{16,32},{24,88},{32,48},{40,104},{48,0},{56,120},{64... | collective-permute-start | bytes 3244040 | tf_op jit(solution)/shard_map/ppermute | solution.py:356
  22.8 15.2 %collective-permute-start.7 = (bf16[66,64,128]{2,1,0:T(8,128)(2,1)S(1)}, bf16[66,64,128]{2,1,0:T(8,128)(2,1)S(1)}, u32[]{:S(2)}, u32[]{:S(2)}) collective-permute-start(bf16[66,64,128]{2,1,0:T(8,128)(2,1)S(1)} %pad_maximum_fusion.refs_0_), channel_id=1, source_target_pairs={{0,48},{8,200},{16,0},{24,216},{32,16},{40,232},{48,32},{56,248},{... | collective-permute-start | bytes 3244040 | tf_op jit(solution)/shard_map/ppermute | solution.py:356
  28.0 21.2 %collective-permute-start.8 = (bf16[66,64,128]{2,1,0:T(8,128)(2,1)S(1)}, bf16[66,64,128]{2,1,0:T(8,128)(2,1)S(1)}, u32[]{:S(2)}, u32[]{:S(2)}) collective-permute-start(bf16[66,64,128]{2,1,0:T(8,128)(2,1)S(1)} %constant_dynamic-update-slice_fusion.refs_1_), channel_id=1, source_target_pairs={{0,16},{8,72},{16,32},{24,88},{32,48},{40,104},{48,0},{56,120},{64... | collective-permute-start | bytes 3244040 | tf_op jit(solution)/shard_map/ppermute | solution.py:356
  30.2 19.3 %collective-permute-start.9 = (bf16[66,64,128]{2,1,0:T(8,128)(2,1)S(1)}, bf16[66,64,128]{2,1,0:T(8,128)(2,1)S(1)}, u32[]{:S(2)}, u32[]{:S(2)}) collective-permute-start(bf16[66,64,128]{2,1,0:T(8,128)(2,1)S(1)} %constant_dynamic-update-slice_fusion.refs_1_), channel_id=1, source_target_pairs={{0,48},{8,200},{16,0},{24,216},{32,16},{40,232},{48,32},{56,248},{... | collective-permute-start | bytes 3244040 | tf_op jit(solution)/shard_map/ppermute | solution.py:356
  38.0 17.0 %collective-permute-start.10 = (bf16[33,64,128]{2,1,0:T(8,128)(2,1)S(1)}, bf16[33,64,128]{2,1,0:T(8,128)(2,1)S(1)}, u32[]{:S(2)}, u32[]{:S(2)}) collective-permute-start(bf16[33,64,128]{2,1,0:T(8,128)(2,1)S(1)} %slice.23), channel_id=1, source_target_pairs={{0,16},{8,72},{16,32},{24,88},{32,48},{40,104},{48,0},{56,120},{64... | collective-permute-start | bytes 1622024 | tf_op jit(solution)/shard_map/ppermute | solution.py:356
  39.7 15.6 %collective-permute-start.11 = (bf16[33,64,128]{2,1,0:T(8,128)(2,1)S(1)}, bf16[33,64,128]{2,1,0:T(8,128)(2,1)S(1)}, u32[]{:S(2)}, u32[]{:S(2)}) collective-permute-start(bf16[33,64,128]{2,1,0:T(8,128)(2,1)S(1)} %slice.24), channel_id=1, source_target_pairs={{0,48},{8,200},{16,0},{24,216},{32,16},{40,232},{48,32},{56,248},{... | collective-permute-start | bytes 1622024 | tf_op jit(solution)/shard_map/ppermute | solution.py:356
  49.6 11.2 %collective-permute-start.12 = (bf16[33,64,128]{2,1,0:T(8,128)(2,1)S(1)}, bf16[33,64,128]{2,1,0:T(8,128)(2,1)S(1)}, u32[]{:S(2)}, u32[]{:S(2)}) collective-permute-start(bf16[33,64,128]{2,1,0:T(8,128)(2,1)S(1)} %slice.25), channel_id=1, source_target_pairs={{0,16},{8,72},{16,32},{24,88},{32,48},{40,104},{48,0},{56,120},{64... | collective-permute-start | bytes 1622024 | tf_op jit(solution)/shard_map/ppermute | solution.py:356
  51.5 11.9 %copy-start.5 = (f32[32,128]{1,0:T(8,128)S(1)}, f32[32,128]{1,0:T(8,128)}, u32[]{:S(2)}) copy-start(f32[32,128]{1,0:T(8,128)} %prior_ref.3) | copy-start | bytes 49156
  51.5 11.9 %copy-start.8 = (bf16[32,256,128]{2,1,0:T(8,128)(2,1)S(1)}, bf16[32,256,128]{2,1,0:T(8,128)(2,1)}, u32[]{:S(2)}) copy-start(bf16[32,256,128]{2,1,0:T(8,128)(2,1)} %table_ref.5) | copy-start | bytes 6291460
  51.5 11.9 %copy-start.9 = (s32[64,32]{0,1:T(8,128)S(1)}, s32[64,32]{0,1:T(8,128)}, u32[]{:S(2)}) copy-start(s32[64,32]{0,1:T(8,128)} %param.9) | copy-start | bytes 24580
  51.5 9.6 %collective-permute-start.13 = (bf16[33,64,128]{2,1,0:T(8,128)(2,1)S(1)}, bf16[33,64,128]{2,1,0:T(8,128)(2,1)S(1)}, u32[]{:S(2)}, u32[]{:S(2)}) collective-permute-start(bf16[33,64,128]{2,1,0:T(8,128)(2,1)S(1)} %slice.26), channel_id=1, source_target_pairs={{0,48},{8,200},{16,0},{24,216},{32,16},{40,232},{48,32},{56,248},{... | collective-permute-start | bytes 1622024 | tf_op jit(solution)/shard_map/ppermute | solution.py:356
  61.1 3.7 %copy-start = (bf16[32,1,4,128,128]{4,3,2,1,0:T(8,128)(2,1)S(1)}, bf16[32,1,4,128,128]{4,3,2,1,0:T(8,128)(2,1)}, u32[]{:S(2)}) copy-start(bf16[32,1,4,128,128]{4,3,2,1,0:T(8,128)(2,1)} %param.13) | copy-start | bytes 12582916
  63.2 3.3 %collective-permute-start.14 = (bf16[65,64,128]{2,1,0:T(8,128)(2,1)S(1)}, bf16[65,64,128]{2,1,0:T(8,128)(2,1)S(1)}, u32[]{:S(2)}, u32[]{:S(2)}) collective-permute-start(bf16[65,64,128]{2,1,0:T(8,128)(2,1)S(1)} %get-tuple-element.49), channel_id=1, source_target_pairs={{0,8},{8,0},{16,24},{24,16},{32,40},{40,32},{48,56},{56,48},{64,72... | collective-permute-start | bytes 3194888 | tf_op jit(solution)/shard_map/ppermute | solution.py:393
  63.4 1.5 %copy-start.6 = (s32[32]{0:T(128)S(1)}, s32[32]{0:T(128)}, u32[]{:S(2)}) copy-start(s32[32]{0:T(128)} %refs_1_.1) | copy-start | bytes 388
  68.7 1.4 %collective-permute-start.15 = (f32[64,128]{1,0:T(8,128)S(1)}, f32[64,128]{1,0:T(8,128)S(1)}, u32[]{:S(2)}, u32[]{:S(2)}) collective-permute-start(f32[64,128]{1,0:T(8,128)S(1)} %get-tuple-element.53.refs_0_), channel_id=1, source_target_pairs={{0,8},{8,0},{16,24},{24,16},{32,40},{40,32},{48,56},{56,48},{64,72... | collective-permute-start | bytes 98312 | tf_op jit(solution)/shard_map/ppermute | solution.py:425
  90.3 6.6 %collective-permute-start.16 = (bf16[16,4,16,128]{3,2,1,0:T(8,128)(2,1)S(1)}, bf16[16,4,16,128]{3,2,1,0:T(8,128)(2,1)S(1)}, u32[]{:S(2)}, u32[]{:S(2)}) collective-permute-start(bf16[16,4,16,128]{3,2,1,0:T(8,128)(2,1)S(1)} %get-tuple-element.65), channel_id=1, source_target_pairs={{0,1},{1,2},{2,3},{3,4},{4,5},{5,6},{6,7},{7,0},{8,9},{9,10},{10,1... | collective-permute-start | bytes 786440 | tf_op jit(solution)/shard_map/ppermute | solution.py:447
  92.3 6.4 %collective-permute-start.17 = (bf16[16,4,16,128]{3,2,1,0:T(8,128)(2,1)S(1)}, bf16[16,4,16,128]{3,2,1,0:T(8,128)(2,1)S(1)}, u32[]{:S(2)}, u32[]{:S(2)}) collective-permute-start(bf16[16,4,16,128]{3,2,1,0:T(8,128)(2,1)S(1)} %get-tuple-element.66), channel_id=1, source_target_pairs={{0,7},{1,0},{2,1},{3,2},{4,3},{5,4},{6,5},{7,6},{8,15},{9,8},{10,9... | collective-permute-start | bytes 786440 | tf_op jit(solution)/shard_map/ppermute | solution.py:447
  98.8 12.2 %collective-permute-start.18 = (bf16[32,4,16,128]{3,2,1,0:T(8,128)(2,1)S(1)}, bf16[32,4,16,128]{3,2,1,0:T(8,128)(2,1)S(1)}, u32[]{:S(2)}, u32[]{:S(2)}) collective-permute-start(bf16[32,4,16,128]{3,2,1,0:T(8,128)(2,1)S(1)} %get-tuple-element.67), channel_id=1, source_target_pairs={{0,1},{1,2},{2,3},{3,4},{4,5},{5,6},{6,7},{7,0},{8,9},{9,10},{10,1... | collective-permute-start | bytes 1572872 | tf_op jit(solution)/shard_map/ppermute | solution.py:447
  102.1 11.8 %collective-permute-start.19 = (bf16[32,4,16,128]{3,2,1,0:T(8,128)(2,1)S(1)}, bf16[32,4,16,128]{3,2,1,0:T(8,128)(2,1)S(1)}, u32[]{:S(2)}, u32[]{:S(2)}) collective-permute-start(bf16[32,4,16,128]{3,2,1,0:T(8,128)(2,1)S(1)} %get-tuple-element.68), channel_id=1, source_target_pairs={{0,7},{1,0},{2,1},{3,2},{4,3},{5,4},{6,5},{7,6},{8,15},{9,8},{10,9... | collective-permute-start | bytes 1572872 | tf_op jit(solution)/shard_map/ppermute | solution.py:447
  114.1 10.3 %collective-permute-start.20 = (bf16[32,4,16,128]{3,2,1,0:T(8,128)(2,1)S(1)}, bf16[32,4,16,128]{3,2,1,0:T(8,128)(2,1)S(1)}, u32[]{:S(2)}, u32[]{:S(2)}) collective-permute-start(bf16[32,4,16,128]{3,2,1,0:T(8,128)(2,1)S(1)} %get-tuple-element.69), channel_id=1, source_target_pairs={{0,1},{1,2},{2,3},{3,4},{4,5},{5,6},{6,7},{7,0},{8,9},{9,10},{10,1... | collective-permute-start | bytes 1572872 | tf_op jit(solution)/shard_map/ppermute | solution.py:447
  116.1 10.1 %collective-permute-start.21 = (bf16[32,4,16,128]{3,2,1,0:T(8,128)(2,1)S(1)}, bf16[32,4,16,128]{3,2,1,0:T(8,128)(2,1)S(1)}, u32[]{:S(2)}, u32[]{:S(2)}) collective-permute-start(bf16[32,4,16,128]{3,2,1,0:T(8,128)(2,1)S(1)} %get-tuple-element.70), channel_id=1, source_target_pairs={{0,7},{1,0},{2,1},{3,2},{4,3},{5,4},{6,5},{7,6},{8,15},{9,8},{10,9... | collective-permute-start | bytes 1572872 | tf_op jit(solution)/shard_map/ppermute | solution.py:447
  126.4 9.3 %collective-permute-start.22 = (bf16[32,4,16,128]{3,2,1,0:T(8,128)(2,1)S(1)}, bf16[32,4,16,128]{3,2,1,0:T(8,128)(2,1)S(1)}, u32[]{:S(2)}, u32[]{:S(2)}) collective-permute-start(bf16[32,4,16,128]{3,2,1,0:T(8,128)(2,1)S(1)} %get-tuple-element.71), channel_id=1, source_target_pairs={{0,1},{1,2},{2,3},{3,4},{4,5},{5,6},{6,7},{7,0},{8,9},{9,10},{10,1... | collective-permute-start | bytes 1572872 | tf_op jit(solution)/shard_map/ppermute | solution.py:447
  128.2 9.2 %collective-permute-start.23 = (bf16[32,4,16,128]{3,2,1,0:T(8,128)(2,1)S(1)}, bf16[32,4,16,128]{3,2,1,0:T(8,128)(2,1)S(1)}, u32[]{:S(2)}, u32[]{:S(2)}) collective-permute-start(bf16[32,4,16,128]{3,2,1,0:T(8,128)(2,1)S(1)} %get-tuple-element.72), channel_id=1, source_target_pairs={{0,7},{1,0},{2,1},{3,2},{4,3},{5,4},{6,5},{7,6},{8,15},{9,8},{10,9... | collective-permute-start | bytes 1572872 | tf_op jit(solution)/shard_map/ppermute | solution.py:447

commit v8 on v7

--- a/solution.py
+++ b/solution.py
@@ -1,3 +1,5 @@
+import functools
+
 import jax
 import jax.numpy as jnp
 from jax import lax
@@ -210,10 +212,13 @@
     refs[-1][...] = merge([r[...] for r in refs[:-1]])
 
 
-def counts_kernel(scale, place_ref, map_ref, stats_ref, *refs):
+def place_rows(place_ref, distance, parts, rows):
+    return pl.multiple_of(lax.rem(place_ref[1] + distance, parts) * rows, rows)
+
+
+def shares_kernel(scale, place_ref, map_ref, stats_ref, *refs):
     root_ref, own_sums_ref, other_sums_ref, own_ref, other_ref, weights_ref = refs[:6]
-    near, far, loglik_ref, posterior = refs[6:13], refs[13:15], refs[15], refs[16]
-    core, place = place_ref[0], place_ref[1]
+    far, (share_ref, loglik_ref, posterior) = refs[6:8], refs[8:]
     stats = merge([stats_ref[i] for i in range(stats_ref.shape[0])])
     lanes = lane_of((S_LOC, BLK))
     norm = stats + pltpu.roll(jnp.log(stats), BLK - P_SIZE, 1)
@@ -224,30 +229,48 @@
     loglik_ref[...] = jnp.broadcast_to(loglik, (S_LOC, BLK))
     for p in range(P_SIZE):
         posterior[p] = jnp.exp(root_ref[p] - norm[:, p : p + 1]).astype(jnp.bfloat16)
-    rows = near[0].shape[2]
+    rows = far[0].shape[2]
     parts = BLK // rows
-    starts = [pl.multiple_of(lax.rem(place + k, parts) * rows, rows) for k in range(parts)]
-    turn = lax.rem(parts - place, parts) * rows
+    first = place_rows(place_ref, parts // 2, parts, rows)
+    turn = lax.rem(BLK - first, BLK)
     for half, (picked_ref, sums_ref) in enumerate(
         ((own_ref, own_sums_ref), (other_ref, other_sums_ref))
     ):
         for k in range(HALF):
-            child = child_at(core, half, k)
+            child = child_at(place_ref[0], half, k)
             share = posterior[map_ref[child]].astype(jnp.float32) / sums_ref[k]
-            share = pltpu.roll(share, turn, 1).astype(jnp.bfloat16)
+            share_ref[half * HALF + k] = share.astype(jnp.bfloat16)
+            share = pltpu.roll(share, turn, 1).astype(jnp.bfloat16)[:, :rows]
             picked = jnp.concatenate([picked_ref[k * NZ + z] for z in range(NZ)], axis=1)
             flow = lax.dot_general(
                 share, picked, (((0,), (0,)), ((), ())), preferred_element_type=jnp.float32
             )
-            for distance in range(parts):
+            for z in range(NZ):
+                weight = weights_ref[child, z, pl.ds(first, rows), :].astype(jnp.float32) * scale
+                block = flow[:, z * BLK : (z + 1) * BLK] * weight
+                far[half][k, z] = block.astype(jnp.bfloat16)
+
+
+def counts_kernel(scale, place_ref, share_ref, own_ref, other_ref, weights_ref, *refs):
+    near, flows = refs[:-1], refs[-1]
+    rows = near[0].shape[2]
+    parts = BLK // rows
+    distances = [d for d in range(parts) if d != parts // 2]
+    starts = [place_rows(place_ref, d, parts, rows) for d in distances]
+    for half, picked_ref in enumerate((own_ref, other_ref)):
+        for k in range(HALF):
+            child = child_at(place_ref[0], half, k)
+            at = half * HALF + k
+            picked = jnp.concatenate([picked_ref[k * NZ + z] for z in range(NZ)], axis=1)
+            flows[at % 4] = lax.dot_general(
+                share_ref[at], picked, (((0,), (0,)), ((), ())), preferred_element_type=jnp.float32
+            )
+            for out_ref, start in zip(near, starts):
+                flow = flows[at % 4, pl.ds(start, rows), :]
                 for z in range(NZ):
-                    weight = weights_ref[child, z, pl.ds(starts[distance], rows), :]
-                    block = flow[distance * rows : (distance + 1) * rows, z * BLK : (z + 1) * BLK]
-                    block = (block * (weight.astype(jnp.float32) * scale)).astype(jnp.bfloat16)
-                    if distance == 4:
-                        far[half][k, z] = block
-                    else:
-                        near[distance if distance < 4 else distance - 1][half * HALF + k, z] = block
+                    weight = weights_ref[child, z, pl.ds(start, rows), :].astype(jnp.float32) * scale
+                    block = flow[:, z * BLK : (z + 1) * BLK] * weight
+                    out_ref[at, z] = block.astype(jnp.bfloat16)
 
 
 def first_step_kernel(up_ref, down_ref, up_in_ref, down_in_ref, up_out_ref, down_out_ref):
@@ -431,15 +454,15 @@
     ]
     scale = K * NZ * BLK / (S_LOC * parts)
     whole, half_set = shape((C, NZ, rows, BLK), bf16), shape((HALF, NZ, rows, BLK), bf16)
-    n0, n1, n2, n3, n5, n6, n7, far_up, far_down, loglik = pl.pallas_call(
-        lambda *refs: counts_kernel(scale, *refs),
-        out_shape=(whole,) * 7 + (half_set,) * 2 + (shape((S_LOC, BLK), f32),),
+    far_up, far_down, shares, loglik = pl.pallas_call(
+        functools.partial(shares_kernel, scale),
+        out_shape=(half_set, half_set, shape((C, S_LOC, BLK), bf16), shape((S_LOC, BLK), f32)),
         in_specs=[SMEM, SMEM] + [VMEM] * 7,
-        out_specs=(VMEM,) * 10,
+        out_specs=(VMEM,) * 4,
         scratch_shapes=[pltpu.VMEM((P_SIZE, S_LOC, BLK), bf16)],
-        compiler_params=params(24),
-        cost_estimate=cost(1 << 29, 13 << 20, 1 << 19),
-        name="counts",
+        compiler_params=params(20),
+        cost_estimate=cost(1 << 26, 12 << 20, 1 << 19),
+        name="shares",
     )(place, parent_map, *others, root, own_sums, other_sums, picked, other, weights)
 
     def ring(up, down):
@@ -447,6 +470,16 @@
         return lax.ppermute(up, "batch", shift(1)), lax.ppermute(down, "batch", shift(-1))
 
     up, down = ring(far_up, far_down)
+    n0, n1, n2, n3, n5, n6, n7 = pl.pallas_call(
+        functools.partial(counts_kernel, scale),
+        out_shape=(whole,) * 7,
+        in_specs=[SMEM] + [VMEM] * 4,
+        out_specs=(VMEM,) * 7,
+        scratch_shapes=[pltpu.VMEM((4, BLK, NZ * BLK), f32)],
+        compiler_params=params(20),
+        cost_estimate=cost(1 << 20, 1 << 20, 1),
+        name="counts",
+    )(place, shares, picked, other, weights)
     for kernel, here_up, here_down in (
         (first_step_kernel, n3, n5),
         (step_kernel, n2, n6),

time: 141 us -> 140 us (level)
  waiting for transfers between devices: 70.2 us -> 67.8 us
    ppermute x4, waiting for transfers between devices: 28 us -> 26.4 us  [ring(): lax.ppermute(up, 'batch', shift(1))]
    pallas_call x1 -> x2, Pallas kernels: 2.79 us -> 4.1 us  [the longest x1 2.08 us: body(): pl.pallas_call(functools.partial(counts_kernel, scale), out_shape=(whole,...]
  transfers between devices with their start and end apart: 24 -> 24, of which waited for: 20 -> 20; matrix products, arithmetic and copies ran while one was open for 1% -> 1% of each run, Pallas kernels for 3% -> 5%
where the time goes in v8:
time: 140 us; the launch traced here: 138 us
  waiting for transfers between devices  67.8 us (48%)
  starting transfers between devices  31.4 us (22%)
  blocking collectives  17.3 us (12%)
  Pallas kernels  16.7 us (12%)
  local copies, waits for them, and re-layouts  3.3 us (2%)
    ppermute x12, waiting for transfers between devices, send(): return lax.ppermute(value, 'region', along(a, b))  33.2 us
    ppermute x4, waiting for transfers between devices, ring(): lax.ppermute(up, 'batch', shift(1))  26.4 us
    ppermute x12, starting transfers between devices, send(): return lax.ppermute(value, 'region', along(a, b))  20.7 us
    all_to_all x1, blocking collectives, body(): lax.all_to_all(jnp.broadcast_to(stats[None], (16, S_LOC, BLK)), 'region',...  17.3 us
    ppermute x4, starting transfers between devices, ring(): lax.ppermute(up, 'batch', shift(1))  8.82 us
    ppermute x4, waiting for transfers between devices, ring(): lax.ppermute(down, 'batch', shift(-1))  7.32 us
  transfers between devices with their start and end apart: 24, of which 20 were waited for; matrix products, arithmetic and copies ran while one was open for 1% of the time, Pallas kernels for 5%

profile of v8, /device:TPU:32, one launch (start us, length us, event | category | flops | bytes accessed | tf_op | source)
XLA Modules:
  0.0 137.6 jit_solution(15748243731020703152)
XLA Ops:
  0.6 1.6 %copy-done.1 = bf16[32,256,128]{2,1,0:T(8,128)(2,1)S(1)} copy-done((bf16[32,256,128]{2,1,0:T(8,128)(2,1)S(1)}, bf16[32,256,128]{2,1,0:T(8,128)(2,1)}, u32[]{:S(2)}) %copy-start.1) | copy-done | bytes 2097176
  2.2 0.7 copy-done.3
  3.0 1.2 child_scores.2
  4.3 0.5 collective-permute-start.1
  4.9 1.2 child_scores.3.own_ref
  6.1 0.6 pack.1
  6.7 1.5 %collective-permute-start.2 = (bf16[33,64,128]{2,1,0:T(8,128)(2,1)S(1)}, bf16[33,64,128]{2,1,0:T(8,128)(2,1)S(1)}, u32[]{:S(2)}, u32[]{:S(2)}) collective-permute-start(bf16[33,64,128]{2,1,0:T(8,128)(2,1)S(1)} %pack.1), channel_id=1, source_target_pairs={{0,64},{8,24},{16,80},{24,40},{32,96},{40,56},{48,112},{56,8},{64,... | collective-permute-start | bytes 1622024 | tf_op jit(solution)/shard_map/ppermute | solution.py:379
  8.3 1.7 %collective-permute-start.3 = (bf16[33,64,128]{2,1,0:T(8,128)(2,1)S(1)}, bf16[33,64,128]{2,1,0:T(8,128)(2,1)S(1)}, u32[]{:S(2)}, u32[]{:S(2)}) collective-permute-start(bf16[33,64,128]{2,1,0:T(8,128)(2,1)S(1)} %pack.1), channel_id=1, source_target_pairs={{0,192},{8,56},{16,208},{24,8},{32,224},{40,24},{48,240},{56,40},{... | collective-permute-start | bytes 1622024 | tf_op jit(solution)/shard_map/ppermute | solution.py:379
  10.0 7.3 %collective-permute-done.2 = bf16[33,64,128]{2,1,0:T(8,128)(2,1)S(1)} collective-permute-done((bf16[33,64,128]{2,1,0:T(8,128)(2,1)S(1)}, bf16[33,64,128]{2,1,0:T(8,128)(2,1)S(1)}, u32[]{:S(2)}, u32[]{:S(2)}) %collective-permute-start.2) | collective-permute-done | bytes 540704 | tf_op jit(solution)/shard_map/ppermute | solution.py:379
  17.7 1.6 %collective-permute-start.4 = (bf16[17,64,128]{2,1,0:T(8,128)(2,1)S(1)}, bf16[17,64,128]{2,1,0:T(8,128)(2,1)S(1)}, u32[]{:S(2)}, u32[]{:S(2)}) collective-permute-start(bf16[17,64,128]{2,1,0:T(8,128)(2,1)S(1)} %slice.21), channel_id=1, source_target_pairs={{0,64},{8,24},{16,80},{24,40},{32,96},{40,56},{48,112},{56,8},{64,... | collective-permute-start | bytes 835592 | tf_op jit(solution)/shard_map/ppermute | solution.py:379
  19.2 1.8 %collective-permute-start.5 = (bf16[16,64,128]{2,1,0:T(8,128)(2,1)S(1)}, bf16[16,64,128]{2,1,0:T(8,128)(2,1)S(1)}, u32[]{:S(2)}, u32[]{:S(2)}) collective-permute-start(bf16[16,64,128]{2,1,0:T(8,128)(2,1)S(1)} %slice.22), channel_id=1, source_target_pairs={{0,192},{8,56},{16,208},{24,8},{32,224},{40,24},{48,240},{56,40},{... | collective-permute-start | bytes 786440 | tf_op jit(solution)/shard_map/ppermute | solution.py:379
  21.2 1.7 %collective-permute-start.6 = (bf16[66,64,128]{2,1,0:T(8,128)(2,1)S(1)}, bf16[66,64,128]{2,1,0:T(8,128)(2,1)S(1)}, u32[]{:S(2)}, u32[]{:S(2)}) collective-permute-start(bf16[66,64,128]{2,1,0:T(8,128)(2,1)S(1)} %pad_maximum_fusion.refs_0_), channel_id=1, source_target_pairs={{0,16},{8,72},{16,32},{24,88},{32,48},{40,104},{48,0},{56,120},{64... | collective-permute-start | bytes 3244040 | tf_op jit(solution)/shard_map/ppermute | solution.py:379
  22.8 1.7 %collective-permute-start.7 = (bf16[66,64,128]{2,1,0:T(8,128)(2,1)S(1)}, bf16[66,64,128]{2,1,0:T(8,128)(2,1)S(1)}, u32[]{:S(2)}, u32[]{:S(2)}) collective-permute-start(bf16[66,64,128]{2,1,0:T(8,128)(2,1)S(1)} %pad_maximum_fusion.refs_0_), channel_id=1, source_target_pairs={{0,48},{8,200},{16,0},{24,216},{32,16},{40,232},{48,32},{56,248},{... | collective-permute-start | bytes 3244040 | tf_op jit(solution)/shard_map/ppermute | solution.py:379
  24.5 3.4 %collective-permute-done.5 = bf16[16,64,128]{2,1,0:T(8,128)(2,1)S(1)} collective-permute-done((bf16[16,64,128]{2,1,0:T(8,128)(2,1)S(1)}, bf16[16,64,128]{2,1,0:T(8,128)(2,1)S(1)}, u32[]{:S(2)}, u32[]{:S(2)}) %collective-permute-start.5) | collective-permute-done | bytes 262176 | tf_op jit(solution)/shard_map/ppermute | solution.py:379
  28.0 2.2 %collective-permute-start.8 = (bf16[66,64,128]{2,1,0:T(8,128)(2,1)S(1)}, bf16[66,64,128]{2,1,0:T(8,128)(2,1)S(1)}, u32[]{:S(2)}, u32[]{:S(2)}) collective-permute-start(bf16[66,64,128]{2,1,0:T(8,128)(2,1)S(1)} %constant_dynamic-update-slice_fusion.refs_1_), channel_id=1, source_target_pairs={{0,16},{8,72},{16,32},{24,88},{32,48},{40,104},{48,0},{56,120},{64... | collective-permute-start | bytes 3244040 | tf_op jit(solution)/shard_map/ppermute | solution.py:379
  30.2 1.5 %collective-permute-start.9 = (bf16[66,64,128]{2,1,0:T(8,128)(2,1)S(1)}, bf16[66,64,128]{2,1,0:T(8,128)(2,1)S(1)}, u32[]{:S(2)}, u32[]{:S(2)}) collective-permute-start(bf16[66,64,128]{2,1,0:T(8,128)(2,1)S(1)} %constant_dynamic-update-slice_fusion.refs_1_), channel_id=1, source_target_pairs={{0,48},{8,200},{16,0},{24,216},{32,16},{40,232},{48,32},{56,248},{... | collective-permute-start | bytes 3244040 | tf_op jit(solution)/shard_map/ppermute | solution.py:379
  31.8 5.9 %collective-permute-done.6.refs_2_ = bf16[66,64,128]{2,1,0:T(8,128)(2,1)S(1)} collective-permute-done((bf16[66,64,128]{2,1,0:T(8,128)(2,1)S(1)}, bf16[66,64,128]{2,1,0:T(8,128)(2,1)S(1)}, u32[]{:S(2)}, u32[]{:S(2)}) %collective-permute-start.6) | collective-permute-done | bytes 1081376 | tf_op jit(solution)/shard_map/ppermute | solution.py:379
  37.6 0.4 collective-permute-done.7.refs_4_
  38.0 1.7 %collective-permute-start.10 = (bf16[33,64,128]{2,1,0:T(8,128)(2,1)S(1)}, bf16[33,64,128]{2,1,0:T(8,128)(2,1)S(1)}, u32[]{:S(2)}, u32[]{:S(2)}) collective-permute-start(bf16[33,64,128]{2,1,0:T(8,128)(2,1)S(1)} %slice.23), channel_id=1, source_target_pairs={{0,16},{8,72},{16,32},{24,88},{32,48},{40,104},{48,0},{56,120},{64... | collective-permute-start | bytes 1622024 | tf_op jit(solution)/shard_map/ppermute | solution.py:379
  39.7 1.7 %collective-permute-start.11 = (bf16[33,64,128]{2,1,0:T(8,128)(2,1)S(1)}, bf16[33,64,128]{2,1,0:T(8,128)(2,1)S(1)}, u32[]{:S(2)}, u32[]{:S(2)}) collective-permute-start(bf16[33,64,128]{2,1,0:T(8,128)(2,1)S(1)} %slice.24), channel_id=1, source_target_pairs={{0,48},{8,200},{16,0},{24,216},{32,16},{40,232},{48,32},{56,248},{... | collective-permute-start | bytes 1622024 | tf_op jit(solution)/shard_map/ppermute | solution.py:379
  41.4 7.7 %collective-permute-done.8.refs_3_ = bf16[66,64,128]{2,1,0:T(8,128)(2,1)S(1)} collective-permute-done((bf16[66,64,128]{2,1,0:T(8,128)(2,1)S(1)}, bf16[66,64,128]{2,1,0:T(8,128)(2,1)S(1)}, u32[]{:S(2)}, u32[]{:S(2)}) %collective-permute-start.8) | collective-permute-done | bytes 1081376 | tf_op jit(solution)/shard_map/ppermute | solution.py:379
  49.6 1.8 %collective-permute-start.12 = (bf16[33,64,128]{2,1,0:T(8,128)(2,1)S(1)}, bf16[33,64,128]{2,1,0:T(8,128)(2,1)S(1)}, u32[]{:S(2)}, u32[]{:S(2)}) collective-permute-start(bf16[33,64,128]{2,1,0:T(8,128)(2,1)S(1)} %slice.25), channel_id=1, source_target_pairs={{0,16},{8,72},{16,32},{24,88},{32,48},{40,104},{48,0},{56,120},{64... | collective-permute-start | bytes 1622024 | tf_op jit(solution)/shard_map/ppermute | solution.py:379
  51.5 1.7 %collective-permute-start.13 = (bf16[33,64,128]{2,1,0:T(8,128)(2,1)S(1)}, bf16[33,64,128]{2,1,0:T(8,128)(2,1)S(1)}, u32[]{:S(2)}, u32[]{:S(2)}) collective-permute-start(bf16[33,64,128]{2,1,0:T(8,128)(2,1)S(1)} %slice.26), channel_id=1, source_target_pairs={{0,48},{8,200},{16,0},{24,216},{32,16},{40,232},{48,32},{56,248},{... | collective-permute-start | bytes 1622024 | tf_op jit(solution)/shard_map/ppermute | solution.py:379
  53.2 1.7 %collective-permute-done.10.refs_6_ = bf16[33,64,128]{2,1,0:T(8,128)(2,1)S(1)} collective-permute-done((bf16[33,64,128]{2,1,0:T(8,128)(2,1)S(1)}, bf16[33,64,128]{2,1,0:T(8,128)(2,1)S(1)}, u32[]{:S(2)}, u32[]{:S(2)}) %collective-permute-start.10) | collective-permute-done | bytes 540704 | tf_op jit(solution)/shard_map/ppermute | solution.py:379
  55.4 5.4 %collective-permute-done.12.refs_8_ = bf16[33,64,128]{2,1,0:T(8,128)(2,1)S(1)} collective-permute-done((bf16[33,64,128]{2,1,0:T(8,128)(2,1)S(1)}, bf16[33,64,128]{2,1,0:T(8,128)(2,1)S(1)}, u32[]{:S(2)}, u32[]{:S(2)}) %collective-permute-start.12) | collective-permute-done | bytes 540704 | tf_op jit(solution)/shard_map/ppermute | solution.py:379
  61.1 2.1 %pick_other.1 = (bf16[65,64,128]{2,1,0:T(8,128)(2,1)S(1)}, bf16[528,64,128]{2,1,0:T(8,128)(2,1)S(1)}, f32[32,64,128]{2,1,0:T(8,128)S(1)}) custom-call(s32[4]{0:T(128)S(1)} %pad_add_fusion.core_ref.place_ref, s32[4,32]{1,0:T(4,128)S(1)} %collective-permute-done.1.columns_ref, bf16[66,64,128]{2,1,0:T(8,128)(2,1)S(1)} %pad_maximum_fusion.refs_0_, ...), custom_call_target="tpu_custom_call" | custom-call | flops 4194304 | bytes 20971520 | tf_op jit(solution)/shard_map/pick_other/pallas_call | solution.py:403
  63.4 1.4 %parent_scores.1.parent_ref = f32[32,64,128]{2,1,0:T(8,128)S(1)} custom-call(s32[32,64]{1,0:T(8,128)S(1)} %bitcast.22, bf16[32,256,128]{2,1,0:T(8,128)(2,1)S(1)} %copy-done.8, f32[32,128]{1,0:T(8,128)S(1)} %copy-done.5), custom_call_target="tpu_custom_call" | custom-call | flops 268435456 | bytes 3145728 | tf_op jit(solution)/shard_map/parent_scores/pallas_call | solution.py:381
  64.9 1.7 %own_sums.1 = (bf16[64,64,128]{2,1,0:T(8,128)(2,1)S(1)}, f32[16,64,128]{2,1,0:T(8,128)S(1)}, f32[32,64,128]{2,1,0:T(8,128)S(1)}) custom-call(s32[4]{0:T(128)S(1)} %pad_add_fusion.core_ref.place_ref, s32[4,32]{1,0:T(4,128)S(1)} %bitcast.21, s32[32]{0:T(128)S(1)} %copy-done.6, bf16[528,64,128]{2,1,0:T(8,128)(2,1)S(1)} %get-tuple-element.51.pool, ...), custom_call_target="tpu_custom_call" | custom-call | flops 268435456 | bytes 8388608 | tf_op jit(solution)/shard_map/own_sums/pallas_call | solution.py:419
  66.6 2.0 %row_sums.1 = (f32[64,128]{1,0:T(8,128)S(1)}, f32[32,64,128]{2,1,0:T(8,128)S(1)}, f32[16,64,128]{2,1,0:T(8,128)S(1)}) custom-call(s32[4]{0:T(128)S(1)} %pad_add_fusion.core_ref.place_ref, s32[32]{0:T(128)S(1)} %copy-done.6, bf16[65,64,128]{2,1,0:T(8,128)(2,1)S(1)} %collective-permute-done.14.other_ref.refs_4_, bf16[32,4,128,128]{3,2,1,0:T(8,128)(2,1)S(1)} %bitcast.15, ...), custom_call_target="tpu_custom_call" | custom-call | flops 268435456 | bytes 8388608 | tf_op jit(solution)/shard_map/row_sums/pallas_call | solution.py:428
  68.6 0.6 collective-permute-start.15
  69.2 0.9 collective-permute-done.15.refs_1_
  70.2 17.3 %all_to_all.5.stats_ref = f32[16,64,128]{2,1,0:T(8,128)S(1)} all-to-all(f32[16,64,128]{2,1,0:T(8,128)S(1)} %broadcast_in_dim.4), channel_id=1, replica_groups={{0,16,32,48,64,80,96,112,128,144,160,176,192,208,224,240},{8,24,40,56,7..., dimensions={0} | all-to-all | bytes 1048576 | tf_op jit(solution)/shard_map/all_to_all | solution.py:451
  87.5 2.0 %shares.1 = (bf16[16,4,16,128]{3,2,1,0:T(8,128)(2,1)S(1)}, bf16[16,4,16,128]{3,2,1,0:T(8,128)(2,1)S(1)}, bf16[32,64,128]{2,1,0:T(8,128)(2,1)S(1)}, f32[64,128]{1,0:T(8,128)S(1)}) custom-call(s32[4]{0:T(128)S(1)} %pad_add_fusion.core_ref.place_ref, s32[32]{0:T(128)S(1)} %copy-done.6, f32[16,64,128]{2,1,0:T(8,128)S(1)} %all_to_all.5.stats_ref, ...), custom_call_target="tpu_custom_call" | custom-call | flops 67108864 | bytes 12582912 | tf_op jit(solution)/shard_map/shares/pallas_call | solution.py:457
  89.5 2.0 %collective-permute-start.16 = (bf16[16,4,16,128]{3,2,1,0:T(8,128)(2,1)S(1)}, bf16[16,4,16,128]{3,2,1,0:T(8,128)(2,1)S(1)}, u32[]{:S(2)}, u32[]{:S(2)}) collective-permute-start(bf16[16,4,16,128]{3,2,1,0:T(8,128)(2,1)S(1)} %get-tuple-element.67), channel_id=1, source_target_pairs={{0,1},{1,2},{2,3},{3,4},{4,5},{5,6},{6,7},{7,0},{8,9},{9,10},{10,1... | collective-permute-start | bytes 786440 | tf_op jit(solution)/shard_map/ppermute | solution.py:470
  91.6 2.1 %counts.1 = (bf16[32,4,16,128]{3,2,1,0:T(8,128)(2,1)S(1)}, bf16[32,4,16,128]{3,2,1,0:T(8,128)(2,1)S(1)}, bf16[32,4,16,128]{3,2,1,0:T(8,128)(2,1)S(1)}, bf16[32,4...) custom-call(s32[4]{0:T(128)S(1)} %pad_add_fusion.core_ref.place_ref,, ...), custom_call_target="tpu_custom_call" | custom-call | flops 1048576 | bytes 1048576 | tf_op jit(solution)/shard_map/counts/pallas_call | solution.py:473
  93.7 2.4 %collective-permute-done.16.up_in_ref = bf16[16,4,16,128]{3,2,1,0:T(8,128)(2,1)S(1)} collective-permute-done((bf16[16,4,16,128]{3,2,1,0:T(8,128)(2,1)S(1)}, bf16[16,4,16,128]{3,2,1,0:T(8,128)(2,1)S(1)}, u32[]{:S(2)}, u32[]{:S(2)}) %collective-permute-start.16) | collective-permute-done | bytes 262176 | tf_op jit(solution)/shard_map/ppermute | solution.py:470
  96.1 1.8 %collective-permute-done.17.down_in_ref = bf16[16,4,16,128]{3,2,1,0:T(8,128)(2,1)S(1)} collective-permute-done((bf16[16,4,16,128]{3,2,1,0:T(8,128)(2,1)S(1)}, bf16[16,4,16,128]{3,2,1,0:T(8,128)(2,1)S(1)}, u32[]{:S(2)}, u32[]{:S(2)}) %collective-permute-start.17) | collective-permute-done | bytes 262176 | tf_op jit(solution)/shard_map/ppermute | solution.py:470
  98.0 3.2 %collective-permute-start.18 = (bf16[32,4,16,128]{3,2,1,0:T(8,128)(2,1)S(1)}, bf16[32,4,16,128]{3,2,1,0:T(8,128)(2,1)S(1)}, u32[]{:S(2)}, u32[]{:S(2)}) collective-permute-start(bf16[32,4,16,128]{3,2,1,0:T(8,128)(2,1)S(1)} %get-tuple-element.69), channel_id=1, source_target_pairs={{0,1},{1,2},{2,3},{3,4},{4,5},{5,6},{6,7},{7,0},{8,9},{9,10},{10,1... | collective-permute-start | bytes 1572872 | tf_op jit(solution)/shard_map/ppermute | solution.py:470
  101.2 9.0 %collective-permute-done.18.up_in_ref = bf16[32,4,16,128]{3,2,1,0:T(8,128)(2,1)S(1)} collective-permute-done((bf16[32,4,16,128]{3,2,1,0:T(8,128)(2,1)S(1)}, bf16[32,4,16,128]{3,2,1,0:T(8,128)(2,1)S(1)}, u32[]{:S(2)}, u32[]{:S(2)}) %collective-permute-start.18) | collective-permute-done | bytes 524320 | tf_op jit(solution)/shard_map/ppermute | solution.py:470
  110.2 2.8 %collective-permute-done.19.down_in_ref = bf16[32,4,16,128]{3,2,1,0:T(8,128)(2,1)S(1)} collective-permute-done((bf16[32,4,16,128]{3,2,1,0:T(8,128)(2,1)S(1)}, bf16[32,4,16,128]{3,2,1,0:T(8,128)(2,1)S(1)}, u32[]{:S(2)}, u32[]{:S(2)}) %collective-permute-start.19) | collective-permute-done | bytes 524320 | tf_op jit(solution)/shard_map/ppermute | solution.py:470
  113.2 1.8 %collective-permute-start.20 = (bf16[32,4,16,128]{3,2,1,0:T(8,128)(2,1)S(1)}, bf16[32,4,16,128]{3,2,1,0:T(8,128)(2,1)S(1)}, u32[]{:S(2)}, u32[]{:S(2)}) collective-permute-start(bf16[32,4,16,128]{3,2,1,0:T(8,128)(2,1)S(1)} %get-tuple-element.71), channel_id=1, source_target_pairs={{0,1},{1,2},{2,3},{3,4},{4,5},{5,6},{6,7},{7,0},{8,9},{9,10},{10,1... | collective-permute-start | bytes 1572872 | tf_op jit(solution)/shard_map/ppermute | solution.py:470
  115.3 8.4 %collective-permute-done.20.up_in_ref = bf16[32,4,16,128]{3,2,1,0:T(8,128)(2,1)S(1)} collective-permute-done((bf16[32,4,16,128]{3,2,1,0:T(8,128)(2,1)S(1)}, bf16[32,4,16,128]{3,2,1,0:T(8,128)(2,1)S(1)}, u32[]{:S(2)}, u32[]{:S(2)}) %collective-permute-start.20) | collective-permute-done | bytes 524320 | tf_op jit(solution)/shard_map/ppermute | solution.py:470
  123.7 0.9 collective-permute-done.21.down_in_ref
  124.9 1.8 %collective-permute-start.22 = (bf16[32,4,16,128]{3,2,1,0:T(8,128)(2,1)S(1)}, bf16[32,4,16,128]{3,2,1,0:T(8,128)(2,1)S(1)}, u32[]{:S(2)}, u32[]{:S(2)}) collective-permute-start(bf16[32,4,16,128]{3,2,1,0:T(8,128)(2,1)S(1)} %get-tuple-element.73), channel_id=1, source_target_pairs={{0,1},{1,2},{2,3},{3,4},{4,5},{5,6},{6,7},{7,0},{8,9},{9,10},{10,1... | collective-permute-start | bytes 1572872 | tf_op jit(solution)/shard_map/ppermute | solution.py:470
  127.0 0.6 slice_reduce_fusion
  127.6 6.6 %collective-permute-done.22.up_in_ref = bf16[32,4,16,128]{3,2,1,0:T(8,128)(2,1)S(1)} collective-permute-done((bf16[32,4,16,128]{3,2,1,0:T(8,128)(2,1)S(1)}, bf16[32,4,16,128]{3,2,1,0:T(8,128)(2,1)S(1)}, u32[]{:S(2)}, u32[]{:S(2)}) %collective-permute-start.22) | collective-permute-done | bytes 524320 | tf_op jit(solution)/shard_map/ppermute | solution.py:470
  134.2 1.8 %collective-permute-done.23.down_in_ref = bf16[32,4,16,128]{3,2,1,0:T(8,128)(2,1)S(1)} collective-permute-done((bf16[32,4,16,128]{3,2,1,0:T(8,128)(2,1)S(1)}, bf16[32,4,16,128]{3,2,1,0:T(8,128)(2,1)S(1)}, u32[]{:S(2)}, u32[]{:S(2)}) %collective-permute-start.23) | collective-permute-done | bytes 524320 | tf_op jit(solution)/shard_map/ppermute | solution.py:470
  136.1 1.5 %ring_last.1 = bf16[32,4,16,128]{3,2,1,0:T(8,128)(2,1)} custom-call(s32[4]{0:T(128)S(1)} %pad_add_fusion.core_ref.place_ref, bf16[32,4,16,128]{3,2,1,0:T(8,128)(2,1)S(1)} %get-tuple-element.60.own_ref, bf16[32,4,16,128]{3,2,1,0:T(8,128)(2,1)S(1)} %collective-permute-done.22.up_in_ref, bf16[32,4,16,128]{3,2,1,0:T(8,128)(2,1)S(1)} %collective-permute-done.23.down_in_ref), custom_call_target="tpu_custom_call" | custom-call | tf_op jit(solution)/shard_map/ring_last/pallas_call | solution.py:498
  (48 shorter events, 3.5 us)
Async XLA Ops:
  0.6 1.6 %copy-start.1 = (bf16[32,256,128]{2,1,0:T(8,128)(2,1)S(1)}, bf16[32,256,128]{2,1,0:T(8,128)(2,1)}, u32[]{:S(2)}) copy-start(bf16[32,256,128]{2,1,0:T(8,128)(2,1)} %table_ref.4) | copy-start | bytes 6291460
  2.2 0.7 copy-start.3
  2.9 1.3 copy-start.7
  3.0 1.9 %copy-start.2 = (bf16[32,256,128]{2,1,0:T(8,128)(2,1)S(1)}, bf16[32,256,128]{2,1,0:T(8,128)(2,1)}, u32[]{:S(2)}) copy-start(bf16[32,256,128]{2,1,0:T(8,128)(2,1)} %table_ref.4) | copy-start | bytes 6291460
  3.0 1.9 %copy-start.4 = (s32[64,32]{0,1:T(8,128)S(1)}, s32[64,32]{0,1:T(8,128)}, u32[]{:S(2)}) copy-start(s32[64,32]{0,1:T(8,128)} %param.8) | copy-start | bytes 24580
  4.2 1.9 %collective-permute-start = (bf16[17,64,128]{2,1,0:T(8,128)(2,1)S(1)}, bf16[17,64,128]{2,1,0:T(8,128)(2,1)S(1)}, u32[]{:S(2)}, u32[]{:S(2)}) collective-permute-start(bf16[17,64,128]{2,1,0:T(8,128)(2,1)S(1)} %child_scores.2), channel_id=1, source_target_pairs={{0,8},{8,0},{16,24},{24,16},{32,40},{40,32},{48,56},{56,48},{64,72... | collective-permute-start | bytes 835592 | tf_op jit(solution)/shard_map/ppermute | solution.py:366
  4.3 1.8 %collective-permute-start.1 = (s32[4,32]{1,0:T(4,128)S(1)}, s32[4,32]{1,0:T(4,128)S(1)}, u32[]{:S(2)}, u32[]{:S(2)}) collective-permute-start(s32[4,32]{1,0:T(4,128)S(1)} %bitcast.20), channel_id=1, source_target_pairs={{0,8},{8,0},{16,24},{24,16},{32,40},{40,32},{48,56},{56,48},{64,72... | collective-permute-start | bytes 1544 | tf_op jit(solution)/shard_map/ppermute | solution.py:366
  6.7 10.6 %collective-permute-start.2 = (bf16[33,64,128]{2,1,0:T(8,128)(2,1)S(1)}, bf16[33,64,128]{2,1,0:T(8,128)(2,1)S(1)}, u32[]{:S(2)}, u32[]{:S(2)}) collective-permute-start(bf16[33,64,128]{2,1,0:T(8,128)(2,1)S(1)} %pack.1), channel_id=1, source_target_pairs={{0,64},{8,24},{16,80},{24,40},{32,96},{40,56},{48,112},{56,8},{64,... | collective-permute-start | bytes 1622024 | tf_op jit(solution)/shard_map/ppermute | solution.py:379
  8.3 9.4 %collective-permute-start.3 = (bf16[33,64,128]{2,1,0:T(8,128)(2,1)S(1)}, bf16[33,64,128]{2,1,0:T(8,128)(2,1)S(1)}, u32[]{:S(2)}, u32[]{:S(2)}) collective-permute-start(bf16[33,64,128]{2,1,0:T(8,128)(2,1)S(1)} %pack.1), channel_id=1, source_target_pairs={{0,192},{8,56},{16,208},{24,8},{32,224},{40,24},{48,240},{56,40},{... | collective-permute-start | bytes 1622024 | tf_op jit(solution)/shard_map/ppermute | solution.py:379
  17.7 10.2 %collective-permute-start.4 = (bf16[17,64,128]{2,1,0:T(8,128)(2,1)S(1)}, bf16[17,64,128]{2,1,0:T(8,128)(2,1)S(1)}, u32[]{:S(2)}, u32[]{:S(2)}) collective-permute-start(bf16[17,64,128]{2,1,0:T(8,128)(2,1)S(1)} %slice.21), channel_id=1, source_target_pairs={{0,64},{8,24},{16,80},{24,40},{32,96},{40,56},{48,112},{56,8},{64,... | collective-permute-start | bytes 835592 | tf_op jit(solution)/shard_map/ppermute | solution.py:379
  19.2 8.6 %collective-permute-start.5 = (bf16[16,64,128]{2,1,0:T(8,128)(2,1)S(1)}, bf16[16,64,128]{2,1,0:T(8,128)(2,1)S(1)}, u32[]{:S(2)}, u32[]{:S(2)}) collective-permute-start(bf16[16,64,128]{2,1,0:T(8,128)(2,1)S(1)} %slice.22), channel_id=1, source_target_pairs={{0,192},{8,56},{16,208},{24,8},{32,224},{40,24},{48,240},{56,40},{... | collective-permute-start | bytes 786440 | tf_op jit(solution)/shard_map/ppermute | solution.py:379
  21.2 16.4 %collective-permute-start.6 = (bf16[66,64,128]{2,1,0:T(8,128)(2,1)S(1)}, bf16[66,64,128]{2,1,0:T(8,128)(2,1)S(1)}, u32[]{:S(2)}, u32[]{:S(2)}) collective-permute-start(bf16[66,64,128]{2,1,0:T(8,128)(2,1)S(1)} %pad_maximum_fusion.refs_0_), channel_id=1, source_target_pairs={{0,16},{8,72},{16,32},{24,88},{32,48},{40,104},{48,0},{56,120},{64... | collective-permute-start | bytes 3244040 | tf_op jit(solution)/shard_map/ppermute | solution.py:379
  22.8 15.2 %collective-permute-start.7 = (bf16[66,64,128]{2,1,0:T(8,128)(2,1)S(1)}, bf16[66,64,128]{2,1,0:T(8,128)(2,1)S(1)}, u32[]{:S(2)}, u32[]{:S(2)}) collective-permute-start(bf16[66,64,128]{2,1,0:T(8,128)(2,1)S(1)} %pad_maximum_fusion.refs_0_), channel_id=1, source_target_pairs={{0,48},{8,200},{16,0},{24,216},{32,16},{40,232},{48,32},{56,248},{... | collective-permute-start | bytes 3244040 | tf_op jit(solution)/shard_map/ppermute | solution.py:379
  28.0 21.2 %collective-permute-start.8 = (bf16[66,64,128]{2,1,0:T(8,128)(2,1)S(1)}, bf16[66,64,128]{2,1,0:T(8,128)(2,1)S(1)}, u32[]{:S(2)}, u32[]{:S(2)}) collective-permute-start(bf16[66,64,128]{2,1,0:T(8,128)(2,1)S(1)} %constant_dynamic-update-slice_fusion.refs_1_), channel_id=1, source_target_pairs={{0,16},{8,72},{16,32},{24,88},{32,48},{40,104},{48,0},{56,120},{64... | collective-permute-start | bytes 3244040 | tf_op jit(solution)/shard_map/ppermute | solution.py:379
  30.2 19.3 %collective-permute-start.9 = (bf16[66,64,128]{2,1,0:T(8,128)(2,1)S(1)}, bf16[66,64,128]{2,1,0:T(8,128)(2,1)S(1)}, u32[]{:S(2)}, u32[]{:S(2)}) collective-permute-start(bf16[66,64,128]{2,1,0:T(8,128)(2,1)S(1)} %constant_dynamic-update-slice_fusion.refs_1_), channel_id=1, source_target_pairs={{0,48},{8,200},{16,0},{24,216},{32,16},{40,232},{48,32},{56,248},{... | collective-permute-start | bytes 3244040 | tf_op jit(solution)/shard_map/ppermute | solution.py:379
  38.0 17.0 %collective-permute-start.10 = (bf16[33,64,128]{2,1,0:T(8,128)(2,1)S(1)}, bf16[33,64,128]{2,1,0:T(8,128)(2,1)S(1)}, u32[]{:S(2)}, u32[]{:S(2)}) collective-permute-start(bf16[33,64,128]{2,1,0:T(8,128)(2,1)S(1)} %slice.23), channel_id=1, source_target_pairs={{0,16},{8,72},{16,32},{24,88},{32,48},{40,104},{48,0},{56,120},{64... | collective-permute-start | bytes 1622024 | tf_op jit(solution)/shard_map/ppermute | solution.py:379
  39.7 15.6 %collective-permute-start.11 = (bf16[33,64,128]{2,1,0:T(8,128)(2,1)S(1)}, bf16[33,64,128]{2,1,0:T(8,128)(2,1)S(1)}, u32[]{:S(2)}, u32[]{:S(2)}) collective-permute-start(bf16[33,64,128]{2,1,0:T(8,128)(2,1)S(1)} %slice.24), channel_id=1, source_target_pairs={{0,48},{8,200},{16,0},{24,216},{32,16},{40,232},{48,32},{56,248},{... | collective-permute-start | bytes 1622024 | tf_op jit(solution)/shard_map/ppermute | solution.py:379
  49.6 11.2 %collective-permute-start.12 = (bf16[33,64,128]{2,1,0:T(8,128)(2,1)S(1)}, bf16[33,64,128]{2,1,0:T(8,128)(2,1)S(1)}, u32[]{:S(2)}, u32[]{:S(2)}) collective-permute-start(bf16[33,64,128]{2,1,0:T(8,128)(2,1)S(1)} %slice.25), channel_id=1, source_target_pairs={{0,16},{8,72},{16,32},{24,88},{32,48},{40,104},{48,0},{56,120},{64... | collective-permute-start | bytes 1622024 | tf_op jit(solution)/shard_map/ppermute | solution.py:379
  51.5 11.9 %copy-start.5 = (f32[32,128]{1,0:T(8,128)S(1)}, f32[32,128]{1,0:T(8,128)}, u32[]{:S(2)}) copy-start(f32[32,128]{1,0:T(8,128)} %prior_ref.3) | copy-start | bytes 49156
  51.5 11.9 %copy-start.8 = (bf16[32,256,128]{2,1,0:T(8,128)(2,1)S(1)}, bf16[32,256,128]{2,1,0:T(8,128)(2,1)}, u32[]{:S(2)}) copy-start(bf16[32,256,128]{2,1,0:T(8,128)(2,1)} %table_ref.5) | copy-start | bytes 6291460
  51.5 11.9 %copy-start.9 = (s32[64,32]{0,1:T(8,128)S(1)}, s32[64,32]{0,1:T(8,128)}, u32[]{:S(2)}) copy-start(s32[64,32]{0,1:T(8,128)} %param.9) | copy-start | bytes 24580
  51.5 9.6 %collective-permute-start.13 = (bf16[33,64,128]{2,1,0:T(8,128)(2,1)S(1)}, bf16[33,64,128]{2,1,0:T(8,128)(2,1)S(1)}, u32[]{:S(2)}, u32[]{:S(2)}) collective-permute-start(bf16[33,64,128]{2,1,0:T(8,128)(2,1)S(1)} %slice.26), channel_id=1, source_target_pairs={{0,48},{8,200},{16,0},{24,216},{32,16},{40,232},{48,32},{56,248},{... | collective-permute-start | bytes 1622024 | tf_op jit(solution)/shard_map/ppermute | solution.py:379
  61.1 3.7 %copy-start = (bf16[32,1,4,128,128]{4,3,2,1,0:T(8,128)(2,1)S(1)}, bf16[32,1,4,128,128]{4,3,2,1,0:T(8,128)(2,1)}, u32[]{:S(2)}) copy-start(bf16[32,1,4,128,128]{4,3,2,1,0:T(8,128)(2,1)} %param.13) | copy-start | bytes 12582916
  63.2 3.3 %collective-permute-start.14 = (bf16[65,64,128]{2,1,0:T(8,128)(2,1)S(1)}, bf16[65,64,128]{2,1,0:T(8,128)(2,1)S(1)}, u32[]{:S(2)}, u32[]{:S(2)}) collective-permute-start(bf16[65,64,128]{2,1,0:T(8,128)(2,1)S(1)} %get-tuple-element.50), channel_id=1, source_target_pairs={{0,8},{8,0},{16,24},{24,16},{32,40},{40,32},{48,56},{56,48},{64,72... | collective-permute-start | bytes 3194888 | tf_op jit(solution)/shard_map/ppermute | solution.py:416
  63.4 1.5 %copy-start.6 = (s32[32]{0:T(128)S(1)}, s32[32]{0:T(128)}, u32[]{:S(2)}) copy-start(s32[32]{0:T(128)} %map_ref.5) | copy-start | bytes 388
  68.6 1.4 %collective-permute-start.15 = (f32[64,128]{1,0:T(8,128)S(1)}, f32[64,128]{1,0:T(8,128)S(1)}, u32[]{:S(2)}, u32[]{:S(2)}) collective-permute-start(f32[64,128]{1,0:T(8,128)S(1)} %get-tuple-element.54.refs_0_), channel_id=1, source_target_pairs={{0,8},{8,0},{16,24},{24,16},{32,40},{40,32},{48,56},{56,48},{64,72... | collective-permute-start | bytes 98312 | tf_op jit(solution)/shard_map/ppermute | solution.py:448
  89.5 6.6 %collective-permute-start.16 = (bf16[16,4,16,128]{3,2,1,0:T(8,128)(2,1)S(1)}, bf16[16,4,16,128]{3,2,1,0:T(8,128)(2,1)S(1)}, u32[]{:S(2)}, u32[]{:S(2)}) collective-permute-start(bf16[16,4,16,128]{3,2,1,0:T(8,128)(2,1)S(1)} %get-tuple-element.67), channel_id=1, source_target_pairs={{0,1},{1,2},{2,3},{3,4},{4,5},{5,6},{6,7},{7,0},{8,9},{9,10},{10,1... | collective-permute-start | bytes 786440 | tf_op jit(solution)/shard_map/ppermute | solution.py:470
  91.5 6.4 %collective-permute-start.17 = (bf16[16,4,16,128]{3,2,1,0:T(8,128)(2,1)S(1)}, bf16[16,4,16,128]{3,2,1,0:T(8,128)(2,1)S(1)}, u32[]{:S(2)}, u32[]{:S(2)}) collective-permute-start(bf16[16,4,16,128]{3,2,1,0:T(8,128)(2,1)S(1)} %get-tuple-element.68), channel_id=1, source_target_pairs={{0,7},{1,0},{2,1},{3,2},{4,3},{5,4},{6,5},{7,6},{8,15},{9,8},{10,9... | collective-permute-start | bytes 786440 | tf_op jit(solution)/shard_map/ppermute | solution.py:470
  98.0 12.2 %collective-permute-start.18 = (bf16[32,4,16,128]{3,2,1,0:T(8,128)(2,1)S(1)}, bf16[32,4,16,128]{3,2,1,0:T(8,128)(2,1)S(1)}, u32[]{:S(2)}, u32[]{:S(2)}) collective-permute-start(bf16[32,4,16,128]{3,2,1,0:T(8,128)(2,1)S(1)} %get-tuple-element.69), channel_id=1, source_target_pairs={{0,1},{1,2},{2,3},{3,4},{4,5},{5,6},{6,7},{7,0},{8,9},{9,10},{10,1... | collective-permute-start | bytes 1572872 | tf_op jit(solution)/shard_map/ppermute | solution.py:470
  101.2 11.8 %collective-permute-start.19 = (bf16[32,4,16,128]{3,2,1,0:T(8,128)(2,1)S(1)}, bf16[32,4,16,128]{3,2,1,0:T(8,128)(2,1)S(1)}, u32[]{:S(2)}, u32[]{:S(2)}) collective-permute-start(bf16[32,4,16,128]{3,2,1,0:T(8,128)(2,1)S(1)} %get-tuple-element.70), channel_id=1, source_target_pairs={{0,7},{1,0},{2,1},{3,2},{4,3},{5,4},{6,5},{7,6},{8,15},{9,8},{10,9... | collective-permute-start | bytes 1572872 | tf_op jit(solution)/shard_map/ppermute | solution.py:470
  113.2 10.5 %collective-permute-start.20 = (bf16[32,4,16,128]{3,2,1,0:T(8,128)(2,1)S(1)}, bf16[32,4,16,128]{3,2,1,0:T(8,128)(2,1)S(1)}, u32[]{:S(2)}, u32[]{:S(2)}) collective-permute-start(bf16[32,4,16,128]{3,2,1,0:T(8,128)(2,1)S(1)} %get-tuple-element.71), channel_id=1, source_target_pairs={{0,1},{1,2},{2,3},{3,4},{4,5},{5,6},{6,7},{7,0},{8,9},{9,10},{10,1... | collective-permute-start | bytes 1572872 | tf_op jit(solution)/shard_map/ppermute | solution.py:470
  115.0 9.6 %collective-permute-start.21 = (bf16[32,4,16,128]{3,2,1,0:T(8,128)(2,1)S(1)}, bf16[32,4,16,128]{3,2,1,0:T(8,128)(2,1)S(1)}, u32[]{:S(2)}, u32[]{:S(2)}) collective-permute-start(bf16[32,4,16,128]{3,2,1,0:T(8,128)(2,1)S(1)} %get-tuple-element.72), channel_id=1, source_target_pairs={{0,7},{1,0},{2,1},{3,2},{4,3},{5,4},{6,5},{7,6},{8,15},{9,8},{10,9... | collective-permute-start | bytes 1572872 | tf_op jit(solution)/shard_map/ppermute | solution.py:470
  124.9 9.3 %collective-permute-start.22 = (bf16[32,4,16,128]{3,2,1,0:T(8,128)(2,1)S(1)}, bf16[32,4,16,128]{3,2,1,0:T(8,128)(2,1)S(1)}, u32[]{:S(2)}, u32[]{:S(2)}) collective-permute-start(bf16[32,4,16,128]{3,2,1,0:T(8,128)(2,1)S(1)} %get-tuple-element.73), channel_id=1, source_target_pairs={{0,1},{1,2},{2,3},{3,4},{4,5},{5,6},{6,7},{7,0},{8,9},{9,10},{10,1... | collective-permute-start | bytes 1572872 | tf_op jit(solution)/shard_map/ppermute | solution.py:470
  126.7 9.4 %collective-permute-start.23 = (bf16[32,4,16,128]{3,2,1,0:T(8,128)(2,1)S(1)}, bf16[32,4,16,128]{3,2,1,0:T(8,128)(2,1)S(1)}, u32[]{:S(2)}, u32[]{:S(2)}) collective-permute-start(bf16[32,4,16,128]{3,2,1,0:T(8,128)(2,1)S(1)} %get-tuple-element.74), channel_id=1, source_target_pairs={{0,7},{1,0},{2,1},{3,2},{4,3},{5,4},{6,5},{7,6},{8,15},{9,8},{10,9... | collective-permute-start | bytes 1572872 | tf_op jit(solution)/shard_map/ppermute | solution.py:470

commit v9 on v8

--- a/solution.py
+++ b/solution.py
@@ -19,7 +19,7 @@
 PIECE = 2 * HALF + 1
 VMEM = pl.BlockSpec(memory_space=pltpu.VMEM)
 SMEM = pl.BlockSpec(memory_space=pltpu.SMEM)
-ANY = pl.BlockSpec(memory_space=pl.ANY)
+HBM = pl.BlockSpec(memory_space=pltpu.HBM)
 
 
 def lane_of(shape):
@@ -35,12 +35,11 @@
     return looked - log_norm
 
 
-def child_kernel(half_ref, values_ref, table_ref, out_ref, inputs):
-    half = half_ref[0]
-    values = values_ref[...].T
+def child_scores(half, values, table_of, out_ref, inputs):
+    values = values.T
     values = jnp.where(half == 0, values[:, :HALF], values[:, HALF:])
     for k in range(HALF):
-        inputs[k] = look_up(values[:, k : k + 1], table_ref[half * HALF + k])
+        inputs[k] = look_up(values[:, k : k + 1], table_of(k))
     powers = jnp.zeros((S_LOC, BLK), jnp.float32)
     lanes = lane_of((S_LOC, BLK))
     for k in range(HALF):
@@ -50,6 +49,31 @@
     powers = powers.astype(jnp.float32) * LN2
     for k in range(HALF):
         out_ref[k] = jnp.exp(inputs[k] - powers[:, k : k + 1]).astype(jnp.bfloat16)
+
+
+def child_kernel(half_ref, values_ref, table_ref, out_ref, inputs):
+    half = half_ref[0]
+    child_scores(half, values_ref[...], lambda k: table_ref[half * HALF + k], out_ref, inputs)
+
+
+def first_child_kernel(half_ref, values_ref, table_ref, out_ref, inputs, values, table, sems):
+    half = half_ref[0]
+    chunks = sems.shape[0] - 1
+    size = HALF // chunks
+    copies = [pltpu.make_async_copy(values_ref, values, sems.at[chunks])]
+    for n in range(chunks):
+        source = table_ref.at[pl.ds(half * HALF + n * size, size)]
+        copies.append(pltpu.make_async_copy(source, table.at[pl.ds(n * size, size)], sems.at[n]))
+    for copy in copies:
+        copy.start()
+    copies[0].wait()
+
+    def table_of(k):
+        if k % size == 0:
+            copies[1 + k // size].wait()
+        return table[k]
+
+    child_scores(half, values[...], table_of, out_ref, inputs)
 
 
 def pack_kernel(core_ref, own_ref, other_ref, out_ref):
@@ -350,22 +374,28 @@
 
     columns = block_cols[:, 0].T
 
-    def scores(half):
+    def scores(kernel, half, in_space, more_scratch, mib):
         return pl.pallas_call(
-            child_kernel,
+            kernel,
             out_shape=shape((HALF + 1, S_LOC, BLK), bf16),
-            in_specs=[SMEM, VMEM, VMEM],
+            in_specs=[SMEM, in_space, in_space],
             out_specs=VMEM,
-            scratch_shapes=[pltpu.VMEM((HALF, S_LOC, BLK), f32)],
-            compiler_params=params(16),
+            scratch_shapes=[pltpu.VMEM((HALF, S_LOC, BLK), f32)] + more_scratch,
+            compiler_params=params(mib),
             cost_estimate=cost(1 << 27, 2 << 20, 1 << 20),
             name="child_scores",
         )(half.reshape(1), child_values.T, child_logits)
 
+    fetched = [
+        pltpu.VMEM((C, S_LOC), i32),
+        pltpu.VMEM((HALF,) + child_logits.shape[1:], bf16),
+        pltpu.SemaphoreType.DMA((5,)),
+    ]
+    given = scores(first_child_kernel, 1 - core, HBM, fetched, 56)
     given, other_columns = lax.optimization_barrier(
-        (lax.ppermute(scores(1 - core), "region", SWAP), lax.ppermute(columns, "region", SWAP))
-    )
-    kept = scores(core)
+        (lax.ppermute(given, "region", SWAP), lax.ppermute(columns, "region", SWAP))
+    )
+    kept = scores(child_kernel, core, VMEM, [], 16)
     own = pl.pallas_call(
         pack_kernel,
         out_shape=shape((PIECE, S_LOC, BLK), bf16),

time: 140 us -> 140 us (level)
  local copies, waits for them, and re-layouts: 3.3 us -> 1 us
  Pallas kernels: 16.7 us -> 18.7 us
    unnamed x22 -> x18, local copies, waits for them, and re-layouts: 2.41 us -> 0.11 us
    pallas_call x2, Pallas kernels: 2.45 us -> 4.45 us  [scores(): pl.pallas_call(kernel, out_shape=shape((HALF + 1, S_LOC, BLK), bf16), in_...]
where the time goes in v9:
time: 140 us; the launch traced here: 137 us
  waiting for transfers between devices  67.8 us (48%)
  starting transfers between devices  31.4 us (22%)
  Pallas kernels  18.7 us (13%)
  blocking collectives  17.3 us (12%)
    ppermute x12, waiting for transfers between devices, send(): return lax.ppermute(value, 'region', along(a, b))  33.2 us
    ppermute x4, waiting for transfers between devices, ring(): lax.ppermute(up, 'batch', shift(1))  26.4 us
    ppermute x12, starting transfers between devices, send(): return lax.ppermute(value, 'region', along(a, b))  20.7 us
    all_to_all x1, blocking collectives, body(): lax.all_to_all(jnp.broadcast_to(stats[None], (16, S_LOC, BLK)), 'region',...  17.3 us
    ppermute x4, starting transfers between devices, ring(): lax.ppermute(up, 'batch', shift(1))  8.82 us
    ppermute x4, waiting for transfers between devices, ring(): lax.ppermute(down, 'batch', shift(-1))  7.32 us
    pallas_call x2, Pallas kernels, scores(): pl.pallas_call(kernel, out_shape=shape((HALF + 1, S_LOC, BLK), bf16), in_...  4.45 us
  transfers between devices with their start and end apart: 24, of which 20 were waited for; matrix products, arithmetic and copies ran while one was open for 1% of the time, Pallas kernels for 5%

profile of v9, /device:TPU:32, one launch (start us, length us, event | category | flops | bytes accessed | tf_op | source)
XLA Modules:
  0.0 137.3 jit_solution(14513031051694868452)
XLA Ops:
  0.7 3.2 %child_scores.2 = bf16[17,64,128]{2,1,0:T(8,128)(2,1)} custom-call(s32[1]{0:T(128)} %bitcast.4.half_ref, s32[32,64]{1,0:T(8,128)} %bitcast.18, bf16[32,256,128]{2,1,0:T(8,128)(2,1)} %table_ref.4), custom_call_target="tpu_custom_call" | custom-call | flops 134217728 | bytes 2097152 | tf_op jit(solution)/shard_map/child_scores/pallas_call | solution.py:378
  4.0 0.5 collective-permute-start.1
  4.6 1.2 child_scores.3.own_ref
  5.8 0.6 pack.1
  6.5 1.5 %collective-permute-start.2 = (bf16[33,64,128]{2,1,0:T(8,128)(2,1)S(1)}, bf16[33,64,128]{2,1,0:T(8,128)(2,1)S(1)}, u32[]{:S(2)}, u32[]{:S(2)}) collective-permute-start(bf16[33,64,128]{2,1,0:T(8,128)(2,1)S(1)} %pack.1), channel_id=1, source_target_pairs={{0,64},{8,24},{16,80},{24,40},{32,96},{40,56},{48,112},{56,8},{64,... | collective-permute-start | bytes 1622024 | tf_op jit(solution)/shard_map/ppermute | solution.py:409
  8.0 1.7 %collective-permute-start.3 = (bf16[33,64,128]{2,1,0:T(8,128)(2,1)S(1)}, bf16[33,64,128]{2,1,0:T(8,128)(2,1)S(1)}, u32[]{:S(2)}, u32[]{:S(2)}) collective-permute-start(bf16[33,64,128]{2,1,0:T(8,128)(2,1)S(1)} %pack.1), channel_id=1, source_target_pairs={{0,192},{8,56},{16,208},{24,8},{32,224},{40,24},{48,240},{56,40},{... | collective-permute-start | bytes 1622024 | tf_op jit(solution)/shard_map/ppermute | solution.py:409
  9.7 7.3 %collective-permute-done.2 = bf16[33,64,128]{2,1,0:T(8,128)(2,1)S(1)} collective-permute-done((bf16[33,64,128]{2,1,0:T(8,128)(2,1)S(1)}, bf16[33,64,128]{2,1,0:T(8,128)(2,1)S(1)}, u32[]{:S(2)}, u32[]{:S(2)}) %collective-permute-start.2) | collective-permute-done | bytes 540704 | tf_op jit(solution)/shard_map/ppermute | solution.py:409
  17.4 1.6 %collective-permute-start.4 = (bf16[17,64,128]{2,1,0:T(8,128)(2,1)S(1)}, bf16[17,64,128]{2,1,0:T(8,128)(2,1)S(1)}, u32[]{:S(2)}, u32[]{:S(2)}) collective-permute-start(bf16[17,64,128]{2,1,0:T(8,128)(2,1)S(1)} %slice.21), channel_id=1, source_target_pairs={{0,64},{8,24},{16,80},{24,40},{32,96},{40,56},{48,112},{56,8},{64,... | collective-permute-start | bytes 835592 | tf_op jit(solution)/shard_map/ppermute | solution.py:409
  19.0 1.8 %collective-permute-start.5 = (bf16[16,64,128]{2,1,0:T(8,128)(2,1)S(1)}, bf16[16,64,128]{2,1,0:T(8,128)(2,1)S(1)}, u32[]{:S(2)}, u32[]{:S(2)}) collective-permute-start(bf16[16,64,128]{2,1,0:T(8,128)(2,1)S(1)} %slice.22), channel_id=1, source_target_pairs={{0,192},{8,56},{16,208},{24,8},{32,224},{40,24},{48,240},{56,40},{... | collective-permute-start | bytes 786440 | tf_op jit(solution)/shard_map/ppermute | solution.py:409
  20.9 1.7 %collective-permute-start.6 = (bf16[66,64,128]{2,1,0:T(8,128)(2,1)S(1)}, bf16[66,64,128]{2,1,0:T(8,128)(2,1)S(1)}, u32[]{:S(2)}, u32[]{:S(2)}) collective-permute-start(bf16[66,64,128]{2,1,0:T(8,128)(2,1)S(1)} %pad_maximum_fusion.refs_0_), channel_id=1, source_target_pairs={{0,16},{8,72},{16,32},{24,88},{32,48},{40,104},{48,0},{56,120},{64... | collective-permute-start | bytes 3244040 | tf_op jit(solution)/shard_map/ppermute | solution.py:409
  22.5 1.7 %collective-permute-start.7 = (bf16[66,64,128]{2,1,0:T(8,128)(2,1)S(1)}, bf16[66,64,128]{2,1,0:T(8,128)(2,1)S(1)}, u32[]{:S(2)}, u32[]{:S(2)}) collective-permute-start(bf16[66,64,128]{2,1,0:T(8,128)(2,1)S(1)} %pad_maximum_fusion.refs_0_), channel_id=1, source_target_pairs={{0,48},{8,200},{16,0},{24,216},{32,16},{40,232},{48,32},{56,248},{... | collective-permute-start | bytes 3244040 | tf_op jit(solution)/shard_map/ppermute | solution.py:409
  24.2 3.4 %collective-permute-done.5 = bf16[16,64,128]{2,1,0:T(8,128)(2,1)S(1)} collective-permute-done((bf16[16,64,128]{2,1,0:T(8,128)(2,1)S(1)}, bf16[16,64,128]{2,1,0:T(8,128)(2,1)S(1)}, u32[]{:S(2)}, u32[]{:S(2)}) %collective-permute-start.5) | collective-permute-done | bytes 262176 | tf_op jit(solution)/shard_map/ppermute | solution.py:409
  27.7 2.2 %collective-permute-start.8 = (bf16[66,64,128]{2,1,0:T(8,128)(2,1)S(1)}, bf16[66,64,128]{2,1,0:T(8,128)(2,1)S(1)}, u32[]{:S(2)}, u32[]{:S(2)}) collective-permute-start(bf16[66,64,128]{2,1,0:T(8,128)(2,1)S(1)} %constant_dynamic-update-slice_fusion.refs_1_), channel_id=1, source_target_pairs={{0,16},{8,72},{16,32},{24,88},{32,48},{40,104},{48,0},{56,120},{64... | collective-permute-start | bytes 3244040 | tf_op jit(solution)/shard_map/ppermute | solution.py:409
  29.9 1.5 %collective-permute-start.9 = (bf16[66,64,128]{2,1,0:T(8,128)(2,1)S(1)}, bf16[66,64,128]{2,1,0:T(8,128)(2,1)S(1)}, u32[]{:S(2)}, u32[]{:S(2)}) collective-permute-start(bf16[66,64,128]{2,1,0:T(8,128)(2,1)S(1)} %constant_dynamic-update-slice_fusion.refs_1_), channel_id=1, source_target_pairs={{0,48},{8,200},{16,0},{24,216},{32,16},{40,232},{48,32},{56,248},{... | collective-permute-start | bytes 3244040 | tf_op jit(solution)/shard_map/ppermute | solution.py:409
  31.5 5.9 %collective-permute-done.6.refs_2_ = bf16[66,64,128]{2,1,0:T(8,128)(2,1)S(1)} collective-permute-done((bf16[66,64,128]{2,1,0:T(8,128)(2,1)S(1)}, bf16[66,64,128]{2,1,0:T(8,128)(2,1)S(1)}, u32[]{:S(2)}, u32[]{:S(2)}) %collective-permute-start.6) | collective-permute-done | bytes 1081376 | tf_op jit(solution)/shard_map/ppermute | solution.py:409
  37.3 0.4 collective-permute-done.7.refs_4_
  37.7 1.6 %collective-permute-start.10 = (bf16[33,64,128]{2,1,0:T(8,128)(2,1)S(1)}, bf16[33,64,128]{2,1,0:T(8,128)(2,1)S(1)}, u32[]{:S(2)}, u32[]{:S(2)}) collective-permute-start(bf16[33,64,128]{2,1,0:T(8,128)(2,1)S(1)} %slice.23), channel_id=1, source_target_pairs={{0,16},{8,72},{16,32},{24,88},{32,48},{40,104},{48,0},{56,120},{64... | collective-permute-start | bytes 1622024 | tf_op jit(solution)/shard_map/ppermute | solution.py:409
  39.4 1.7 %collective-permute-start.11 = (bf16[33,64,128]{2,1,0:T(8,128)(2,1)S(1)}, bf16[33,64,128]{2,1,0:T(8,128)(2,1)S(1)}, u32[]{:S(2)}, u32[]{:S(2)}) collective-permute-start(bf16[33,64,128]{2,1,0:T(8,128)(2,1)S(1)} %slice.24), channel_id=1, source_target_pairs={{0,48},{8,200},{16,0},{24,216},{32,16},{40,232},{48,32},{56,248},{... | collective-permute-start | bytes 1622024 | tf_op jit(solution)/shard_map/ppermute | solution.py:409
  41.2 7.7 %collective-permute-done.8.refs_3_ = bf16[66,64,128]{2,1,0:T(8,128)(2,1)S(1)} collective-permute-done((bf16[66,64,128]{2,1,0:T(8,128)(2,1)S(1)}, bf16[66,64,128]{2,1,0:T(8,128)(2,1)S(1)}, u32[]{:S(2)}, u32[]{:S(2)}) %collective-permute-start.8) | collective-permute-done | bytes 1081376 | tf_op jit(solution)/shard_map/ppermute | solution.py:409
  48.9 0.4 collective-permute-done.9.refs_5_
  49.3 1.8 %collective-permute-start.12 = (bf16[33,64,128]{2,1,0:T(8,128)(2,1)S(1)}, bf16[33,64,128]{2,1,0:T(8,128)(2,1)S(1)}, u32[]{:S(2)}, u32[]{:S(2)}) collective-permute-start(bf16[33,64,128]{2,1,0:T(8,128)(2,1)S(1)} %slice.25), channel_id=1, source_target_pairs={{0,16},{8,72},{16,32},{24,88},{32,48},{40,104},{48,0},{56,120},{64... | collective-permute-start | bytes 1622024 | tf_op jit(solution)/shard_map/ppermute | solution.py:409
  51.2 1.7 %collective-permute-start.13 = (bf16[33,64,128]{2,1,0:T(8,128)(2,1)S(1)}, bf16[33,64,128]{2,1,0:T(8,128)(2,1)S(1)}, u32[]{:S(2)}, u32[]{:S(2)}) collective-permute-start(bf16[33,64,128]{2,1,0:T(8,128)(2,1)S(1)} %slice.26), channel_id=1, source_target_pairs={{0,48},{8,200},{16,0},{24,216},{32,16},{40,232},{48,32},{56,248},{... | collective-permute-start | bytes 1622024 | tf_op jit(solution)/shard_map/ppermute | solution.py:409
  53.0 1.7 %collective-permute-done.10.refs_6_ = bf16[33,64,128]{2,1,0:T(8,128)(2,1)S(1)} collective-permute-done((bf16[33,64,128]{2,1,0:T(8,128)(2,1)S(1)}, bf16[33,64,128]{2,1,0:T(8,128)(2,1)S(1)}, u32[]{:S(2)}, u32[]{:S(2)}) %collective-permute-start.10) | collective-permute-done | bytes 540704 | tf_op jit(solution)/shard_map/ppermute | solution.py:409
  54.7 0.4 collective-permute-done.11.refs_7_
  55.1 5.4 %collective-permute-done.12.refs_8_ = bf16[33,64,128]{2,1,0:T(8,128)(2,1)S(1)} collective-permute-done((bf16[33,64,128]{2,1,0:T(8,128)(2,1)S(1)}, bf16[33,64,128]{2,1,0:T(8,128)(2,1)S(1)}, u32[]{:S(2)}, u32[]{:S(2)}) %collective-permute-start.12) | collective-permute-done | bytes 540704 | tf_op jit(solution)/shard_map/ppermute | solution.py:409
  60.9 2.1 %pick_other.1 = (bf16[65,64,128]{2,1,0:T(8,128)(2,1)S(1)}, bf16[528,64,128]{2,1,0:T(8,128)(2,1)S(1)}, f32[32,64,128]{2,1,0:T(8,128)S(1)}) custom-call(s32[4]{0:T(128)S(1)} %pad_add_fusion.core_ref.place_ref, s32[4,32]{1,0:T(4,128)S(1)} %collective-permute-done.1.columns_ref, bf16[66,64,128]{2,1,0:T(8,128)(2,1)S(1)} %pad_maximum_fusion.refs_0_, ...), custom_call_target="tpu_custom_call" | custom-call | flops 4194304 | bytes 20971520 | tf_op jit(solution)/shard_map/pick_other/pallas_call | solution.py:433
  63.1 1.4 %parent_scores.1.parent_ref = f32[32,64,128]{2,1,0:T(8,128)S(1)} custom-call(s32[32,64]{1,0:T(8,128)S(1)} %bitcast.22, bf16[32,256,128]{2,1,0:T(8,128)(2,1)S(1)} %copy-done.6, f32[32,128]{1,0:T(8,128)S(1)} %copy-done.3), custom_call_target="tpu_custom_call" | custom-call | flops 268435456 | bytes 3145728 | tf_op jit(solution)/shard_map/parent_scores/pallas_call | solution.py:411
  64.6 1.7 %own_sums.1 = (bf16[64,64,128]{2,1,0:T(8,128)(2,1)S(1)}, f32[16,64,128]{2,1,0:T(8,128)S(1)}, f32[32,64,128]{2,1,0:T(8,128)S(1)}) custom-call(s32[4]{0:T(128)S(1)} %pad_add_fusion.core_ref.place_ref, s32[4,32]{1,0:T(4,128)S(1)} %bitcast.21, s32[32]{0:T(128)S(1)} %copy-done.4, bf16[528,64,128]{2,1,0:T(8,128)(2,1)S(1)} %get-tuple-element.51.pool, ...), custom_call_target="tpu_custom_call" | custom-call | flops 268435456 | bytes 8388608 | tf_op jit(solution)/shard_map/own_sums/pallas_call | solution.py:449
  66.3 2.0 %row_sums.1 = (f32[64,128]{1,0:T(8,128)S(1)}, f32[32,64,128]{2,1,0:T(8,128)S(1)}, f32[16,64,128]{2,1,0:T(8,128)S(1)}) custom-call(s32[4]{0:T(128)S(1)} %pad_add_fusion.core_ref.place_ref, s32[32]{0:T(128)S(1)} %copy-done.4, bf16[65,64,128]{2,1,0:T(8,128)(2,1)S(1)} %collective-permute-done.14.other_ref.refs_4_, bf16[32,4,128,128]{3,2,1,0:T(8,128)(2,1)S(1)} %bitcast.15, ...), custom_call_target="tpu_custom_call" | custom-call | flops 268435456 | bytes 8388608 | tf_op jit(solution)/shard_map/row_sums/pallas_call | solution.py:458
  68.3 0.6 collective-permute-start.15
  68.9 0.9 collective-permute-done.15.refs_1_
  69.9 17.3 %all_to_all.5.stats_ref = f32[16,64,128]{2,1,0:T(8,128)S(1)} all-to-all(f32[16,64,128]{2,1,0:T(8,128)S(1)} %broadcast_in_dim.4), channel_id=1, replica_groups={{0,16,32,48,64,80,96,112,128,144,160,176,192,208,224,240},{8,24,40,56,7..., dimensions={0} | all-to-all | bytes 1048576 | tf_op jit(solution)/shard_map/all_to_all | solution.py:481
  87.2 2.0 %shares.1 = (bf16[16,4,16,128]{3,2,1,0:T(8,128)(2,1)S(1)}, bf16[16,4,16,128]{3,2,1,0:T(8,128)(2,1)S(1)}, bf16[32,64,128]{2,1,0:T(8,128)(2,1)S(1)}, f32[64,128]{1,0:T(8,128)S(1)}) custom-call(s32[4]{0:T(128)S(1)} %pad_add_fusion.core_ref.place_ref, s32[32]{0:T(128)S(1)} %copy-done.4, f32[16,64,128]{2,1,0:T(8,128)S(1)} %all_to_all.5.stats_ref, ...), custom_call_target="tpu_custom_call" | custom-call | flops 67108864 | bytes 12582912 | tf_op jit(solution)/shard_map/shares/pallas_call | solution.py:487
  89.2 2.0 %collective-permute-start.16 = (bf16[16,4,16,128]{3,2,1,0:T(8,128)(2,1)S(1)}, bf16[16,4,16,128]{3,2,1,0:T(8,128)(2,1)S(1)}, u32[]{:S(2)}, u32[]{:S(2)}) collective-permute-start(bf16[16,4,16,128]{3,2,1,0:T(8,128)(2,1)S(1)} %get-tuple-element.67), channel_id=1, source_target_pairs={{0,1},{1,2},{2,3},{3,4},{4,5},{5,6},{6,7},{7,0},{8,9},{9,10},{10,1... | collective-permute-start | bytes 786440 | tf_op jit(solution)/shard_map/ppermute | solution.py:500
  91.3 2.1 %counts.1 = (bf16[32,4,16,128]{3,2,1,0:T(8,128)(2,1)S(1)}, bf16[32,4,16,128]{3,2,1,0:T(8,128)(2,1)S(1)}, bf16[32,4,16,128]{3,2,1,0:T(8,128)(2,1)S(1)}, bf16[32,4...) custom-call(s32[4]{0:T(128)S(1)} %pad_add_fusion.core_ref.place_ref,, ...), custom_call_target="tpu_custom_call" | custom-call | flops 1048576 | bytes 1048576 | tf_op jit(solution)/shard_map/counts/pallas_call | solution.py:503
  93.4 2.4 %collective-permute-done.16.up_in_ref = bf16[16,4,16,128]{3,2,1,0:T(8,128)(2,1)S(1)} collective-permute-done((bf16[16,4,16,128]{3,2,1,0:T(8,128)(2,1)S(1)}, bf16[16,4,16,128]{3,2,1,0:T(8,128)(2,1)S(1)}, u32[]{:S(2)}, u32[]{:S(2)}) %collective-permute-start.16) | collective-permute-done | bytes 262176 | tf_op jit(solution)/shard_map/ppermute | solution.py:500
  95.8 1.8 %collective-permute-done.17.down_in_ref = bf16[16,4,16,128]{3,2,1,0:T(8,128)(2,1)S(1)} collective-permute-done((bf16[16,4,16,128]{3,2,1,0:T(8,128)(2,1)S(1)}, bf16[16,4,16,128]{3,2,1,0:T(8,128)(2,1)S(1)}, u32[]{:S(2)}, u32[]{:S(2)}) %collective-permute-start.17) | collective-permute-done | bytes 262176 | tf_op jit(solution)/shard_map/ppermute | solution.py:500
  97.7 3.2 %collective-permute-start.18 = (bf16[32,4,16,128]{3,2,1,0:T(8,128)(2,1)S(1)}, bf16[32,4,16,128]{3,2,1,0:T(8,128)(2,1)S(1)}, u32[]{:S(2)}, u32[]{:S(2)}) collective-permute-start(bf16[32,4,16,128]{3,2,1,0:T(8,128)(2,1)S(1)} %get-tuple-element.69), channel_id=1, source_target_pairs={{0,1},{1,2},{2,3},{3,4},{4,5},{5,6},{6,7},{7,0},{8,9},{9,10},{10,1... | collective-permute-start | bytes 1572872 | tf_op jit(solution)/shard_map/ppermute | solution.py:500
  100.9 9.0 %collective-permute-done.18.up_in_ref = bf16[32,4,16,128]{3,2,1,0:T(8,128)(2,1)S(1)} collective-permute-done((bf16[32,4,16,128]{3,2,1,0:T(8,128)(2,1)S(1)}, bf16[32,4,16,128]{3,2,1,0:T(8,128)(2,1)S(1)}, u32[]{:S(2)}, u32[]{:S(2)}) %collective-permute-start.18) | collective-permute-done | bytes 524320 | tf_op jit(solution)/shard_map/ppermute | solution.py:500
  109.9 2.8 %collective-permute-done.19.down_in_ref = bf16[32,4,16,128]{3,2,1,0:T(8,128)(2,1)S(1)} collective-permute-done((bf16[32,4,16,128]{3,2,1,0:T(8,128)(2,1)S(1)}, bf16[32,4,16,128]{3,2,1,0:T(8,128)(2,1)S(1)}, u32[]{:S(2)}, u32[]{:S(2)}) %collective-permute-start.19) | collective-permute-done | bytes 524320 | tf_op jit(solution)/shard_map/ppermute | solution.py:500
  112.9 1.8 %collective-permute-start.20 = (bf16[32,4,16,128]{3,2,1,0:T(8,128)(2,1)S(1)}, bf16[32,4,16,128]{3,2,1,0:T(8,128)(2,1)S(1)}, u32[]{:S(2)}, u32[]{:S(2)}) collective-permute-start(bf16[32,4,16,128]{3,2,1,0:T(8,128)(2,1)S(1)} %get-tuple-element.71), channel_id=1, source_target_pairs={{0,1},{1,2},{2,3},{3,4},{4,5},{5,6},{6,7},{7,0},{8,9},{9,10},{10,1... | collective-permute-start | bytes 1572872 | tf_op jit(solution)/shard_map/ppermute | solution.py:500
  115.0 8.4 %collective-permute-done.20.up_in_ref = bf16[32,4,16,128]{3,2,1,0:T(8,128)(2,1)S(1)} collective-permute-done((bf16[32,4,16,128]{3,2,1,0:T(8,128)(2,1)S(1)}, bf16[32,4,16,128]{3,2,1,0:T(8,128)(2,1)S(1)}, u32[]{:S(2)}, u32[]{:S(2)}) %collective-permute-start.20) | collective-permute-done | bytes 524320 | tf_op jit(solution)/shard_map/ppermute | solution.py:500
  123.4 0.9 collective-permute-done.21.down_in_ref
  124.6 1.8 %collective-permute-start.22 = (bf16[32,4,16,128]{3,2,1,0:T(8,128)(2,1)S(1)}, bf16[32,4,16,128]{3,2,1,0:T(8,128)(2,1)S(1)}, u32[]{:S(2)}, u32[]{:S(2)}) collective-permute-start(bf16[32,4,16,128]{3,2,1,0:T(8,128)(2,1)S(1)} %get-tuple-element.73), channel_id=1, source_target_pairs={{0,1},{1,2},{2,3},{3,4},{4,5},{5,6},{6,7},{7,0},{8,9},{9,10},{10,1... | collective-permute-start | bytes 1572872 | tf_op jit(solution)/shard_map/ppermute | solution.py:500
  126.7 0.6 slice_reduce_fusion
  127.3 6.6 %collective-permute-done.22.up_in_ref = bf16[32,4,16,128]{3,2,1,0:T(8,128)(2,1)S(1)} collective-permute-done((bf16[32,4,16,128]{3,2,1,0:T(8,128)(2,1)S(1)}, bf16[32,4,16,128]{3,2,1,0:T(8,128)(2,1)S(1)}, u32[]{:S(2)}, u32[]{:S(2)}) %collective-permute-start.22) | collective-permute-done | bytes 524320 | tf_op jit(solution)/shard_map/ppermute | solution.py:500
  133.9 1.8 %collective-permute-done.23.down_in_ref = bf16[32,4,16,128]{3,2,1,0:T(8,128)(2,1)S(1)} collective-permute-done((bf16[32,4,16,128]{3,2,1,0:T(8,128)(2,1)S(1)}, bf16[32,4,16,128]{3,2,1,0:T(8,128)(2,1)S(1)}, u32[]{:S(2)}, u32[]{:S(2)}) %collective-permute-start.23) | collective-permute-done | bytes 524320 | tf_op jit(solution)/shard_map/ppermute | solution.py:500
  135.8 1.5 %ring_last.1 = bf16[32,4,16,128]{3,2,1,0:T(8,128)(2,1)} custom-call(s32[4]{0:T(128)S(1)} %pad_add_fusion.core_ref.place_ref, bf16[32,4,16,128]{3,2,1,0:T(8,128)(2,1)S(1)} %get-tuple-element.60.own_ref, bf16[32,4,16,128]{3,2,1,0:T(8,128)(2,1)S(1)} %collective-permute-done.22.up_in_ref, bf16[32,4,16,128]{3,2,1,0:T(8,128)(2,1)S(1)} %collective-permute-done.23.down_in_ref), custom_call_target="tpu_custom_call" | custom-call | tf_op jit(solution)/shard_map/ring_last/pallas_call | solution.py:528
  (44 shorter events, 2.8 us)
Async XLA Ops:
  0.6 3.4 %copy-start.5 = (s32[32,1,4]{0,2,1:T(4,128)S(1)}, s32[32,1,4]{0,2,1:T(4,128)}, u32[]{:S(2)}) copy-start(s32[32,1,4]{0,2,1:T(4,128)} %param.14) | copy-start | bytes 1540
  0.6 3.9 %copy-start.1 = (bf16[32,256,128]{2,1,0:T(8,128)(2,1)S(1)}, bf16[32,256,128]{2,1,0:T(8,128)(2,1)}, u32[]{:S(2)}) copy-start(bf16[32,256,128]{2,1,0:T(8,128)(2,1)} %table_ref.4) | copy-start | bytes 6291460
  0.7 3.9 %copy-start.2 = (s32[64,32]{0,1:T(8,128)S(1)}, s32[64,32]{0,1:T(8,128)}, u32[]{:S(2)}) copy-start(s32[64,32]{0,1:T(8,128)} %param.8) | copy-start | bytes 24580
  3.9 1.9 %collective-permute-start = (bf16[17,64,128]{2,1,0:T(8,128)(2,1)}, bf16[17,64,128]{2,1,0:T(8,128)(2,1)S(1)}, u32[]{:S(2)}, u32[]{:S(2)}) collective-permute-start(bf16[17,64,128]{2,1,0:T(8,128)(2,1)} %child_scores.2), channel_id=1, source_target_pairs={{0,8},{8,0},{16,24},{24,16},{32,40},{40,32},{48,56},{56,48},{64,72... | collective-permute-start | bytes 835592 | tf_op jit(solution)/shard_map/ppermute | solution.py:396
  4.0 1.8 %collective-permute-start.1 = (s32[4,32]{1,0:T(4,128)S(1)}, s32[4,32]{1,0:T(4,128)S(1)}, u32[]{:S(2)}, u32[]{:S(2)}) collective-permute-start(s32[4,32]{1,0:T(4,128)S(1)} %bitcast.20), channel_id=1, source_target_pairs={{0,8},{8,0},{16,24},{24,16},{32,40},{40,32},{48,56},{56,48},{64,72... | collective-permute-start | bytes 1544 | tf_op jit(solution)/shard_map/ppermute | solution.py:396
  6.5 10.6 %collective-permute-start.2 = (bf16[33,64,128]{2,1,0:T(8,128)(2,1)S(1)}, bf16[33,64,128]{2,1,0:T(8,128)(2,1)S(1)}, u32[]{:S(2)}, u32[]{:S(2)}) collective-permute-start(bf16[33,64,128]{2,1,0:T(8,128)(2,1)S(1)} %pack.1), channel_id=1, source_target_pairs={{0,64},{8,24},{16,80},{24,40},{32,96},{40,56},{48,112},{56,8},{64,... | collective-permute-start | bytes 1622024 | tf_op jit(solution)/shard_map/ppermute | solution.py:409
  8.0 9.4 %collective-permute-start.3 = (bf16[33,64,128]{2,1,0:T(8,128)(2,1)S(1)}, bf16[33,64,128]{2,1,0:T(8,128)(2,1)S(1)}, u32[]{:S(2)}, u32[]{:S(2)}) collective-permute-start(bf16[33,64,128]{2,1,0:T(8,128)(2,1)S(1)} %pack.1), channel_id=1, source_target_pairs={{0,192},{8,56},{16,208},{24,8},{32,224},{40,24},{48,240},{56,40},{... | collective-permute-start | bytes 1622024 | tf_op jit(solution)/shard_map/ppermute | solution.py:409
  17.4 10.2 %collective-permute-start.4 = (bf16[17,64,128]{2,1,0:T(8,128)(2,1)S(1)}, bf16[17,64,128]{2,1,0:T(8,128)(2,1)S(1)}, u32[]{:S(2)}, u32[]{:S(2)}) collective-permute-start(bf16[17,64,128]{2,1,0:T(8,128)(2,1)S(1)} %slice.21), channel_id=1, source_target_pairs={{0,64},{8,24},{16,80},{24,40},{32,96},{40,56},{48,112},{56,8},{64,... | collective-permute-start | bytes 835592 | tf_op jit(solution)/shard_map/ppermute | solution.py:409
  19.0 8.6 %collective-permute-start.5 = (bf16[16,64,128]{2,1,0:T(8,128)(2,1)S(1)}, bf16[16,64,128]{2,1,0:T(8,128)(2,1)S(1)}, u32[]{:S(2)}, u32[]{:S(2)}) collective-permute-start(bf16[16,64,128]{2,1,0:T(8,128)(2,1)S(1)} %slice.22), channel_id=1, source_target_pairs={{0,192},{8,56},{16,208},{24,8},{32,224},{40,24},{48,240},{56,40},{... | collective-permute-start | bytes 786440 | tf_op jit(solution)/shard_map/ppermute | solution.py:409
  20.9 16.4 %collective-permute-start.6 = (bf16[66,64,128]{2,1,0:T(8,128)(2,1)S(1)}, bf16[66,64,128]{2,1,0:T(8,128)(2,1)S(1)}, u32[]{:S(2)}, u32[]{:S(2)}) collective-permute-start(bf16[66,64,128]{2,1,0:T(8,128)(2,1)S(1)} %pad_maximum_fusion.refs_0_), channel_id=1, source_target_pairs={{0,16},{8,72},{16,32},{24,88},{32,48},{40,104},{48,0},{56,120},{64... | collective-permute-start | bytes 3244040 | tf_op jit(solution)/shard_map/ppermute | solution.py:409
  22.5 15.2 %collective-permute-start.7 = (bf16[66,64,128]{2,1,0:T(8,128)(2,1)S(1)}, bf16[66,64,128]{2,1,0:T(8,128)(2,1)S(1)}, u32[]{:S(2)}, u32[]{:S(2)}) collective-permute-start(bf16[66,64,128]{2,1,0:T(8,128)(2,1)S(1)} %pad_maximum_fusion.refs_0_), channel_id=1, source_target_pairs={{0,48},{8,200},{16,0},{24,216},{32,16},{40,232},{48,32},{56,248},{... | collective-permute-start | bytes 3244040 | tf_op jit(solution)/shard_map/ppermute | solution.py:409
  27.7 21.2 %collective-permute-start.8 = (bf16[66,64,128]{2,1,0:T(8,128)(2,1)S(1)}, bf16[66,64,128]{2,1,0:T(8,128)(2,1)S(1)}, u32[]{:S(2)}, u32[]{:S(2)}) collective-permute-start(bf16[66,64,128]{2,1,0:T(8,128)(2,1)S(1)} %constant_dynamic-update-slice_fusion.refs_1_), channel_id=1, source_target_pairs={{0,16},{8,72},{16,32},{24,88},{32,48},{40,104},{48,0},{56,120},{64... | collective-permute-start | bytes 3244040 | tf_op jit(solution)/shard_map/ppermute | solution.py:409
  29.9 19.3 %collective-permute-start.9 = (bf16[66,64,128]{2,1,0:T(8,128)(2,1)S(1)}, bf16[66,64,128]{2,1,0:T(8,128)(2,1)S(1)}, u32[]{:S(2)}, u32[]{:S(2)}) collective-permute-start(bf16[66,64,128]{2,1,0:T(8,128)(2,1)S(1)} %constant_dynamic-update-slice_fusion.refs_1_), channel_id=1, source_target_pairs={{0,48},{8,200},{16,0},{24,216},{32,16},{40,232},{48,32},{56,248},{... | collective-permute-start | bytes 3244040 | tf_op jit(solution)/shard_map/ppermute | solution.py:409
  37.7 17.0 %collective-permute-start.10 = (bf16[33,64,128]{2,1,0:T(8,128)(2,1)S(1)}, bf16[33,64,128]{2,1,0:T(8,128)(2,1)S(1)}, u32[]{:S(2)}, u32[]{:S(2)}) collective-permute-start(bf16[33,64,128]{2,1,0:T(8,128)(2,1)S(1)} %slice.23), channel_id=1, source_target_pairs={{0,16},{8,72},{16,32},{24,88},{32,48},{40,104},{48,0},{56,120},{64... | collective-permute-start | bytes 1622024 | tf_op jit(solution)/shard_map/ppermute | solution.py:409
  39.4 15.7 %collective-permute-start.11 = (bf16[33,64,128]{2,1,0:T(8,128)(2,1)S(1)}, bf16[33,64,128]{2,1,0:T(8,128)(2,1)S(1)}, u32[]{:S(2)}, u32[]{:S(2)}) collective-permute-start(bf16[33,64,128]{2,1,0:T(8,128)(2,1)S(1)} %slice.24), channel_id=1, source_target_pairs={{0,48},{8,200},{16,0},{24,216},{32,16},{40,232},{48,32},{56,248},{... | collective-permute-start | bytes 1622024 | tf_op jit(solution)/shard_map/ppermute | solution.py:409
  49.3 11.2 %collective-permute-start.12 = (bf16[33,64,128]{2,1,0:T(8,128)(2,1)S(1)}, bf16[33,64,128]{2,1,0:T(8,128)(2,1)S(1)}, u32[]{:S(2)}, u32[]{:S(2)}) collective-permute-start(bf16[33,64,128]{2,1,0:T(8,128)(2,1)S(1)} %slice.25), channel_id=1, source_target_pairs={{0,16},{8,72},{16,32},{24,88},{32,48},{40,104},{48,0},{56,120},{64... | collective-permute-start | bytes 1622024 | tf_op jit(solution)/shard_map/ppermute | solution.py:409
  51.2 11.9 %copy-start.3 = (f32[32,128]{1,0:T(8,128)S(1)}, f32[32,128]{1,0:T(8,128)}, u32[]{:S(2)}) copy-start(f32[32,128]{1,0:T(8,128)} %prior_ref.3) | copy-start | bytes 49156
  51.2 11.9 %copy-start.6 = (bf16[32,256,128]{2,1,0:T(8,128)(2,1)S(1)}, bf16[32,256,128]{2,1,0:T(8,128)(2,1)}, u32[]{:S(2)}) copy-start(bf16[32,256,128]{2,1,0:T(8,128)(2,1)} %table_ref.5) | copy-start | bytes 6291460
  51.2 11.9 %copy-start.7 = (s32[64,32]{0,1:T(8,128)S(1)}, s32[64,32]{0,1:T(8,128)}, u32[]{:S(2)}) copy-start(s32[64,32]{0,1:T(8,128)} %param.9) | copy-start | bytes 24580
  51.2 9.6 %collective-permute-start.13 = (bf16[33,64,128]{2,1,0:T(8,128)(2,1)S(1)}, bf16[33,64,128]{2,1,0:T(8,128)(2,1)S(1)}, u32[]{:S(2)}, u32[]{:S(2)}) collective-permute-start(bf16[33,64,128]{2,1,0:T(8,128)(2,1)S(1)} %slice.26), channel_id=1, source_target_pairs={{0,48},{8,200},{16,0},{24,216},{32,16},{40,232},{48,32},{56,248},{... | collective-permute-start | bytes 1622024 | tf_op jit(solution)/shard_map/ppermute | solution.py:409
  60.9 3.7 %copy-start = (bf16[32,1,4,128,128]{4,3,2,1,0:T(8,128)(2,1)S(1)}, bf16[32,1,4,128,128]{4,3,2,1,0:T(8,128)(2,1)}, u32[]{:S(2)}) copy-start(bf16[32,1,4,128,128]{4,3,2,1,0:T(8,128)(2,1)} %param.13) | copy-start | bytes 12582916
  63.0 3.3 %collective-permute-start.14 = (bf16[65,64,128]{2,1,0:T(8,128)(2,1)S(1)}, bf16[65,64,128]{2,1,0:T(8,128)(2,1)S(1)}, u32[]{:S(2)}, u32[]{:S(2)}) collective-permute-start(bf16[65,64,128]{2,1,0:T(8,128)(2,1)S(1)} %get-tuple-element.50), channel_id=1, source_target_pairs={{0,8},{8,0},{16,24},{24,16},{32,40},{40,32},{48,56},{56,48},{64,72... | collective-permute-start | bytes 3194888 | tf_op jit(solution)/shard_map/ppermute | solution.py:446
  63.1 1.5 %copy-start.4 = (s32[32]{0:T(128)S(1)}, s32[32]{0:T(128)}, u32[]{:S(2)}) copy-start(s32[32]{0:T(128)} %map_ref.5) | copy-start | bytes 388
  68.3 1.4 %collective-permute-start.15 = (f32[64,128]{1,0:T(8,128)S(1)}, f32[64,128]{1,0:T(8,128)S(1)}, u32[]{:S(2)}, u32[]{:S(2)}) collective-permute-start(f32[64,128]{1,0:T(8,128)S(1)} %get-tuple-element.54.refs_0_), channel_id=1, source_target_pairs={{0,8},{8,0},{16,24},{24,16},{32,40},{40,32},{48,56},{56,48},{64,72... | collective-permute-start | bytes 98312 | tf_op jit(solution)/shard_map/ppermute | solution.py:478
  89.2 6.6 %collective-permute-start.16 = (bf16[16,4,16,128]{3,2,1,0:T(8,128)(2,1)S(1)}, bf16[16,4,16,128]{3,2,1,0:T(8,128)(2,1)S(1)}, u32[]{:S(2)}, u32[]{:S(2)}) collective-permute-start(bf16[16,4,16,128]{3,2,1,0:T(8,128)(2,1)S(1)} %get-tuple-element.67), channel_id=1, source_target_pairs={{0,1},{1,2},{2,3},{3,4},{4,5},{5,6},{6,7},{7,0},{8,9},{9,10},{10,1... | collective-permute-start | bytes 786440 | tf_op jit(solution)/shard_map/ppermute | solution.py:500
  91.2 6.4 %collective-permute-start.17 = (bf16[16,4,16,128]{3,2,1,0:T(8,128)(2,1)S(1)}, bf16[16,4,16,128]{3,2,1,0:T(8,128)(2,1)S(1)}, u32[]{:S(2)}, u32[]{:S(2)}) collective-permute-start(bf16[16,4,16,128]{3,2,1,0:T(8,128)(2,1)S(1)} %get-tuple-element.68), channel_id=1, source_target_pairs={{0,7},{1,0},{2,1},{3,2},{4,3},{5,4},{6,5},{7,6},{8,15},{9,8},{10,9... | collective-permute-start | bytes 786440 | tf_op jit(solution)/shard_map/ppermute | solution.py:500
  97.7 12.2 %collective-permute-start.18 = (bf16[32,4,16,128]{3,2,1,0:T(8,128)(2,1)S(1)}, bf16[32,4,16,128]{3,2,1,0:T(8,128)(2,1)S(1)}, u32[]{:S(2)}, u32[]{:S(2)}) collective-permute-start(bf16[32,4,16,128]{3,2,1,0:T(8,128)(2,1)S(1)} %get-tuple-element.69), channel_id=1, source_target_pairs={{0,1},{1,2},{2,3},{3,4},{4,5},{5,6},{6,7},{7,0},{8,9},{9,10},{10,1... | collective-permute-start | bytes 1572872 | tf_op jit(solution)/shard_map/ppermute | solution.py:500
  100.9 11.8 %collective-permute-start.19 = (bf16[32,4,16,128]{3,2,1,0:T(8,128)(2,1)S(1)}, bf16[32,4,16,128]{3,2,1,0:T(8,128)(2,1)S(1)}, u32[]{:S(2)}, u32[]{:S(2)}) collective-permute-start(bf16[32,4,16,128]{3,2,1,0:T(8,128)(2,1)S(1)} %get-tuple-element.70), channel_id=1, source_target_pairs={{0,7},{1,0},{2,1},{3,2},{4,3},{5,4},{6,5},{7,6},{8,15},{9,8},{10,9... | collective-permute-start | bytes 1572872 | tf_op jit(solution)/shard_map/ppermute | solution.py:500
  112.9 10.5 %collective-permute-start.20 = (bf16[32,4,16,128]{3,2,1,0:T(8,128)(2,1)S(1)}, bf16[32,4,16,128]{3,2,1,0:T(8,128)(2,1)S(1)}, u32[]{:S(2)}, u32[]{:S(2)}) collective-permute-start(bf16[32,4,16,128]{3,2,1,0:T(8,128)(2,1)S(1)} %get-tuple-element.71), channel_id=1, source_target_pairs={{0,1},{1,2},{2,3},{3,4},{4,5},{5,6},{6,7},{7,0},{8,9},{9,10},{10,1... | collective-permute-start | bytes 1572872 | tf_op jit(solution)/shard_map/ppermute | solution.py:500
  114.7 9.6 %collective-permute-start.21 = (bf16[32,4,16,128]{3,2,1,0:T(8,128)(2,1)S(1)}, bf16[32,4,16,128]{3,2,1,0:T(8,128)(2,1)S(1)}, u32[]{:S(2)}, u32[]{:S(2)}) collective-permute-start(bf16[32,4,16,128]{3,2,1,0:T(8,128)(2,1)S(1)} %get-tuple-element.72), channel_id=1, source_target_pairs={{0,7},{1,0},{2,1},{3,2},{4,3},{5,4},{6,5},{7,6},{8,15},{9,8},{10,9... | collective-permute-start | bytes 1572872 | tf_op jit(solution)/shard_map/ppermute | solution.py:500
  124.6 9.3 %collective-permute-start.22 = (bf16[32,4,16,128]{3,2,1,0:T(8,128)(2,1)S(1)}, bf16[32,4,16,128]{3,2,1,0:T(8,128)(2,1)S(1)}, u32[]{:S(2)}, u32[]{:S(2)}) collective-permute-start(bf16[32,4,16,128]{3,2,1,0:T(8,128)(2,1)S(1)} %get-tuple-element.73), channel_id=1, source_target_pairs={{0,1},{1,2},{2,3},{3,4},{4,5},{5,6},{6,7},{7,0},{8,9},{9,10},{10,1... | collective-permute-start | bytes 1572872 | tf_op jit(solution)/shard_map/ppermute | solution.py:500
  126.4 9.4 %collective-permute-start.23 = (bf16[32,4,16,128]{3,2,1,0:T(8,128)(2,1)S(1)}, bf16[32,4,16,128]{3,2,1,0:T(8,128)(2,1)S(1)}, u32[]{:S(2)}, u32[]{:S(2)}) collective-permute-start(bf16[32,4,16,128]{3,2,1,0:T(8,128)(2,1)S(1)} %get-tuple-element.74), channel_id=1, source_target_pairs={{0,7},{1,0},{2,1},{3,2},{4,3},{5,4},{6,5},{7,6},{8,15},{9,8},{10,9... | collective-permute-start | bytes 1572872 | tf_op jit(solution)/shard_map/ppermute | solution.py:500
